TPU v7x, 32 devices: a whole 2x2x4 slice. The times are simulated.
32 devices in a mesh: wide: 8 (over z, y), narrow: 4 (over x, core).
Axes of the slice: x: 2, y: 2, z: 4, core: 2. Of those that a mesh axis runs over, the one named last changes fastest.
Arguments:
- layer_input: bfloat16 [8, 2048, 1024], P(None, ('wide', 'narrow')), may hold values from -6 to 6
- query_weight: bfloat16 [1024, 1024], P('wide', 'narrow'), may hold values from -0.1875 to 0.1875
- key_weight: bfloat16 [1024, 1024], P('wide', 'narrow'), may hold values from -0.1875 to 0.1875
- value_weight: bfloat16 [1024, 1024], P('wide', 'narrow'), may hold values from -0.1875 to 0.1875
- modulate_weight: bfloat16 [1024, 1024], P('wide', 'narrow'), may hold values from -0.1875 to 0.1875
- output_weight: bfloat16 [1024, 1024], P('wide', 'narrow'), may hold values from -0.1875 to 0.1875
- gate_matrix: bfloat16 [1024, 2816], P(None, ('wide', 'narrow')), may hold values from -0.1875 to 0.1875
- lift_matrix: bfloat16 [1024, 2816], P(None, ('wide', 'narrow')), may hold values from -0.1875 to 0.1875
- down_matrix: bfloat16 [1024, 2816], P(None, ('wide', 'narrow')), may hold values from -0.109375 to 0.109375
- decay_factor: float32 [8], P('narrow'), may hold values from 0.96 to 1, as said below
- valid_lengths: int32 [8], replicated, may hold values from 512 to 2048, as said below
- output_cotangent: bfloat16 [8, 2048, 1024], P(None, ('wide', 'narrow')), may hold values from -6 to 6
Outputs:
- layer_output: bfloat16 [8, 2048, 1024], P(None, ('wide', 'narrow'))
- input_gradient: float32 [8, 2048, 1024], P(None, ('wide', 'narrow'))
- query_gradient: float32 [1024, 1024], P('wide', 'narrow')
- key_gradient: float32 [1024, 1024], P('wide', 'narrow')
- value_gradient: float32 [1024, 1024], P('wide', 'narrow')
- modulate_gradient: float32 [1024, 1024], P('wide', 'narrow')
- output_gradient: float32 [1024, 1024], P('wide', 'narrow')
- gate_gradient: float32 [1024, 2816], P(None, ('wide', 'narrow'))
- lift_gradient: float32 [1024, 2816], P(None, ('wide', 'narrow'))
- down_gradient: float32 [1024, 2816], P(None, ('wide', 'narrow'))
Inputs may be any that keep to these rules, and one draw needn't show every extreme that they name: `decay_factor`: decay per position of each head, below one. `valid_lengths`: valid positions of each slot; in every draw one slot, drawn from the seed, is full (2048 positions).
All inputs are finite; a program needn't handle non-finite values.
Results may differ from a plain program's by a relative error of at most 0.014.
Values may be sent and summed in bfloat16 or wider, within the bound.
No kernel may reach another device: no remote copies, remote signals or barrier semaphores. Data moves between devices by JAX's collectives and lax.ppermute only.
A program may use at most 256 MiB of HBM per device.

v0:
```python
import math

import jax
import jax.numpy as jnp
from jax import lax
from jax.sharding import PartitionSpec as P

EPS = 1e-06
HIGH = lax.Precision.HIGHEST


def carried_in(x, axis, combine, identity, reverse):
    size, mine = (lax.axis_size(axis), lax.axis_index(axis))
    everything = jax.tree.map(lambda part: lax.all_gather(part, axis), x)
    start = jax.tree.map(
        lambda part, zero: jnp.broadcast_to(jnp.asarray(zero, part.dtype), part.shape), x, identity
    )

    def step(k, before):
        at = size - 1 - k if reverse else k
        reached = at > mine if reverse else at < mine
        new = combine(before, jax.tree.map(lambda part: part[at], everything))
        return jax.tree.map(lambda a, b: jnp.where(reached, a, b), new, before)

    return lax.fori_loop(0, size, step, start)


def cut_along(x, dim, size):
    before, after = (x.shape[:dim], x.shape[dim + 1 :])
    return jnp.moveaxis(x.reshape(*before, size, -1, *after), dim, 0)


def summed_on_arrival(x, axis, dim):
    size = lax.axis_size(axis)
    blocks = lax.all_to_all(cut_along(x, dim, size), axis, 0, 0, tiled=True)
    return jnp.sum(blocks.astype(jnp.float32), axis=0)


def in_one_piece(arrays, axis, dim, along):
    ends, at = ([], 0)
    for a in arrays[:-1]:
        at += a.shape[along]
        ends.append(at)
    both = jnp.concatenate(arrays, axis=along)
    return tuple(jnp.split(summed_on_arrival(both, axis, dim), ends, axis=along))


def simple_norm(values):
    return values * lax.rsqrt(jnp.mean(values * values, axis=-1, keepdims=True) + EPS)


def norm_backward(values, cotangent):
    return jax.vjp(simple_norm, values)[1](cotangent)[0]


def apply_swish(values):
    return values * jax.nn.sigmoid(values)


def swish_slope(values):
    sigmoid_value = jax.nn.sigmoid(values)
    return sigmoid_value + values * sigmoid_value * (1.0 - sigmoid_value)


def rotation_tables(positions, head_size):
    half_width = head_size // 2
    frequency = jnp.exp(-math.log(10000.0) * jnp.arange(half_width, dtype=jnp.float32) / half_width)
    phase_angle = positions.astype(jnp.float32)[:, None] * frequency[None, :]
    return (jnp.cos(phase_angle)[:, None, :], jnp.sin(phase_angle)[:, None, :])


def rotate(values, cosine_table, sine_table):
    half_width = values.shape[-1] // 2
    first_half = values[..., :half_width]
    second_half = values[..., half_width:]
    return jnp.concatenate(
        [
            first_half * cosine_table - second_half * sine_table,
            first_half * sine_table + second_half * cosine_table,
        ],
        axis=-1,
    )


def decay_tables(log_decay, block_length):
    position_index = jnp.arange(block_length, dtype=jnp.float32)
    position_gap = position_index[:, None] - position_index[None, :]
    decay_grid = jnp.where(
        position_gap[None] >= 0.0,
        jnp.exp(jnp.maximum(position_gap, 0.0)[None] * log_decay[:, None, None]),
        0.0,
    )
    query_decay = jnp.exp((position_index[:, None] + 1.0) * log_decay[None, :])
    key_decay = jnp.exp((block_length - 1.0 - position_index[:, None]) * log_decay[None, :])
    block_decay = jnp.exp(block_length * log_decay)
    return (decay_grid, query_decay, key_decay, block_decay)


def combine_states(earlier, later):
    return (earlier[0] * later[0], later[0][..., None, None] * earlier[1] + later[1])


def block_gather(values):
    return lax.all_gather(values, "narrow", axis=1, tiled=True)


def quarter_total(values):
    return lax.psum_scatter(values, "narrow", scatter_dimension=1, tiled=True)


def hidden_total(values):
    return lax.psum_scatter(values, "narrow", scatter_dimension=1, tiled=True)


def glu_pass(normed_rows, grad_rows, gate_cols, lift_cols, down_cols):
    gate_pre = jnp.einsum("brd,df->brf", normed_rows, gate_cols, preferred_element_type=jnp.float32)
    lift_pre = jnp.einsum("brd,df->brf", normed_rows, lift_cols, preferred_element_type=jnp.float32)
    gate_act = apply_swish(gate_pre)
    inner_act = (gate_act * lift_pre).astype(jnp.bfloat16)
    branch = jnp.einsum("brf,df->brd", inner_act, down_cols, preferred_element_type=jnp.float32)
    inner_grad = jnp.einsum("brd,df->brf", grad_rows, down_cols, preferred_element_type=jnp.float32)
    down_grad = jnp.einsum("brd,brf->df", grad_rows, inner_act, preferred_element_type=jnp.float32)
    gate_pre_grad = (inner_grad * lift_pre * swish_slope(gate_pre)).astype(jnp.bfloat16)
    lift_pre_grad = (inner_grad * gate_act).astype(jnp.bfloat16)
    gate_grad = jnp.einsum(
        "brd,brf->df", normed_rows, gate_pre_grad, preferred_element_type=jnp.float32
    )
    lift_grad = jnp.einsum(
        "brd,brf->df", normed_rows, lift_pre_grad, preferred_element_type=jnp.float32
    )
    normed_grad = jnp.einsum(
        "brf,df->brd", gate_pre_grad, gate_cols, preferred_element_type=jnp.float32
    ) + jnp.einsum("brf,df->brd", lift_pre_grad, lift_cols, preferred_element_type=jnp.float32)
    return (branch, normed_grad, gate_grad, lift_grad, down_grad)


def on_device(
    layer_input,
    query_weight,
    key_weight,
    value_weight,
    modulate_weight,
    output_weight,
    gate_matrix,
    lift_matrix,
    down_matrix,
    decay_factor,
    valid_lengths,
    output_cotangent,
):
    narrow_count = lax.axis_size("narrow")
    wide_index = lax.axis_index("wide")
    narrow_index = lax.axis_index("narrow")
    batch_size, quarter, model_width = layer_input.shape
    block_length = quarter * narrow_count
    head_local = decay_factor.shape[0]
    local_width = query_weight.shape[1]
    head_size = local_width // head_local
    block_start = wide_index * block_length
    block_positions = block_start + jnp.arange(block_length, dtype=jnp.int32)
    quarter_positions = block_start + narrow_index * quarter + jnp.arange(quarter, dtype=jnp.int32)
    block_mask = (block_positions[None, :] < valid_lengths[:, None]).astype(jnp.float32)
    quarter_mask = (quarter_positions[None, :] < valid_lengths[:, None]).astype(jnp.float32)
    mask_heads = block_mask[:, :, None, None]
    quarter_weight = quarter_mask[:, :, None]
    gathered_input = block_gather(layer_input)
    full_query, full_key, full_value, full_modulate, full_output = (
        lax.all_gather(query_weight, "wide", axis=0, tiled=True),
        lax.all_gather(key_weight, "wide", axis=0, tiled=True),
        lax.all_gather(value_weight, "wide", axis=0, tiled=True),
        lax.all_gather(modulate_weight, "wide", axis=0, tiled=True),
        lax.all_gather(output_weight, "wide", axis=0, tiled=True),
    )
    normed = simple_norm(gathered_input.astype(jnp.float32)).astype(jnp.bfloat16)
    flat_normed = normed.reshape(batch_size * block_length, model_width)

    def project(matrix):
        return jnp.dot(flat_normed, matrix, preferred_element_type=jnp.float32).reshape(
            batch_size, block_length, head_local, head_size
        )

    query_pre = project(full_query)
    key_pre = project(full_key)
    value_pre = project(full_value)
    modulate_pre = project(full_modulate)
    cosine_table, sine_table = rotation_tables(block_positions, head_size)
    queries = rotate(apply_swish(query_pre), cosine_table, sine_table).astype(jnp.bfloat16)
    key_rows = (mask_heads * rotate(apply_swish(key_pre), cosine_table, sine_table)).astype(
        jnp.bfloat16
    )
    value_rows = (mask_heads * value_pre).astype(jnp.bfloat16)
    log_decay = jnp.log(decay_factor)
    decay_grid, query_decay, key_decay, block_decay = decay_tables(log_decay, block_length)
    scores = (
        jnp.einsum("bihd,bjhd->bhij", queries, key_rows, preferred_element_type=jnp.float32)
        * decay_grid[None]
    ).astype(jnp.bfloat16)
    intra_part = jnp.einsum(
        "bhij,bjhd->bihd", scores, value_rows, preferred_element_type=jnp.float32
    )
    key_scaled = key_rows.astype(jnp.float32) * key_decay[None, :, :, None]
    value_float = value_rows.astype(jnp.float32)
    local_state = jnp.einsum("bjhd,bjhe->bhde", key_scaled, value_float, precision=HIGH)
    decay_pairs = jnp.broadcast_to(block_decay[None, :], (batch_size, head_local))
    unit_pairs = jnp.ones_like(decay_pairs)
    zero_state = jnp.zeros_like(local_state)
    state_in = carried_in(
        (decay_pairs, local_state), "wide", combine_states, (unit_pairs, zero_state), False
    )[1]
    query_scaled = queries.astype(jnp.float32) * query_decay[None, :, :, None]
    inter_part = jnp.einsum("bihd,bhde->bihe", query_scaled, state_in, precision=HIGH)
    mixed_heads = intra_part + inter_part
    normed_heads = simple_norm(mixed_heads)
    modulate_masked = modulate_pre * mask_heads
    gated_heads = (
        (normed_heads * modulate_masked)
        .astype(jnp.bfloat16)
        .reshape(batch_size, block_length, local_width)
    )
    partial_out = jnp.einsum(
        "ble,oe->blo", gated_heads, full_output, preferred_element_type=jnp.float32
    )
    attended = quarter_total(partial_out)
    middle = layer_input.astype(jnp.float32) + attended
    normed_two = simple_norm(middle).astype(jnp.bfloat16)
    cotangent = output_cotangent.astype(jnp.float32)
    branch_grad = (quarter_weight * cotangent).astype(jnp.bfloat16)
    part_gate, part_lift, part_down = (
        lax.all_gather(gate_matrix, "wide", axis=1, tiled=True),
        lax.all_gather(lift_matrix, "wide", axis=1, tiled=True),
        lax.all_gather(down_matrix, "wide", axis=1, tiled=True),
    )
    rows_normed, rows_grad = (
        lax.all_gather(normed_two, "narrow", axis=1, tiled=True),
        lax.all_gather(branch_grad, "narrow", axis=1, tiled=True),
    )
    branch_part, normed_part, gate_grad, lift_grad, down_grad = glu_pass(
        rows_normed, rows_grad, part_gate, part_lift, part_down
    )
    branch = hidden_total(branch_part)
    normed_two_grad = hidden_total(normed_part)
    gate_gradient, lift_gradient, down_gradient = (
        lax.psum_scatter(gate_grad, "wide", scatter_dimension=1, tiled=True),
        lax.psum_scatter(lift_grad, "wide", scatter_dimension=1, tiled=True),
        lax.psum_scatter(down_grad, "wide", scatter_dimension=1, tiled=True),
    )
    layer_output = (middle + quarter_weight * branch).astype(jnp.bfloat16)
    middle_grad = cotangent + norm_backward(middle, normed_two_grad)
    attended_grad = block_gather(middle_grad.astype(jnp.bfloat16))
    gated_grad = jnp.einsum(
        "blo,oe->ble", attended_grad, full_output, preferred_element_type=jnp.float32
    ).reshape(batch_size, block_length, head_local, head_size)
    output_grad = jnp.einsum(
        "blo,ble->oe", attended_grad, gated_heads, preferred_element_type=jnp.float32
    )
    modulate_grad = (gated_grad * mask_heads * normed_heads).astype(jnp.bfloat16)
    mixed_grad = norm_backward(mixed_heads, gated_grad * modulate_masked).astype(jnp.bfloat16)
    score_grad = (
        jnp.einsum("bihe,bjhe->bhij", mixed_grad, value_rows, preferred_element_type=jnp.float32)
        * decay_grid[None]
    ).astype(jnp.bfloat16)
    value_grad = jnp.einsum(
        "bhij,bihe->bjhe", scores, mixed_grad, preferred_element_type=jnp.float32
    )
    query_grad = jnp.einsum(
        "bhij,bjhd->bihd", score_grad, key_rows, preferred_element_type=jnp.float32
    )
    key_grad = jnp.einsum(
        "bhij,bihd->bjhd", score_grad, queries, preferred_element_type=jnp.float32
    )
    mixed_float = mixed_grad.astype(jnp.float32)
    query_grad = (
        query_grad
        + jnp.einsum("bihe,bhde->bihd", mixed_float, state_in, precision=HIGH)
        * query_decay[None, :, :, None]
    )
    state_grad = jnp.einsum("bihd,bihe->bhde", query_scaled, mixed_float, precision=HIGH)
    later_grad = carried_in(
        (decay_pairs, state_grad), "wide", combine_states, (unit_pairs, zero_state), True
    )[1]
    key_grad = (
        key_grad
        + jnp.einsum("bjhe,bhde->bjhd", value_float, later_grad, precision=HIGH)
        * key_decay[None, :, :, None]
    )
    value_grad = value_grad + jnp.einsum("bjhd,bhde->bjhe", key_scaled, later_grad, precision=HIGH)
    query_pre_grad = (
        rotate(query_grad, cosine_table, -sine_table) * swish_slope(query_pre)
    ).astype(jnp.bfloat16)
    key_pre_grad = (
        rotate(key_grad * mask_heads, cosine_table, -sine_table) * swish_slope(key_pre)
    ).astype(jnp.bfloat16)
    value_pre_grad = (value_grad * mask_heads).astype(jnp.bfloat16)
    flat_count = batch_size * block_length
    pre_grads = [
        grad_heads.reshape(flat_count, local_width)
        for grad_heads in (query_pre_grad, key_pre_grad, value_pre_grad, modulate_grad)
    ]
    matrices = (full_query, full_key, full_value, full_modulate)
    normed_grad = jnp.einsum(
        "ne,de->nd", pre_grads[0], matrices[0], preferred_element_type=jnp.float32
    )
    for position_rank in range(1, 4):
        normed_grad = normed_grad + jnp.einsum(
            "ne,de->nd",
            pre_grads[position_rank],
            matrices[position_rank],
            preferred_element_type=jnp.float32,
        )
    row_grad = quarter_total(normed_grad.reshape(batch_size, block_length, model_width))
    input_gradient = middle_grad + norm_backward(layer_input.astype(jnp.float32), row_grad)
    weight_terms = [
        jnp.einsum("nd,ne->de", flat_normed, grad_flat, preferred_element_type=jnp.float32)
        for grad_flat in pre_grads
    ]
    query_gradient, key_gradient, value_gradient, modulate_gradient, output_gradient = in_one_piece(
        (
            weight_terms[0].astype(jnp.bfloat16),
            weight_terms[1].astype(jnp.bfloat16),
            weight_terms[2].astype(jnp.bfloat16),
            weight_terms[3].astype(jnp.bfloat16),
            output_grad.astype(jnp.bfloat16),
        ),
        "wide",
        0,
        1,
    )
    return (
        layer_output,
        input_gradient,
        query_gradient,
        key_gradient,
        value_gradient,
        modulate_gradient,
        output_gradient,
        gate_gradient,
        lift_gradient,
        down_gradient,
    )


def solution(mesh):
    placed = (
        P(None, ("wide", "narrow"), None),
        P("wide", "narrow"),
        P("wide", "narrow"),
        P("wide", "narrow"),
        P("wide", "narrow"),
        P("wide", "narrow"),
        P(None, ("wide", "narrow")),
        P(None, ("wide", "narrow")),
        P(None, ("wide", "narrow")),
        P("narrow"),
        P(),
        P(None, ("wide", "narrow"), None),
    )
    return jax.shard_map(
        on_device,
        mesh=mesh,
        in_specs=placed,
        out_specs=(
            P(None, ("wide", "narrow"), None),
            P(None, ("wide", "narrow"), None),
            P("wide", "narrow"),
            P("wide", "narrow"),
            P("wide", "narrow"),
            P("wide", "narrow"),
            P("wide", "narrow"),
            P(None, ("wide", "narrow")),
            P(None, ("wide", "narrow")),
            P(None, ("wide", "narrow")),
        ),
        check_vma=False,
    )
```

profile of v0, /device:TPU:0, one launch (start us, length us, event | category | flops | bytes accessed | tf_op | source)
XLA Modules:
  0.0 1291.3 jit_solution(3669256976879687703)
XLA Ops:
  8.0 33.2 %all_gather.53 = bf16[1024,256]{1,0:T(8,128)(2,1)S(1)} all-gather(bf16[128,256]{1,0:T(8,128)(2,1)} %param.19), channel_id=1, replica_groups=mesh['wide'=8,'narrow'=4] {'wide'}, dimensions={0}, use_global_device_ids=true | all-gather | bytes 589824 | tf_op jit(solution)/shard_map/all_gather | solution.py:170
  42.2 31.6 %all_gather.55 = bf16[1024,256]{1,0:T(8,128)(2,1)S(1)} all-gather(bf16[128,256]{1,0:T(8,128)(2,1)S(1)} %copy-done.57), channel_id=1, replica_groups=mesh['wide'=8,'narrow'=4] {'wide'}, dimensions={0}, use_global_device_ids=true | all-gather | bytes 589824 | tf_op jit(solution)/shard_map/all_gather | solution.py:169
  74.8 31.2 %all_gather.54 = bf16[1024,256]{1,0:T(8,128)(2,1)S(1)} all-gather(bf16[128,256]{1,0:T(8,128)(2,1)S(1)} %copy-done.58), channel_id=1, replica_groups=mesh['wide'=8,'narrow'=4] {'wide'}, dimensions={0}, use_global_device_ids=true | all-gather | bytes 589824 | tf_op jit(solution)/shard_map/all_gather | solution.py:168
  126.9 22.1 %all-reduce = f32[16]{0:T(128)S(1)} all-reduce(f32[16]{0:T(128)S(1)} %copy-done.75), channel_id=3, replica_groups=mesh['wide'=8,'narrow'=4] {'wide'}, use_global_device_ids=true, to_apply=%add | all-reduce | flops 16 | bytes 128
  149.1 33.0 %all_gather.59 = bf16[1024,256]{1,0:T(8,128)(2,1)S(1)} all-gather(bf16[128,256]{1,0:T(8,128)(2,1)S(1)} %copy-done.59), channel_id=1, replica_groups=mesh['wide'=8,'narrow'=4] {'wide'}, dimensions={0}, use_global_device_ids=true | all-gather | bytes 589824 | tf_op jit(solution)/shard_map/all_gather | solution.py:171
  183.2 35.7 %all_gather.60 = bf16[1024,256]{1,0:T(8,128)(2,1)} all-gather(bf16[128,256]{1,0:T(8,128)(2,1)S(1)} %copy-done.60), channel_id=1, replica_groups=mesh['wide'=8,'narrow'=4] {'wide'}, dimensions={0}, use_global_device_ids=true | all-gather | bytes 589824 | tf_op jit(solution)/shard_map/all_gather | solution.py:172
  225.4 37.6 %all-gather.27.cloned.1.call-done = f32[64,2,128,128]{3,2,1,0:T(8,128)} async-done(((f32[8,2,128,128]{3,2,1,0:T(8,128)}), f32[64,2,128,128]{3,2,1,0:T(8,128)}) %all-gather.27.cloned.1.call-update) | async-done | bytes 8388624 | tf_op jit(solution)/shard_map/all_gather | solution.py:14
  263.1 12.6 while.30
  289.5 70.1 %reduce-scatter.8.cloned.1.call-done = f32[8,64,1024]{2,1,0:T(8,128)} async-done(((f32[8,256,1024]{2,1,0:T(8,128)}), f32[8,64,1024]{2,1,0:T(8,128)}) %reduce-scatter.8.cloned.1.call-update) | async-done | bytes 2097168 | tf_op jit(solution)/shard_map/reduce_scatter | solution.py:108
  367.2 37.9 %all-gather.19.cloned.1.call-done = bf16[1024,704]{0,1:T(8,128)(2,1)} async-done(((bf16[1024,88]{0,1:T(8,128)(2,1)}), bf16[1024,704]{0,1:T(8,128)(2,1)}) %all-gather.19.cloned.1.call-update) | async-done | bytes 1441808 | tf_op jit(solution)/shard_map/all_gather | solution.py:230
  405.0 34.9 %all-gather.15.cloned.1.call-done = bf16[8,256,1024]{2,1,0:T(8,128)(2,1)} async-done(((bf16[8,64,1024]{2,1,0:T(8,128)(2,1)}), bf16[8,256,1024]{2,1,0:T(8,128)(2,1)}) %all-gather.15.cloned.1.call-update) | async-done | bytes 4194320 | tf_op jit(solution)/shard_map/all_gather | solution.py:234
  448.2 37.1 %all-gather.17.cloned.1.call-done = bf16[1024,704]{0,1:T(8,128)(2,1)} async-done(((bf16[1024,88]{0,1:T(8,128)(2,1)}), bf16[1024,704]{0,1:T(8,128)(2,1)}) %all-gather.17.cloned.1.call-update) | async-done | bytes 1441808 | tf_op jit(solution)/shard_map/all_gather | solution.py:229
  493.6 35.6 %all-gather.21.cloned.1.call-done = bf16[1024,704]{0,1:T(8,128)(2,1)} async-done(((bf16[1024,88]{0,1:T(8,128)(2,1)}), bf16[1024,704]{0,1:T(8,128)(2,1)}) %all-gather.21.cloned.1.call-update) | async-done | bytes 1441808 | tf_op jit(solution)/shard_map/all_gather | solution.py:231
  529.1 34.5 %all-gather.23.cloned.1.call-done = bf16[8,256,1024]{2,1,0:T(8,128)(2,1)} async-done(((bf16[8,64,1024]{2,1,0:T(8,128)(2,1)}), bf16[8,256,1024]{2,1,0:T(8,128)(2,1)}) %all-gather.23.cloned.1.call-update) | async-done | bytes 4194320 | tf_op jit(solution)/shard_map/all_gather | solution.py:235
  563.6 20.1 %multiply_convert_fusion = (bf16[8,256,704]{1,2,0:T(8,128)(2,1)S(1)}, bf16[8,256,704]{1,2,0:T(8,128)(2,1)S(1)}, bf16[8,256,704]{1,2,0:T(8,128)(2,1)}) fusion(f32[8,256,704]{1,2,0:T(8,128)} %fusion.44, f32[8,256,704]{1,2,0:T(8,128)} %fusion.40, bf16[8,256,1024]{2,1,0:T(8,128)(2,1)} %all-gather.23.cloned.1.call-done, ...), kind=kOutput, calls=%fused_computation.11 | convolution fusion | flops 2972975104 | bytes 25821184 | tf_op jit(solution)/shard_map/brd,df->brf/dot_general | solution.py:121
  593.1 71.8 %reduce-scatter.12.cloned.1.call-done = f32[8,64,1024]{2,1,0:T(8,128)} async-done(((f32[8,256,1024]{2,1,0:T(8,128)}), f32[8,64,1024]{2,1,0:T(8,128)}) %reduce-scatter.12.cloned.1.call-update) | async-done | bytes 2097168 | tf_op jit(solution)/shard_map/reduce_scatter | solution.py:112
  669.5 34.6 %all-gather.25.cloned.1.call-done = bf16[8,256,1024]{2,1,0:T(8,128)(2,1)} async-done(((bf16[8,64,1024]{2,1,0:T(8,128)(2,1)}), bf16[8,256,1024]{2,1,0:T(8,128)(2,1)}) %all-gather.25.cloned.1.call-update) | async-done | bytes 4194320 | tf_op jit(solution)/shard_map/all_gather | solution.py:104
  735.7 112.7 %all-gather.29.cloned.1.call-done = f32[64,2,128,128]{3,2,1,0:T(8,128)} async-done(((f32[8,2,128,128]{3,2,1,0:T(8,128)}), f32[64,2,128,128]{3,2,1,0:T(8,128)}) %all-gather.29.cloned.1.call-update) | async-done | bytes 8388624 | tf_op jit(solution)/shard_map/all_gather | solution.py:14
  848.4 22.0 %while.31 = (s32[]{:T(128)}, f32[8,2,128,128]{3,2,1,0:T(8,128)}, s32[]{:T(128)}, f32[8,8,2]{1,2,0:T(2,128)S(1)}, f32[8,8,2,128,128]{4,3,2,1,0:T(8,128)}, /*index=5*/s32[]{:T(128)}, s32[]{:T(128)}, s32[]{:T(128)}, s32[]{:T(128)}) while((s32[]{:T(128)}, f32[8,2,128,128]{3,2,1,0:T(8,128)}, s32[]{:T(128)}, ...), condition=%wide.region_11.12_spmd.clone, body=%wide.region_10.11_spmd.clone.sunk | while | flops 1048584 | bytes 3146223 | solution.py:25
  968.1 50.8 %all-to-all-done = bf16[8,128,1280]{1,2,0:T(8,128)(2,1)} async-done(((bf16[8,128,1280]{1,2,0:T(8,128)(2,1)}), bf16[8,128,1280]{1,2,0:T(8,128)(2,1)}, u32[]{:S(2)}, u32[]{:S(2)}) %all-to-all-start) | async-done | bytes 2621472 | tf_op jit(solution)/shard_map/all_to_all | solution.py:35
  1029.6 29.5 %reduce-scatter.10.cloned.1.call-done = f32[8,64,1024]{2,1,0:T(8,128)} async-done(((f32[8,256,1024]{2,1,0:T(8,128)}), f32[8,64,1024]{2,1,0:T(8,128)}) %reduce-scatter.10.cloned.1.call-update) | async-done | bytes 2097168 | tf_op jit(solution)/shard_map/reduce_scatter | solution.py:112
  1063.9 70.9 %reduce-scatter.20.cloned.1.call-done = f32[1024,88]{0,1:T(8,128)} async-done(((f32[1024,704]{0,1:T(8,128)}), f32[1024,88]{0,1:T(8,128)}) %reduce-scatter.20.cloned.1.call-update) | async-done | bytes 360464 | tf_op jit(solution)/shard_map/reduce_scatter | solution.py:245
  1134.8 74.9 %reduce-scatter.16.cloned.1.call-done = f32[1024,88]{0,1:T(8,128)} async-done(((f32[1024,704]{0,1:T(8,128)}), f32[1024,88]{0,1:T(8,128)}) %reduce-scatter.16.cloned.1.call-update) | async-done | bytes 360464 | tf_op jit(solution)/shard_map/reduce_scatter | solution.py:243
  1209.7 74.9 %reduce-scatter.18.cloned.1.call-done = f32[1024,88]{0,1:T(8,128)} async-done(((f32[1024,704]{0,1:T(8,128)}), f32[1024,88]{0,1:T(8,128)}) %reduce-scatter.18.cloned.1.call-update) | async-done | bytes 360464 | tf_op jit(solution)/shard_map/reduce_scatter | solution.py:244
  (342 shorter events, 260.9 us)
Async XLA Ops:
  7.2 67.6 %copy-start.58 = (bf16[128,256]{1,0:T(8,128)(2,1)S(1)}, bf16[128,256]{1,0:T(8,128)(2,1)}, u32[]{:S(2)}) copy-start(bf16[128,256]{1,0:T(8,128)(2,1)} %param.17) | copy-start | bytes 196612
  7.2 101.9 %all-gather.13.cloned.1.call-start = ((), (), s32[]{:S(2)}) async-start(), calls=%async_computation.8 | async-start | bytes 5242880 | tf_op jit(solution)/shard_map/all_gather | solution.py:104
  7.9 255.1 %all-gather.27.cloned.1.call-start = ((), (), s32[]{:S(2)}) async-start(), calls=%async_computation.22 | async-start | bytes 9437184 | tf_op jit(solution)/shard_map/all_gather | solution.py:14
  41.2 67.3 %copy-start.68 = (s32[8]{0:T(128)S(1)}, s32[8]{0:T(128)}, u32[]{:S(2)}) copy-start(s32[8]{0:T(128)} %param.26) | copy-start | bytes 100
  108.5 167.2 %copy-start.63 = (f32[256,2]{0,1:T(2,128)}, f32[256,2]{0,1:T(2,128)S(1)}, u32[]{:S(2)}) copy-start(f32[256,2]{0,1:T(2,128)S(1)} %get-tuple-element.355) | copy-start | bytes 6148
  123.9 97.3 %copy-start.14 = (bf16[8,256,2,128]{3,1,2,0:T(8,128)(2,1)}, bf16[8,256,2,128]{3,1,2,0:T(8,128)(2,1)S(1)}, u32[]{:S(2)}) copy-start(bf16[8,256,2,128]{3,1,2,0:T(8,128)(2,1)S(1)} %fusion.18) | copy-start | bytes 3145732
  126.8 92.1 %copy-start.67 = (f32[2]{0:T(128)S(1)}, f32[2]{0:T(128)}, u32[]{:S(2)}) copy-start(f32[2]{0:T(128)} %copy-done.66) | copy-start | bytes 28
  126.9 232.8 %reduce-scatter.8.cloned.1.call-start = ((), (), s32[]{:S(2)}) async-start(), calls=%async_computation.9 | async-start | bytes 10485760 | tf_op jit(solution)/shard_map/reduce_scatter | solution.py:108
  288.9 70.8 %copy-start.1 = (bf16[8,64,1024]{2,1,0:T(8,128)(2,1)S(1)}, bf16[8,64,1024]{2,1,0:T(8,128)(2,1)}, u32[]{:S(2)}) copy-start(bf16[8,64,1024]{2,1,0:T(8,128)(2,1)} %param.16) | copy-start | bytes 3145732
  288.9 116.1 %all-gather.19.cloned.1.call-start = ((), (), s32[]{:S(2)}) async-start(), calls=%async_computation.12 | async-start | bytes 1622016 | tf_op jit(solution)/shard_map/all_gather | solution.py:230
  289.5 150.4 %all-gather.15.cloned.1.call-start = ((), (), s32[]{:S(2)}) async-start(), calls=%async_computation.10 | async-start | bytes 5242880 | tf_op jit(solution)/shard_map/all_gather | solution.py:234
  363.1 122.1 %all-gather.17.cloned.1.call-start = ((), (), s32[]{:S(2)}) async-start(), calls=%async_computation.11 | async-start | bytes 1622016 | tf_op jit(solution)/shard_map/all_gather | solution.py:229
  363.7 165.4 %all-gather.21.cloned.1.call-start = ((), (), s32[]{:S(2)}) async-start(), calls=%async_computation.13 | async-start | bytes 1622016 | tf_op jit(solution)/shard_map/all_gather | solution.py:231
  364.5 199.1 %all-gather.23.cloned.1.call-start = ((), (), s32[]{:S(2)}) async-start(), calls=%async_computation.15 | async-start | bytes 5242880 | tf_op jit(solution)/shard_map/all_gather | solution.py:235
  364.6 83.6 %copy-start.61 = (f32[8,64]{1,0:T(8,128)}, f32[8,64]{1,0:T(8,128)S(1)}, u32[]{:S(2)}) copy-start(f32[8,64]{1,0:T(8,128)S(1)} %compare_convert_fusion.1) | copy-start | bytes 6148
  367.1 297.9 %reduce-scatter.12.cloned.1.call-start = ((), (), s32[]{:S(2)}) async-start(), calls=%async_computation.16 | async-start | bytes 10485760 | tf_op jit(solution)/shard_map/reduce_scatter | solution.py:112
  593.1 111.0 %all-gather.25.cloned.1.call-start = ((), (), s32[]{:S(2)}) async-start(), calls=%async_computation.17 | async-start | bytes 5242880 | tf_op jit(solution)/shard_map/all_gather | solution.py:104
  669.5 178.9 %all-gather.29.cloned.1.call-start = ((), (), s32[]{:S(2)}) async-start(), calls=%async_computation.23 | async-start | bytes 9437184 | tf_op jit(solution)/shard_map/all_gather | solution.py:14
  723.3 304.4 %reduce-scatter.14.cloned.1.call-start = ((), (), s32[]{:S(2)}) async-start(), calls=%async_computation.18 | async-start | bytes 10485760 | tf_op jit(solution)/shard_map/reduce_scatter | solution.py:108
  914.4 144.6 %reduce-scatter.10.cloned.1.call-start = ((), (), s32[]{:S(2)}) async-start(), calls=%async_computation.14 | async-start | bytes 10485760 | tf_op jit(solution)/shard_map/reduce_scatter | solution.py:112
  925.2 209.6 %reduce-scatter.20.cloned.1.call-start = ((), (), s32[]{:S(2)}) async-start(), calls=%async_computation.21 | async-start | bytes 3244032 | tf_op jit(solution)/shard_map/reduce_scatter | solution.py:245
  934.0 275.7 %reduce-scatter.16.cloned.1.call-start = ((), (), s32[]{:S(2)}) async-start(), calls=%async_computation.19 | async-start | bytes 3244032 | tf_op jit(solution)/shard_map/reduce_scatter | solution.py:243
  955.4 63.5 %all-to-all-start = ((bf16[8,128,1280]{1,2,0:T(8,128)(2,1)}), bf16[8,128,1280]{1,2,0:T(8,128)(2,1)}, u32[]{:S(2)}, u32[]{:S(2)}) async-start(bf16[8,128,1280]{1,2,0:T(8,128)(2,1)} %copy_bitcast_fusion), calls=%async_computation.4 | async-start | bytes 5242880 | tf_op jit(solution)/shard_map/all_to_all | solution.py:35
  959.8 324.7 %reduce-scatter.18.cloned.1.call-start = ((), (), s32[]{:S(2)}) async-start(), calls=%async_computation.20 | async-start | bytes 3244032 | tf_op jit(solution)/shard_map/reduce_scatter | solution.py:244
  (72 other events, 656.9 us)
Sparse Core Ops, SparseCore 0:
  9.6 37.1 all-gather.12
  127.0 136.0 all-gather.26
  289.0 70.5 reduce-scatter.7
  361.9 43.0 all-gather.18
  407.1 32.7 all-gather.14
  442.2 43.0 all-gather.16
  487.7 41.3 all-gather.20
  530.8 32.7 all-gather.22
  593.2 71.7 reduce-scatter.11
  669.6 34.4 all-gather.24
  723.4 124.9 all-gather.28
  914.6 69.9 reduce-scatter.13
  987.3 71.6 reduce-scatter.9
  1063.0 71.7 reduce-scatter.19
  1138.7 70.9 reduce-scatter.15
  1213.6 70.8 reduce-scatter.17
where the time goes:
time: 1300 us; the launch traced here: 1290 us
  waiting for transfers between devices  810 us (62%)
  blocking collectives  187 us (14%)
  matrix products  151 us (12%)
  other arithmetic  78.8 us (6%)
  local copies, waits for them, and re-layouts  43.2 us (3%)
  between operations  15.8 us (1%)
    all_gather x2, waiting for transfers between devices, carried_in(): everything = jax.tree.map(lambda part: lax.all_gather(part, axis), x)  150 us
    reduce_scatter x2, waiting for transfers between devices, hidden_total(): return lax.psum_scatter(values, 'narrow', scatter_dimension=1, tiled=True)  101 us
    reduce_scatter x1, waiting for transfers between devices, on_device(): lax.psum_scatter(gate_grad, 'wide', scatter_dimension=1, tiled=True)  74.9 us
    reduce_scatter x1, waiting for transfers between devices, on_device(): lax.psum_scatter(lift_grad, 'wide', scatter_dimension=1, tiled=True)  74.9 us
    reduce_scatter x1, waiting for transfers between devices, on_device(): lax.psum_scatter(down_grad, 'wide', scatter_dimension=1, tiled=True)  70.9 us
    reduce_scatter x2, waiting for transfers between devices, quarter_total(): return lax.psum_scatter(values, 'narrow', scatter_dimension=1, tiled=True)  70.1 us
    all_to_all x1, waiting for transfers between devices, summed_on_arrival(): blocks = lax.all_to_all(cut_along(x, dim, size), axis, 0, 0, tiled=True)  50.8 us
    all_gather x1, waiting for transfers between devices, on_device(): lax.all_gather(lift_matrix, 'wide', axis=1, tiled=True)  37.9 us
  transfers between devices with their start and end apart: 17, of which 15 were waited for; matrix products, arithmetic and copies ran while one was open for 8% of the time, Pallas kernels for 0%

commit v1 on v0

v1 whole, which is shorter than its diff:
```python
import math

import jax
import jax.numpy as jnp
from jax import lax
from jax.sharding import PartitionSpec as P

EPS = 1e-06
AXES = ("wide", "narrow")
BF16 = jnp.bfloat16
F32 = jnp.float32


def simple_norm(values):
    return values * lax.rsqrt(jnp.mean(values * values, axis=-1, keepdims=True) + EPS)


def norm_backward(values, cotangent):
    scale = lax.rsqrt(jnp.mean(values * values, axis=-1, keepdims=True) + EPS)
    inner = jnp.mean(values * cotangent, axis=-1, keepdims=True)
    return scale * cotangent - values * (scale * scale * scale * inner)


def apply_swish(values):
    return values * jax.nn.sigmoid(values)


def swish_slope(values):
    sigmoid_value = jax.nn.sigmoid(values)
    return sigmoid_value + values * sigmoid_value * (1.0 - sigmoid_value)


def rotation_tables(positions, head_size):
    half_width = head_size // 2
    frequency = jnp.exp(-math.log(10000.0) * jnp.arange(half_width, dtype=F32) / half_width)
    phase_angle = positions.astype(F32)[:, None] * frequency[None, :]
    return (jnp.cos(phase_angle)[:, None, :], jnp.sin(phase_angle)[:, None, :])


def rotate(values, cosine_table, sine_table):
    half_width = values.shape[-1] // 2
    first_half = values[..., :half_width]
    second_half = values[..., half_width:]
    return jnp.concatenate(
        [
            first_half * cosine_table - second_half * sine_table,
            first_half * sine_table + second_half * cosine_table,
        ],
        axis=-1,
    )


def exchange(x, mask):
    count = lax.axis_size(AXES)
    return lax.ppermute(x, AXES, [(i, i ^ mask) for i in range(count)])


def shift_z(x, step, reverse):
    count, unit = lax.axis_size(AXES), 2 * lax.axis_size("narrow")
    pairs = [(i, i + step * unit) for i in range(count - step * unit)]
    if reverse:
        pairs = [(b, a) for a, b in pairs]
    return lax.ppermute(x, AXES, pairs)


def gather_plane(x, masks):
    held = x[None]
    for mask in masks:
        held = jnp.concatenate([held, exchange(held, mask)], axis=0)
    return held


def gather_hidden(x, masks, swapped):
    held = gather_plane(x, masks)
    if swapped:
        held = jnp.swapaxes(held.reshape(2, 2, -1, *x.shape), 0, 1)
    return held.reshape(-1, x.shape[-1])


def scatter_plane(x, masks):
    for mask in reversed(masks):
        half = x.shape[0] // 2
        got = exchange(x[half:], mask)
        total = x[:half].astype(F32) + got.astype(F32)
        x = total.astype(BF16) if half > 1 else total
    return x[0]


def relative(masks, index):
    out = 0
    for k, mask in enumerate(masks):
        out ^= mask * ((index >> k) & 1)
    return out


def block_place(masks, wide_count):
    own = lax.axis_index(AXES)
    narrow_count = lax.axis_size("narrow")
    count = 1 << len(masks)
    ids = jnp.array([relative(masks, i) for i in range(count)], jnp.int32) ^ own
    return (ids // narrow_count) * (narrow_count // 2) + (ids % narrow_count) // 2


def to_canonical(blocks, masks, wide_count):
    own = lax.axis_index(AXES)
    count, rows, cols = blocks.shape
    narrow_count = lax.axis_size("narrow")
    sides = narrow_count // 2
    inverse = {relative(masks, i): i for i in range(count)}
    out = jnp.zeros((wide_count * rows, sides * cols), blocks.dtype)
    for i in range(count):
        ids = relative(masks, i) ^ own
        w, side = ids // narrow_count, (ids % narrow_count) // 2
        out = lax.dynamic_update_slice(out, blocks[i], (w * rows, side * cols))
    return out


def to_relative(full, masks, rows, cols):
    own = lax.axis_index(AXES)
    narrow_count = lax.axis_size("narrow")
    pieces = []
    for i in range(1 << len(masks)):
        ids = relative(masks, i) ^ own
        w, side = ids // narrow_count, (ids % narrow_count) // 2
        pieces.append(lax.dynamic_slice(full, (w * rows, side * cols), (rows, cols)))
    return jnp.stack(pieces)


def carried(local, block_decay, reverse):
    narrow_count = lax.axis_size("narrow")
    z_count = lax.axis_size("wide") // 2
    n, w = lax.axis_index("narrow"), lax.axis_index("wide")
    member = 2 * (w % 2) + n // 2
    masks = [0, 2, narrow_count, narrow_count + 2]
    slots = local.shape[0]
    share = slots // 4
    rank = lambda m: 3 - m if reverse else m
    log_decay = jnp.log(block_decay)
    power = lambda e: jnp.exp(e * log_decay)[None, :, None, None]

    def part(m):
        return lax.dynamic_slice_in_dim(local, m * share, share, 0)

    held = [part(member)] + [exchange(part(member ^ k), masks[k]) for k in range(1, 4)]
    held = [h.astype(F32) for h in held]
    ranks = [rank(member ^ k) for k in range(4)]
    total = sum(power((3 - ranks[k]).astype(F32)) * held[k] for k in range(4))
    before, span, step = 0.0, total, 1
    while step < z_count:
        got = shift_z(span.astype(BF16), step, reverse).astype(F32)
        before = before + power(4.0 * (step - 1)) * got
        span = span + power(4.0 * step) * got
        step *= 2
    sent = []
    for k in range(4):
        state = power(ranks[k].astype(F32)) * before
        for j in range(4):
            gap = (ranks[k] - 1 - ranks[j]).astype(F32)
            state = state + jnp.where(gap >= 0, power(jnp.maximum(gap, 0.0)), 0.0) * held[j]
        sent.append(state.astype(BF16))
    out = jnp.zeros(local.shape, BF16)
    for k in range(4):
        got = sent[0] if k == 0 else exchange(sent[k], masks[k])
        out = lax.dynamic_update_slice_in_dim(out, got, (member ^ k) * share, 0)
    return out


def on_device(
    layer_input,
    query_weight,
    key_weight,
    value_weight,
    modulate_weight,
    output_weight,
    gate_matrix,
    lift_matrix,
    down_matrix,
    decay_factor,
    valid_lengths,
    output_cotangent,
):
    narrow_count, wide_count = lax.axis_size("narrow"), lax.axis_size("wide")
    wide_index, narrow_index = lax.axis_index("wide"), lax.axis_index("narrow")
    core, side = narrow_index % 2, narrow_index // 2
    slots, quarter, width = layer_input.shape
    block = 2 * quarter
    rows, cols = query_weight.shape
    heads = 2 * decay_factor.shape[0]
    head_size = cols // decay_factor.shape[0]
    x_mask = 2
    wide_masks = []
    bit = narrow_count
    while bit < narrow_count * wide_count:
        wide_masks.append(bit)
        bit *= 2
    y_mask, z_masks = wide_masks[0], wide_masks[:0:-1]
    order_yx = z_masks + [y_mask, x_mask]
    order_xy = z_masks + [x_mask, y_mask]

    base = wide_index * (quarter * narrow_count) + side * block
    offsets = jnp.concatenate(
        [core * quarter + jnp.arange(quarter), (1 - core) * quarter + jnp.arange(quarter)]
    ).astype(jnp.int32)
    positions = base + offsets
    mask = (positions[None, :] < valid_lengths[:, None]).astype(F32)
    mask_rows = mask[:, :quarter, None]
    mask_heads = mask[:, :, None, None]

    def pair(mine):
        return jnp.concatenate([mine, exchange(mine, 1)], axis=1)

    def core_sum(partial):
        return partial[:, :quarter] + exchange(partial[:, quarter:].astype(BF16), 1).astype(F32)

    other_decay = exchange(decay_factor, x_mask)
    decay = jnp.concatenate(
        [jnp.where(side == 0, decay_factor, other_decay), jnp.where(side == 0, other_decay, decay_factor)]
    )
    log_decay = jnp.log(decay)

    def gathered(weight, masks):
        return to_canonical(gather_plane(weight, masks), masks, wide_count)

    full_key = gathered(key_weight, order_yx)
    full_value = gathered(value_weight, order_xy)
    full_query = gathered(query_weight, order_yx)
    full_modulate = gathered(modulate_weight, order_xy)
    full_output = gathered(output_weight, order_yx)
    gate_t = gather_hidden(gate_matrix.T, order_yx, False)
    lift_t = gather_hidden(lift_matrix.T, order_xy, True)
    down_t = gather_hidden(down_matrix.T, order_yx, False)

    input_rows = layer_input.astype(F32)
    normed = pair(simple_norm(input_rows).astype(BF16))

    def project(matrix):
        return jnp.einsum("bld,de->ble", normed, matrix, preferred_element_type=F32).reshape(
            slots, block, heads, head_size
        )

    cosine_table, sine_table = rotation_tables(positions, head_size)
    key_pre = project(full_key)
    value_pre = project(full_value)
    keys = (mask_heads * rotate(apply_swish(key_pre), cosine_table, sine_table)).astype(BF16)
    values = (mask_heads * value_pre).astype(BF16)
    spot = offsets.astype(F32)
    gap = spot[:, None] - spot[None, :]
    decay_grid = jnp.where(
        gap[None] >= 0.0, jnp.exp(jnp.maximum(gap, 0.0)[None] * log_decay[:, None, None]), 0.0
    )
    query_decay = jnp.exp((spot[:, None] + 1.0) * log_decay[None, :])[None, :, :, None]
    key_decay = jnp.exp((block - 1.0 - spot[:, None]) * log_decay[None, :])[None, :, :, None]
    block_decay = jnp.exp(block * log_decay)
    keys_scaled = (keys.astype(F32) * key_decay).astype(BF16)
    local_state = jnp.einsum("bjhd,bjhe->bhde", keys_scaled, values, preferred_element_type=F32)
    state = carried(local_state.astype(BF16), block_decay, False)

    query_pre = project(full_query)
    modulate_pre = project(full_modulate)
    queries = rotate(apply_swish(query_pre), cosine_table, sine_table).astype(BF16)
    scores = (
        jnp.einsum("bihd,bjhd->bhij", queries, keys, preferred_element_type=F32) * decay_grid[None]
    ).astype(BF16)
    queries_scaled = (queries.astype(F32) * query_decay).astype(BF16)
    mixed = jnp.einsum("bhij,bjhd->bihd", scores, values, preferred_element_type=F32)
    mixed = mixed + jnp.einsum("bihd,bhde->bihe", queries_scaled, state, preferred_element_type=F32)
    normed_heads = simple_norm(mixed)
    modulate_masked = modulate_pre * mask_heads
    gated = (normed_heads * modulate_masked).astype(BF16).reshape(slots, block, heads * head_size)
    attended = core_sum(jnp.einsum("ble,oe->blo", gated, full_output, preferred_element_type=F32))
    middle = input_rows + attended
    normed_two = pair(simple_norm(middle).astype(BF16))
    cotangent = output_cotangent.astype(F32)
    branch_grad = pair((mask_rows * cotangent).astype(BF16))

    def hidden(rows_in, matrix):
        return jnp.einsum("bld,fd->blf", rows_in, matrix, preferred_element_type=F32)

    def outer(a, b):
        return jnp.einsum("blf,bld->fd", a, b, preferred_element_type=F32).astype(BF16)

    gate_pre = hidden(normed_two, gate_t)
    lift_pre = hidden(normed_two, lift_t)
    inner_grad = hidden(branch_grad, down_t)
    gate_act = apply_swish(gate_pre)
    inner = (gate_act * lift_pre).astype(BF16)
    gate_grad = (inner_grad * lift_pre * swish_slope(gate_pre)).astype(BF16)
    lift_grad = (inner_grad * gate_act).astype(BF16)
    normed_grad = jnp.einsum("blf,fd->bld", gate_grad, gate_t, preferred_element_type=F32)
    normed_grad = normed_grad + jnp.einsum("blf,fd->bld", lift_grad, lift_t, preferred_element_type=F32)
    middle_grad = cotangent + norm_backward(middle, core_sum(normed_grad))
    branch = core_sum(jnp.einsum("blf,fd->bld", inner, down_t, preferred_element_type=F32))
    layer_output = (middle + mask_rows * branch).astype(BF16)

    def scattered(grad, masks, swapped):
        members = 1 << len(masks)
        if swapped:
            grad = jnp.swapaxes(grad.reshape(2, 2, -1, width), 0, 1)
        return scatter_plane(grad.reshape(members, -1, width), masks).T

    gate_gradient = scattered(outer(gate_grad, normed_two), order_yx, False)
    lift_gradient = scattered(outer(lift_grad, normed_two), order_xy, True)
    down_gradient = scattered(outer(inner, branch_grad), order_yx, False)

    attended_grad = pair(middle_grad.astype(BF16))
    gated_grad = jnp.einsum(
        "blo,oe->ble", attended_grad, full_output, preferred_element_type=F32
    ).reshape(slots, block, heads, head_size)
    modulate_grad = (gated_grad * mask_heads * normed_heads).astype(BF16)
    mixed_grad = norm_backward(mixed, gated_grad * modulate_masked).astype(BF16)
    state_grad = jnp.einsum("bihd,bihe->bhde", queries_scaled, mixed_grad, preferred_element_type=F32)
    later = carried(state_grad.astype(BF16), block_decay, True)
    score_grad = (
        jnp.einsum("bihe,bjhe->bhij", mixed_grad, values, preferred_element_type=F32)
        * decay_grid[None]
    ).astype(BF16)
    value_grad = jnp.einsum("bhij,bihe->bjhe", scores, mixed_grad, preferred_element_type=F32)
    query_grad = jnp.einsum("bhij,bjhd->bihd", score_grad, keys, preferred_element_type=F32)
    key_grad = jnp.einsum("bhij,bihd->bjhd", score_grad, queries, preferred_element_type=F32)
    query_grad = (
        query_grad
        + jnp.einsum("bihe,bhde->bihd", mixed_grad, state, preferred_element_type=F32) * query_decay
    )
    key_grad = (
        key_grad
        + jnp.einsum("bjhe,bhde->bjhd", values, later, preferred_element_type=F32) * key_decay
    )
    value_grad = value_grad + jnp.einsum(
        "bjhd,bhde->bjhe", keys_scaled, later, preferred_element_type=F32
    )
    query_pre_grad = (rotate(query_grad, cosine_table, -sine_table) * swish_slope(query_pre)).astype(BF16)
    key_pre_grad = (
        rotate(key_grad * mask_heads, cosine_table, -sine_table) * swish_slope(key_pre)
    ).astype(BF16)
    value_pre_grad = (value_grad * mask_heads).astype(BF16)
    grads = [
        g.reshape(slots, block, heads * head_size)
        for g in (query_pre_grad, key_pre_grad, value_pre_grad, modulate_grad)
    ]
    matrices = (full_query, full_key, full_value, full_modulate)
    row_grad = sum(
        jnp.einsum("ble,de->bld", g, m, preferred_element_type=F32) for g, m in zip(grads, matrices)
    )
    input_gradient = middle_grad + norm_backward(input_rows, core_sum(row_grad))

    def square(a, b, masks):
        full = jnp.einsum("bld,ble->de", a, b, preferred_element_type=F32)
        return scatter_plane(to_relative(full.astype(BF16), masks, rows, cols), masks)

    output_gradient = square(attended_grad, gated, order_yx)
    modulate_gradient = square(normed, grads[3], order_xy)
    query_gradient = square(normed, grads[0], order_yx)
    key_gradient = square(normed, grads[1], order_xy)
    value_gradient = square(normed, grads[2], order_yx)
    return (
        layer_output,
        input_gradient,
        query_gradient,
        key_gradient,
        value_gradient,
        modulate_gradient,
        output_gradient,
        gate_gradient,
        lift_gradient,
        down_gradient,
    )


def solution(mesh):
    placed = (
        P(None, ("wide", "narrow"), None),
        P("wide", "narrow"),
        P("wide", "narrow"),
        P("wide", "narrow"),
        P("wide", "narrow"),
        P("wide", "narrow"),
        P(None, ("wide", "narrow")),
        P(None, ("wide", "narrow")),
        P(None, ("wide", "narrow")),
        P("narrow"),
        P(),
        P(None, ("wide", "narrow"), None),
    )
    return jax.shard_map(
        on_device,
        mesh=mesh,
        in_specs=placed,
        out_specs=(
            P(None, ("wide", "narrow"), None),
            P(None, ("wide", "narrow"), None),
            P("wide", "narrow"),
            P("wide", "narrow"),
            P("wide", "narrow"),
            P("wide", "narrow"),
            P("wide", "narrow"),
            P(None, ("wide", "narrow")),
            P(None, ("wide", "narrow")),
            P(None, ("wide", "narrow")),
        ),
        check_vma=False,
    )
```

time: 1300 us -> 627 us (0.48)
  waiting for transfers between devices: 810 us -> 230 us
  blocking collectives: 187 us -> 0 us
  starting transfers between devices: 5.42 us -> 98.1 us
  local copies, waits for them, and re-layouts: 43.2 us -> 107 us
  matrix products: 151 us -> 103 us
    reduce_scatter x7 -> x0, waiting for transfers between devices: 392 us -> none  [the longest x2 101 us: hidden_total(): return lax.psum_scatter(values, 'narrow', scatter_dimension=1, tiled=True)]
    all_gather x9 -> x0, waiting for transfers between devices: 365 us -> none  [the longest x2 150 us: carried_in(): everything = jax.tree.map(lambda part: lax.all_gather(part, axis), x)]
    ppermute x0 -> x89, waiting for transfers between devices: none -> 230 us  [the longest x85 225 us: exchange(): return lax.ppermute(x, AXES, [(i, i ^ mask) for i in range(count)])]
    all_gather x5 -> x0, blocking collectives: 165 us -> none  [the longest x1 35.7 us: on_device(): lax.all_gather(output_weight, 'wide', axis=0, tiled=True)]
    ppermute x0 -> x89, starting transfers between devices: none -> 98.1 us  [the longest x85 85.6 us: exchange(): return lax.ppermute(x, AXES, [(i, i ^ mask) for i in range(count)])]
    all_to_all x1 -> x0, waiting for transfers between devices: 50.8 us -> none  [summed_on_arrival(): blocks = lax.all_to_all(cut_along(x, dim, size), axis, 0, 0, tiled=True)]
    dot_general x33, matrix products: 143 us -> 95.3 us  [the longest x3 20.9 us: hidden(): jnp.einsum('bld,fd->blf', rows_in, matrix, preferred_element_type=F32)]
    dynamic_update_slice x0 -> x86, local copies, waits for them, and re-layouts: none -> 42.7 us  [the longest x78 33.9 us: to_canonical(): out = lax.dynamic_update_slice(out, blocks[i], (w * rows, side * cols))]
  transfers between devices with their start and end apart: 17 -> 89, of which waited for: 15 -> 43; matrix products, arithmetic and copies ran while one was open for 8% -> 38% of each run, Pallas kernels for 0% -> 0%
where the time goes in v1:
time: 627 us; the launch traced here: 620 us
  waiting for transfers between devices  230 us (37%)
  local copies, waits for them, and re-layouts  107 us (17%)
  matrix products  103 us (16%)
  starting transfers between devices  98.1 us (16%)
  other arithmetic  78.1 us (12%)
    ppermute x85, waiting for transfers between devices, exchange(): return lax.ppermute(x, AXES, [(i, i ^ mask) for i in range(count)])  225 us
    ppermute x85, starting transfers between devices, exchange(): return lax.ppermute(x, AXES, [(i, i ^ mask) for i in range(count)])  85.6 us
    dynamic_update_slice x78, local copies, waits for them, and re-layouts, to_canonical(): out = lax.dynamic_update_slice(out, blocks[i], (w * rows, side * cols))  33.9 us
    unnamed x315, local copies, waits for them, and re-layouts  30.2 us
    dot_general x3, matrix products, hidden(): jnp.einsum('bld,fd->blf', rows_in, matrix, preferred_element_type=F32)  20.9 us
    concatenate x24, other arithmetic, gather_plane(): held = jnp.concatenate([held, exchange(held, mask)], axis=0)  16.6 us
    dot_general x4, matrix products, project(): jnp.einsum('bld,de->ble', normed, matrix, preferred_element_type=F32)  13.4 us
    dot_general x3, matrix products, outer(): jnp.einsum('blf,bld->fd', a, b, preferred_element_type=F32).astype(BF16)  12.8 us
  transfers between devices with their start and end apart: 89, of which 43 were waited for; matrix products, arithmetic and copies ran while one was open for 38% of the time, Pallas kernels for 0%

profile of v1, /device:TPU:0, one launch (start us, length us, event | category | flops | bytes accessed | tf_op | source)
XLA Modules:
  0.0 619.7 jit_solution(10368559004546820093)
XLA Ops:
  53.1 8.4 %collective-permute-done.32 = bf16[1,88,1024]{2,1,0:T(8,128)(2,1)S(1)} collective-permute-done((bf16[1,88,1024]{2,1,0:T(8,128)(2,1)S(1)}, bf16[1,88,1024]{2,1,0:T(8,128)(2,1)S(1)}, u32[]{:S(2)}, u32[]{:S(2)}) %collective-permute-start.32) | collective-permute-done | bytes 180256 | tf_op jit(solution)/shard_map/ppermute | solution.py:55
  63.1 4.3 collective-permute-done.36
  115.3 6.1 collective-permute-done.25
  121.4 7.6 %collective-permute-done.4 = bf16[8,128,256]{2,1,0:T(8,128)(2,1)S(1)} collective-permute-done((bf16[8,128,256]{2,1,0:T(8,128)(2,1)S(1)}, bf16[8,128,256]{2,1,0:T(8,128)(2,1)S(1)}, u32[]{:S(2)}, u32[]{:S(2)}) %collective-permute-start.4) | collective-permute-done | bytes 524320 | tf_op jit(solution)/shard_map/ppermute | solution.py:55
  132.9 11.1 %collective-permute-done.12 = bf16[8,128,256]{2,1,0:T(8,128)(2,1)S(1)} collective-permute-done((bf16[8,128,256]{2,1,0:T(8,128)(2,1)S(1)}, bf16[8,128,256]{2,1,0:T(8,128)(2,1)S(1)}, u32[]{:S(2)}, u32[]{:S(2)}) %collective-permute-start.12) | collective-permute-done | bytes 524320 | tf_op jit(solution)/shard_map/ppermute | solution.py:55
  144.0 9.0 %collective-permute-done.29 = bf16[8,128,256]{2,1,0:T(8,128)(2,1)S(1)} collective-permute-done((bf16[8,128,256]{2,1,0:T(8,128)(2,1)S(1)}, bf16[8,128,256]{2,1,0:T(8,128)(2,1)S(1)}, u32[]{:S(2)}, u32[]{:S(2)}) %collective-permute-start.29) | collective-permute-done | bytes 524320 | tf_op jit(solution)/shard_map/ppermute | solution.py:55
  182.7 4.7 fusion.36
  199.4 7.8 %collective-permute-start.18 = (bf16[2,4,128,128]{3,2,1,0:T(8,128)(2,1)S(1)}, bf16[2,4,128,128]{3,2,1,0:T(8,128)(2,1)S(1)}, u32[]{:S(2)}, u32[]{:S(2)}) collective-permute-start(bf16[2,4,128,128]{3,2,1,0:T(8,128)(2,1)S(1)} %fusion.51), channel_id=1, source_target_pairs={{0,16},{1,17},{2,18},{3,19},{4,20},{5,21},{6,22},{7,23},{8,24},{9,... | collective-permute-start | bytes 786440 | tf_op jit(solution)/shard_map/ppermute | solution.py:63
  259.2 14.2 %collective-permute-done.38 = bf16[4,88,1024]{2,1,0:T(8,128)(2,1)S(1)} collective-permute-done((bf16[4,88,1024]{2,1,0:T(8,128)(2,1)S(1)}, bf16[4,88,1024]{2,1,0:T(8,128)(2,1)S(1)}, u32[]{:S(2)}, u32[]{:S(2)}) %collective-permute-start.38) | collective-permute-done | bytes 720928 | tf_op jit(solution)/shard_map/ppermute | solution.py:55
  281.4 24.0 %collective-permute-done.39 = bf16[8,88,1024]{2,1,0:T(8,128)(2,1)S(1)} collective-permute-done((bf16[8,88,1024]{2,1,0:T(8,128)(2,1)S(1)}, bf16[8,88,1024]{2,1,0:T(8,128)(2,1)S(1)}, u32[]{:S(2)}, u32[]{:S(2)}) %collective-permute-start.39) | collective-permute-done | bytes 1441824 | tf_op jit(solution)/shard_map/ppermute | solution.py:55
  306.0 27.7 %collective-permute-done.43 = bf16[8,88,1024]{2,1,0:T(8,128)(2,1)S(1)} collective-permute-done((bf16[8,88,1024]{2,1,0:T(8,128)(2,1)S(1)}, bf16[8,88,1024]{2,1,0:T(8,128)(2,1)S(1)}, u32[]{:S(2)}, u32[]{:S(2)}) %collective-permute-start.43) | collective-permute-done | bytes 1441824 | tf_op jit(solution)/shard_map/ppermute | solution.py:55
  333.9 5.3 fusion.180
  339.3 5.4 fusion.179
  344.7 10.1 %multiply_convert_fusion.1 = (bf16[8,128,1408]{2,1,0:T(8,128)(2,1)S(1)}, bf16[8,128,1408]{2,1,0:T(8,128)(2,1)S(1)}, bf16[8,128,1408]{2,1,0:T(8,128)(2,1)}) fusion(f32[8,128,1408]{2,1,0:T(8,128)} %fusion.179, f32[8,128,1408]{2,1,0:T(8,128)} %fusion.180, bf16[1408,1024,1]{1,0,2:T(8,128)(2,1)S(1)} %bitcast.731, ...), kind=kOutput, calls=%fused_computation.4 | convolution fusion | flops 2977169408 | bytes 25165824 | tf_op jit(solution)/shard_map/bld,fd->blf/dot_general | solution.py:277
  359.9 5.6 bitcast_convert_fusion
  388.5 11.8 %collective-permute-done.85 = bf16[8,88,1024]{2,1,0:T(8,128)(2,1)S(1)} collective-permute-done((bf16[8,88,1024]{2,1,0:T(8,128)(2,1)S(1)}, bf16[8,88,1024]{2,1,0:T(8,128)(2,1)S(1)}, u32[]{:S(2)}, u32[]{:S(2)}) %collective-permute-start.85) | collective-permute-done | bytes 1441824 | tf_op jit(solution)/shard_map/ppermute | solution.py:55
  402.2 11.8 %collective-permute-done.81 = bf16[8,88,1024]{2,1,0:T(8,128)(2,1)S(1)} collective-permute-done((bf16[8,88,1024]{2,1,0:T(8,128)(2,1)S(1)}, bf16[8,88,1024]{2,1,0:T(8,128)(2,1)S(1)}, u32[]{:S(2)}, u32[]{:S(2)}) %collective-permute-start.81) | collective-permute-done | bytes 1441824 | tf_op jit(solution)/shard_map/ppermute | solution.py:55
  416.5 14.8 %collective-permute-done.77 = bf16[8,88,1024]{2,1,0:T(8,128)(2,1)S(1)} collective-permute-done((bf16[8,88,1024]{2,1,0:T(8,128)(2,1)S(1)}, bf16[8,88,1024]{2,1,0:T(8,128)(2,1)S(1)}, u32[]{:S(2)}, u32[]{:S(2)}) %collective-permute-start.77) | collective-permute-done | bytes 1441824 | tf_op jit(solution)/shard_map/ppermute | solution.py:55
  433.2 4.3 fusion.30
  480.6 4.9 collective-permute-done.49
  492.4 7.8 %collective-permute-done.83 = bf16[2,88,1024]{2,1,0:T(8,128)(2,1)S(1)} collective-permute-done((bf16[2,88,1024]{2,1,0:T(8,128)(2,1)S(1)}, bf16[2,88,1024]{2,1,0:T(8,128)(2,1)S(1)}, u32[]{:S(2)}, u32[]{:S(2)}) %collective-permute-start.83) | collective-permute-done | bytes 360480 | tf_op jit(solution)/shard_map/ppermute | solution.py:55
  500.5 6.2 %collective-permute-done.79 = bf16[2,88,1024]{2,1,0:T(8,128)(2,1)S(1)} collective-permute-done((bf16[2,88,1024]{2,1,0:T(8,128)(2,1)S(1)}, bf16[2,88,1024]{2,1,0:T(8,128)(2,1)S(1)}, u32[]{:S(2)}, u32[]{:S(2)}) %collective-permute-start.79) | collective-permute-done | bytes 360480 | tf_op jit(solution)/shard_map/ppermute | solution.py:55
  517.0 9.4 %collective-permute-done.84 = bf16[1,88,1024]{2,1,0:T(8,128)(2,1)S(1)} collective-permute-done((bf16[1,88,1024]{2,1,0:T(8,128)(2,1)S(1)}, bf16[1,88,1024]{2,1,0:T(8,128)(2,1)S(1)}, u32[]{:S(2)}, u32[]{:S(2)}) %collective-permute-start.84) | collective-permute-done | bytes 180256 | tf_op jit(solution)/shard_map/ppermute | solution.py:55
  590.8 4.6 collective-permute-done.57
  (758 shorter events, 389.0 us)
Async XLA Ops:
  0.7 39.7 %collective-permute-start.22 = (bf16[1,128,256]{2,1,0:T(8,128)(2,1)}, bf16[1,128,256]{2,1,0:T(8,128)(2,1)}, u32[]{:S(2)}, u32[]{:S(2)}) collective-permute-start(bf16[1,128,256]{2,1,0:T(8,128)(2,1)} %bitcast.713), channel_id=1, source_target_pairs={{0,16},{1,17},{2,18},{3,19},{4,20},{5,21},{6,22},{7,23},{8,24},{9,... | collective-permute-start | bytes 196616 | tf_op jit(solution)/shard_map/ppermute | solution.py:55
  4.8 39.1 %collective-permute-start.1 = (bf16[1,128,256]{2,1,0:T(8,128)(2,1)}, bf16[1,128,256]{2,1,0:T(8,128)(2,1)}, u32[]{:S(2)}, u32[]{:S(2)}) collective-permute-start(bf16[1,128,256]{2,1,0:T(8,128)(2,1)} %bitcast.717), channel_id=1, source_target_pairs={{0,16},{1,17},{2,18},{3,19},{4,20},{5,21},{6,22},{7,23},{8,24},{9,... | collective-permute-start | bytes 196616 | tf_op jit(solution)/shard_map/ppermute | solution.py:55
  10.0 152.6 %collective-permute-start = (bf16[8,64,1024]{2,1,0:T(8,128)(2,1)}, bf16[8,64,1024]{2,1,0:T(8,128)(2,1)}, u32[]{:S(2)}, u32[]{:S(2)}) collective-permute-start(bf16[8,64,1024]{2,1,0:T(8,128)(2,1)} %fusion.6), channel_id=1, source_target_pairs={{0,1},{1,0},{2,3},{3,2},{4,5},{5,4},{6,7},{7,6},{8,9},{9,8},{10,11... | collective-permute-start | bytes 3145736 | tf_op jit(solution)/shard_map/ppermute | solution.py:55
  10.0 36.0 %collective-permute-start.5 = (bf16[1,128,256]{2,1,0:T(8,128)(2,1)}, bf16[1,128,256]{2,1,0:T(8,128)(2,1)}, u32[]{:S(2)}, u32[]{:S(2)}) collective-permute-start(bf16[1,128,256]{2,1,0:T(8,128)(2,1)} %bitcast.17), channel_id=1, source_target_pairs={{0,16},{1,17},{2,18},{3,19},{4,20},{5,21},{6,22},{7,23},{8,24},{9,... | collective-permute-start | bytes 196616 | tf_op jit(solution)/shard_map/ppermute | solution.py:55
  50.4 294.3 %collective-permute-start.45 = (bf16[8,64,1024]{2,1,0:T(8,128)(2,1)}, bf16[8,64,1024]{2,1,0:T(8,128)(2,1)}, u32[]{:S(2)}, u32[]{:S(2)}) collective-permute-start(bf16[8,64,1024]{2,1,0:T(8,128)(2,1)} %fusion.4), channel_id=1, source_target_pairs={{0,1},{1,0},{2,3},{3,2},{4,5},{5,4},{6,7},{7,6},{8,9},{9,8},{10,11... | collective-permute-start | bytes 3145736 | tf_op jit(solution)/shard_map/ppermute | solution.py:55
  77.7 36.5 %collective-permute-start.33 = (bf16[2,88,1024]{2,1,0:T(8,128)(2,1)S(1)}, bf16[2,88,1024]{2,1,0:T(8,128)(2,1)S(1)}, u32[]{:S(2)}, u32[]{:S(2)}) collective-permute-start(bf16[2,88,1024]{2,1,0:T(8,128)(2,1)S(1)} %pad_maximum_fusion.20), channel_id=1, source_target_pairs={{0,8},{1,9},{2,10},{3,11},{4,12},{5,13},{6,14},{7,15},{8,0},{9,1},... | collective-permute-start | bytes 1081352 | tf_op jit(solution)/shard_map/ppermute | solution.py:55
  114.3 138.0 %collective-permute-start.37 = (bf16[2,88,1024]{2,1,0:T(8,128)(2,1)}, bf16[2,88,1024]{2,1,0:T(8,128)(2,1)}, u32[]{:S(2)}, u32[]{:S(2)}) collective-permute-start(bf16[2,88,1024]{2,1,0:T(8,128)(2,1)} %pad_maximum_fusion.21), channel_id=1, source_target_pairs={{0,8},{1,9},{2,10},{3,11},{4,12},{5,13},{6,14},{7,15},{8,0},{9,1},... | collective-permute-start | bytes 1081352 | tf_op jit(solution)/shard_map/ppermute | solution.py:55
  224.3 30.8 %collective-permute-start.41 = (bf16[2,88,1024]{2,1,0:T(8,128)(2,1)}, bf16[2,88,1024]{2,1,0:T(8,128)(2,1)}, u32[]{:S(2)}, u32[]{:S(2)}) collective-permute-start(bf16[2,88,1024]{2,1,0:T(8,128)(2,1)} %pad_maximum_fusion.22), channel_id=1, source_target_pairs={{0,8},{1,9},{2,10},{3,11},{4,12},{5,13},{6,14},{7,15},{8,0},{9,1},... | collective-permute-start | bytes 1081352 | tf_op jit(solution)/shard_map/ppermute | solution.py:55
  230.2 26.6 %collective-permute-start.34 = (bf16[4,88,1024]{2,1,0:T(8,128)(2,1)}, bf16[4,88,1024]{2,1,0:T(8,128)(2,1)}, u32[]{:S(2)}, u32[]{:S(2)}) collective-permute-start(bf16[4,88,1024]{2,1,0:T(8,128)(2,1)} %pad_maximum_fusion.12), channel_id=1, source_target_pairs={{0,4},{1,5},{2,6},{3,7},{4,0},{5,1},{6,2},{7,3},{8,12},{9,13},{10,... | collective-permute-start | bytes 2162696 | tf_op jit(solution)/shard_map/ppermute | solution.py:55
  252.2 24.8 %collective-permute-start.30 = (bf16[8,64,1024]{2,1,0:T(8,128)(2,1)S(1)}, bf16[8,64,1024]{2,1,0:T(8,128)(2,1)S(1)}, u32[]{:S(2)}, u32[]{:S(2)}) collective-permute-start(bf16[8,64,1024]{2,1,0:T(8,128)(2,1)S(1)} %slice.1020), channel_id=1, source_target_pairs={{0,1},{1,0},{2,3},{3,2},{4,5},{5,4},{6,7},{7,6},{8,9},{9,8},{10,11... | collective-permute-start | bytes 3145736 | tf_op jit(solution)/shard_map/ppermute | solution.py:55
  258.0 47.9 %collective-permute-start.35 = (bf16[8,88,1024]{2,1,0:T(8,128)(2,1)S(1)}, bf16[8,88,1024]{2,1,0:T(8,128)(2,1)S(1)}, u32[]{:S(2)}, u32[]{:S(2)}) collective-permute-start(bf16[8,88,1024]{2,1,0:T(8,128)(2,1)S(1)} %pad_maximum_fusion.4), channel_id=1, source_target_pairs={{0,2},{1,3},{2,0},{3,1},{4,6},{5,7},{6,4},{7,5},{8,10},{9,11},{10,... | collective-permute-start | bytes 4325384 | tf_op jit(solution)/shard_map/ppermute | solution.py:55
  274.5 30.8 %collective-permute-start.39 = (bf16[8,88,1024]{2,1,0:T(8,128)(2,1)S(1)}, bf16[8,88,1024]{2,1,0:T(8,128)(2,1)S(1)}, u32[]{:S(2)}, u32[]{:S(2)}) collective-permute-start(bf16[8,88,1024]{2,1,0:T(8,128)(2,1)S(1)} %pad_maximum_fusion.5), channel_id=1, source_target_pairs={{0,4},{1,5},{2,6},{3,7},{4,0},{5,1},{6,2},{7,3},{8,12},{9,13},{10,... | collective-permute-start | bytes 4325384 | tf_op jit(solution)/shard_map/ppermute | solution.py:55
  276.0 57.8 %collective-permute-start.43 = (bf16[8,88,1024]{2,1,0:T(8,128)(2,1)S(1)}, bf16[8,88,1024]{2,1,0:T(8,128)(2,1)S(1)}, u32[]{:S(2)}, u32[]{:S(2)}) collective-permute-start(bf16[8,88,1024]{2,1,0:T(8,128)(2,1)S(1)} %pad_maximum_fusion.6), channel_id=1, source_target_pairs={{0,2},{1,3},{2,0},{3,1},{4,6},{5,7},{6,4},{7,5},{8,10},{9,11},{10,... | collective-permute-start | bytes 4325384 | tf_op jit(solution)/shard_map/ppermute | solution.py:55
  277.7 56.2 %collective-permute-start.31 = (bf16[8,64,1024]{2,1,0:T(8,128)(2,1)S(1)}, bf16[8,64,1024]{2,1,0:T(8,128)(2,1)S(1)}, u32[]{:S(2)}, u32[]{:S(2)}) collective-permute-start(bf16[8,64,1024]{2,1,0:T(8,128)(2,1)S(1)} %multiply_convert_fusion.6), channel_id=1, source_target_pairs={{0,1},{1,0},{2,3},{3,2},{4,5},{5,4},{6,7},{7,6},{8,9},{9,8},{10,11... | collective-permute-start | bytes 3145736 | tf_op jit(solution)/shard_map/ppermute | solution.py:55
  365.8 34.6 %collective-permute-start.85 = (bf16[8,88,1024]{2,1,0:T(8,128)(2,1)S(1)}, bf16[8,88,1024]{2,1,0:T(8,128)(2,1)S(1)}, u32[]{:S(2)}, u32[]{:S(2)}) collective-permute-start(bf16[8,88,1024]{2,1,0:T(8,128)(2,1)S(1)} %bitcast.710), channel_id=1, source_target_pairs={{0,2},{1,3},{2,0},{3,1},{4,6},{5,7},{6,4},{7,5},{8,10},{9,11},{10,... | collective-permute-start | bytes 4325384 | tf_op jit(solution)/shard_map/ppermute | solution.py:55
  379.4 34.6 %collective-permute-start.81 = (bf16[8,88,1024]{2,1,0:T(8,128)(2,1)S(1)}, bf16[8,88,1024]{2,1,0:T(8,128)(2,1)S(1)}, u32[]{:S(2)}, u32[]{:S(2)}) collective-permute-start(bf16[8,88,1024]{2,1,0:T(8,128)(2,1)S(1)} %bitcast.711), channel_id=1, source_target_pairs={{0,4},{1,5},{2,6},{3,7},{4,0},{5,1},{6,2},{7,3},{8,12},{9,13},{10,... | collective-permute-start | bytes 4325384 | tf_op jit(solution)/shard_map/ppermute | solution.py:55
  385.1 46.2 %collective-permute-start.77 = (bf16[8,88,1024]{2,1,0:T(8,128)(2,1)S(1)}, bf16[8,88,1024]{2,1,0:T(8,128)(2,1)S(1)}, u32[]{:S(2)}, u32[]{:S(2)}) collective-permute-start(bf16[8,88,1024]{2,1,0:T(8,128)(2,1)S(1)} %bitcast.712), channel_id=1, source_target_pairs={{0,2},{1,3},{2,0},{3,1},{4,6},{5,7},{6,4},{7,5},{8,10},{9,11},{10,... | collective-permute-start | bytes 4325384 | tf_op jit(solution)/shard_map/ppermute | solution.py:55
  388.5 44.7 %collective-permute-start.47 = (bf16[8,64,1024]{2,1,0:T(8,128)(2,1)S(1)}, bf16[8,64,1024]{2,1,0:T(8,128)(2,1)S(1)}, u32[]{:S(2)}, u32[]{:S(2)}) collective-permute-start(bf16[8,64,1024]{2,1,0:T(8,128)(2,1)S(1)} %get-tuple-element.14), channel_id=1, source_target_pairs={{0,1},{1,0},{2,3},{3,2},{4,5},{5,4},{6,7},{7,6},{8,9},{9,8},{10,11... | collective-permute-start | bytes 3145736 | tf_op jit(solution)/shard_map/ppermute | solution.py:55
  402.0 69.8 %collective-permute-start.86 = (bf16[4,88,1024]{2,1,0:T(8,128)(2,1)}, bf16[4,88,1024]{2,1,0:T(8,128)(2,1)}, u32[]{:S(2)}, u32[]{:S(2)}) collective-permute-start(bf16[4,88,1024]{2,1,0:T(8,128)(2,1)} %slice.738), channel_id=1, source_target_pairs={{0,4},{1,5},{2,6},{3,7},{4,0},{5,1},{6,2},{7,3},{8,12},{9,13},{10,... | collective-permute-start | bytes 2162696 | tf_op jit(solution)/shard_map/ppermute | solution.py:55
  415.7 59.4 %collective-permute-start.82 = (bf16[4,88,1024]{2,1,0:T(8,128)(2,1)}, bf16[4,88,1024]{2,1,0:T(8,128)(2,1)}, u32[]{:S(2)}, u32[]{:S(2)}) collective-permute-start(bf16[4,88,1024]{2,1,0:T(8,128)(2,1)} %slice.730), channel_id=1, source_target_pairs={{0,2},{1,3},{2,0},{3,1},{4,6},{5,7},{6,4},{7,5},{8,10},{9,11},{10,... | collective-permute-start | bytes 2162696 | tf_op jit(solution)/shard_map/ppermute | solution.py:55
  432.9 44.6 %collective-permute-start.78 = (bf16[4,88,1024]{2,1,0:T(8,128)(2,1)}, bf16[4,88,1024]{2,1,0:T(8,128)(2,1)}, u32[]{:S(2)}, u32[]{:S(2)}) collective-permute-start(bf16[4,88,1024]{2,1,0:T(8,128)(2,1)} %slice.722), channel_id=1, source_target_pairs={{0,4},{1,5},{2,6},{3,7},{4,0},{5,1},{6,2},{7,3},{8,12},{9,13},{10,... | collective-permute-start | bytes 2162696 | tf_op jit(solution)/shard_map/ppermute | solution.py:55
  458.2 49.9 %collective-permute-start.73 = (bf16[8,128,256]{2,1,0:T(8,128)(2,1)}, bf16[8,128,256]{2,1,0:T(8,128)(2,1)}, u32[]{:S(2)}, u32[]{:S(2)}) collective-permute-start(bf16[8,128,256]{2,1,0:T(8,128)(2,1)} %get-tuple-element.53), channel_id=1, source_target_pairs={{0,2},{1,3},{2,0},{3,1},{4,6},{5,7},{6,4},{7,5},{8,10},{9,11},{10,... | collective-permute-start | bytes 1572872 | tf_op jit(solution)/shard_map/ppermute | solution.py:55
  479.0 32.0 %collective-permute-start.69 = (bf16[8,128,256]{2,1,0:T(8,128)(2,1)S(1)}, bf16[8,128,256]{2,1,0:T(8,128)(2,1)S(1)}, u32[]{:S(2)}, u32[]{:S(2)}) collective-permute-start(bf16[8,128,256]{2,1,0:T(8,128)(2,1)S(1)} %get-tuple-element.69), channel_id=1, source_target_pairs={{0,4},{1,5},{2,6},{3,7},{4,0},{5,1},{6,2},{7,3},{8,12},{9,13},{10,... | collective-permute-start | bytes 1572872 | tf_op jit(solution)/shard_map/ppermute | solution.py:55
  587.2 28.9 %collective-permute-start.56 = (bf16[8,64,1024]{2,1,0:T(8,128)(2,1)S(1)}, bf16[8,64,1024]{2,1,0:T(8,128)(2,1)S(1)}, u32[]{:S(2)}, u32[]{:S(2)}) collective-permute-start(bf16[8,64,1024]{2,1,0:T(8,128)(2,1)S(1)} %slice.1017), channel_id=1, source_target_pairs={{0,1},{1,0},{2,3},{3,2},{4,5},{5,4},{6,7},{7,6},{8,9},{9,8},{10,11... | collective-permute-start | bytes 3145736 | tf_op jit(solution)/shard_map/ppermute | solution.py:55
  (199 other events, 3033.5 us)

commit v2 on v1

v2 whole, which is shorter than its diff:
```python
import functools
import math

import jax
import jax.numpy as jnp
from jax import lax
from jax.experimental import pallas as pl
from jax.experimental.pallas import tpu as pltpu
from jax.sharding import PartitionSpec as P

EPS = 1e-06
AXES = ("wide", "narrow")
BF16 = jnp.bfloat16
F32 = jnp.float32


def simple_norm(values):
    return values * lax.rsqrt(jnp.mean(values * values, axis=-1, keepdims=True) + EPS)


def norm_backward(values, cotangent):
    scale = lax.rsqrt(jnp.mean(values * values, axis=-1, keepdims=True) + EPS)
    inner = jnp.mean(values * cotangent, axis=-1, keepdims=True)
    return scale * cotangent - values * (scale * scale * scale * inner)


def apply_swish(values):
    return values * jax.nn.sigmoid(values)


def swish_slope(values):
    sigmoid_value = jax.nn.sigmoid(values)
    return sigmoid_value + values * sigmoid_value * (1.0 - sigmoid_value)


def exchange(x, mask):
    count = lax.axis_size(AXES)
    return lax.ppermute(x, AXES, [(i, i ^ mask) for i in range(count)])


def shift_z(x, step, reverse):
    count, unit = lax.axis_size(AXES), 2 * lax.axis_size("narrow")
    pairs = [(i, i + step * unit) for i in range(count - step * unit)]
    if reverse:
        pairs = [(b, a) for a, b in pairs]
    return lax.ppermute(x, AXES, pairs)


def gather_plane(x, masks):
    return gather_more(x[None], masks)


def gather_more(held, masks):
    for mask in masks:
        held = jnp.concatenate([held, exchange(held, mask)], axis=0)
    return held


def gather_hidden(x, masks, swapped):
    held = gather_plane(x, masks)
    if swapped:
        held = jnp.swapaxes(held.reshape(2, 2, -1, *x.shape), 0, 1)
    return held.reshape(-1, x.shape[-1])


def scatter_plane(x, masks):
    for mask in reversed(masks):
        half = x.shape[0] // 2
        got = exchange(x[half:], mask)
        total = x[:half].astype(F32) + got.astype(F32)
        x = total.astype(BF16) if half > 1 else total
    return x[0]


def relative(masks, index):
    out = 0
    for k, mask in enumerate(masks):
        out ^= mask * ((index >> k) & 1)
    return out


NT = (((1,), (1,)), ((), ()))
NN = (((1,), (0,)), ((), ()))
TN = (((0,), (0,)), ((), ()))


def mm(a, b, dims=NN):
    return lax.dot_general(a, b, dims, preferred_element_type=F32)


def turn(v, cosine, sine):
    return v * cosine + pltpu.roll(v, v.shape[-1] // 2, 1) * sine


def block_spots(masks):
    own = lax.axis_index(AXES)
    narrow_count = lax.axis_size("narrow")
    ids = jnp.array([relative(masks, i) for i in range(1 << len(masks))], jnp.int32) ^ own
    return jnp.stack([ids // narrow_count, (ids % narrow_count) // 2], axis=1)


def block_copy(spots, which, i, rows, cols, whole, part, sem, out):
    at = (
        pl.ds(pl.multiple_of(spots[which, i, 0] * rows, rows), rows),
        pl.ds(pl.multiple_of(spots[which, i, 1] * cols, cols), cols),
    )
    if out:
        return pltpu.make_async_copy(whole.at[at], part, sem)
    return pltpu.make_async_copy(part, whole.at[at], sem)


def each_block(spots, jobs, out=False):
    def go(method):
        for order, k, near, far, whole, sems in jobs:
            half, _, rows, cols = near.shape

            def step(i, _):
                for at, part in enumerate((near, far)):
                    copy = block_copy(
                        spots, order, i + at * half, rows, cols, whole, part.at[i, k],
                        sems.at[i + at * half], out,
                    )
                    getattr(copy, method)()
                return 0

            lax.fori_loop(0, half, step, 0)

    go("start")
    go("wait")


def both(near, far):
    rows = near.shape[0] * near.shape[1]
    return jnp.concatenate([near.reshape(rows, -1), far.reshape(rows, -1)], axis=0)


def slot_rows(x, s, size, count):
    return jnp.concatenate(
        [x[s * size : (s + 1) * size], x[(count + s) * size : (count + s + 1) * size]], axis=0
    )


def slot_back(parts, size):
    return jnp.concatenate([p[:size] for p in parts] + [p[size:] for p in parts], axis=0)


def put(ref, lanes, value):
    two, count, size, _ = ref.shape
    ref[:, :, :, lanes] = value.reshape(two, count, size, -1).astype(ref.dtype)


def get(ref, lanes=slice(None)):
    two, count, size, width = ref.shape
    x = ref[:, :, :, lanes]
    return x.reshape(two * count * size, x.shape[-1])


def key_value_kernel(
    spots, near, far, mask, cosine, sine, key_decay, kw0, kw1, vw0, vw1,
    key_pre, keys, values, state, wk, wv, sems
):
    @pl.when(pl.program_id(0) == 0)
    def _():
        each_block(spots, [(0, 0, kw0, kw1, wk, sems.at[0]), (1, 0, vw0, vw1, wv, sems.at[1])])

    count, size = near.shape[0], near.shape[1]
    x = both(near[...], far[...])
    valid = get(mask)
    head = cosine.shape[-1]
    pre = mm(x, wk[...])
    val_pre = mm(x, wv[...])
    for h in range(pre.shape[-1] // head):
        lanes = slice(h * head, (h + 1) * head)
        kp = pre[:, lanes]
        put(key_pre, lanes, kp)
        key = (valid * turn(kp * jax.nn.sigmoid(kp), cosine[...], sine[...])).astype(BF16)
        val = (valid * val_pre[:, lanes]).astype(BF16)
        put(keys, lanes, key)
        put(values, lanes, val)
        scaled = (key.astype(F32) * key_decay[:, lanes]).astype(BF16)
        for s in range(count):
            state[s, h] = mm(
                slot_rows(scaled, s, size, count), slot_rows(val, s, size, count), TN
            ).astype(BF16)


def query_kernel(
    spots, near, far, mask, cosine, sine, grid, keys, values, w0, w1,
    query_pre, queries, modulate, intra, wq, wm, sems
):
    @pl.when(pl.program_id(0) == 0)
    def _():
        each_block(spots, [(0, 0, w0, w1, wq, sems.at[0]), (0, 1, w0, w1, wm, sems.at[1])])

    count, size = near.shape[0], near.shape[1]
    x = both(near[...], far[...])
    valid = get(mask)
    head = cosine.shape[-1]
    pre = mm(x, wq[...])
    mod = mm(x, wm[...])
    for h in range(pre.shape[-1] // head):
        lanes = slice(h * head, (h + 1) * head)
        qp = pre[:, lanes]
        put(query_pre, lanes, qp)
        put(modulate, lanes, mod[:, lanes] * valid)
        q = turn(qp * jax.nn.sigmoid(qp), cosine[...], sine[...]).astype(BF16)
        put(queries, lanes, q)
        k, v = get(keys, lanes), get(values, lanes)
        parts = []
        for s in range(count):
            scores = mm(slot_rows(q, s, size, count), slot_rows(k, s, size, count), NT) * grid[h]
            parts.append(mm(scores.astype(BF16), slot_rows(v, s, size, count)))
        put(intra, lanes, slot_back(parts, size))


def load_states(spots, pieces, held, sems):
    member = spots[2, 0, 0]
    copies = [
        pltpu.make_async_copy(p, held.at[member ^ k], sems.at[k]) for k, p in enumerate(pieces)
    ]
    for c in copies:
        c.start()
    for c in copies:
        c.wait()


def mixed_kernel(
    spots, queries, intra, modulate, query_decay, s0, s1, s2, s3, w0, w1,
    mixed, gated, near_out, far_out, wo, held, sems, state_sems
):
    @pl.when(pl.program_id(0) == 0)
    def _():
        load_states(spots, (s0, s1, s2, s3), held, state_sems)
        each_block(spots, [(0, 0, w0, w1, wo, sems)])

    step = pl.program_id(0)
    _, count, size, width = queries.shape
    heads = held.shape[2]
    head = width // heads
    gates = []
    for h in range(heads):
        lanes = slice(h * head, (h + 1) * head)
        q = (get(queries, lanes).astype(F32) * query_decay[:, lanes]).astype(BF16)
        parts = [mm(slot_rows(q, s, size, count), held[step, s, h]) for s in range(count)]
        mix = get(intra, lanes) + slot_back(parts, size)
        put(mixed, lanes, mix)
        scale = lax.rsqrt(jnp.mean(mix * mix, axis=-1, keepdims=True) + EPS)
        gates.append((mix * scale * get(modulate, lanes)).astype(BF16))
    gate = jnp.concatenate(gates, axis=1)
    put(gated, slice(None), gate)
    out = mm(gate, wo[...], NT)
    near_out[...] = out[: count * size].reshape(near_out.shape)
    far_out[...] = out[count * size :].astype(BF16).reshape(far_out.shape)


def mixed_back_kernel(
    spots, near, far, mixed, modulate, queries, query_pre, keys, values, mask, cosine, sine,
    query_decay, grid, s0, s1, s2, s3, w0, w1,
    modulate_grad, query_grad, key_grad, value_grad, state_grad, wo, held, sems, state_sems
):
    @pl.when(pl.program_id(0) == 0)
    def _():
        load_states(spots, (s0, s1, s2, s3), held, state_sems)
        each_block(spots, [(0, 0, w0, w1, wo, sems)])

    step = pl.program_id(0)
    _, count, size, width = queries.shape
    heads = held.shape[2]
    head = width // heads
    gate_grad = mm(both(near[...], far[...]), wo[...])
    valid = get(mask)
    for h in range(heads):
        lanes = slice(h * head, (h + 1) * head)
        mix = get(mixed, lanes)
        scale = lax.rsqrt(jnp.mean(mix * mix, axis=-1, keepdims=True) + EPS)
        gg = gate_grad[:, lanes]
        put(modulate_grad, lanes, gg * valid * (mix * scale))
        cot = gg * get(modulate, lanes)
        inner = jnp.mean(mix * cot, axis=-1, keepdims=True)
        gm = (scale * cot - mix * (scale * scale * scale * inner)).astype(BF16)
        q, k, v = get(queries, lanes), get(keys, lanes), get(values, lanes)
        qs = (q.astype(F32) * query_decay[:, lanes]).astype(BF16)
        gq, gk, gv = [], [], []
        for s in range(count):
            pick = lambda x: slot_rows(x, s, size, count)
            gms, qq, kk, vv = pick(gm), pick(q), pick(k), pick(v)
            gs = (mm(gms, vv, NT) * grid[h]).astype(BF16)
            sc = (mm(qq, kk, NT) * grid[h]).astype(BF16)
            gv.append(mm(sc, gms, TN))
            gk.append(mm(gs, qq, TN))
            decay = slot_rows(query_decay[:, lanes], s, size, count)
            gq.append(mm(gs, kk) + mm(gms, held[step, s, h], NT) * decay)
            state_grad[s, h] = mm(pick(qs), gms, TN).astype(BF16)
        put(key_grad, lanes, slot_back(gk, size))
        put(value_grad, lanes, slot_back(gv, size))
        qp = get(query_pre, lanes)
        sg = jax.nn.sigmoid(qp)
        slope = sg + qp * sg * (1.0 - sg)
        put(query_grad, lanes, turn(slot_back(gq, size), cosine[...], -sine[...]) * slope)


def rows_kernel(spots, query_grad, modulate_grad, w0, w1, out, wq, wm, sems):
    @pl.when(pl.program_id(0) == 0)
    def _():
        each_block(spots, [(0, 0, w0, w1, wq, sems.at[0]), (0, 1, w0, w1, wm, sems.at[1])])

    put(out, slice(None), mm(get(query_grad), wq[...], NT) + mm(get(modulate_grad), wm[...], NT))


def key_back_kernel(
    spots, key_grad, value_grad, keys, values, key_pre, mask, cosine, sine, key_decay, rows_in,
    g0, g1, g2, g3, kw0, kw1, vw0, vw1,
    key_out, value_out, near_out, far_out, wk, wv, held, sems, state_sems
):
    @pl.when(pl.program_id(0) == 0)
    def _():
        load_states(spots, (g0, g1, g2, g3), held, state_sems)
        each_block(spots, [(0, 0, kw0, kw1, wk, sems.at[0]), (1, 0, vw0, vw1, wv, sems.at[1])])

    step = pl.program_id(0)
    _, count, size, width = keys.shape
    heads = held.shape[2]
    head = width // heads
    valid = get(mask)
    gks, gvs = [], []
    for h in range(heads):
        lanes = slice(h * head, (h + 1) * head)
        decay = key_decay[:, lanes]
        k, v = get(keys, lanes), get(values, lanes)
        scaled = (k.astype(F32) * decay).astype(BF16)
        pk = [mm(slot_rows(v, s, size, count), held[step, s, h], NT) for s in range(count)]
        pv = [mm(slot_rows(scaled, s, size, count), held[step, s, h]) for s in range(count)]
        gk = get(key_grad, lanes) + slot_back(pk, size) * decay
        gv = get(value_grad, lanes) + slot_back(pv, size)
        kp = get(key_pre, lanes)
        sg = jax.nn.sigmoid(kp)
        slope = sg + kp * sg * (1.0 - sg)
        gks.append((turn(gk * valid, cosine[...], -sine[...]) * slope).astype(BF16))
        gvs.append((gv * valid).astype(BF16))
    gk, gv = jnp.concatenate(gks, axis=1), jnp.concatenate(gvs, axis=1)
    put(key_out, slice(None), gk)
    put(value_out, slice(None), gv)
    out = get(rows_in) + mm(gk, wk[...], NT) + mm(gv, wv[...], NT)
    near_out[...] = out[: count * size].reshape(near_out.shape)
    far_out[...] = out[count * size :].astype(BF16).reshape(far_out.shape)


def outer_kernel(order, spots, near, far, *refs):
    count = (len(refs) - 4) // 1
    grads, (keep, send, whole, sems) = refs[:count], refs[count:]
    rows = near.shape[0] * near.shape[1]
    width = near.shape[2]
    tile = 256
    for c in range(0, width, tile):
        a = near[:, :, c : c + tile].reshape(rows, tile)
        b = far[:, :, c : c + tile].reshape(rows, tile)
        for k, g in enumerate(grads):
            g0 = g[0].reshape(rows, -1)
            g1 = g[1].reshape(rows, -1)
            whole[k, c : c + tile, :] = (mm(a, g0, TN) + mm(b, g1, TN)).astype(BF16)
    each_block(
        spots, [(order, k, keep, send, whole.at[k], sems.at[k]) for k in range(count)], out=True
    )


ANY = pl.BlockSpec(memory_space=pl.ANY)
VMEM = pl.BlockSpec(memory_space=pltpu.VMEM)


def run(kernel, name, spots, inputs, outputs, scratch, steps, flops):
    def spec(shape, kind):
        if kind == "any":
            return ANY
        if kind == "rows":
            size = shape[0] // steps
            return pl.BlockSpec((size, *shape[1:]), lambda i, _: (i,) + (0,) * (len(shape) - 1))
        if kind == "pair":
            size = shape[1] // steps
            return pl.BlockSpec(
                (2, size, *shape[2:]), lambda i, _: (0, i) + (0,) * (len(shape) - 2)
            )
        return pl.BlockSpec(shape, lambda i, _: (0,) * len(shape))

    moved = sum(a.size * a.dtype.itemsize for a, _ in inputs)
    moved += sum(math.prod(s) * jnp.dtype(d).itemsize for s, d, _ in outputs)
    return pl.pallas_call(
        kernel,
        out_shape=[jax.ShapeDtypeStruct(s, d) for s, d, _ in outputs],
        grid_spec=pltpu.PrefetchScalarGridSpec(
            num_scalar_prefetch=1,
            grid=(steps,),
            in_specs=[spec(a.shape, kind) for a, kind in inputs],
            out_specs=[spec(s, kind) for s, _, kind in outputs],
            scratch_shapes=scratch,
        ),
        compiler_params=pltpu.CompilerParams(vmem_limit_bytes=40 * 2**20),
        cost_estimate=pl.CostEstimate(flops=flops, bytes_accessed=moved, transcendentals=0),
        name=name,
    )(spots, *[a for a, _ in inputs])


def carried(local, block_decay, reverse):
    narrow_count = lax.axis_size("narrow")
    z_count = lax.axis_size("wide") // 2
    n, w = lax.axis_index("narrow"), lax.axis_index("wide")
    member = 2 * (w % 2) + n // 2
    masks = [0, 2, narrow_count, narrow_count + 2]
    slots = local.shape[0]
    share = slots // 4
    rank = lambda m: 3 - m if reverse else m
    log_decay = jnp.log(block_decay)
    power = lambda e: jnp.exp(e * log_decay)[None, :, None, None]

    def part(m):
        return lax.dynamic_slice_in_dim(local, m * share, share, 0)

    held = [part(member)] + [exchange(part(member ^ k), masks[k]) for k in range(1, 4)]
    held = [h.astype(F32) for h in held]
    ranks = [rank(member ^ k) for k in range(4)]
    total = sum(power((3 - ranks[k]).astype(F32)) * held[k] for k in range(4))
    before, span, step = 0.0, total, 1
    while step < z_count:
        got = shift_z(span.astype(BF16), step, reverse).astype(F32)
        before = before + power(4.0 * (step - 1)) * got
        span = span + power(4.0 * step) * got
        step *= 2
    sent = []
    for k in range(4):
        state = power(ranks[k].astype(F32)) * before
        for j in range(4):
            gap = (ranks[k] - 1 - ranks[j]).astype(F32)
            state = state + jnp.where(gap >= 0, power(jnp.maximum(gap, 0.0)), 0.0) * held[j]
        sent.append(state.astype(BF16))
    return [sent[0]] + [exchange(sent[k], masks[k]) for k in range(1, 4)]


def on_device(
    layer_input,
    query_weight,
    key_weight,
    value_weight,
    modulate_weight,
    output_weight,
    gate_matrix,
    lift_matrix,
    down_matrix,
    decay_factor,
    valid_lengths,
    output_cotangent,
):
    narrow_count, wide_count = lax.axis_size("narrow"), lax.axis_size("wide")
    wide_index, narrow_index = lax.axis_index("wide"), lax.axis_index("narrow")
    core, side = narrow_index % 2, narrow_index // 2
    slots, quarter, width = layer_input.shape
    block = 2 * quarter
    rows, cols = query_weight.shape
    heads = 2 * decay_factor.shape[0]
    head_size = cols // decay_factor.shape[0]
    x_mask = 2
    wide_masks = []
    bit = narrow_count
    while bit < narrow_count * wide_count:
        wide_masks.append(bit)
        bit *= 2
    y_mask, z_masks = wide_masks[0], wide_masks[:0:-1]
    order_yx = z_masks + [y_mask, x_mask]
    order_xy = z_masks + [x_mask, y_mask]
    members = 1 << len(order_yx)
    half = members // 2

    base = wide_index * (quarter * narrow_count) + side * block
    offsets = jnp.stack(
        [core * quarter + jnp.arange(quarter), (1 - core) * quarter + jnp.arange(quarter)]
    ).astype(jnp.int32)
    mask = ((base + offsets)[:, None, :] < valid_lengths[None, :, None]).astype(F32)
    mask_rows = mask[0][:, :, None]
    mask_wide = jnp.broadcast_to(mask[..., None], (2, slots, quarter, head_size))
    member = 2 * (wide_index % 2) + side
    spots = jnp.concatenate(
        [
            block_spots(order_xy)[None],
            block_spots(order_yx)[None],
            jnp.broadcast_to(member, (1, members, 2)).astype(jnp.int32),
        ]
    )

    def core_sum(near, far):
        return near + exchange(far, 1).astype(F32)

    other_decay = exchange(decay_factor, x_mask)
    decay = jnp.concatenate(
        [jnp.where(side == 0, decay_factor, other_decay), jnp.where(side == 0, other_decay, decay_factor)]
    )
    log_decay = jnp.log(decay)
    block_decay = jnp.exp(block * log_decay)
    steps = 4
    count = slots // steps

    def table(values):
        lanes = values.shape[-1]
        return jnp.broadcast_to(values[:, None], (2, count, quarter, lanes)).reshape(-1, lanes)

    half_head = head_size // 2
    frequency = jnp.exp(-math.log(10000.0) * jnp.arange(half_head, dtype=F32) / half_head)
    phase = (base + offsets).astype(F32)[..., None] * frequency
    cosine, sine = jnp.cos(phase), jnp.sin(phase)
    cosine = table(jnp.concatenate([cosine, cosine], axis=-1))
    sine = table(jnp.concatenate([-sine, sine], axis=-1))
    spot = offsets.astype(F32)
    log_lanes = jnp.repeat(log_decay, head_size)
    query_decay = table(jnp.exp((spot[..., None] + 1.0) * log_lanes))
    key_decay = table(jnp.exp((block - 1.0 - spot[..., None]) * log_lanes))
    flat = spot.reshape(-1)
    gap = flat[:, None] - flat[None, :]
    decay_grid = jnp.where(
        gap[None] >= 0.0, jnp.exp(jnp.maximum(gap, 0.0)[None] * log_decay[:, None, None]), 0.0
    )

    def halves(x, masks):
        held = gather_plane(x, masks[:-1])
        return held, exchange(held, masks[-1])

    def bundle(*weights):
        return jnp.stack(weights)

    key_value = gather_plane(bundle(key_weight, value_weight), z_masks)
    key_near = gather_more(key_value[:, :1], [x_mask])
    value_near = gather_more(key_value[:, 1:], [y_mask])
    key_parts = (key_near, exchange(key_near, y_mask))
    value_parts = (value_near, exchange(value_near, x_mask))
    query_parts = halves(bundle(query_weight, modulate_weight), order_xy)
    output_parts = halves(bundle(output_weight), order_xy)
    gate_t = gather_hidden(gate_matrix.T, order_yx, False)
    lift_t = gather_hidden(lift_matrix.T, order_xy, True)
    down_t = gather_hidden(down_matrix.T, order_yx, False)

    input_rows = layer_input.astype(F32)
    normed = simple_norm(input_rows).astype(BF16)
    normed_pair = (normed, exchange(normed, 1))
    inner_width = heads * head_size
    chip_shape = (2, slots, quarter, inner_width)
    row_shape = (slots, quarter, width)
    state_shape = (slots, heads, head_size, head_size)
    square_flops = 2 * 2 * slots * quarter * width * inner_width
    wide_scratch = pltpu.VMEM((width, inner_width), BF16)
    held_scratch = pltpu.VMEM((4, slots // 4, heads, head_size, head_size), BF16)
    dma = pltpu.SemaphoreType.DMA

    key_pre, keys, values, local_state = run(
        key_value_kernel, "key_value", spots,
        [
            (normed_pair[0], "rows"), (normed_pair[1], "rows"), (mask_wide, "pair"),
            (cosine, "whole"), (sine, "whole"), (key_decay, "whole"),
            (key_parts[0], "any"), (key_parts[1], "any"),
            (value_parts[0], "any"), (value_parts[1], "any"),
        ],
        [
            (chip_shape, F32, "pair"), (chip_shape, BF16, "pair"), (chip_shape, BF16, "pair"),
            (state_shape, BF16, "rows"),
        ],
        [wide_scratch, wide_scratch, dma((2, members))],
        steps, 2 * square_flops,
    )
    state_parts = carried(local_state, block_decay, False)
    query_pre, queries, modulate, intra = run(
        query_kernel, "query", spots,
        [
            (normed_pair[0], "rows"), (normed_pair[1], "rows"), (mask_wide, "pair"),
            (cosine, "whole"), (sine, "whole"), (decay_grid, "whole"),
            (keys, "pair"), (values, "pair"), (query_parts[0], "any"), (query_parts[1], "any"),
        ],
        [
            (chip_shape, F32, "pair"), (chip_shape, BF16, "pair"), (chip_shape, F32, "pair"),
            (chip_shape, F32, "pair"),
        ],
        [wide_scratch, wide_scratch, dma((2, members))],
        steps, 2 * square_flops,
    )
    state_inputs = [(p, "any") for p in state_parts]
    output_inputs = [(p, "any") for p in output_parts]
    mixed, gated, near_att, far_att = run(
        mixed_kernel, "mixed", spots,
        [
            (queries, "pair"), (intra, "pair"), (modulate, "pair"), (query_decay, "whole"),
            *state_inputs, *output_inputs,
        ],
        [
            (chip_shape, F32, "pair"), (chip_shape, BF16, "pair"), (row_shape, F32, "rows"),
            (row_shape, BF16, "rows"),
        ],
        [wide_scratch, held_scratch, dma((members,)), dma((4,))],
        steps, square_flops,
    )
    middle = input_rows + core_sum(near_att, far_att)

    def pair(mine):
        return jnp.stack([mine, exchange(mine, 1)])

    normed_two = pair(simple_norm(middle).astype(BF16))
    cotangent = output_cotangent.astype(F32)
    branch_grad = pair((mask_rows * cotangent).astype(BF16))

    def hidden(rows_in, matrix):
        return jnp.einsum("pbld,fd->pblf", rows_in, matrix, preferred_element_type=F32)

    def outer(a, b):
        return jnp.einsum("pblf,pbld->fd", a, b, preferred_element_type=F32).astype(BF16)

    gate_pre = hidden(normed_two, gate_t)
    lift_pre = hidden(normed_two, lift_t)
    inner_grad = hidden(branch_grad, down_t)
    gate_act = apply_swish(gate_pre)
    inner = (gate_act * lift_pre).astype(BF16)
    gate_grad = (inner_grad * lift_pre * swish_slope(gate_pre)).astype(BF16)
    lift_grad = (inner_grad * gate_act).astype(BF16)
    normed_grad = jnp.einsum("pblf,fd->pbld", gate_grad, gate_t, preferred_element_type=F32)
    normed_grad = normed_grad + jnp.einsum(
        "pblf,fd->pbld", lift_grad, lift_t, preferred_element_type=F32
    )
    middle_grad = cotangent + norm_backward(
        middle, core_sum(normed_grad[0], normed_grad[1].astype(BF16))
    )
    branch = jnp.einsum("pblf,fd->pbld", inner, down_t, preferred_element_type=F32)
    branch = core_sum(branch[0], branch[1].astype(BF16))
    layer_output = (middle + mask_rows * branch).astype(BF16)

    def scattered(grad, masks, swapped):
        if swapped:
            grad = jnp.swapaxes(grad.reshape(2, 2, -1, width), 0, 1)
        return scatter_plane(grad.reshape(members, -1, width), masks).T

    gate_gradient = scattered(outer(gate_grad, normed_two), order_yx, False)
    lift_gradient = scattered(outer(lift_grad, normed_two), order_xy, True)
    down_gradient = scattered(outer(inner, branch_grad), order_yx, False)

    attended_grad = middle_grad.astype(BF16)
    attended_pair = (attended_grad, exchange(attended_grad, 1))
    modulate_grad, query_grad, key_grad, value_grad, state_grad = run(
        mixed_back_kernel, "mixed_back", spots,
        [
            (attended_pair[0], "rows"), (attended_pair[1], "rows"), (mixed, "pair"),
            (modulate, "pair"), (queries, "pair"), (query_pre, "pair"), (keys, "pair"),
            (values, "pair"), (mask_wide, "pair"), (cosine, "whole"), (sine, "whole"),
            (query_decay, "whole"), (decay_grid, "whole"), *state_inputs, *output_inputs,
        ],
        [
            (chip_shape, BF16, "pair"), (chip_shape, BF16, "pair"), (chip_shape, F32, "pair"),
            (chip_shape, F32, "pair"), (state_shape, BF16, "rows"),
        ],
        [wide_scratch, held_scratch, dma((members,)), dma((4,))],
        steps, 2 * square_flops,
    )
    later_inputs = [(p, "any") for p in carried(state_grad, block_decay, True)]
    part_shape = (half, 1, rows, cols)

    def square(name, order, a, *grads):
        shape = (half, len(grads), rows, cols)
        return run(
            functools.partial(outer_kernel, order), name, spots,
            [(a[0], "whole"), (a[1], "whole"), *[(g, "whole") for g in grads]],
            [(shape, BF16, "any"), (shape, BF16, "any")],
            [pltpu.VMEM((len(grads), width, inner_width), BF16), dma((len(grads), members))],
            1, len(grads) * square_flops,
        )

    def finish(parts, masks):
        total = (parts[0].astype(F32) + exchange(parts[1], masks[-1]).astype(F32)).astype(BF16)
        return scatter_plane(total, masks[:-1])

    output_gradient = finish(square("output_outer", 0, attended_pair, gated), order_xy)[0]
    (query_rows,) = run(
        rows_kernel, "query_rows", spots,
        [(query_grad, "pair"), (modulate_grad, "pair"), (query_parts[0], "any"), (query_parts[1], "any")],
        [((2, *row_shape), F32, "pair")],
        [wide_scratch, wide_scratch, dma((2, members))],
        steps, 2 * square_flops,
    )
    query_gradient, modulate_gradient = finish(
        square("query_outer", 0, normed_pair, query_grad, modulate_grad), order_xy
    )
    key_out, value_out, near_rows, far_rows = run(
        key_back_kernel, "key_back", spots,
        [
            (key_grad, "pair"), (value_grad, "pair"), (keys, "pair"), (values, "pair"),
            (key_pre, "pair"), (mask_wide, "pair"), (cosine, "whole"), (sine, "whole"),
            (key_decay, "whole"), (query_rows, "pair"), *later_inputs,
            (key_parts[0], "any"), (key_parts[1], "any"),
            (value_parts[0], "any"), (value_parts[1], "any"),
        ],
        [
            (chip_shape, BF16, "pair"), (chip_shape, BF16, "pair"), (row_shape, F32, "rows"),
            (row_shape, BF16, "rows"),
        ],
        [wide_scratch, wide_scratch, held_scratch, dma((2, members)), dma((4,))],
        steps, 2 * square_flops,
    )
    key_gradient = finish(square("key_outer", 0, normed_pair, key_out), order_xy)[0]
    value_gradient = finish(square("value_outer", 1, normed_pair, value_out), order_yx)[0]
    input_gradient = middle_grad + norm_backward(input_rows, core_sum(near_rows, far_rows))
    return (
        layer_output,
        input_gradient,
        query_gradient,
        key_gradient,
        value_gradient,
        modulate_gradient,
        output_gradient,
        gate_gradient,
        lift_gradient,
        down_gradient,
    )


def solution(mesh):
    placed = (
        P(None, ("wide", "narrow"), None),
        P("wide", "narrow"),
        P("wide", "narrow"),
        P("wide", "narrow"),
        P("wide", "narrow"),
        P("wide", "narrow"),
        P(None, ("wide", "narrow")),
        P(None, ("wide", "narrow")),
        P(None, ("wide", "narrow")),
        P("narrow"),
        P(),
        P(None, ("wide", "narrow"), None),
    )
    return jax.shard_map(
        on_device,
        mesh=mesh,
        in_specs=placed,
        out_specs=(
            P(None, ("wide", "narrow"), None),
            P(None, ("wide", "narrow"), None),
            P("wide", "narrow"),
            P("wide", "narrow"),
            P("wide", "narrow"),
            P("wide", "narrow"),
            P("wide", "narrow"),
            P(None, ("wide", "narrow")),
            P(None, ("wide", "narrow")),
            P(None, ("wide", "narrow")),
        ),
        check_vma=False,
    )
```

time: 627 us -> 517 us (0.82)
  local copies, waits for them, and re-layouts: 107 us -> 24.8 us
  Pallas kernels: 0 us -> 64.1 us
  matrix products: 103 us -> 47.2 us
  other arithmetic: 78.1 us -> 41.8 us
  waiting for transfers between devices: 230 us -> 244 us
  starting transfers between devices: 98.1 us -> 85.4 us
    pallas_call x0 -> x10, Pallas kernels: none -> 64.1 us  [run(): pl.pallas_call(kernel, out_shape=[jax.ShapeDtypeStruct(s, d) for s, d, _...]
    dot_general x36 -> x9, matrix products: 103 us -> 47.2 us  [the longest x3 21.3 us: hidden(): jnp.einsum('pbld,fd->pblf', rows_in, matrix, preferred_element_type=F32)]
    dynamic_update_slice x86 -> x0, local copies, waits for them, and re-layouts: 42.7 us -> none  [the longest x78 33.9 us: to_canonical(): out = lax.dynamic_update_slice(out, blocks[i], (w * rows, side * cols))]
    unnamed x315 -> x160, local copies, waits for them, and re-layouts: 30.2 us -> 16 us
    ppermute x85 -> x75, waiting for transfers between devices: 225 us -> 237 us  [exchange(): return lax.ppermute(x, AXES, [(i, i ^ mask) for i in range(count)])]
    concatenate x25 -> x22, other arithmetic: 18.8 us -> 8.79 us  [the longest x19 7.28 us: gather_more(): held = jnp.concatenate([held, exchange(held, mask)], axis=0)]
    ppermute x6 -> x0, local copies, waits for them, and re-layouts: 9.42 us -> none  [exchange(): return lax.ppermute(x, AXES, [(i, i ^ mask) for i in range(count)])]
    ppermute x85 -> x75, starting transfers between devices: 85.6 us -> 76.8 us  [exchange(): return lax.ppermute(x, AXES, [(i, i ^ mask) for i in range(count)])]
  transfers between devices with their start and end apart: 89 -> 79, of which waited for: 43 -> 32; matrix products, arithmetic and copies ran while one was open for 38% -> 13% of each run, Pallas kernels for 0% -> 13%
where the time goes in v2:
time: 517 us; the launch traced here: 510 us
  waiting for transfers between devices  244 us (47%)
  starting transfers between devices  85.4 us (17%)
  Pallas kernels  64.1 us (12%)
  matrix products  47.2 us (9%)
  other arithmetic  41.8 us (8%)
  local copies, waits for them, and re-layouts  24.8 us (5%)
    ppermute x75, waiting for transfers between devices, exchange(): return lax.ppermute(x, AXES, [(i, i ^ mask) for i in range(count)])  237 us
    ppermute x75, starting transfers between devices, exchange(): return lax.ppermute(x, AXES, [(i, i ^ mask) for i in range(count)])  76.8 us
    pallas_call x10, Pallas kernels, run(): pl.pallas_call(kernel, out_shape=[jax.ShapeDtypeStruct(s, d) for s, d, _...  64.1 us
    dot_general x3, matrix products, hidden(): jnp.einsum('pbld,fd->pblf', rows_in, matrix, preferred_element_type=F32)  21.3 us
    unnamed x160, local copies, waits for them, and re-layouts  16 us
    dot_general x3, matrix products, outer(): jnp.einsum('pblf,pbld->fd', a, b, preferred_element_type=F32).astype(BF16)  12.3 us
  transfers between devices with their start and end apart: 79, of which 32 were waited for; matrix products, arithmetic and copies ran while one was open for 13% of the time, Pallas kernels for 13%

profile of v2, /device:TPU:0, one launch (start us, length us, event | category | flops | bytes accessed | tf_op | source)
XLA Modules:
  0.0 510.5 jit_solution(2716515605102660335)
XLA Ops:
  26.2 6.3 %collective-permute-done.3 = bf16[2,2,128,256]{3,2,1,0:T(8,128)(2,1)S(1)} collective-permute-done((bf16[2,2,128,256]{3,2,1,0:T(8,128)(2,1)S(1)}, bf16[2,2,128,256]{3,2,1,0:T(8,128)(2,1)S(1)}, u32[]{:S(2)}, u32[]{:S(2)}) %collective-permute-start.3) | collective-permute-done | bytes 262176 | tf_op jit(solution)/shard_map/ppermute | solution.py:38
  49.5 8.7 %collective-permute-done.26 = bf16[1,88,1024]{2,1,0:T(8,128)(2,1)S(1)} collective-permute-done((bf16[1,88,1024]{2,1,0:T(8,128)(2,1)S(1)}, bf16[1,88,1024]{2,1,0:T(8,128)(2,1)S(1)}, u32[]{:S(2)}, u32[]{:S(2)}) %collective-permute-start.26) | collective-permute-done | bytes 180256 | tf_op jit(solution)/shard_map/ppermute | solution.py:38
  60.8 6.0 %key_value.1 = (f32[2,8,64,512]{3,2,1,0:T(8,128)S(1)}, bf16[2,8,64,512]{3,2,1,0:T(8,128)(2,1)S(1)}, bf16[2,8,64,512]{3,2,1,0:T(8,128)(2,1)S(1)}, bf16[8,4,128,128]{3,2,1,0:T(8,128)(2,1)S(1)}) custom-call(s32[3,16,2]{2,1,0:T(8,128)S(1)} %copy.35.spots, bf16[8,64,1024]{2,1,0:T(8,128)(2,1)S(1)} %fusion.9.near, ...), custom_call_target="tpu_custom_call" | custom-call | flops 2147483648 | bytes 10747904 | tf_op jit(solution)/shard_map/key_value/pallas_call | solution.py:386
  108.4 23.8 %collective-permute-done.23.w1 = bf16[8,1,128,256]{3,2,1,0:T(8,128)(2,1)S(1)} collective-permute-done((bf16[8,1,128,256]{3,2,1,0:T(8,128)(2,1)S(1)}, bf16[8,1,128,256]{3,2,1,0:T(8,128)(2,1)S(1)}, u32[]{:S(2)}, u32[]{:S(2)}) %collective-permute-start.23) | collective-permute-done | bytes 524320 | tf_op jit(solution)/shard_map/ppermute | solution.py:38
  135.8 11.0 %query.1 = (f32[2,8,64,512]{3,2,1,0:T(8,128)S(1)}, bf16[2,8,64,512]{3,2,1,0:T(8,128)(2,1)S(1)}, f32[2,8,64,512]{3,2,1,0:T(8,128)S(1)}, f32[2,8,64,512]{3,2,1,0:T(8,128)}) custom-call(s32[3,16,2]{2,1,0:T(8,128)S(1)} %copy.35.spots, bf16[8,64,1024]{2,1,0:T(8,128)(2,1)S(1)} %fusion.9.near, bf16[8,64,1024]{2,1,0:T(8,128)(2,1)S(1)} %collective-permute-done.far, ...), custom_call_target="tpu_custom_call" | custom-call | flops 2147483648 | bytes 14680064 | tf_op jit(solution)/shard_map/query/pallas_call | solution.py:386
  161.5 5.9 %collective-permute-done.32 = bf16[4,88,1024]{2,1,0:T(8,128)(2,1)S(1)} collective-permute-done((bf16[4,88,1024]{2,1,0:T(8,128)(2,1)}, bf16[4,88,1024]{2,1,0:T(8,128)(2,1)S(1)}, u32[]{:S(2)}, u32[]{:S(2)}) %collective-permute-start.32) | collective-permute-done | bytes 720928 | tf_op jit(solution)/shard_map/ppermute | solution.py:38
  168.5 6.6 %collective-permute-done.36 = bf16[4,88,1024]{2,1,0:T(8,128)(2,1)S(1)} collective-permute-done((bf16[4,88,1024]{2,1,0:T(8,128)(2,1)S(1)}, bf16[4,88,1024]{2,1,0:T(8,128)(2,1)S(1)}, u32[]{:S(2)}, u32[]{:S(2)}) %collective-permute-start.36) | collective-permute-done | bytes 720928 | tf_op jit(solution)/shard_map/ppermute | solution.py:38
  180.3 25.1 %collective-permute-done.33 = bf16[8,88,1024]{2,1,0:T(8,128)(2,1)S(1)} collective-permute-done((bf16[8,88,1024]{2,1,0:T(8,128)(2,1)S(1)}, bf16[8,88,1024]{2,1,0:T(8,128)(2,1)S(1)}, u32[]{:S(2)}, u32[]{:S(2)}) %collective-permute-start.33) | collective-permute-done | bytes 1441824 | tf_op jit(solution)/shard_map/ppermute | solution.py:38
  206.1 22.6 %collective-permute-done.37 = bf16[8,88,1024]{2,1,0:T(8,128)(2,1)S(1)} collective-permute-done((bf16[8,88,1024]{2,1,0:T(8,128)(2,1)S(1)}, bf16[8,88,1024]{2,1,0:T(8,128)(2,1)S(1)}, u32[]{:S(2)}, u32[]{:S(2)}) %collective-permute-start.37) | collective-permute-done | bytes 1441824 | tf_op jit(solution)/shard_map/ppermute | solution.py:38
  229.0 5.3 %fusion.85 = f32[2,8,64,1408]{3,2,1,0:T(8,128)} fusion(bf16[1408,1024,1,1]{1,0,3,2:T(8,128)(2,1)S(1)} %bitcast.182, bf16[1,8,64,1024]{3,2,1,0:T(8,128)(2,1)S(1)} %bitcast.184, bf16[1,8,64,1024]{3,2,1,0:T(8,128)(2,1)S(1)} %fusion.108), kind=kOutput, calls=%fused_computation.310 | convolution fusion | flops 2953838592 | bytes 10747904 | tf_op jit(solution)/shard_map/pbld,fd->pblf/dot_general | solution.py:604
  234.3 5.3 %fusion.84 = f32[2,8,64,1408]{3,2,1,0:T(8,128)} fusion(bf16[1408,1024,1,1]{1,0,3,2:T(8,128)(2,1)S(1)} %bitcast.160, bf16[1,8,64,1024]{3,2,1,0:T(8,128)(2,1)S(1)} %bitcast.185, bf16[1,8,64,1024]{3,2,1,0:T(8,128)(2,1)S(1)} %fusion.108), kind=kOutput, calls=%fused_computation.309 | convolution fusion | flops 2953838592 | bytes 10747904 | tf_op jit(solution)/shard_map/pbld,fd->pblf/dot_general | solution.py:604
  239.6 10.7 %multiply_convert_fusion.1 = (bf16[2,8,64,1408]{3,2,1,0:T(8,128)(2,1)}, bf16[2,8,64,1408]{3,2,1,0:T(8,128)(2,1)}, bf16[2,8,64,1408]{3,2,1,0:T(8,128)(2,1)}) fusion(f32[2,8,64,1408]{3,2,1,0:T(8,128)} %fusion.84, f32[2,8,64,1408]{3,2,1,0:T(8,128)} %fusion.85, bf16[1408,1024,1,1]{1,0,3,2:T(8,128)(2,1)S(1)} %bitcast.180, bf16[1,8,64,1024]{3,2,1,0:T(8,128)(2,1)} %bitcast.44, ...), kind=kOutput, calls=%fused_computation.4 | convolution fusion | flops 2974023680 | bytes 25165824 | tf_op jit(solution)/shard_map/pbld,fd->pblf/dot_general | solution.py:604
  250.4 5.4 %bitcast_convert_fusion = bf16[1408,1024]{1,0:T(8,128)(2,1)S(1)} fusion(bf16[2,8,64,1408]{3,2,1,0:T(8,128)(2,1)} %get-tuple-element.85, bf16[1,8,64,1024]{3,2,1,0:T(8,128)(2,1)} %bitcast.44, bf16[1,8,64,1024]{3,2,1,0:T(8,128)(2,1)S(1)} %copy-done.47), kind=kOutput, calls=%fused_computation | convolution fusion | flops 2955280384 | bytes 7864320 | tf_op jit(solution)/shard_map/pblf,pbld->fd/dot_general | solution.py:607
  286.2 26.5 %collective-permute-done.75 = bf16[8,88,1024]{2,1,0:T(8,128)(2,1)S(1)} collective-permute-done((bf16[8,88,1024]{2,1,0:T(8,128)(2,1)}, bf16[8,88,1024]{2,1,0:T(8,128)(2,1)S(1)}, u32[]{:S(2)}, u32[]{:S(2)}) %collective-permute-start.75) | collective-permute-done | bytes 1441824 | tf_op jit(solution)/shard_map/ppermute | solution.py:38
  318.2 25.4 %collective-permute-done.67 = bf16[8,88,1024]{2,1,0:T(8,128)(2,1)S(1)} collective-permute-done((bf16[8,88,1024]{2,1,0:T(8,128)(2,1)S(1)}, bf16[8,88,1024]{2,1,0:T(8,128)(2,1)S(1)}, u32[]{:S(2)}, u32[]{:S(2)}) %collective-permute-start.67) | collective-permute-done | bytes 1441824 | tf_op jit(solution)/shard_map/ppermute | solution.py:38
  350.0 15.5 %mixed_back.1 = (bf16[2,8,64,512]{3,2,1,0:T(8,128)(2,1)S(1)}, bf16[2,8,64,512]{3,2,1,0:T(8,128)(2,1)S(1)}, f32[2,8,64,512]{3,2,1,0:T(8,128)S(1)}, f32[2,8,64,512]{3,2,1,0:T(8,128)}, bf16[8,4,128,128]{3,2,1,0:T(8,128)(2,1)S(1)}) custom-call(s32[3,16,2]{2,1,0:T(8,128)S(1)} %copy.35.spots, bf16[8,64,1024]{2,1,0:T(8,128)(2,1)S(1)} %get-tuple-element.72.near, ...), custom_call_target="tpu_custom_call" | custom-call | flops 2147483648 | bytes 22544384 | tf_op jit(solution)/shard_map/mixed_back/pallas_call | solution.py:386
  366.5 5.3 %query_rows.1.rows_in = f32[2,8,64,1024]{3,2,1,0:T(8,128)S(1)} custom-call(s32[3,16,2]{2,1,0:T(8,128)S(1)} %copy.35.spots, bf16[2,8,64,512]{3,2,1,0:T(8,128)(2,1)S(1)} %get-tuple-element.52.query_grad.refs_0_, bf16[2,8,64,512]{3,2,1,0:T(8,128)(2,1)S(1)} %get-tuple-element.53.modulate_grad.refs_1_, bf16[8,2,128,256]{3,2,1,0:T(8,128)(2,1)S(1)} %pad_maximum_fusion.5.w0, ...), custom_call_target="tpu_custom_call" | custom-call | flops 2147483648 | bytes 8388608 | tf_op jit(solution)/shard_map/query_rows/pallas_call | solution.py:386
  385.3 7.7 %collective-permute-done.43 = bf16[2,4,128,128]{3,2,1,0:T(8,128)(2,1)S(1)} collective-permute-done((bf16[2,4,128,128]{3,2,1,0:T(8,128)(2,1)S(1)}, bf16[2,4,128,128]{3,2,1,0:T(8,128)(2,1)S(1)}, u32[]{:S(2)}, u32[]{:S(2)}) %collective-permute-start.43) | collective-permute-done | bytes 262176 | tf_op jit(solution)/shard_map/ppermute | solution.py:38
  396.7 10.2 %collective-permute-done.73 = bf16[2,88,1024]{2,1,0:T(8,128)(2,1)S(1)} collective-permute-done((bf16[2,88,1024]{2,1,0:T(8,128)(2,1)S(1)}, bf16[2,88,1024]{2,1,0:T(8,128)(2,1)S(1)}, u32[]{:S(2)}, u32[]{:S(2)}) %collective-permute-start.73) | collective-permute-done | bytes 360480 | tf_op jit(solution)/shard_map/ppermute | solution.py:38
  407.0 9.3 %collective-permute-done.69 = bf16[2,88,1024]{2,1,0:T(8,128)(2,1)S(1)} collective-permute-done((bf16[2,88,1024]{2,1,0:T(8,128)(2,1)S(1)}, bf16[2,88,1024]{2,1,0:T(8,128)(2,1)S(1)}, u32[]{:S(2)}, u32[]{:S(2)}) %collective-permute-start.69) | collective-permute-done | bytes 360480 | tf_op jit(solution)/shard_map/ppermute | solution.py:38
  423.8 9.8 %collective-permute-done.74 = bf16[1,88,1024]{2,1,0:T(8,128)(2,1)S(1)} collective-permute-done((bf16[1,88,1024]{2,1,0:T(8,128)(2,1)S(1)}, bf16[1,88,1024]{2,1,0:T(8,128)(2,1)S(1)}, u32[]{:S(2)}, u32[]{:S(2)}) %collective-permute-start.74) | collective-permute-done | bytes 180256 | tf_op jit(solution)/shard_map/ppermute | solution.py:38
  453.5 9.3 %key_back.1 = (bf16[2,8,64,512]{3,2,1,0:T(8,128)(2,1)S(1)}, bf16[2,8,64,512]{3,2,1,0:T(8,128)(2,1)S(1)}, f32[8,64,1024]{2,1,0:T(8,128)S(1)}, bf16[8,64,1024]{2,1,0:T(8,128)(2,1)S(1)}) custom-call(s32[3,16,2]{2,1,0:T(8,128)S(1)} %copy.35.spots, f32[2,8,64,512]{3,2,1,0:T(8,128)S(1)} %get-tuple-element.49.key_grad, ...), custom_call_target="tpu_custom_call" | custom-call | flops 2147483648 | bytes 22282240 | tf_op jit(solution)/shard_map/key_back/pallas_call | solution.py:386
  472.1 8.3 %collective-permute-done.59 = bf16[8,1,128,256]{3,2,1,0:T(8,128)(2,1)S(1)} collective-permute-done((bf16[8,1,128,256]{3,2,1,0:T(8,128)(2,1)S(1)}, bf16[8,1,128,256]{3,2,1,0:T(8,128)(2,1)S(1)}, u32[]{:S(2)}, u32[]{:S(2)}) %collective-permute-start.59) | collective-permute-done | bytes 524320 | tf_op jit(solution)/shard_map/ppermute | solution.py:38
  483.2 5.6 %collective-permute-done.52 = bf16[4,2,128,256]{3,2,1,0:T(8,128)(2,1)S(1)} collective-permute-done((bf16[4,2,128,256]{3,2,1,0:T(8,128)(2,1)S(1)}, bf16[4,2,128,256]{3,2,1,0:T(8,128)(2,1)S(1)}, u32[]{:S(2)}, u32[]{:S(2)}) %collective-permute-start.52) | collective-permute-done | bytes 524320 | tf_op jit(solution)/shard_map/ppermute | solution.py:38
  (452 shorter events, 232.2 us)
Async XLA Ops:
  10.2 48.0 %collective-permute-start = (bf16[8,64,1024]{2,1,0:T(8,128)(2,1)S(1)}, bf16[8,64,1024]{2,1,0:T(8,128)(2,1)S(1)}, u32[]{:S(2)}, u32[]{:S(2)}) collective-permute-start(bf16[8,64,1024]{2,1,0:T(8,128)(2,1)S(1)} %fusion.9.near), channel_id=1, source_target_pairs={{0,1},{1,0},{2,3},{3,2},{4,5},{5,4},{6,7},{7,6},{8,9},{9,8},{10,11... | collective-permute-start | bytes 3145736 | tf_op jit(solution)/shard_map/ppermute | solution.py:38
  10.4 36.1 %collective-permute-start.8 = (bf16[1,2,128,256]{3,2,1,0:T(8,128)(2,1)S(1)}, bf16[1,2,128,256]{3,2,1,0:T(8,128)(2,1)S(1)}, u32[]{:S(2)}, u32[]{:S(2)}) collective-permute-start(bf16[1,2,128,256]{3,2,1,0:T(8,128)(2,1)S(1)} %maximum_bitcast_fusion.1), channel_id=1, source_target_pairs={{0,16},{1,17},{2,18},{3,19},{4,20},{5,21},{6,22},{7,23},{8,24},{9,... | collective-permute-start | bytes 393224 | tf_op jit(solution)/shard_map/ppermute | solution.py:38
  10.8 34.8 %collective-permute-start.20 = (bf16[1,1,128,256]{3,2,1,0:T(8,128)(2,1)}, bf16[1,1,128,256]{3,2,1,0:T(8,128)(2,1)}, u32[]{:S(2)}, u32[]{:S(2)}) collective-permute-start(bf16[1,1,128,256]{3,2,1,0:T(8,128)(2,1)} %bitcast.17), channel_id=1, source_target_pairs={{0,16},{1,17},{2,18},{3,19},{4,20},{5,21},{6,22},{7,23},{8,24},{9,... | collective-permute-start | bytes 196616 | tf_op jit(solution)/shard_map/ppermute | solution.py:38
  76.2 31.3 %collective-permute-start.31 = (bf16[2,88,1024]{2,1,0:T(8,128)(2,1)S(1)}, bf16[2,88,1024]{2,1,0:T(8,128)(2,1)S(1)}, u32[]{:S(2)}, u32[]{:S(2)}) collective-permute-start(bf16[2,88,1024]{2,1,0:T(8,128)(2,1)S(1)} %pad_maximum_fusion.15), channel_id=1, source_target_pairs={{0,8},{1,9},{2,10},{3,11},{4,12},{5,13},{6,14},{7,15},{8,0},{9,1},... | collective-permute-start | bytes 1081352 | tf_op jit(solution)/shard_map/ppermute | solution.py:38
  92.0 42.7 %collective-permute-start.11 = (bf16[8,2,128,256]{3,2,1,0:T(8,128)(2,1)S(1)}, bf16[8,2,128,256]{3,2,1,0:T(8,128)(2,1)S(1)}, u32[]{:S(2)}, u32[]{:S(2)}) collective-permute-start(bf16[8,2,128,256]{3,2,1,0:T(8,128)(2,1)S(1)} %pad_maximum_fusion.5.w0), channel_id=1, source_target_pairs={{0,4},{1,5},{2,6},{3,7},{4,0},{5,1},{6,2},{7,3},{8,12},{9,13},{10,... | collective-permute-start | bytes 3145736 | tf_op jit(solution)/shard_map/ppermute | solution.py:38
  99.3 56.7 %collective-permute-start.35 = (bf16[2,88,1024]{2,1,0:T(8,128)(2,1)}, bf16[2,88,1024]{2,1,0:T(8,128)(2,1)S(1)}, u32[]{:S(2)}, u32[]{:S(2)}) collective-permute-start(bf16[2,88,1024]{2,1,0:T(8,128)(2,1)} %pad_maximum_fusion.16), channel_id=1, source_target_pairs={{0,8},{1,9},{2,10},{3,11},{4,12},{5,13},{6,14},{7,15},{8,0},{9,1},... | collective-permute-start | bytes 1081352 | tf_op jit(solution)/shard_map/ppermute | solution.py:38
  103.2 29.0 %collective-permute-start.23 = (bf16[8,1,128,256]{3,2,1,0:T(8,128)(2,1)S(1)}, bf16[8,1,128,256]{3,2,1,0:T(8,128)(2,1)S(1)}, u32[]{:S(2)}, u32[]{:S(2)}) collective-permute-start(bf16[8,1,128,256]{3,2,1,0:T(8,128)(2,1)S(1)} %pad_maximum_fusion.13.w0), channel_id=1, source_target_pairs={{0,4},{1,5},{2,6},{3,7},{4,0},{5,1},{6,2},{7,3},{8,12},{9,13},{10,... | collective-permute-start | bytes 1572872 | tf_op jit(solution)/shard_map/ppermute | solution.py:38
  105.9 42.3 %collective-permute-start.17 = (bf16[2,4,128,128]{3,2,1,0:T(8,128)(2,1)S(1)}, bf16[2,4,128,128]{3,2,1,0:T(8,128)(2,1)S(1)}, u32[]{:S(2)}, u32[]{:S(2)}) collective-permute-start(bf16[2,4,128,128]{3,2,1,0:T(8,128)(2,1)S(1)} %get-tuple-element.100), channel_id=1, source_target_pairs={{0,2},{1,3},{2,0},{3,1},{4,6},{5,7},{6,4},{7,5},{8,10},{9,11},{10,... | collective-permute-start | bytes 786440 | tf_op jit(solution)/shard_map/ppermute | solution.py:38
  107.5 40.6 %collective-permute-start.18 = (bf16[2,4,128,128]{3,2,1,0:T(8,128)(2,1)S(1)}, bf16[2,4,128,128]{3,2,1,0:T(8,128)(2,1)S(1)}, u32[]{:S(2)}, u32[]{:S(2)}) collective-permute-start(bf16[2,4,128,128]{3,2,1,0:T(8,128)(2,1)S(1)} %get-tuple-element.99), channel_id=1, source_target_pairs={{0,4},{1,5},{2,6},{3,7},{4,0},{5,1},{6,2},{7,3},{8,12},{9,13},{10,... | collective-permute-start | bytes 786440 | tf_op jit(solution)/shard_map/ppermute | solution.py:38
  148.2 91.4 %collective-permute-start.39 = (bf16[8,64,1024]{2,1,0:T(8,128)(2,1)}, bf16[8,64,1024]{2,1,0:T(8,128)(2,1)}, u32[]{:S(2)}, u32[]{:S(2)}) collective-permute-start(bf16[8,64,1024]{2,1,0:T(8,128)(2,1)} %fusion.7), channel_id=1, source_target_pairs={{0,1},{1,0},{2,3},{3,2},{4,5},{5,4},{6,7},{7,6},{8,9},{9,8},{10,11... | collective-permute-start | bytes 3145736 | tf_op jit(solution)/shard_map/ppermute | solution.py:38
  160.8 45.2 %collective-permute-start.29 = (bf16[8,88,1024]{2,1,0:T(8,128)(2,1)S(1)}, bf16[8,88,1024]{2,1,0:T(8,128)(2,1)S(1)}, u32[]{:S(2)}, u32[]{:S(2)}) collective-permute-start(bf16[8,88,1024]{2,1,0:T(8,128)(2,1)S(1)} %pad_maximum_fusion.2), channel_id=1, source_target_pairs={{0,2},{1,3},{2,0},{3,1},{4,6},{5,7},{6,4},{7,5},{8,10},{9,11},{10,... | collective-permute-start | bytes 4325384 | tf_op jit(solution)/shard_map/ppermute | solution.py:38
  167.6 37.9 %collective-permute-start.33 = (bf16[8,88,1024]{2,1,0:T(8,128)(2,1)S(1)}, bf16[8,88,1024]{2,1,0:T(8,128)(2,1)S(1)}, u32[]{:S(2)}, u32[]{:S(2)}) collective-permute-start(bf16[8,88,1024]{2,1,0:T(8,128)(2,1)S(1)} %pad_maximum_fusion.3), channel_id=1, source_target_pairs={{0,4},{1,5},{2,6},{3,7},{4,0},{5,1},{6,2},{7,3},{8,12},{9,13},{10,... | collective-permute-start | bytes 4325384 | tf_op jit(solution)/shard_map/ppermute | solution.py:38
  175.3 53.5 %collective-permute-start.37 = (bf16[8,88,1024]{2,1,0:T(8,128)(2,1)S(1)}, bf16[8,88,1024]{2,1,0:T(8,128)(2,1)S(1)}, u32[]{:S(2)}, u32[]{:S(2)}) collective-permute-start(bf16[8,88,1024]{2,1,0:T(8,128)(2,1)S(1)} %pad_maximum_fusion.4), channel_id=1, source_target_pairs={{0,2},{1,3},{2,0},{3,1},{4,6},{5,7},{6,4},{7,5},{8,10},{9,11},{10,... | collective-permute-start | bytes 4325384 | tf_op jit(solution)/shard_map/ppermute | solution.py:38
  177.2 51.9 %collective-permute-start.25 = (bf16[8,64,1024]{2,1,0:T(8,128)(2,1)S(1)}, bf16[8,64,1024]{2,1,0:T(8,128)(2,1)S(1)}, u32[]{:S(2)}, u32[]{:S(2)}) collective-permute-start(bf16[8,64,1024]{2,1,0:T(8,128)(2,1)S(1)} %multiply_convert_fusion.3), channel_id=1, source_target_pairs={{0,1},{1,0},{2,3},{3,2},{4,5},{5,4},{6,7},{7,6},{8,9},{9,8},{10,11... | collective-permute-start | bytes 3145736 | tf_op jit(solution)/shard_map/ppermute | solution.py:38
  278.1 34.6 %collective-permute-start.75 = (bf16[8,88,1024]{2,1,0:T(8,128)(2,1)}, bf16[8,88,1024]{2,1,0:T(8,128)(2,1)S(1)}, u32[]{:S(2)}, u32[]{:S(2)}) collective-permute-start(bf16[8,88,1024]{2,1,0:T(8,128)(2,1)} %bitcast.77), channel_id=1, source_target_pairs={{0,2},{1,3},{2,0},{3,1},{4,6},{5,7},{6,4},{7,5},{8,10},{9,11},{10,... | collective-permute-start | bytes 4325384 | tf_op jit(solution)/shard_map/ppermute | solution.py:38
  280.8 34.3 %collective-permute-start.71 = (bf16[8,88,1024]{2,1,0:T(8,128)(2,1)}, bf16[8,88,1024]{2,1,0:T(8,128)(2,1)S(1)}, u32[]{:S(2)}, u32[]{:S(2)}) collective-permute-start(bf16[8,88,1024]{2,1,0:T(8,128)(2,1)} %bitcast.71), channel_id=1, source_target_pairs={{0,4},{1,5},{2,6},{3,7},{4,0},{5,1},{6,2},{7,3},{8,12},{9,13},{10,... | collective-permute-start | bytes 4325384 | tf_op jit(solution)/shard_map/ppermute | solution.py:38
  282.6 61.0 %collective-permute-start.67 = (bf16[8,88,1024]{2,1,0:T(8,128)(2,1)S(1)}, bf16[8,88,1024]{2,1,0:T(8,128)(2,1)S(1)}, u32[]{:S(2)}, u32[]{:S(2)}) collective-permute-start(bf16[8,88,1024]{2,1,0:T(8,128)(2,1)S(1)} %bitcast.175), channel_id=1, source_target_pairs={{0,2},{1,3},{2,0},{3,1},{4,6},{5,7},{6,4},{7,5},{8,10},{9,11},{10,... | collective-permute-start | bytes 4325384 | tf_op jit(solution)/shard_map/ppermute | solution.py:38
  286.2 60.0 %collective-permute-start.41 = (bf16[8,64,1024]{2,1,0:T(8,128)(2,1)S(1)}, bf16[8,64,1024]{2,1,0:T(8,128)(2,1)S(1)}, u32[]{:S(2)}, u32[]{:S(2)}) collective-permute-start(bf16[8,64,1024]{2,1,0:T(8,128)(2,1)S(1)} %get-tuple-element.72.near), channel_id=1, source_target_pairs={{0,1},{1,0},{2,3},{3,2},{4,5},{5,4},{6,7},{7,6},{8,9},{9,8},{10,11... | collective-permute-start | bytes 3145736 | tf_op jit(solution)/shard_map/ppermute | solution.py:38
  314.2 63.8 %collective-permute-start.76 = (bf16[4,88,1024]{2,1,0:T(8,128)(2,1)}, bf16[4,88,1024]{2,1,0:T(8,128)(2,1)S(1)}, u32[]{:S(2)}, u32[]{:S(2)}) collective-permute-start(bf16[4,88,1024]{2,1,0:T(8,128)(2,1)} %slice.289), channel_id=1, source_target_pairs={{0,4},{1,5},{2,6},{3,7},{4,0},{5,1},{6,2},{7,3},{8,12},{9,13},{10,... | collective-permute-start | bytes 2162696 | tf_op jit(solution)/shard_map/ppermute | solution.py:38
  316.8 63.2 %collective-permute-start.72 = (bf16[4,88,1024]{2,1,0:T(8,128)(2,1)}, bf16[4,88,1024]{2,1,0:T(8,128)(2,1)}, u32[]{:S(2)}, u32[]{:S(2)}) collective-permute-start(bf16[4,88,1024]{2,1,0:T(8,128)(2,1)} %slice.281), channel_id=1, source_target_pairs={{0,2},{1,3},{2,0},{3,1},{4,6},{5,7},{6,4},{7,5},{8,10},{9,11},{10,... | collective-permute-start | bytes 2162696 | tf_op jit(solution)/shard_map/ppermute | solution.py:38
  345.2 37.3 %collective-permute-start.68 = (bf16[4,88,1024]{2,1,0:T(8,128)(2,1)}, bf16[4,88,1024]{2,1,0:T(8,128)(2,1)}, u32[]{:S(2)}, u32[]{:S(2)}) collective-permute-start(bf16[4,88,1024]{2,1,0:T(8,128)(2,1)} %slice.273), channel_id=1, source_target_pairs={{0,4},{1,5},{2,6},{3,7},{4,0},{5,1},{6,2},{7,3},{8,12},{9,13},{10,... | collective-permute-start | bytes 2162696 | tf_op jit(solution)/shard_map/ppermute | solution.py:38
  348.8 67.7 %collective-permute-start.63 = (bf16[8,1,128,256]{3,2,1,0:T(8,128)(2,1)S(1)}, bf16[8,1,128,256]{3,2,1,0:T(8,128)(2,1)S(1)}, u32[]{:S(2)}, u32[]{:S(2)}) collective-permute-start(bf16[8,1,128,256]{3,2,1,0:T(8,128)(2,1)S(1)} %get-tuple-element.67), channel_id=1, source_target_pairs={{0,4},{1,5},{2,6},{3,7},{4,0},{5,1},{6,2},{7,3},{8,12},{9,13},{10,... | collective-permute-start | bytes 1572872 | tf_op jit(solution)/shard_map/ppermute | solution.py:38
  384.3 86.9 %collective-permute-start.51 = (bf16[8,2,128,256]{3,2,1,0:T(8,128)(2,1)S(1)}, bf16[8,2,128,256]{3,2,1,0:T(8,128)(2,1)S(1)}, u32[]{:S(2)}, u32[]{:S(2)}) collective-permute-start(bf16[8,2,128,256]{3,2,1,0:T(8,128)(2,1)S(1)} %get-tuple-element.58), channel_id=1, source_target_pairs={{0,4},{1,5},{2,6},{3,7},{4,0},{5,1},{6,2},{7,3},{8,12},{9,13},{10,... | collective-permute-start | bytes 3145736 | tf_op jit(solution)/shard_map/ppermute | solution.py:38
  472.1 34.5 %collective-permute-start.50 = (bf16[8,64,1024]{2,1,0:T(8,128)(2,1)S(1)}, bf16[8,64,1024]{2,1,0:T(8,128)(2,1)S(1)}, u32[]{:S(2)}, u32[]{:S(2)}) collective-permute-start(bf16[8,64,1024]{2,1,0:T(8,128)(2,1)S(1)} %get-tuple-element.56), channel_id=1, source_target_pairs={{0,1},{1,0},{2,3},{3,2},{4,5},{5,4},{6,7},{7,6},{8,9},{9,8},{10,11... | collective-permute-start | bytes 3145736 | tf_op jit(solution)/shard_map/ppermute | solution.py:38
  (129 other events, 1898.4 us)

commit v3 on v2

--- a/solution.py
+++ b/solution.py
@@ -36,6 +36,10 @@
 def exchange(x, mask):
     count = lax.axis_size(AXES)
     return lax.ppermute(x, AXES, [(i, i ^ mask) for i in range(count)])
+
+
+def after(x, *others):
+    return lax.optimization_barrier((x, *others))[0]
 
 
 def shift_z(x, step, reverse):
@@ -231,7 +235,7 @@
     @pl.when(pl.program_id(0) == 0)
     def _():
         load_states(spots, (s0, s1, s2, s3), held, state_sems)
-        each_block(spots, [(0, 0, w0, w1, wo, sems)])
+        each_block(spots, [(1, 0, w0, w1, wo, sems)])
 
     step = pl.program_id(0)
     _, count, size, width = queries.shape
@@ -261,7 +265,7 @@
     @pl.when(pl.program_id(0) == 0)
     def _():
         load_states(spots, (s0, s1, s2, s3), held, state_sems)
-        each_block(spots, [(0, 0, w0, w1, wo, sems)])
+        each_block(spots, [(1, 0, w0, w1, wo, sems)])
 
     step = pl.program_id(0)
     _, count, size, width = queries.shape
@@ -399,39 +403,48 @@
     )(spots, *[a for a, _ in inputs])
 
 
-def carried(local, block_decay, reverse):
-    narrow_count = lax.axis_size("narrow")
-    z_count = lax.axis_size("wide") // 2
-    n, w = lax.axis_index("narrow"), lax.axis_index("wide")
-    member = 2 * (w % 2) + n // 2
-    masks = [0, 2, narrow_count, narrow_count + 2]
-    slots = local.shape[0]
-    share = slots // 4
-    rank = lambda m: 3 - m if reverse else m
-    log_decay = jnp.log(block_decay)
-    power = lambda e: jnp.exp(e * log_decay)[None, :, None, None]
-
-    def part(m):
-        return lax.dynamic_slice_in_dim(local, m * share, share, 0)
-
-    held = [part(member)] + [exchange(part(member ^ k), masks[k]) for k in range(1, 4)]
-    held = [h.astype(F32) for h in held]
-    ranks = [rank(member ^ k) for k in range(4)]
-    total = sum(power((3 - ranks[k]).astype(F32)) * held[k] for k in range(4))
-    before, span, step = 0.0, total, 1
-    while step < z_count:
-        got = shift_z(span.astype(BF16), step, reverse).astype(F32)
-        before = before + power(4.0 * (step - 1)) * got
-        span = span + power(4.0 * step) * got
-        step *= 2
-    sent = []
-    for k in range(4):
-        state = power(ranks[k].astype(F32)) * before
-        for j in range(4):
-            gap = (ranks[k] - 1 - ranks[j]).astype(F32)
-            state = state + jnp.where(gap >= 0, power(jnp.maximum(gap, 0.0)), 0.0) * held[j]
-        sent.append(state.astype(BF16))
-    return [sent[0]] + [exchange(sent[k], masks[k]) for k in range(1, 4)]
+class Carry:
+    def __init__(self, local, block_decay, reverse):
+        self.local, self.reverse = local, reverse
+        narrow_count = lax.axis_size("narrow")
+        self.member = 2 * (lax.axis_index("wide") % 2) + lax.axis_index("narrow") // 2
+        self.masks = [0, 2, narrow_count, narrow_count + 2]
+        ranks = [self.member ^ k for k in range(4)]
+        self.ranks = [3 - r if reverse else r for r in ranks]
+        self.log_decay = jnp.log(block_decay)
+
+    def power(self, e):
+        return jnp.exp(e * self.log_decay)[None, :, None, None]
+
+    def spread(self):
+        share = self.local.shape[0] // 4
+        parts = [
+            lax.dynamic_slice_in_dim(self.local, (self.member ^ k) * share, share, 0)
+            for k in range(4)
+        ]
+        self.got = [parts[0]] + [exchange(parts[k], self.masks[k]) for k in range(1, 4)]
+
+    def along(self):
+        self.held = [h.astype(F32) for h in self.got]
+        span = sum(self.power((3 - self.ranks[k]).astype(F32)) * self.held[k] for k in range(4))
+        before, step = 0.0, 1
+        while step < lax.axis_size("wide") // 2:
+            got = shift_z(span.astype(BF16), step, self.reverse).astype(F32)
+            before = before + self.power(4.0 * (step - 1)) * got
+            span = span + self.power(4.0 * step) * got
+            step *= 2
+        self.before = before
+
+    def back(self):
+        sent = []
+        for k in range(4):
+            state = self.power(self.ranks[k].astype(F32)) * self.before
+            for j in range(4):
+                gap = (self.ranks[k] - 1 - self.ranks[j]).astype(F32)
+                scale = jnp.where(gap >= 0, self.power(jnp.maximum(gap, 0.0)), 0.0)
+                state = state + scale * self.held[j]
+            sent.append(state.astype(BF16))
+        return [sent[0]] + [exchange(sent[k], self.masks[k]) for k in range(1, 4)]
 
 
 def on_device(
@@ -516,27 +529,42 @@
         gap[None] >= 0.0, jnp.exp(jnp.maximum(gap, 0.0)[None] * log_decay[:, None, None]), 0.0
     )
 
-    def halves(x, masks):
-        held = gather_plane(x, masks[:-1])
-        return held, exchange(held, masks[-1])
-
-    def bundle(*weights):
-        return jnp.stack(weights)
-
-    key_value = gather_plane(bundle(key_weight, value_weight), z_masks)
-    key_near = gather_more(key_value[:, :1], [x_mask])
-    value_near = gather_more(key_value[:, 1:], [y_mask])
-    key_parts = (key_near, exchange(key_near, y_mask))
-    value_parts = (value_near, exchange(value_near, x_mask))
-    query_parts = halves(bundle(query_weight, modulate_weight), order_xy)
-    output_parts = halves(bundle(output_weight), order_xy)
-    gate_t = gather_hidden(gate_matrix.T, order_yx, False)
-    lift_t = gather_hidden(lift_matrix.T, order_xy, True)
-    down_t = gather_hidden(down_matrix.T, order_yx, False)
-
+    def join(*parts):
+        return jnp.concatenate(parts, axis=0)
+
+    z_far, z_near = z_masks[:-1], z_masks[-1]
+    swap = exchange
+
+    def tie(*arrays):
+        return lax.optimization_barrier(arrays)
+
+    def far_steps(x):
+        for m in z_far:
+            x = join(x, swap(x, m))
+        return x
+
+    kv = jnp.stack([key_weight, value_weight])[None]
+    dn = down_matrix.T[None]
+    gl = jnp.stack([gate_matrix.T, lift_matrix.T])[None]
+    qmo = jnp.stack([query_weight, modulate_weight, output_weight])[None]
     input_rows = layer_input.astype(F32)
     normed = simple_norm(input_rows).astype(BF16)
-    normed_pair = (normed, exchange(normed, 1))
+    normed_pair = (normed, swap(normed, 1))
+    kv, dn_x = tie(far_steps(kv), swap(dn, x_mask))
+    dn = join(dn, dn_x)
+    kv_z, dn_y = tie(swap(kv, z_near), swap(dn, y_mask))
+    kv, dn = join(kv, kv_z), join(dn, dn_y)
+    k_half, v_half = kv[:, :1], kv[:, 1:]
+    qmo, k_half, v_half = tie(qmo, k_half, v_half)
+    k_x, v_y, qmo = tie(swap(k_half, x_mask), swap(v_half, y_mask), far_steps(qmo))
+    k_half, v_half = join(k_half, k_x), join(v_half, v_y)
+    k_far, v_far, qmo_z = tie(swap(k_half, y_mask), swap(v_half, x_mask), swap(qmo, z_near))
+    key_parts, value_parts = (k_half, k_far), (v_half, v_far)
+    qmo = join(qmo, qmo_z)
+    qm, out_w = qmo[:, :2], qmo[:, 2:]
+    gl = after(gl, qmo_z)
+    qm_x, o_y = swap(qm, x_mask), swap(out_w, y_mask)
+    gl = far_steps(gl)
     inner_width = heads * head_size
     chip_shape = (2, slots, quarter, inner_width)
     row_shape = (slots, quarter, width)
@@ -561,7 +589,20 @@
         [wide_scratch, wide_scratch, dma((2, members))],
         steps, 2 * square_flops,
     )
-    state_parts = carried(local_state, block_decay, False)
+    local_state, qm_x, o_y = tie(local_state, qm_x, o_y)
+    qm, out_w = join(qm, qm_x), join(out_w, o_y)
+    scan = Carry(local_state, block_decay, False)
+    scan.spread()
+    *scan.got, gl = tie(*scan.got, gl)
+    qm_y, o_x = swap(qm, y_mask), swap(out_w, x_mask)
+    gl_z = swap(gl, z_near)
+    scan.along()
+    scan.before, qm_y, o_x, gl_z = tie(scan.before, qm_y, o_x, gl_z)
+    gl = join(gl, gl_z)
+    query_parts, output_parts = (qm, qm_y), (out_w, o_x)
+    dn = after(dn, gl_z)
+    dn = far_steps(dn)
+    state_parts = scan.back()
     query_pre, queries, modulate, intra = run(
         query_kernel, "query", spots,
         [
@@ -576,6 +617,9 @@
         [wide_scratch, wide_scratch, dma((2, members))],
         steps, 2 * square_flops,
     )
+    *state_parts, queries = tie(*state_parts, queries)
+    gate_w, lift_w = after(gl, *state_parts)[:, 0], after(gl, *state_parts)[:, 1]
+    gate_y, lift_x = swap(gate_w, y_mask), swap(lift_w, x_mask)
     state_inputs = [(p, "any") for p in state_parts]
     output_inputs = [(p, "any") for p in output_parts]
     mixed, gated, near_att, far_att = run(
@@ -591,7 +635,17 @@
         [wide_scratch, held_scratch, dma((members,)), dma((4,))],
         steps, square_flops,
     )
+    near_att, gate_y, lift_x, dn = tie(near_att, gate_y, lift_x, dn)
+    gate_w, lift_w = join(gate_w, gate_y), join(lift_w, lift_x)
+    gate_x, lift_y, dn_z = swap(gate_w, x_mask), swap(lift_w, y_mask), swap(dn, z_near)
     middle = input_rows + core_sum(near_att, far_att)
+    bulk = half // 2
+    gate_t = join(gate_w, gate_x).reshape(-1, width)
+    lift_t = jnp.stack(
+        [lift_w.reshape(2, bulk, -1, width), lift_y.reshape(2, bulk, -1, width)], axis=1
+    ).reshape(-1, width)
+    down_t = jnp.moveaxis(join(dn, dn_z).reshape(bulk, 4, -1, width), 0, 1)
+    down_t = jnp.swapaxes(down_t.reshape(2, 2, bulk, -1, width), 0, 1).reshape(-1, width)
 
     def pair(mine):
         return jnp.stack([mine, exchange(mine, 1)])
@@ -624,15 +678,18 @@
     branch = core_sum(branch[0], branch[1].astype(BF16))
     layer_output = (middle + mask_rows * branch).astype(BF16)
 
-    def scattered(grad, masks, swapped):
-        if swapped:
-            grad = jnp.swapaxes(grad.reshape(2, 2, -1, width), 0, 1)
-        return scatter_plane(grad.reshape(members, -1, width), masks).T
-
-    gate_gradient = scattered(outer(gate_grad, normed_two), order_yx, False)
-    lift_gradient = scattered(outer(lift_grad, normed_two), order_xy, True)
-    down_gradient = scattered(outer(inner, branch_grad), order_yx, False)
-
+    def fold(mine, got):
+        return (mine.astype(F32) + got.astype(F32)).astype(BF16)
+
+    def final(mine, got):
+        return mine.astype(F32) + got.astype(F32)
+
+    gate_g = outer(gate_grad, normed_two).reshape(2, half, -1, width)
+    lift_g = outer(lift_grad, normed_two).reshape(2, 2, bulk, -1, width)
+    down_g = outer(inner, branch_grad).reshape(2, 2, 2, bulk // 2, -1, width)
+    gate_x = swap(gate_g[1], x_mask)
+    lift_y = swap(lift_g[:, 1], y_mask)
+    down_z = swap(down_g[:, :, 1], z_near)
     attended_grad = middle_grad.astype(BF16)
     attended_pair = (attended_grad, exchange(attended_grad, 1))
     modulate_grad, query_grad, key_grad, value_grad, state_grad = run(
@@ -650,8 +707,11 @@
         [wide_scratch, held_scratch, dma((members,)), dma((4,))],
         steps, 2 * square_flops,
     )
-    later_inputs = [(p, "any") for p in carried(state_grad, block_decay, True)]
-    part_shape = (half, 1, rows, cols)
+    state_grad, gate_x, lift_y = tie(state_grad, gate_x, lift_y)
+    gate_g = fold(gate_g[0], gate_x)
+    lift_g = fold(lift_g[:, 0], lift_y)
+    scan = Carry(state_grad, block_decay, True)
+    scan.spread()
 
     def square(name, order, a, *grads):
         shape = (half, len(grads), rows, cols)
@@ -663,11 +723,8 @@
             1, len(grads) * square_flops,
         )
 
-    def finish(parts, masks):
-        total = (parts[0].astype(F32) + exchange(parts[1], masks[-1]).astype(F32)).astype(BF16)
-        return scatter_plane(total, masks[:-1])
-
-    output_gradient = finish(square("output_outer", 0, attended_pair, gated), order_xy)[0]
+    output_keep, output_send = square("output_outer", 1, attended_pair, gated)
+    query_keep, query_send = square("query_outer", 0, normed_pair, query_grad, modulate_grad)
     (query_rows,) = run(
         rows_kernel, "query_rows", spots,
         [(query_grad, "pair"), (modulate_grad, "pair"), (query_parts[0], "any"), (query_parts[1], "any")],
@@ -675,9 +732,38 @@
         [wide_scratch, wide_scratch, dma((2, members))],
         steps, 2 * square_flops,
     )
-    query_gradient, modulate_gradient = finish(
-        square("query_outer", 0, normed_pair, query_grad, modulate_grad), order_xy
-    )
+    *scan.got, down_z, gate_g, lift_g = tie(*scan.got, down_z, gate_g, lift_g)
+    gate_y, lift_x = swap(gate_g[bulk:], y_mask), swap(lift_g[1], x_mask)
+    output_x, query_y = swap(output_send, x_mask), swap(query_send, y_mask)
+    down_g = fold(down_g[:, :, 0], down_z)
+    scan.along()
+    scan.before, gate_y, lift_x, output_x, query_y, query_rows = tie(
+        scan.before, gate_y, lift_x, output_x, query_y, query_rows
+    )
+    later_parts = scan.back()
+    gate_lift = jnp.stack([fold(gate_g[:bulk], gate_y), fold(lift_g[0], lift_x)], axis=1)
+    output_g, query_g = fold(output_keep, output_x), fold(query_keep, query_y)
+    near = bulk // 2
+    gl_z = swap(gate_lift[near:], z_near)
+    *later_parts, gl_z = tie(*later_parts, gl_z)
+    gate_lift = fold(gate_lift[:near], gl_z)
+    later_inputs = [(p, "any") for p in later_parts]
+    quad = half // 2
+    down_g, output_g, query_g = tie(down_g, output_g, query_g, *later_parts)[:3]
+    output_y, query_x = swap(output_g[quad:], y_mask), swap(query_g[quad:], x_mask)
+
+    def far_folds(x):
+        for m in reversed(z_far):
+            size = x.shape[0] // 2
+            x = (fold if size > 1 else final)(x[:size], swap(x[size:], m))
+        return x[0]
+
+    down_far = jnp.moveaxis(down_g, 2, 0)
+    for m in reversed(z_far):
+        size = down_far.shape[0] // 2
+        down_far = fold(down_far[:size], swap(down_far[size:], m))
+    down_g = down_far[0]
+    gate_lift = far_folds(gate_lift)
     key_out, value_out, near_rows, far_rows = run(
         key_back_kernel, "key_back", spots,
         [
@@ -694,8 +780,26 @@
         [wide_scratch, wide_scratch, held_scratch, dma((2, members)), dma((4,))],
         steps, 2 * square_flops,
     )
-    key_gradient = finish(square("key_outer", 0, normed_pair, key_out), order_xy)[0]
-    value_gradient = finish(square("value_outer", 1, normed_pair, value_out), order_yx)[0]
+    key_out, value_out, output_y, query_x = tie(key_out, value_out, output_y, query_x)
+    key_keep, key_send = square("key_outer", 0, normed_pair, key_out)
+    value_keep, value_send = square("value_outer", 1, normed_pair, value_out)
+    key_y, value_x = swap(key_send, y_mask), swap(value_send, x_mask)
+    qmo_g = jnp.concatenate(
+        [fold(query_g[:quad], query_x), fold(output_g[:quad], output_y)], axis=1
+    )
+    qmo_z = swap(qmo_g[near:], z_near)
+    down_y = swap(down_g[:, 1], y_mask)
+    key_g, value_g = fold(key_keep, key_y), fold(value_keep, value_x)
+    down_g = fold(down_g[:, 0], down_y)
+    qmo_g = fold(qmo_g[:near], qmo_z)
+    key_x, value_y = swap(key_g[quad:], x_mask), swap(value_g[quad:], y_mask)
+    down_x = swap(down_g[1], x_mask)
+    query_gradient, modulate_gradient, output_gradient = far_folds(qmo_g)
+    down_gradient = final(down_g[0], down_x).T
+    gate_gradient, lift_gradient = gate_lift[0].T, gate_lift[1].T
+    kv_g = jnp.concatenate([fold(key_g[:quad], key_x), fold(value_g[:quad], value_y)], axis=1)
+    kv_z = swap(kv_g[near:], z_near)
+    key_gradient, value_gradient = far_folds(fold(kv_g[:near], kv_z))
     input_gradient = middle_grad + norm_backward(input_rows, core_sum(near_rows, far_rows))
     return (
         layer_output,

time: 517 us -> 452 us (0.87)
  waiting for transfers between devices: 244 us -> 176 us
  local copies, waits for them, and re-layouts: 24.8 us -> 17 us
  other arithmetic: 41.8 us -> 48.1 us
    ppermute x75 -> x65, waiting for transfers between devices: 237 us -> 150 us  [exchange(): return lax.ppermute(x, AXES, [(i, i ^ mask) for i in range(count)])]
    ppermute x4, waiting for transfers between devices: 7.56 us -> 25.1 us  [shift_z(): return lax.ppermute(x, AXES, pairs)]
    unnamed x160 -> x223, local copies, waits for them, and re-layouts: 16 us -> 6.48 us
    ppermute x4, starting transfers between devices: 8.64 us -> 14.6 us  [shift_z(): return lax.ppermute(x, AXES, pairs)]
    convert_element_type x29 -> x23, other arithmetic: 9.61 us -> 13.5 us  [the longest x15 9.83 us: fold(): return (mine.astype(F32) + got.astype(F32)).astype(BF16)]
    ppermute x75 -> x65, starting transfers between devices: 76.8 us -> 74.8 us  [exchange(): return lax.ppermute(x, AXES, [(i, i ^ mask) for i in range(count)])]
  transfers between devices with their start and end apart: 79 -> 69, of which waited for: 32 -> 29; matrix products, arithmetic and copies ran while one was open for 13% -> 18% of each run, Pallas kernels for 13% -> 15%
where the time goes in v3:
time: 452 us; the launch traced here: 445 us
  waiting for transfers between devices  176 us (39%)
  starting transfers between devices  89.4 us (20%)
  Pallas kernels  64.7 us (14%)
  other arithmetic  48.1 us (11%)
  matrix products  47.3 us (10%)
  local copies, waits for them, and re-layouts  17 us (4%)
    ppermute x65, waiting for transfers between devices, exchange(): return lax.ppermute(x, AXES, [(i, i ^ mask) for i in range(count)])  150 us
    ppermute x65, starting transfers between devices, exchange(): return lax.ppermute(x, AXES, [(i, i ^ mask) for i in range(count)])  74.8 us
    pallas_call x10, Pallas kernels, run(): pl.pallas_call(kernel, out_shape=[jax.ShapeDtypeStruct(s, d) for s, d, _...  64.7 us
    ppermute x4, waiting for transfers between devices, shift_z(): return lax.ppermute(x, AXES, pairs)  25.1 us
    dot_general x3, matrix products, hidden(): jnp.einsum('pbld,fd->pblf', rows_in, matrix, preferred_element_type=F32)  23.4 us
    ppermute x4, starting transfers between devices, shift_z(): return lax.ppermute(x, AXES, pairs)  14.6 us
    dot_general x3, matrix products, outer(): jnp.einsum('pblf,pbld->fd', a, b, preferred_element_type=F32).astype(BF16)  13.6 us
    convert_element_type x15, other arithmetic, fold(): return (mine.astype(F32) + got.astype(F32)).astype(BF16)  9.83 us
  transfers between devices with their start and end apart: 69, of which 29 were waited for; matrix products, arithmetic and copies ran while one was open for 18% of the time, Pallas kernels for 15%

profile of v3, /device:TPU:0, one launch (start us, length us, event | category | flops | bytes accessed | tf_op | source)
XLA Modules:
  0.0 445.2 jit_solution(15851965902289315056)
XLA Ops:
  19.9 5.6 %collective-permute-done.4 = bf16[2,2,128,256]{3,2,1,0:T(8,128)(2,1)} collective-permute-done((bf16[2,2,128,256]{3,2,1,0:T(8,128)(2,1)S(1)}, bf16[2,2,128,256]{3,2,1,0:T(8,128)(2,1)}, u32[]{:S(2)}, u32[]{:S(2)}) %collective-permute-start.4) | collective-permute-done | bytes 262176 | tf_op jit(solution)/shard_map/ppermute | solution.py:38
  30.3 8.2 %collective-permute-done.8 = bf16[1,3,128,256]{3,2,1,0:T(8,128)(2,1)S(1)} collective-permute-done((bf16[1,3,128,256]{3,2,1,0:T(8,128)(2,1)S(1)}, bf16[1,3,128,256]{3,2,1,0:T(8,128)(2,1)S(1)}, u32[]{:S(2)}, u32[]{:S(2)}) %collective-permute-start.8) | collective-permute-done | bytes 196640 | tf_op jit(solution)/shard_map/ppermute | solution.py:38
  42.7 8.6 %collective-permute-done.11 = bf16[2,3,128,256]{3,2,1,0:T(8,128)(2,1)S(1)} collective-permute-done((bf16[2,3,128,256]{3,2,1,0:T(8,128)(2,1)S(1)}, bf16[2,3,128,256]{3,2,1,0:T(8,128)(2,1)S(1)}, u32[]{:S(2)}, u32[]{:S(2)}) %collective-permute-start.11) | collective-permute-done | bytes 393248 | tf_op jit(solution)/shard_map/ppermute | solution.py:38
  56.2 5.9 %key_value.1 = (f32[2,8,64,512]{3,2,1,0:T(8,128)S(1)}, bf16[2,8,64,512]{3,2,1,0:T(8,128)(2,1)S(1)}, bf16[2,8,64,512]{3,2,1,0:T(8,128)(2,1)S(1)}, bf16[8,4,128,128]{3,2,1,0:T(8,128)(2,1)S(1)}) custom-call(s32[3,16,2]{2,1,0:T(8,128)S(1)} %copy.71.spots, bf16[8,64,1024]{2,1,0:T(8,128)(2,1)S(1)} %fusion.9.near, ...), custom_call_target="tpu_custom_call" | custom-call | flops 2147483648 | bytes 10747904 | tf_op jit(solution)/shard_map/key_value/pallas_call | solution.py:390
  77.4 5.0 %collective-permute-start.18 = (bf16[2,4,128,128]{3,2,1,0:T(8,128)(2,1)S(1)}, bf16[2,4,128,128]{3,2,1,0:T(8,128)(2,1)S(1)}, u32[]{:S(2)}, u32[]{:S(2)}) collective-permute-start(bf16[2,4,128,128]{3,2,1,0:T(8,128)(2,1)S(1)} %get-tuple-element.206), channel_id=1, source_target_pairs={{0,8},{1,9},{2,10},{3,11},{4,12},{5,13},{6,14},{7,15},{8,16},{9,17... | collective-permute-start | bytes 786440 | tf_op jit(solution)/shard_map/ppermute | solution.py:50
  83.6 5.5 %collective-permute-done.18 = bf16[2,4,128,128]{3,2,1,0:T(8,128)(2,1)S(1)} collective-permute-done((bf16[2,4,128,128]{3,2,1,0:T(8,128)(2,1)S(1)}, bf16[2,4,128,128]{3,2,1,0:T(8,128)(2,1)S(1)}, u32[]{:S(2)}, u32[]{:S(2)}) %collective-permute-start.18) | collective-permute-done | bytes 262176 | tf_op jit(solution)/shard_map/ppermute | solution.py:50
  89.2 6.9 %collective-permute-start.19 = (bf16[2,4,128,128]{3,2,1,0:T(8,128)(2,1)S(1)}, bf16[2,4,128,128]{3,2,1,0:T(8,128)(2,1)S(1)}, u32[]{:S(2)}, u32[]{:S(2)}) collective-permute-start(bf16[2,4,128,128]{3,2,1,0:T(8,128)(2,1)S(1)} %fusion.31), channel_id=1, source_target_pairs={{0,16},{1,17},{2,18},{3,19},{4,20},{5,21},{6,22},{7,23},{8,24},{9,... | collective-permute-start | bytes 786440 | tf_op jit(solution)/shard_map/ppermute | solution.py:50
  97.8 5.9 %collective-permute-done.19 = bf16[2,4,128,128]{3,2,1,0:T(8,128)(2,1)S(1)} collective-permute-done((bf16[2,4,128,128]{3,2,1,0:T(8,128)(2,1)S(1)}, bf16[2,4,128,128]{3,2,1,0:T(8,128)(2,1)S(1)}, u32[]{:S(2)}, u32[]{:S(2)}) %collective-permute-start.19) | collective-permute-done | bytes 262176 | tf_op jit(solution)/shard_map/ppermute | solution.py:50
  112.2 11.1 %query.1 = (f32[2,8,64,512]{3,2,1,0:T(8,128)S(1)}, bf16[2,8,64,512]{3,2,1,0:T(8,128)(2,1)S(1)}, f32[2,8,64,512]{3,2,1,0:T(8,128)S(1)}, f32[2,8,64,512]{3,2,1,0:T(8,128)}) custom-call(s32[3,16,2]{2,1,0:T(8,128)S(1)} %copy-done.40, bf16[8,64,1024]{2,1,0:T(8,128)(2,1)S(1)} %copy-done.37, bf16[8,64,1024]{2,1,0:T(8,128)(2,1)S(1)} %copy-done.47, ...), custom_call_target="tpu_custom_call" | custom-call | flops 2147483648 | bytes 14680064 | tf_op jit(solution)/shard_map/query/pallas_call | solution.py:390
  126.6 5.0 %mixed.1 = (f32[2,8,64,512]{3,2,1,0:T(8,128)S(1)}, bf16[2,8,64,512]{3,2,1,0:T(8,128)(2,1)S(1)}, f32[8,64,1024]{2,1,0:T(8,128)S(1)}, bf16[8,64,1024]{2,1,0:T(8,128)(2,1)S(1)}) custom-call(s32[3,16,2]{2,1,0:T(8,128)S(1)} %copy-done.40, bf16[2,8,64,512]{3,2,1,0:T(8,128)(2,1)S(1)} %get-tuple-element.131.queries, f32[2,8,64,512]{3,2,1,0:T(8,128)S(1)} %copy-done.13, ...), custom_call_target="tpu_custom_call" | custom-call | flops 1073741824 | bytes 14155776 | tf_op jit(solution)/shard_map/mixed/pallas_call | solution.py:390
  138.4 12.1 %collective-permute-done.26 = bf16[4,88,1024]{2,1,0:T(8,128)(2,1)S(1)} collective-permute-done((bf16[4,88,1024]{2,1,0:T(8,128)(2,1)S(1)}, bf16[4,88,1024]{2,1,0:T(8,128)(2,1)S(1)}, u32[]{:S(2)}, u32[]{:S(2)}) %collective-permute-start.26) | collective-permute-done | bytes 720928 | tf_op jit(solution)/shard_map/ppermute | solution.py:38
  162.9 22.6 %collective-permute-done.31 = bf16[8,88,1024]{2,1,0:T(8,128)(2,1)} collective-permute-done((bf16[8,88,1024]{2,1,0:T(8,128)(2,1)}, bf16[8,88,1024]{2,1,0:T(8,128)(2,1)}, u32[]{:S(2)}, u32[]{:S(2)}) %collective-permute-start.31) | collective-permute-done | bytes 1441824 | tf_op jit(solution)/shard_map/ppermute | solution.py:38
  187.1 6.5 %fusion.94 = f32[2,8,64,1408]{3,2,1,0:T(8,128)} fusion(bf16[1408,1024,1,1]{1,0,3,2:T(8,128)(2,1)S(1)} %bitcast.211, bf16[1,8,64,1024]{3,2,1,0:T(8,128)(2,1)} %bitcast.30, bf16[1,8,64,1024]{3,2,1,0:T(8,128)(2,1)S(1)} %fusion.116), kind=kOutput, calls=%fused_computation.329 | convolution fusion | flops 2953838592 | bytes 10747904 | tf_op jit(solution)/shard_map/pbld,fd->pblf/dot_general | solution.py:658
  198.1 6.6 %fusion.93 = f32[2,8,64,1408]{3,2,1,0:T(8,128)} fusion(bf16[1408,1024,1,1]{1,0,3,2:T(8,128)(2,1)S(1)} %bitcast.215, bf16[1,8,64,1024]{3,2,1,0:T(8,128)(2,1)} %bitcast.30, bf16[1,8,64,1024]{3,2,1,0:T(8,128)(2,1)S(1)} %fusion.116), kind=kOutput, calls=%fused_computation.328 | convolution fusion | flops 2953838592 | bytes 10747904 | tf_op jit(solution)/shard_map/pbld,fd->pblf/dot_general | solution.py:658
  204.7 10.3 %multiply_convert_fusion.1 = (bf16[2,8,64,1408]{3,2,1,0:T(8,128)(2,1)}, bf16[2,8,64,1408]{3,2,1,0:T(8,128)(2,1)}, bf16[2,8,64,1408]{3,2,1,0:T(8,128)(2,1)S(1)}) fusion(f32[2,8,64,1408]{3,2,1,0:T(8,128)} %fusion.93, f32[2,8,64,1408]{3,2,1,0:T(8,128)} %fusion.94, bf16[1408,1024,1,1]{1,0,3,2:T(8,128)(2,1)S(1)} %bitcast.213, ...), kind=kOutput, calls=%fused_computation.4 | convolution fusion | flops 2974023680 | bytes 25165824 | tf_op jit(solution)/shard_map/pbld,fd->pblf/dot_general | solution.py:658
  253.4 15.4 %mixed_back.1 = (bf16[2,8,64,512]{3,2,1,0:T(8,128)(2,1)S(1)}, bf16[2,8,64,512]{3,2,1,0:T(8,128)(2,1)S(1)}, f32[2,8,64,512]{3,2,1,0:T(8,128)S(1)}, f32[2,8,64,512]{3,2,1,0:T(8,128)}, bf16[8,4,128,128]{3,2,1,0:T(8,128)(2,1)S(1)}) custom-call(s32[3,16,2]{2,1,0:T(8,128)S(1)} %copy-done.41, bf16[8,64,1024]{2,1,0:T(8,128)(2,1)S(1)} %get-tuple-element.202.near, ...), custom_call_target="tpu_custom_call" | custom-call | flops 2147483648 | bytes 22544384 | tf_op jit(solution)/shard_map/mixed_back/pallas_call | solution.py:390
  283.1 5.7 %query_rows.1.rows_in = f32[2,8,64,1024]{3,2,1,0:T(8,128)S(1)} custom-call(s32[3,16,2]{2,1,0:T(8,128)S(1)} %copy-done.41, bf16[2,8,64,512]{3,2,1,0:T(8,128)(2,1)S(1)} %get-tuple-element.166.refs_0_.query_grad, bf16[2,8,64,512]{3,2,1,0:T(8,128)(2,1)S(1)} %get-tuple-element.167.refs_1_.modulate_grad, bf16[8,2,128,256]{3,2,1,0:T(8,128)(2,1)S(1)} %copy-done.11, ...), custom_call_target="tpu_custom_call" | custom-call | flops 2147483648 | bytes 8388608 | tf_op jit(solution)/shard_map/query_rows/pallas_call | solution.py:390
  288.8 20.8 %collective-permute-done.41 = bf16[2,4,128,128]{3,2,1,0:T(8,128)(2,1)S(1)} collective-permute-done((bf16[2,4,128,128]{3,2,1,0:T(8,128)(2,1)S(1)}, bf16[2,4,128,128]{3,2,1,0:T(8,128)(2,1)S(1)}, u32[]{:S(2)}, u32[]{:S(2)}) %collective-permute-start.41) | collective-permute-done | bytes 262176 | tf_op jit(solution)/shard_map/ppermute | solution.py:38
  323.1 11.8 %collective-permute-done.45 = bf16[2,4,128,128]{3,2,1,0:T(8,128)(2,1)S(1)} collective-permute-done((bf16[2,4,128,128]{3,2,1,0:T(8,128)(2,1)S(1)}, bf16[2,4,128,128]{3,2,1,0:T(8,128)(2,1)S(1)}, u32[]{:S(2)}, u32[]{:S(2)}) %collective-permute-start.45) | collective-permute-done | bytes 262176 | tf_op jit(solution)/shard_map/ppermute | solution.py:50
  335.1 7.8 %collective-permute-done.47 = bf16[4,88,1024]{2,1,0:T(8,128)(2,1)S(1)} collective-permute-done((bf16[4,88,1024]{2,1,0:T(8,128)(2,1)S(1)}, bf16[4,88,1024]{2,1,0:T(8,128)(2,1)S(1)}, u32[]{:S(2)}, u32[]{:S(2)}) %collective-permute-start.47) | collective-permute-done | bytes 720928 | tf_op jit(solution)/shard_map/ppermute | solution.py:38
  367.7 9.5 %key_back.1 = (bf16[2,8,64,512]{3,2,1,0:T(8,128)(2,1)S(1)}, bf16[2,8,64,512]{3,2,1,0:T(8,128)(2,1)S(1)}, f32[8,64,1024]{2,1,0:T(8,128)S(1)}, bf16[8,64,1024]{2,1,0:T(8,128)(2,1)S(1)}) custom-call(s32[3,16,2]{2,1,0:T(8,128)S(1)} %copy-done.41, f32[2,8,64,512]{3,2,1,0:T(8,128)S(1)} %get-tuple-element.151.key_grad, ...), custom_call_target="tpu_custom_call" | custom-call | flops 2147483648 | bytes 22282240 | tf_op jit(solution)/shard_map/key_back/pallas_call | solution.py:390
  377.2 16.8 %collective-permute-done.65 = bf16[1,2,88,1024]{3,2,1,0:T(8,128)(2,1)} collective-permute-done((bf16[1,2,88,1024]{3,2,1,0:T(8,128)(2,1)S(1)}, bf16[1,2,88,1024]{3,2,1,0:T(8,128)(2,1)}, u32[]{:S(2)}, u32[]{:S(2)}) %collective-permute-start.65) | collective-permute-done | bytes 360480 | tf_op jit(solution)/shard_map/ppermute | solution.py:38
  410.4 6.6 %collective-permute-done.57 = bf16[2,3,128,256]{3,2,1,0:T(8,128)(2,1)S(1)} collective-permute-done((bf16[2,3,128,256]{3,2,1,0:T(8,128)(2,1)S(1)}, bf16[2,3,128,256]{3,2,1,0:T(8,128)(2,1)S(1)}, u32[]{:S(2)}, u32[]{:S(2)}) %collective-permute-start.57) | collective-permute-done | bytes 393248 | tf_op jit(solution)/shard_map/ppermute | solution.py:38
  425.5 5.4 %collective-permute-done.60 = bf16[4,1,128,256]{3,2,1,0:T(8,128)(2,1)S(1)} collective-permute-done((bf16[4,1,128,256]{3,2,1,0:T(8,128)(2,1)S(1)}, bf16[4,1,128,256]{3,2,1,0:T(8,128)(2,1)S(1)}, u32[]{:S(2)}, u32[]{:S(2)}) %collective-permute-start.60) | collective-permute-done | bytes 262176 | tf_op jit(solution)/shard_map/ppermute | solution.py:38
  (487 shorter events, 216.4 us)
Async XLA Ops:
  7.3 34.5 %collective-permute-start = (f32[2]{0:T(128)}, f32[2]{0:T(128)S(1)}, u32[]{:S(2)}, u32[]{:S(2)}) collective-permute-start(f32[2]{0:T(128)} %param.23), channel_id=1, source_target_pairs={{0,2},{1,3},{2,0},{3,1},{4,6},{5,7},{6,4},{7,5},{8,10},{9,11},{10,... | collective-permute-start | bytes 32 | tf_op jit(solution)/shard_map/ppermute | solution.py:38
  10.8 45.0 %collective-permute-start.1 = (bf16[8,64,1024]{2,1,0:T(8,128)(2,1)S(1)}, bf16[8,64,1024]{2,1,0:T(8,128)(2,1)S(1)}, u32[]{:S(2)}, u32[]{:S(2)}) collective-permute-start(bf16[8,64,1024]{2,1,0:T(8,128)(2,1)S(1)} %fusion.9.near), channel_id=1, source_target_pairs={{0,1},{1,0},{2,3},{3,2},{4,5},{5,4},{6,7},{7,6},{8,9},{9,8},{10,11... | collective-permute-start | bytes 3145736 | tf_op jit(solution)/shard_map/ppermute | solution.py:38
  71.5 32.4 %collective-permute-start.20 = (bf16[8,2,128,256]{3,2,1,0:T(8,128)(2,1)S(1)}, bf16[8,2,128,256]{3,2,1,0:T(8,128)(2,1)S(1)}, u32[]{:S(2)}, u32[]{:S(2)}) collective-permute-start(bf16[8,2,128,256]{3,2,1,0:T(8,128)(2,1)S(1)} %pad_maximum_fusion.9.w0), channel_id=1, source_target_pairs={{0,4},{1,5},{2,6},{3,7},{4,0},{5,1},{6,2},{7,3},{8,12},{9,13},{10,... | collective-permute-start | bytes 3145736 | tf_op jit(solution)/shard_map/ppermute | solution.py:38
  82.6 21.3 %collective-permute-start.21 = (bf16[8,1,128,256]{3,2,1,0:T(8,128)(2,1)S(1)}, bf16[8,1,128,256]{3,2,1,0:T(8,128)(2,1)S(1)}, u32[]{:S(2)}, u32[]{:S(2)}) collective-permute-start(bf16[8,1,128,256]{3,2,1,0:T(8,128)(2,1)S(1)} %pad_maximum_fusion.13.w0), channel_id=1, source_target_pairs={{0,2},{1,3},{2,0},{3,1},{4,6},{5,7},{6,4},{7,5},{8,10},{9,11},{10,... | collective-permute-start | bytes 1572872 | tf_op jit(solution)/shard_map/ppermute | solution.py:38
  108.7 28.5 %collective-permute-start.28 = (bf16[4,88,1024]{2,1,0:T(8,128)(2,1)S(1)}, bf16[4,88,1024]{2,1,0:T(8,128)(2,1)S(1)}, u32[]{:S(2)}, u32[]{:S(2)}) collective-permute-start(bf16[4,88,1024]{2,1,0:T(8,128)(2,1)S(1)} %pad_maximum_fusion.12), channel_id=1, source_target_pairs={{0,16},{1,17},{2,18},{3,19},{4,20},{5,21},{6,22},{7,23},{8,24},{9,... | collective-permute-start | bytes 2162696 | tf_op jit(solution)/shard_map/ppermute | solution.py:38
  131.7 22.0 %collective-permute-start.29 = (bf16[8,64,1024]{2,1,0:T(8,128)(2,1)S(1)}, bf16[8,64,1024]{2,1,0:T(8,128)(2,1)S(1)}, u32[]{:S(2)}, u32[]{:S(2)}) collective-permute-start(bf16[8,64,1024]{2,1,0:T(8,128)(2,1)S(1)} %get-tuple-element.145), channel_id=1, source_target_pairs={{0,1},{1,0},{2,3},{3,2},{4,5},{5,4},{6,7},{7,6},{8,9},{9,8},{10,11... | collective-permute-start | bytes 3145736 | tf_op jit(solution)/shard_map/ppermute | solution.py:38
  152.3 33.2 %collective-permute-start.31 = (bf16[8,88,1024]{2,1,0:T(8,128)(2,1)}, bf16[8,88,1024]{2,1,0:T(8,128)(2,1)}, u32[]{:S(2)}, u32[]{:S(2)}) collective-permute-start(bf16[8,88,1024]{2,1,0:T(8,128)(2,1)} %pad_maximum_fusion.7), channel_id=1, source_target_pairs={{0,2},{1,3},{2,0},{3,1},{4,6},{5,7},{6,4},{7,5},{8,10},{9,11},{10,... | collective-permute-start | bytes 4325384 | tf_op jit(solution)/shard_map/ppermute | solution.py:38
  155.4 31.7 %collective-permute-start.30 = (bf16[8,64,1024]{2,1,0:T(8,128)(2,1)}, bf16[8,64,1024]{2,1,0:T(8,128)(2,1)}, u32[]{:S(2)}, u32[]{:S(2)}) collective-permute-start(bf16[8,64,1024]{2,1,0:T(8,128)(2,1)} %multiply_convert_fusion.3), channel_id=1, source_target_pairs={{0,1},{1,0},{2,3},{3,2},{4,5},{5,4},{6,7},{7,6},{8,9},{9,8},{10,11... | collective-permute-start | bytes 3145736 | tf_op jit(solution)/shard_map/ppermute | solution.py:38
  157.0 47.8 %collective-permute-start.35 = (bf16[8,64,1024]{2,1,0:T(8,128)(2,1)}, bf16[8,64,1024]{2,1,0:T(8,128)(2,1)}, u32[]{:S(2)}, u32[]{:S(2)}) collective-permute-start(bf16[8,64,1024]{2,1,0:T(8,128)(2,1)} %fusion.7), channel_id=1, source_target_pairs={{0,1},{1,0},{2,3},{3,2},{4,5},{5,4},{6,7},{7,6},{8,9},{9,8},{10,11... | collective-permute-start | bytes 3145736 | tf_op jit(solution)/shard_map/ppermute | solution.py:38
  157.2 36.5 %collective-permute-start.33 = (bf16[8,88,1024]{2,1,0:T(8,128)(2,1)}, bf16[8,88,1024]{2,1,0:T(8,128)(2,1)}, u32[]{:S(2)}, u32[]{:S(2)}) collective-permute-start(bf16[8,88,1024]{2,1,0:T(8,128)(2,1)} %pad_maximum_fusion.6), channel_id=1, source_target_pairs={{0,8},{1,9},{2,10},{3,11},{4,12},{5,13},{6,14},{7,15},{8,0},{9,1},... | collective-permute-start | bytes 4325384 | tf_op jit(solution)/shard_map/ppermute | solution.py:38
  161.1 34.9 %collective-permute-start.32 = (bf16[8,88,1024]{2,1,0:T(8,128)(2,1)}, bf16[8,88,1024]{2,1,0:T(8,128)(2,1)}, u32[]{:S(2)}, u32[]{:S(2)}) collective-permute-start(bf16[8,88,1024]{2,1,0:T(8,128)(2,1)} %pad_maximum_fusion.8), channel_id=1, source_target_pairs={{0,4},{1,5},{2,6},{3,7},{4,0},{5,1},{6,2},{7,3},{8,12},{9,13},{10,... | collective-permute-start | bytes 4325384 | tf_op jit(solution)/shard_map/ppermute | solution.py:38
  236.9 37.6 %collective-permute-start.39 = (bf16[2,4,88,1024]{3,2,1,0:T(8,128)(2,1)}, bf16[2,4,88,1024]{3,2,1,0:T(8,128)(2,1)S(1)}, u32[]{:S(2)}, u32[]{:S(2)}) collective-permute-start(bf16[2,4,88,1024]{3,2,1,0:T(8,128)(2,1)} %slice_bitcast_fusion.3), channel_id=1, source_target_pairs={{0,4},{1,5},{2,6},{3,7},{4,0},{5,1},{6,2},{7,3},{8,12},{9,13},{10,... | collective-permute-start | bytes 4325384 | tf_op jit(solution)/shard_map/ppermute | solution.py:38
  239.6 34.9 %collective-permute-start.38 = (bf16[8,88,1024]{2,1,0:T(8,128)(2,1)}, bf16[8,88,1024]{2,1,0:T(8,128)(2,1)}, u32[]{:S(2)}, u32[]{:S(2)}) collective-permute-start(bf16[8,88,1024]{2,1,0:T(8,128)(2,1)} %bitcast.65), channel_id=1, source_target_pairs={{0,2},{1,3},{2,0},{3,1},{4,6},{5,7},{6,4},{7,5},{8,10},{9,11},{10,... | collective-permute-start | bytes 4325384 | tf_op jit(solution)/shard_map/ppermute | solution.py:38
  250.5 38.3 %collective-permute-start.43 = (bf16[2,2,2,88,1024]{4,3,0,1,2:T(8,128)(2,1)}, bf16[2,2,2,88,1024]{4,3,0,1,2:T(8,128)(2,1)}, u32[]{:S(2)}, u32[]{:S(2)}) collective-permute-start(bf16[2,2,2,88,1024]{4,3,0,1,2:T(8,128)(2,1)} %bitcast.192), channel_id=1, source_target_pairs={{0,8},{1,9},{2,10},{3,11},{4,12},{5,13},{6,14},{7,15},{8,0},{9,1},... | collective-permute-start | bytes 4325384 | tf_op jit(solution)/shard_map/ppermute | solution.py:38
  273.1 69.8 %collective-permute-start.49 = (bf16[8,2,128,256]{3,2,1,0:T(8,128)(2,1)S(1)}, bf16[8,2,128,256]{3,2,1,0:T(8,128)(2,1)}, u32[]{:S(2)}, u32[]{:S(2)}) collective-permute-start(bf16[8,2,128,256]{3,2,1,0:T(8,128)(2,1)S(1)} %get-tuple-element.168), channel_id=1, source_target_pairs={{0,4},{1,5},{2,6},{3,7},{4,0},{5,1},{6,2},{7,3},{8,12},{9,13},{10,... | collective-permute-start | bytes 3145736 | tf_op jit(solution)/shard_map/ppermute | solution.py:38
  275.4 34.3 %collective-permute-start.41 = (bf16[2,4,128,128]{3,2,1,0:T(8,128)(2,1)S(1)}, bf16[2,4,128,128]{3,2,1,0:T(8,128)(2,1)S(1)}, u32[]{:S(2)}, u32[]{:S(2)}) collective-permute-start(bf16[2,4,128,128]{3,2,1,0:T(8,128)(2,1)S(1)} %get-tuple-element.231), channel_id=1, source_target_pairs={{0,4},{1,5},{2,6},{3,7},{4,0},{5,1},{6,2},{7,3},{8,12},{9,13},{10,... | collective-permute-start | bytes 786440 | tf_op jit(solution)/shard_map/ppermute | solution.py:38
  276.1 33.6 %collective-permute-start.42 = (bf16[2,4,128,128]{3,2,1,0:T(8,128)(2,1)S(1)}, bf16[2,4,128,128]{3,2,1,0:T(8,128)(2,1)S(1)}, u32[]{:S(2)}, u32[]{:S(2)}) collective-permute-start(bf16[2,4,128,128]{3,2,1,0:T(8,128)(2,1)S(1)} %get-tuple-element.230), channel_id=1, source_target_pairs={{0,6},{1,7},{2,4},{3,5},{4,2},{5,3},{6,0},{7,1},{8,14},{9,15},{10,... | collective-permute-start | bytes 786440 | tf_op jit(solution)/shard_map/ppermute | solution.py:38
  316.4 26.5 %collective-permute-start.47 = (bf16[4,88,1024]{2,1,0:T(8,128)(2,1)S(1)}, bf16[4,88,1024]{2,1,0:T(8,128)(2,1)S(1)}, u32[]{:S(2)}, u32[]{:S(2)}) collective-permute-start(bf16[4,88,1024]{2,1,0:T(8,128)(2,1)S(1)} %slice_bitcast_fusion.4), channel_id=1, source_target_pairs={{0,2},{1,3},{2,0},{3,1},{4,6},{5,7},{6,4},{7,5},{8,10},{9,11},{10,... | collective-permute-start | bytes 2162696 | tf_op jit(solution)/shard_map/ppermute | solution.py:38
  361.4 32.7 %collective-permute-start.65 = (bf16[1,2,88,1024]{3,2,1,0:T(8,128)(2,1)S(1)}, bf16[1,2,88,1024]{3,2,1,0:T(8,128)(2,1)}, u32[]{:S(2)}, u32[]{:S(2)}) collective-permute-start(bf16[1,2,88,1024]{3,2,1,0:T(8,128)(2,1)S(1)} %slice.237), channel_id=1, source_target_pairs={{0,16},{1,17},{2,18},{3,19},{4,20},{5,21},{6,22},{7,23},{8,24},{9,... | collective-permute-start | bytes 1081352 | tf_op jit(solution)/shard_map/ppermute | solution.py:38
  364.9 43.8 %collective-permute-start.66 = (bf16[1,2,2,88,1024]{4,3,1,2,0:T(8,128)(2,1)}, bf16[1,2,2,88,1024]{4,3,1,2,0:T(8,128)(2,1)S(1)}, u32[]{:S(2)}, u32[]{:S(2)}) collective-permute-start(bf16[1,2,2,88,1024]{4,3,1,2,0:T(8,128)(2,1)} %slice.241), channel_id=1, source_target_pairs={{0,16},{1,17},{2,18},{3,19},{4,20},{5,21},{6,22},{7,23},{8,24},{9,... | collective-permute-start | bytes 2162696 | tf_op jit(solution)/shard_map/ppermute | solution.py:38
  365.5 30.6 %collective-permute-start.56 = (bf16[4,2,128,256]{3,2,1,0:T(8,128)(2,1)S(1)}, bf16[4,2,128,256]{3,2,1,0:T(8,128)(2,1)S(1)}, u32[]{:S(2)}, u32[]{:S(2)}) collective-permute-start(bf16[4,2,128,256]{3,2,1,0:T(8,128)(2,1)S(1)} %slice.182), channel_id=1, source_target_pairs={{0,2},{1,3},{2,0},{3,1},{4,6},{5,7},{6,4},{7,5},{8,10},{9,11},{10,... | collective-permute-start | bytes 1572872 | tf_op jit(solution)/shard_map/ppermute | solution.py:38
  366.2 29.8 %collective-permute-start.55 = (bf16[4,1,128,256]{3,2,1,0:T(8,128)(2,1)S(1)}, bf16[4,1,128,256]{3,2,1,0:T(8,128)(2,1)S(1)}, u32[]{:S(2)}, u32[]{:S(2)}) collective-permute-start(bf16[4,1,128,256]{3,2,1,0:T(8,128)(2,1)S(1)} %slice.181), channel_id=1, source_target_pairs={{0,4},{1,5},{2,6},{3,7},{4,0},{5,1},{6,2},{7,3},{8,12},{9,13},{10,... | collective-permute-start | bytes 786440 | tf_op jit(solution)/shard_map/ppermute | solution.py:38
  377.1 40.8 %collective-permute-start.54 = (bf16[8,64,1024]{2,1,0:T(8,128)(2,1)S(1)}, bf16[8,64,1024]{2,1,0:T(8,128)(2,1)S(1)}, u32[]{:S(2)}, u32[]{:S(2)}) collective-permute-start(bf16[8,64,1024]{2,1,0:T(8,128)(2,1)S(1)} %get-tuple-element.178), channel_id=1, source_target_pairs={{0,1},{1,0},{2,3},{3,2},{4,5},{5,4},{6,7},{7,6},{8,9},{9,8},{10,11... | collective-permute-start | bytes 3145736 | tf_op jit(solution)/shard_map/ppermute | solution.py:38
  398.7 22.7 %collective-permute-start.59 = (bf16[8,1,128,256]{3,2,1,0:T(8,128)(2,1)S(1)}, bf16[8,1,128,256]{3,2,1,0:T(8,128)(2,1)S(1)}, u32[]{:S(2)}, u32[]{:S(2)}) collective-permute-start(bf16[8,1,128,256]{3,2,1,0:T(8,128)(2,1)S(1)} %get-tuple-element.192), channel_id=1, source_target_pairs={{0,4},{1,5},{2,6},{3,7},{4,0},{5,1},{6,2},{7,3},{8,12},{9,13},{10,... | collective-permute-start | bytes 1572872 | tf_op jit(solution)/shard_map/ppermute | solution.py:38
  (154 other events, 2075.0 us)

commit v4 on v3

--- a/solution.py
+++ b/solution.py
@@ -74,6 +74,14 @@
         total = x[:half].astype(F32) + got.astype(F32)
         x = total.astype(BF16) if half > 1 else total
     return x[0]
+
+
+def fold(mine, got, dtype=BF16):
+    return (mine.astype(F32) + got.astype(F32)).astype(dtype)
+
+
+def final(mine, got):
+    return fold(mine, got, F32)
 
 
 def relative(masks, index):
@@ -165,11 +173,11 @@
 ):
     @pl.when(pl.program_id(0) == 0)
     def _():
-        each_block(spots, [(0, 0, kw0, kw1, wk, sems.at[0]), (1, 0, vw0, vw1, wv, sems.at[1])])
+        each_block(spots, [(0, 0, kw0, kw1, wk, sems.at[0]), (2, 0, vw0, vw1, wv, sems.at[1])])
 
     count, size = near.shape[0], near.shape[1]
     x = both(near[...], far[...])
-    valid = get(mask)
+    valid = get(mask).astype(F32)
     head = cosine.shape[-1]
     pre = mm(x, wk[...])
     val_pre = mm(x, wv[...])
@@ -198,7 +206,7 @@
 
     count, size = near.shape[0], near.shape[1]
     x = both(near[...], far[...])
-    valid = get(mask)
+    valid = get(mask).astype(F32)
     head = cosine.shape[-1]
     pre = mm(x, wq[...])
     mod = mm(x, wm[...])
@@ -210,15 +218,12 @@
         q = turn(qp * jax.nn.sigmoid(qp), cosine[...], sine[...]).astype(BF16)
         put(queries, lanes, q)
         k, v = get(keys, lanes), get(values, lanes)
-        parts = []
-        for s in range(count):
-            scores = mm(slot_rows(q, s, size, count), slot_rows(k, s, size, count), NT) * grid[h]
-            parts.append(mm(scores.astype(BF16), slot_rows(v, s, size, count)))
-        put(intra, lanes, slot_back(parts, size))
+        scores = (mm(q, k, NT) * grid[h]).astype(BF16)
+        put(intra, lanes, mm(scores, v))
 
 
 def load_states(spots, pieces, held, sems):
-    member = spots[2, 0, 0]
+    member = spots[3, 0, 0]
     copies = [
         pltpu.make_async_copy(p, held.at[member ^ k], sems.at[k]) for k, p in enumerate(pieces)
     ]
@@ -246,10 +251,10 @@
         lanes = slice(h * head, (h + 1) * head)
         q = (get(queries, lanes).astype(F32) * query_decay[:, lanes]).astype(BF16)
         parts = [mm(slot_rows(q, s, size, count), held[step, s, h]) for s in range(count)]
-        mix = get(intra, lanes) + slot_back(parts, size)
+        mix = get(intra, lanes).astype(F32) + slot_back(parts, size)
         put(mixed, lanes, mix)
         scale = lax.rsqrt(jnp.mean(mix * mix, axis=-1, keepdims=True) + EPS)
-        gates.append((mix * scale * get(modulate, lanes)).astype(BF16))
+        gates.append((mix * scale * get(modulate, lanes).astype(F32)).astype(BF16))
     gate = jnp.concatenate(gates, axis=1)
     put(gated, slice(None), gate)
     out = mm(gate, wo[...], NT)
@@ -259,7 +264,7 @@
 
 def mixed_back_kernel(
     spots, near, far, mixed, modulate, queries, query_pre, keys, values, mask, cosine, sine,
-    query_decay, grid, s0, s1, s2, s3, w0, w1,
+    query_decay, grid, grid_t, s0, s1, s2, s3, w0, w1,
     modulate_grad, query_grad, key_grad, value_grad, state_grad, wo, held, sems, state_sems
 ):
     @pl.when(pl.program_id(0) == 0)
@@ -272,35 +277,34 @@
     heads = held.shape[2]
     head = width // heads
     gate_grad = mm(both(near[...], far[...]), wo[...])
-    valid = get(mask)
+    valid = get(mask).astype(F32)
     for h in range(heads):
         lanes = slice(h * head, (h + 1) * head)
-        mix = get(mixed, lanes)
+        mix = get(mixed, lanes).astype(F32)
         scale = lax.rsqrt(jnp.mean(mix * mix, axis=-1, keepdims=True) + EPS)
         gg = gate_grad[:, lanes]
         put(modulate_grad, lanes, gg * valid * (mix * scale))
-        cot = gg * get(modulate, lanes)
+        cot = gg * get(modulate, lanes).astype(F32)
         inner = jnp.mean(mix * cot, axis=-1, keepdims=True)
         gm = (scale * cot - mix * (scale * scale * scale * inner)).astype(BF16)
         q, k, v = get(queries, lanes), get(keys, lanes), get(values, lanes)
         qs = (q.astype(F32) * query_decay[:, lanes]).astype(BF16)
-        gq, gk, gv = [], [], []
+        gst = (mm(v, gm, NT) * grid_t[h]).astype(BF16)
+        gs = (mm(gm, v, NT) * grid[h]).astype(BF16)
+        sct = (mm(k, q, NT) * grid_t[h]).astype(BF16)
+        put(value_grad, lanes, mm(sct, gm))
+        put(key_grad, lanes, mm(gst, q))
+        gq = []
         for s in range(count):
             pick = lambda x: slot_rows(x, s, size, count)
-            gms, qq, kk, vv = pick(gm), pick(q), pick(k), pick(v)
-            gs = (mm(gms, vv, NT) * grid[h]).astype(BF16)
-            sc = (mm(qq, kk, NT) * grid[h]).astype(BF16)
-            gv.append(mm(sc, gms, TN))
-            gk.append(mm(gs, qq, TN))
-            decay = slot_rows(query_decay[:, lanes], s, size, count)
-            gq.append(mm(gs, kk) + mm(gms, held[step, s, h], NT) * decay)
+            gms = pick(gm)
+            gq.append(mm(gms, held[step, s, h], NT))
             state_grad[s, h] = mm(pick(qs), gms, TN).astype(BF16)
-        put(key_grad, lanes, slot_back(gk, size))
-        put(value_grad, lanes, slot_back(gv, size))
-        qp = get(query_pre, lanes)
+        gq = mm(gs, k) + slot_back(gq, size) * query_decay[:, lanes]
+        qp = get(query_pre, lanes).astype(F32)
         sg = jax.nn.sigmoid(qp)
         slope = sg + qp * sg * (1.0 - sg)
-        put(query_grad, lanes, turn(slot_back(gq, size), cosine[...], -sine[...]) * slope)
+        put(query_grad, lanes, turn(gq, cosine[...], -sine[...]) * slope)
 
 
 def rows_kernel(spots, query_grad, modulate_grad, w0, w1, out, wq, wm, sems):
@@ -319,13 +323,13 @@
     @pl.when(pl.program_id(0) == 0)
     def _():
         load_states(spots, (g0, g1, g2, g3), held, state_sems)
-        each_block(spots, [(0, 0, kw0, kw1, wk, sems.at[0]), (1, 0, vw0, vw1, wv, sems.at[1])])
+        each_block(spots, [(0, 0, kw0, kw1, wk, sems.at[0]), (2, 0, vw0, vw1, wv, sems.at[1])])
 
     step = pl.program_id(0)
     _, count, size, width = keys.shape
     heads = held.shape[2]
     head = width // heads
-    valid = get(mask)
+    valid = get(mask).astype(F32)
     gks, gvs = [], []
     for h in range(heads):
         lanes = slice(h * head, (h + 1) * head)
@@ -334,9 +338,9 @@
         scaled = (k.astype(F32) * decay).astype(BF16)
         pk = [mm(slot_rows(v, s, size, count), held[step, s, h], NT) for s in range(count)]
         pv = [mm(slot_rows(scaled, s, size, count), held[step, s, h]) for s in range(count)]
-        gk = get(key_grad, lanes) + slot_back(pk, size) * decay
-        gv = get(value_grad, lanes) + slot_back(pv, size)
-        kp = get(key_pre, lanes)
+        gk = get(key_grad, lanes).astype(F32) + slot_back(pk, size) * decay
+        gv = get(value_grad, lanes).astype(F32) + slot_back(pv, size)
+        kp = get(key_pre, lanes).astype(F32)
         sg = jax.nn.sigmoid(kp)
         slope = sg + kp * sg * (1.0 - sg)
         gks.append((turn(gk * valid, cosine[...], -sine[...]) * slope).astype(BF16))
@@ -344,7 +348,7 @@
     gk, gv = jnp.concatenate(gks, axis=1), jnp.concatenate(gvs, axis=1)
     put(key_out, slice(None), gk)
     put(value_out, slice(None), gv)
-    out = get(rows_in) + mm(gk, wk[...], NT) + mm(gv, wv[...], NT)
+    out = get(rows_in).astype(F32) + mm(gk, wk[...], NT) + mm(gv, wv[...], NT)
     near_out[...] = out[: count * size].reshape(near_out.shape)
     far_out[...] = out[count * size :].astype(BF16).reshape(far_out.shape)
 
@@ -367,7 +371,7 @@
     )
 
 
-ANY = pl.BlockSpec(memory_space=pl.ANY)
+ANY = pl.BlockSpec(memory_space=pltpu.HBM)
 VMEM = pl.BlockSpec(memory_space=pltpu.VMEM)
 
 
@@ -424,12 +428,12 @@
         ]
         self.got = [parts[0]] + [exchange(parts[k], self.masks[k]) for k in range(1, 4)]
 
-    def along(self):
+    def along(self, between=lambda step, got: got):
         self.held = [h.astype(F32) for h in self.got]
         span = sum(self.power((3 - self.ranks[k]).astype(F32)) * self.held[k] for k in range(4))
         before, step = 0.0, 1
         while step < lax.axis_size("wide") // 2:
-            got = shift_z(span.astype(BF16), step, self.reverse).astype(F32)
+            got = between(step, shift_z(span.astype(BF16), step, self.reverse)).astype(F32)
             before = before + self.power(4.0 * (step - 1)) * got
             span = span + self.power(4.0 * step) * got
             step *= 2
@@ -478,6 +482,7 @@
     y_mask, z_masks = wide_masks[0], wide_masks[:0:-1]
     order_yx = z_masks + [y_mask, x_mask]
     order_xy = z_masks + [x_mask, y_mask]
+    order_v = [y_mask] + z_masks + [x_mask]
     members = 1 << len(order_yx)
     half = members // 2
 
@@ -487,12 +492,13 @@
     ).astype(jnp.int32)
     mask = ((base + offsets)[:, None, :] < valid_lengths[None, :, None]).astype(F32)
     mask_rows = mask[0][:, :, None]
-    mask_wide = jnp.broadcast_to(mask[..., None], (2, slots, quarter, head_size))
+    mask_wide = jnp.broadcast_to(mask[..., None], (2, slots, quarter, head_size)).astype(BF16)
     member = 2 * (wide_index % 2) + side
     spots = jnp.concatenate(
         [
             block_spots(order_xy)[None],
             block_spots(order_yx)[None],
+            block_spots(order_v)[None],
             jnp.broadcast_to(member, (1, members, 2)).astype(jnp.int32),
         ]
     )
@@ -523,11 +529,14 @@
     log_lanes = jnp.repeat(log_decay, head_size)
     query_decay = table(jnp.exp((spot[..., None] + 1.0) * log_lanes))
     key_decay = table(jnp.exp((block - 1.0 - spot[..., None]) * log_lanes))
-    flat = spot.reshape(-1)
+    flat = jnp.broadcast_to(spot[:, None], (2, count, quarter)).reshape(-1)
+    slot_of = jnp.broadcast_to(jnp.arange(count)[None, :, None], (2, count, quarter)).reshape(-1)
     gap = flat[:, None] - flat[None, :]
+    seen = (gap >= 0.0) & (slot_of[:, None] == slot_of[None, :])
     decay_grid = jnp.where(
-        gap[None] >= 0.0, jnp.exp(jnp.maximum(gap, 0.0)[None] * log_decay[:, None, None]), 0.0
-    )
+        seen[None], jnp.exp(jnp.maximum(gap, 0.0)[None] * log_decay[:, None, None]), 0.0
+    )
+    decay_grid_t = jnp.swapaxes(decay_grid, 1, 2)
 
     def join(*parts):
         return jnp.concatenate(parts, axis=0)
@@ -538,33 +547,35 @@
     def tie(*arrays):
         return lax.optimization_barrier(arrays)
 
-    def far_steps(x):
-        for m in z_far:
+    def far_open(x):
+        for m in z_far[:-1]:
             x = join(x, swap(x, m))
-        return x
-
-    kv = jnp.stack([key_weight, value_weight])[None]
+        return x, swap(x, z_far[-1])
+
+    key_w, value_w = key_weight[None, None], value_weight[None, None]
     dn = down_matrix.T[None]
     gl = jnp.stack([gate_matrix.T, lift_matrix.T])[None]
     qmo = jnp.stack([query_weight, modulate_weight, output_weight])[None]
     input_rows = layer_input.astype(F32)
     normed = simple_norm(input_rows).astype(BF16)
+    cotangent = output_cotangent.astype(F32)
+    cotangent_x = [swap(output_cotangent[: slots // 2], x_mask)]
+    key_w, k_got = far_open(key_w)
+    k_got, v_got = tie(k_got, swap(value_w, y_mask))
+    key_w, value_w = join(key_w, k_got), join(value_w, v_got)
+    value_w, v_got = far_open(value_w)
+    k_got, v_got, dn_y, cotangent_x[0] = tie(
+        swap(key_w, z_near), v_got, swap(dn, y_mask), cotangent_x[0]
+    )
+    key_w, value_w, dn = join(key_w, k_got), join(value_w, v_got), join(dn, dn_y)
     normed_pair = (normed, swap(normed, 1))
-    kv, dn_x = tie(far_steps(kv), swap(dn, x_mask))
-    dn = join(dn, dn_x)
-    kv_z, dn_y = tie(swap(kv, z_near), swap(dn, y_mask))
-    kv, dn = join(kv, kv_z), join(dn, dn_y)
-    k_half, v_half = kv[:, :1], kv[:, 1:]
-    qmo, k_half, v_half = tie(qmo, k_half, v_half)
-    k_x, v_y, qmo = tie(swap(k_half, x_mask), swap(v_half, y_mask), far_steps(qmo))
-    k_half, v_half = join(k_half, k_x), join(v_half, v_y)
-    k_far, v_far, qmo_z = tie(swap(k_half, y_mask), swap(v_half, x_mask), swap(qmo, z_near))
-    key_parts, value_parts = (k_half, k_far), (v_half, v_far)
-    qmo = join(qmo, qmo_z)
-    qm, out_w = qmo[:, :2], qmo[:, 2:]
-    gl = after(gl, qmo_z)
-    qm_x, o_y = swap(qm, x_mask), swap(out_w, y_mask)
-    gl = far_steps(gl)
+    k_got, v_got = tie(swap(key_w, x_mask), swap(value_w, z_near))
+    key_w, value_w, qmo = join(key_w, k_got), join(value_w, v_got), tie(qmo, k_got)[0]
+    qmo, q_got = far_open(qmo)
+    k_got, v_got, q_got = tie(swap(key_w, y_mask), swap(value_w, x_mask), q_got)
+    key_parts, value_parts = (key_w, k_got), (value_w, v_got)
+    qmo = join(qmo, q_got)
+    qmo_z = swap(qmo, z_near)
     inner_width = heads * head_size
     chip_shape = (2, slots, quarter, inner_width)
     row_shape = (slots, quarter, width)
@@ -583,25 +594,41 @@
             (value_parts[0], "any"), (value_parts[1], "any"),
         ],
         [
-            (chip_shape, F32, "pair"), (chip_shape, BF16, "pair"), (chip_shape, BF16, "pair"),
+            (chip_shape, BF16, "pair"), (chip_shape, BF16, "pair"), (chip_shape, BF16, "pair"),
             (state_shape, BF16, "rows"),
         ],
         [wide_scratch, wide_scratch, dma((2, members))],
         steps, 2 * square_flops,
     )
-    local_state, qm_x, o_y = tie(local_state, qm_x, o_y)
-    qm, out_w = join(qm, qm_x), join(out_w, o_y)
+    local_state, qmo_z = tie(local_state, qmo_z)
+    qmo = join(qmo, qmo_z)
+    qm, out_w = qmo[:, :2], qmo[:, 2:]
     scan = Carry(local_state, block_decay, False)
     scan.spread()
-    *scan.got, gl = tie(*scan.got, gl)
-    qm_y, o_x = swap(qm, y_mask), swap(out_w, x_mask)
-    gl_z = swap(gl, z_near)
-    scan.along()
-    scan.before, qm_y, o_x, gl_z = tie(scan.before, qm_y, o_x, gl_z)
-    gl = join(gl, gl_z)
-    query_parts, output_parts = (qm, qm_y), (out_w, o_x)
-    dn = after(dn, gl_z)
-    dn = far_steps(dn)
+    gl, gl_got = far_open(tie(gl, qmo_z)[0])
+    scan.got[1], scan.got[2], scan.got[3], qm, out_w = tie(*scan.got[1:], qm, out_w)
+    qm_x, o_y = swap(qm, x_mask), swap(out_w, y_mask)
+    held = {}
+
+    def forward_step(step, got):
+        if step == 1:
+            got, qx, oy, held["gl"] = tie(got, qm_x, o_y, gl_got)
+            held["qm"], held["out"] = join(qm, qx), join(out_w, oy)
+            held["gl"] = join(gl, held["gl"])
+            held["more"] = [
+                swap(held["qm"], y_mask), swap(held["out"], x_mask), swap(held["gl"], z_near),
+                swap(tie(output_cotangent[slots // 2 :], oy)[0], x_mask),
+            ]
+        if step == 2:
+            got, *held["more"] = tie(got, *held["more"])
+        return got
+
+    scan.along(forward_step)
+    qm_y, o_x, gl_z, more_x = held["more"]
+    cotangent_x.append(more_x)
+    gl = join(held["gl"], gl_z)
+    query_parts, output_parts = (held["qm"], qm_y), (held["out"], o_x)
+    dn, dn_got = far_open(tie(dn, gl_z)[0])
     state_parts = scan.back()
     query_pre, queries, modulate, intra = run(
         query_kernel, "query", spots,
@@ -611,15 +638,14 @@
             (keys, "pair"), (values, "pair"), (query_parts[0], "any"), (query_parts[1], "any"),
         ],
         [
-            (chip_shape, F32, "pair"), (chip_shape, BF16, "pair"), (chip_shape, F32, "pair"),
-            (chip_shape, F32, "pair"),
+            (chip_shape, BF16, "pair"), (chip_shape, BF16, "pair"), (chip_shape, BF16, "pair"),
+            (chip_shape, BF16, "pair"),
         ],
         [wide_scratch, wide_scratch, dma((2, members))],
         steps, 2 * square_flops,
     )
-    *state_parts, queries = tie(*state_parts, queries)
-    gate_w, lift_w = after(gl, *state_parts)[:, 0], after(gl, *state_parts)[:, 1]
-    gate_y, lift_x = swap(gate_w, y_mask), swap(lift_w, x_mask)
+    *state_parts, queries, dn_got = tie(*state_parts, queries, dn_got)
+    dn = join(dn, dn_got)
     state_inputs = [(p, "any") for p in state_parts]
     output_inputs = [(p, "any") for p in output_parts]
     mixed, gated, near_att, far_att = run(
@@ -629,30 +655,35 @@
             *state_inputs, *output_inputs,
         ],
         [
-            (chip_shape, F32, "pair"), (chip_shape, BF16, "pair"), (row_shape, F32, "rows"),
+            (chip_shape, BF16, "pair"), (chip_shape, BF16, "pair"), (row_shape, F32, "rows"),
             (row_shape, BF16, "rows"),
         ],
         [wide_scratch, held_scratch, dma((members,)), dma((4,))],
         steps, square_flops,
     )
-    near_att, gate_y, lift_x, dn = tie(near_att, gate_y, lift_x, dn)
-    gate_w, lift_w = join(gate_w, gate_y), join(lift_w, lift_x)
-    gate_x, lift_y, dn_z = swap(gate_w, x_mask), swap(lift_w, y_mask), swap(dn, z_near)
     middle = input_rows + core_sum(near_att, far_att)
+    two = simple_norm(middle).astype(BF16)
+    two_x, gl_y = tie(swap(two, x_mask), swap(gl, y_mask))
+    dn_z = swap(dn, z_near)
+
+    def quarters(mine, got_x):
+        return jnp.stack([mine, got_x, swap(mine, 1), swap(got_x, 1)])
+
+    def core_part(parts):
+        parts = parts.astype(BF16)
+        got = swap(parts[2:], 1)
+        return fold(parts[0], got[0], F32), fold(parts[1], got[1])
+
+    normed_two = quarters(two, two_x)
+    row_starts = (narrow_index ^ jnp.array([0, x_mask, 1, 1 + x_mask], jnp.int32)) * quarter
+    row_spots = wide_index * (quarter * narrow_count) + row_starts[:, None] + jnp.arange(quarter)
+    row_mask = (row_spots[:, None, :] < valid_lengths[None, :, None]).astype(F32)[..., None]
+    branch_rows = quarters(output_cotangent, jnp.concatenate(cotangent_x))
+    branch_rows = (row_mask * branch_rows.astype(F32)).astype(BF16)
+    gate_t = join(gl[:, 0], gl_y[:, 0]).reshape(-1, width)
+    lift_t = join(gl[:, 1], gl_y[:, 1]).reshape(-1, width)
     bulk = half // 2
-    gate_t = join(gate_w, gate_x).reshape(-1, width)
-    lift_t = jnp.stack(
-        [lift_w.reshape(2, bulk, -1, width), lift_y.reshape(2, bulk, -1, width)], axis=1
-    ).reshape(-1, width)
-    down_t = jnp.moveaxis(join(dn, dn_z).reshape(bulk, 4, -1, width), 0, 1)
-    down_t = jnp.swapaxes(down_t.reshape(2, 2, bulk, -1, width), 0, 1).reshape(-1, width)
-
-    def pair(mine):
-        return jnp.stack([mine, exchange(mine, 1)])
-
-    normed_two = pair(simple_norm(middle).astype(BF16))
-    cotangent = output_cotangent.astype(F32)
-    branch_grad = pair((mask_rows * cotangent).astype(BF16))
+    down_t = jnp.swapaxes(join(dn, dn_z).reshape(bulk, 2, -1, width), 0, 1).reshape(-1, width)
 
     def hidden(rows_in, matrix):
         return jnp.einsum("pbld,fd->pblf", rows_in, matrix, preferred_element_type=F32)
@@ -662,7 +693,7 @@
 
     gate_pre = hidden(normed_two, gate_t)
     lift_pre = hidden(normed_two, lift_t)
-    inner_grad = hidden(branch_grad, down_t)
+    inner_grad = hidden(branch_rows, down_t)
     gate_act = apply_swish(gate_pre)
     inner = (gate_act * lift_pre).astype(BF16)
     gate_grad = (inner_grad * lift_pre * swish_slope(gate_pre)).astype(BF16)
@@ -671,25 +702,19 @@
     normed_grad = normed_grad + jnp.einsum(
         "pblf,fd->pbld", lift_grad, lift_t, preferred_element_type=F32
     )
-    middle_grad = cotangent + norm_backward(
-        middle, core_sum(normed_grad[0], normed_grad[1].astype(BF16))
-    )
-    branch = jnp.einsum("pblf,fd->pbld", inner, down_t, preferred_element_type=F32)
-    branch = core_sum(branch[0], branch[1].astype(BF16))
-    layer_output = (middle + mask_rows * branch).astype(BF16)
-
-    def fold(mine, got):
-        return (mine.astype(F32) + got.astype(F32)).astype(BF16)
-
-    def final(mine, got):
-        return mine.astype(F32) + got.astype(F32)
-
-    gate_g = outer(gate_grad, normed_two).reshape(2, half, -1, width)
-    lift_g = outer(lift_grad, normed_two).reshape(2, 2, bulk, -1, width)
-    down_g = outer(inner, branch_grad).reshape(2, 2, 2, bulk // 2, -1, width)
-    gate_x = swap(gate_g[1], x_mask)
-    lift_y = swap(lift_g[:, 1], y_mask)
-    down_z = swap(down_g[:, :, 1], z_near)
+    row_mine, row_send = core_part(normed_grad)
+    row_got = swap(row_send, x_mask)
+    gate_grad, lift_grad, inner, row_send = tie(gate_grad, lift_grad, inner, row_send)
+    gate_g = outer(gate_grad, normed_two).reshape(2, bulk, -1, width)
+    gate_y = swap(gate_g[1], y_mask)
+    lift_grad, inner, gate_g = tie(lift_grad, inner, gate_g)
+    lift_g = outer(lift_grad, normed_two).reshape(2, bulk, -1, width)
+    down_g = outer(inner, branch_rows).reshape(2, 2, bulk // 2, -1, width)
+    down_z = swap(down_g[:, 1], z_near)
+    row_got, gate_y = tie(row_got, gate_y)
+    lift_y = swap(tie(lift_g, gate_y)[0][1], y_mask)
+    middle_grad = cotangent + norm_backward(middle, row_mine + row_got.astype(F32))
+
     attended_grad = middle_grad.astype(BF16)
     attended_pair = (attended_grad, exchange(attended_grad, 1))
     modulate_grad, query_grad, key_grad, value_grad, state_grad = run(
@@ -698,18 +723,23 @@
             (attended_pair[0], "rows"), (attended_pair[1], "rows"), (mixed, "pair"),
             (modulate, "pair"), (queries, "pair"), (query_pre, "pair"), (keys, "pair"),
             (values, "pair"), (mask_wide, "pair"), (cosine, "whole"), (sine, "whole"),
-            (query_decay, "whole"), (decay_grid, "whole"), *state_inputs, *output_inputs,
+            (query_decay, "whole"), (decay_grid, "whole"), (decay_grid_t, "whole"),
+            *state_inputs, *output_inputs,
         ],
         [
-            (chip_shape, BF16, "pair"), (chip_shape, BF16, "pair"), (chip_shape, F32, "pair"),
-            (chip_shape, F32, "pair"), (state_shape, BF16, "rows"),
+            (chip_shape, BF16, "pair"), (chip_shape, BF16, "pair"), (chip_shape, BF16, "pair"),
+            (chip_shape, BF16, "pair"), (state_shape, BF16, "rows"),
         ],
         [wide_scratch, held_scratch, dma((members,)), dma((4,))],
         steps, 2 * square_flops,
     )
-    state_grad, gate_x, lift_y = tie(state_grad, gate_x, lift_y)
-    gate_g = fold(gate_g[0], gate_x)
-    lift_g = fold(lift_g[:, 0], lift_y)
+    state_grad, lift_y, down_z, gated = tie(state_grad, lift_y, down_z, gated)
+    near = bulk // 2
+    down_g = jnp.moveaxis(fold(down_g[:, 0], down_z), 1, 0)
+    for m in z_far[:0:-1]:
+        size = down_g.shape[0] // 2
+        down_g = fold(down_g[:size], swap(down_g[size:], m))
+    down_far = swap(down_g[1], z_far[0])
     scan = Carry(state_grad, block_decay, True)
     scan.spread()
 
@@ -728,42 +758,55 @@
     (query_rows,) = run(
         rows_kernel, "query_rows", spots,
         [(query_grad, "pair"), (modulate_grad, "pair"), (query_parts[0], "any"), (query_parts[1], "any")],
-        [((2, *row_shape), F32, "pair")],
+        [((2, *row_shape), BF16, "pair")],
         [wide_scratch, wide_scratch, dma((2, members))],
         steps, 2 * square_flops,
     )
-    *scan.got, down_z, gate_g, lift_g = tie(*scan.got, down_z, gate_g, lift_g)
-    gate_y, lift_x = swap(gate_g[bulk:], y_mask), swap(lift_g[1], x_mask)
-    output_x, query_y = swap(output_send, x_mask), swap(query_send, y_mask)
-    down_g = fold(down_g[:, :, 0], down_z)
-    scan.along()
-    scan.before, gate_y, lift_x, output_x, query_y, query_rows = tie(
-        scan.before, gate_y, lift_x, output_x, query_y, query_rows
-    )
-    later_parts = scan.back()
-    gate_lift = jnp.stack([fold(gate_g[:bulk], gate_y), fold(lift_g[0], lift_x)], axis=1)
-    output_g, query_g = fold(output_keep, output_x), fold(query_keep, query_y)
-    near = bulk // 2
-    gl_z = swap(gate_lift[near:], z_near)
-    *later_parts, gl_z = tie(*later_parts, gl_z)
-    gate_lift = fold(gate_lift[:near], gl_z)
+    *scan.got, down_far, query_keep, query_send, output_keep, output_send, inner = tie(
+        *scan.got, down_far, query_keep, query_send, output_keep, output_send, inner
+    )
+    branch = jnp.einsum("pblf,fd->pbld", inner, down_t, preferred_element_type=F32)
+    branch_mine, branch_send = core_part(branch)
+    down_g = fold(down_g[0], down_far)
+    gl_g = jnp.stack([fold(gate_g[0], gate_y), fold(lift_g[0], lift_y)], axis=1)
+
+    query_y, output_x = swap(query_send[:, :1], y_mask), swap(output_send, x_mask)
+
+    def backward_step(step, got):
+        if step == 1:
+            got, held["y"], mod_send = tie(got, query_y, query_send[:, 1:])
+            held["more"] = swap(mod_send, y_mask)
+        if step == 2:
+            got, held["more"], held["x"] = tie(got, held["more"], output_x)
+        return got
+
+    scan.along(backward_step)
+    query_y = jnp.concatenate([held["y"], held["more"]], axis=1)
+    scan.before, query_rows, branch_send = tie(scan.before, query_rows, branch_send)
+    later_parts = list(tie(*scan.back()))
+    gl_g, query_keep, output_keep, branch_send = tie(
+        gl_g, query_keep, output_keep, branch_send, *later_parts
+    )[:4]
+    query_g, output_g = fold(query_keep, query_y), fold(output_keep, held["x"])
+    quad = half // 2
+    gl_z = swap(gl_g[near:], z_near)
+    query_x, output_y = swap(query_g[quad:], x_mask), swap(output_g[quad:], y_mask)
+    branch_got = swap(branch_send, x_mask)
     later_inputs = [(p, "any") for p in later_parts]
     quad = half // 2
-    down_g, output_g, query_g = tie(down_g, output_g, query_g, *later_parts)[:3]
-    output_y, query_x = swap(output_g[quad:], y_mask), swap(query_g[quad:], x_mask)
+    def far_pairs(x):
+        x = x.reshape(-1, 2, *x.shape[1:])
+        for m in reversed(z_far):
+            size = x.shape[0] // 2
+            x = fold(x[:size], swap(x[size:], m))
+        return x[0]
 
     def far_folds(x):
         for m in reversed(z_far):
             size = x.shape[0] // 2
             x = (fold if size > 1 else final)(x[:size], swap(x[size:], m))
-        return x[0]
-
-    down_far = jnp.moveaxis(down_g, 2, 0)
-    for m in reversed(z_far):
-        size = down_far.shape[0] // 2
-        down_far = fold(down_far[:size], swap(down_far[size:], m))
-    down_g = down_far[0]
-    gate_lift = far_folds(gate_lift)
+        return x
+
     key_out, value_out, near_rows, far_rows = run(
         key_back_kernel, "key_back", spots,
         [
@@ -780,26 +823,37 @@
         [wide_scratch, wide_scratch, held_scratch, dma((2, members)), dma((4,))],
         steps, 2 * square_flops,
     )
-    key_out, value_out, output_y, query_x = tie(key_out, value_out, output_y, query_x)
     key_keep, key_send = square("key_outer", 0, normed_pair, key_out)
-    value_keep, value_send = square("value_outer", 1, normed_pair, value_out)
+    value_keep, value_send = square("value_outer", 2, normed_pair, value_out)
+    key_send, value_send, gl_z, query_x, output_y = tie(
+        key_send, value_send, gl_z, query_x, output_y
+    )
+    gl_g = fold(gl_g[:near], gl_z)
+    for m in z_far[:0:-1]:
+        size = gl_g.shape[0] // 2
+        gl_g = fold(gl_g[:size], swap(gl_g[size:], m))
+    gl_far = swap(gl_g[1], z_far[0])
     key_y, value_x = swap(key_send, y_mask), swap(value_send, x_mask)
+    key_y, value_x, gl_far = tie(key_y, value_x, gl_far)
+    down_y = swap(down_g[1], y_mask)
+    gate_lift = final(gl_g[0], gl_far)
+    key_g, value_g = fold(key_keep, key_y), fold(value_keep, value_x)
+    key_x, value_z = swap(key_g[quad:], x_mask), swap(value_g[quad:], z_near)
     qmo_g = jnp.concatenate(
         [fold(query_g[:quad], query_x), fold(output_g[:quad], output_y)], axis=1
     )
     qmo_z = swap(qmo_g[near:], z_near)
-    down_y = swap(down_g[:, 1], y_mask)
-    key_g, value_g = fold(key_keep, key_y), fold(value_keep, value_x)
-    down_g = fold(down_g[:, 0], down_y)
-    qmo_g = fold(qmo_g[:near], qmo_z)
-    key_x, value_y = swap(key_g[quad:], x_mask), swap(value_g[quad:], y_mask)
-    down_x = swap(down_g[1], x_mask)
-    query_gradient, modulate_gradient, output_gradient = far_folds(qmo_g)
-    down_gradient = final(down_g[0], down_x).T
+    key_x, value_z, down_y, qmo_z, branch_got = tie(key_x, value_z, down_y, qmo_z, branch_got)
+    layer_output = (middle + mask_rows * (branch_mine + branch_got.astype(F32))).astype(BF16)
+    key_g, value_g = fold(key_g[:quad], key_x), fold(value_g[:quad], value_z)
+    key_z, value_far = swap(key_g[near:], z_near), far_pairs(value_g)
+    qmo_g = far_folds(fold(qmo_g[:near], qmo_z))[0]
+    key_gradient = far_folds(fold(key_g[:near], key_z))[0][0]
+    value_y = swap(value_far[1], y_mask)
+    value_gradient = final(value_far[0], value_y)[0]
+    query_gradient, modulate_gradient, output_gradient = qmo_g
+    down_gradient = final(down_g[0], down_y).T
     gate_gradient, lift_gradient = gate_lift[0].T, gate_lift[1].T
-    kv_g = jnp.concatenate([fold(key_g[:quad], key_x), fold(value_g[:quad], value_y)], axis=1)
-    kv_z = swap(kv_g[near:], z_near)
-    key_gradient, value_gradient = far_folds(fold(kv_g[:near], kv_z))
     input_gradient = middle_grad + norm_backward(input_rows, core_sum(near_rows, far_rows))
     return (
         layer_output,

time: 452 us -> 424 us (0.938)
  waiting for transfers between devices: 176 us -> 149 us
  local copies, waits for them, and re-layouts: 17 us -> 28 us
  starting transfers between devices: 89.4 us -> 78.8 us
    ppermute x65 -> x70, waiting for transfers between devices: 150 us -> 126 us  [exchange(): return lax.ppermute(x, AXES, [(i, i ^ mask) for i in range(count)])]
    unnamed x223 -> x296, local copies, waits for them, and re-layouts: 6.48 us -> 15.1 us
    ppermute x4, starting transfers between devices: 14.6 us -> 8.47 us  [shift_z(): return lax.ppermute(x, AXES, pairs)]
    ppermute x65 -> x70, starting transfers between devices: 74.8 us -> 70.3 us  [exchange(): return lax.ppermute(x, AXES, [(i, i ^ mask) for i in range(count)])]
    convert_element_type x21 -> x22, other arithmetic: 13 us -> 15 us  [the longest x15 8.72 us: fold(): return (mine.astype(F32) + got.astype(F32)).astype(dtype)]
  transfers between devices with their start and end apart: 69 -> 74, of which waited for: 29 -> 31; matrix products, arithmetic and copies ran while one was open for 18% -> 17% of each run, Pallas kernels for 15% -> 14%
where the time goes in v4:
time: 424 us; the launch traced here: 417 us
  waiting for transfers between devices  149 us (35%)
  starting transfers between devices  78.8 us (19%)
  Pallas kernels  61.9 us (15%)
  matrix products  51.2 us (12%)
  other arithmetic  44.8 us (11%)
  local copies, waits for them, and re-layouts  28 us (7%)
    ppermute x70, waiting for transfers between devices, exchange(): return lax.ppermute(x, AXES, [(i, i ^ mask) for i in range(count)])  126 us
    ppermute x70, starting transfers between devices, exchange(): return lax.ppermute(x, AXES, [(i, i ^ mask) for i in range(count)])  70.3 us
    pallas_call x10, Pallas kernels, run(): pl.pallas_call(kernel, out_shape=[jax.ShapeDtypeStruct(s, d) for s, d, _...  61.9 us
    ppermute x4, waiting for transfers between devices, shift_z(): return lax.ppermute(x, AXES, pairs)  22.3 us
    dot_general x3, matrix products, hidden(): jnp.einsum('pbld,fd->pblf', rows_in, matrix, preferred_element_type=F32)  21.5 us
    unnamed x296, local copies, waits for them, and re-layouts  15.1 us
    dot_general x3, matrix products, outer(): jnp.einsum('pblf,pbld->fd', a, b, preferred_element_type=F32).astype(BF16)  12.4 us
    convert_element_type x15, other arithmetic, fold(): return (mine.astype(F32) + got.astype(F32)).astype(dtype)  8.72 us
  transfers between devices with their start and end apart: 74, of which 31 were waited for; matrix products, arithmetic and copies ran while one was open for 17% of the time, Pallas kernels for 14%

profile of v4, /device:TPU:0, one launch (start us, length us, event | category | flops | bytes accessed | tf_op | source)
XLA Modules:
  0.0 416.9 jit_solution(7901806902188280674)
XLA Ops:
  16.5 4.7 %collective-permute-done.5 = bf16[2,1,128,256]{3,2,1,0:T(8,128)(2,1)S(1)} collective-permute-done((bf16[2,1,128,256]{3,2,1,0:T(8,128)(2,1)S(1)}, bf16[2,1,128,256]{3,2,1,0:T(8,128)(2,1)S(1)}, u32[]{:S(2)}, u32[]{:S(2)}) %collective-permute-start.5) | collective-permute-done | bytes 131104 | tf_op jit(solution)/shard_map/ppermute | solution.py:38
  38.4 7.5 %collective-permute-done.12 = bf16[1,3,128,256]{3,2,1,0:T(8,128)(2,1)S(1)} collective-permute-done((bf16[1,3,128,256]{3,2,1,0:T(8,128)(2,1)S(1)}, bf16[1,3,128,256]{3,2,1,0:T(8,128)(2,1)S(1)}, u32[]{:S(2)}, u32[]{:S(2)}) %collective-permute-start.12) | collective-permute-done | bytes 196640 | tf_op jit(solution)/shard_map/ppermute | solution.py:38
  47.6 6.0 %key_value.1 = (bf16[2,8,64,512]{3,2,1,0:T(8,128)(2,1)S(1)}, bf16[2,8,64,512]{3,2,1,0:T(8,128)(2,1)S(1)}, bf16[2,8,64,512]{3,2,1,0:T(8,128)(2,1)S(1)}, bf16[8,4,128,128]{3,2,1,0:T(8,128)(2,1)S(1)}) custom-call(s32[4,16,2]{2,1,0:T(8,128)S(1)} %add_add_fusion.spots, bf16[8,64,1024]{2,1,0:T(8,128)(2,1)S(1)} %fusion.11.near, ...), custom_call_target="tpu_custom_call" | custom-call | flops 2147483648 | bytes 9437184 | tf_op jit(solution)/shard_map/key_value/pallas_call | solution.py:394
  68.9 4.6 %collective-permute-start.17 = (bf16[2,4,128,128]{3,2,1,0:T(8,128)(2,1)S(1)}, bf16[2,4,128,128]{3,2,1,0:T(8,128)(2,1)S(1)}, u32[]{:S(2)}, u32[]{:S(2)}) collective-permute-start(bf16[2,4,128,128]{3,2,1,0:T(8,128)(2,1)S(1)} %get-tuple-element.260), channel_id=1, source_target_pairs={{0,8},{1,9},{2,10},{3,11},{4,12},{5,13},{6,14},{7,15},{8,16},{9,17... | collective-permute-start | bytes 786440 | tf_op jit(solution)/shard_map/ppermute | solution.py:50
  74.5 4.7 %collective-permute-done.17 = bf16[2,4,128,128]{3,2,1,0:T(8,128)(2,1)S(1)} collective-permute-done((bf16[2,4,128,128]{3,2,1,0:T(8,128)(2,1)S(1)}, bf16[2,4,128,128]{3,2,1,0:T(8,128)(2,1)S(1)}, u32[]{:S(2)}, u32[]{:S(2)}) %collective-permute-start.17) | collective-permute-done | bytes 262176 | tf_op jit(solution)/shard_map/ppermute | solution.py:50
  91.9 7.5 %collective-permute-done.21 = bf16[2,4,128,128]{3,2,1,0:T(8,128)(2,1)S(1)} collective-permute-done((bf16[2,4,128,128]{3,2,1,0:T(8,128)(2,1)S(1)}, bf16[2,4,128,128]{3,2,1,0:T(8,128)(2,1)S(1)}, u32[]{:S(2)}, u32[]{:S(2)}) %collective-permute-start.21) | collective-permute-done | bytes 262176 | tf_op jit(solution)/shard_map/ppermute | solution.py:50
  112.2 8.2 %query.1 = (bf16[2,8,64,512]{3,2,1,0:T(8,128)(2,1)S(1)}, bf16[2,8,64,512]{3,2,1,0:T(8,128)(2,1)S(1)}, bf16[2,8,64,512]{3,2,1,0:T(8,128)(2,1)S(1)}, bf16[2,8,64,512]{3,2,1,0:T(8,128)(2,1)S(1)}) custom-call(s32[4,16,2]{2,1,0:T(8,128)S(1)} %copy-done.41, bf16[8,64,1024]{2,1,0:T(8,128)(2,1)S(1)} %copy-done.27, bf16[8,64,1024]{2,1,0:T(8,128)(2,1)S(1)} %copy-done.51, ...), custom_call_target="tpu_custom_call" | custom-call | flops 2147483648 | bytes 12058624 | tf_op jit(solution)/shard_map/query/pallas_call | solution.py:394
  120.7 4.9 %mixed.1 = (bf16[2,8,64,512]{3,2,1,0:T(8,128)(2,1)S(1)}, bf16[2,8,64,512]{3,2,1,0:T(8,128)(2,1)S(1)}, f32[8,64,1024]{2,1,0:T(8,128)S(1)}, bf16[8,64,1024]{2,1,0:T(8,128)(2,1)S(1)}) custom-call(s32[4,16,2]{2,1,0:T(8,128)S(1)} %copy-done.41, bf16[2,8,64,512]{3,2,1,0:T(8,128)(2,1)S(1)} %get-tuple-element.163.queries, ...), custom_call_target="tpu_custom_call" | custom-call | flops 1073741824 | bytes 11010048 | tf_op jit(solution)/shard_map/mixed/pallas_call | solution.py:394
  133.1 16.0 %collective-permute-done.33 = bf16[4,88,1024]{2,1,0:T(8,128)(2,1)S(1)} collective-permute-done((bf16[4,88,1024]{2,1,0:T(8,128)(2,1)S(1)}, bf16[4,88,1024]{2,1,0:T(8,128)(2,1)S(1)}, u32[]{:S(2)}, u32[]{:S(2)}) %collective-permute-start.33) | collective-permute-done | bytes 720928 | tf_op jit(solution)/shard_map/ppermute | solution.py:38
  149.5 12.6 %collective-permute-done.35 = bf16[4,2,88,1024]{3,2,0,1:T(8,128)(2,1)S(1)} collective-permute-done((bf16[4,2,88,1024]{3,2,0,1:T(8,128)(2,1)S(1)}, bf16[4,2,88,1024]{3,2,0,1:T(8,128)(2,1)S(1)}, u32[]{:S(2)}, u32[]{:S(2)}) %collective-permute-start.35) | collective-permute-done | bytes 1441824 | tf_op jit(solution)/shard_map/ppermute | solution.py:38
  162.1 5.4 %fusion.119 = f32[4,8,64,704]{3,2,1,0:T(8,128)} fusion(bf16[704,1024,1,1]{1,0,3,2:T(8,128)(2,1)S(1)} %bitcast.219, bf16[1,8,64,1024]{3,2,1,0:T(8,128)(2,1)S(1)} %bitcast.250, bf16[1,8,64,1024]{3,2,1,0:T(8,128)(2,1)S(1)} %bitcast.248, bf16[1,8,64,1024]{3,2,1,0:T(8,128)(2,1)S(1)} %bitcast.239, bf16[1,8,64,1024]{3,2,1,0:T(8,128)(2,1)S(1)} %bitcast.216, ...), kind=kOutput, calls=%fused_computation.356 | convolution fusion | flops 2965372928 | bytes 11411456 | tf_op jit(solution)/shard_map/pbld,fd->pblf/dot_general | solution.py:689
  168.1 5.4 %fusion.108 = f32[4,8,64,704]{3,2,1,0:T(8,128)} fusion(bf16[704,1024,1,1]{1,0,3,2:T(8,128)(2,1)S(1)} %bitcast.224, bf16[1,8,64,1024]{3,2,1,0:T(8,128)(2,1)S(1)} %bitcast.260, bf16[1,8,64,1024]{3,2,1,0:T(8,128)(2,1)S(1)} %bitcast.256, bf16[1,8,64,1024]{3,2,1,0:T(8,128)(2,1)S(1)} %bitcast.252, bf16[1,8,64,1024]{3,2,1,0:T(8,128)(2,1)S(1)} %fusion.131), kind=kOutput, calls=%fused_computation.347 | convolution fusion | flops 2959081472 | bytes 11403264 | tf_op jit(solution)/shard_map/pbld,fd->pblf/dot_general | solution.py:689
  173.5 10.7 %multiply_convert_fusion.1 = (bf16[4,8,64,704]{3,2,1,0:T(8,128)(2,1)}, bf16[4,8,64,704]{3,2,1,0:T(8,128)(2,1)}, bf16[4,8,64,704]{3,2,1,0:T(8,128)(2,1)}) fusion(f32[4,8,64,704]{3,2,1,0:T(8,128)} %fusion.108, f32[4,8,64,704]{3,2,1,0:T(8,128)} %fusion.119, bf16[704,1024,1,1]{1,0,3,2:T(8,128)(2,1)S(1)} %bitcast.226, bf16[1,8,64,1024]{3,2,1,0:T(8,128)(2,1)S(1)} %bitcast.261, ...), kind=kOutput, calls=%fused_computation.2 | convolution fusion | flops 2979266560 | bytes 25821184 | tf_op jit(solution)/shard_map/pbld,fd->pblf/dot_general | solution.py:689
  184.3 7.7 %fusion.120 = f32[4,8,64,1024]{3,2,1,0:T(8,128)} fusion(bf16[4,8,64,704]{3,2,1,0:T(8,128)(2,1)} %get-tuple-element.178, bf16[704,1024,1,1]{1,0,3,2:T(8,128)(2,1)S(1)} %bitcast.225), kind=kOutput, calls=%fused_computation.357 | convolution fusion | flops 2952790016 | bytes 12713984 | tf_op jit(solution)/shard_map/pblf,fd->pbld/dot_general | solution.py:701
  191.9 6.0 %add_convert_fusion = bf16[4,8,64,1024]{3,2,1,0:T(8,128)(2,1)S(1)} fusion(f32[4,8,64,1024]{3,2,1,0:T(8,128)} %fusion.120, bf16[4,8,64,704]{3,2,1,0:T(8,128)(2,1)S(1)} %copy-done.140, bf16[704,1024,1,1]{1,0,3,2:T(8,128)(2,1)S(1)} %bitcast.227), kind=kOutput, calls=%fused_computation | convolution fusion | flops 2956984320 | bytes 16908288 | tf_op jit(solution)/shard_map/pblf,fd->pbld/dot_general | solution.py:702
  207.1 5.8 %bitcast_convert_fusion = bf16[704,1024]{1,0:T(8,128)(2,1)S(1)} fusion(bf16[4,8,64,704]{3,2,1,0:T(8,128)(2,1)} %get-tuple-element.199, bf16[1,8,64,1024]{3,2,1,0:T(8,128)(2,1)S(1)} %bitcast.251, bf16[1,8,64,1024]{3,2,1,0:T(8,128)(2,1)S(1)} %bitcast.249, bf16[1,8,64,1024]{3,2,1,0:T(8,128)(2,1)S(1)} %bitcast.240, bf16[1,8,64,1024]{3,2,1,0:T(8,128)(2,1)S(1)} %bitcast.217, ...), kind=kOutput, calls=%fused_computation.22 | convolution fusion | flops 2966093824 | bytes 8527872 | tf_op jit(solution)/shard_map/pblf,pbld->fd/dot_general | solution.py:692
  217.3 13.8 %collective-permute-done.40 = bf16[4,88,1024]{2,1,0:T(8,128)(2,1)S(1)} collective-permute-done((bf16[4,88,1024]{2,1,0:T(8,128)(2,1)S(1)}, bf16[4,88,1024]{2,1,0:T(8,128)(2,1)S(1)}, u32[]{:S(2)}, u32[]{:S(2)}) %collective-permute-start.40) | collective-permute-done | bytes 720928 | tf_op jit(solution)/shard_map/ppermute | solution.py:38
  248.7 12.6 %mixed_back.1 = (bf16[2,8,64,512]{3,2,1,0:T(8,128)(2,1)S(1)}, bf16[2,8,64,512]{3,2,1,0:T(8,128)(2,1)S(1)}, bf16[2,8,64,512]{3,2,1,0:T(8,128)(2,1)S(1)}, bf16[2,8...) custom-call(s32[4,16,2]{2,1,0:T(8,128)S(1)} %copy-done.42, bf16[8,64,1024]{2,1,0:T(8,128)(2,1)} %get-tuple-element.256.near, ...), custom_call_target="tpu_custom_call" | custom-call | flops 2147483648 | bytes 18874368 | tf_op jit(solution)/shard_map/mixed_back/pallas_call | solution.py:394
  293.4 5.8 %collective-permute-done.49 = bf16[2,4,128,128]{3,2,1,0:T(8,128)(2,1)S(1)} collective-permute-done((bf16[2,4,128,128]{3,2,1,0:T(8,128)(2,1)S(1)}, bf16[2,4,128,128]{3,2,1,0:T(8,128)(2,1)S(1)}, u32[]{:S(2)}, u32[]{:S(2)}) %collective-permute-start.49) | collective-permute-done | bytes 262176 | tf_op jit(solution)/shard_map/ppermute | solution.py:50
  305.2 6.2 %query_rows.1.rows_in = bf16[2,8,64,1024]{3,2,1,0:T(8,128)(2,1)S(1)} custom-call(s32[4,16,2]{2,1,0:T(8,128)S(1)} %copy-done.42, bf16[2,8,64,512]{3,2,1,0:T(8,128)(2,1)S(1)} %get-tuple-element.192.refs_0_.query_grad, bf16[2,8,64,512]{3,2,1,0:T(8,128)(2,1)S(1)} %get-tuple-element.193.refs_1_.modulate_grad, bf16[8,2,128,256]{3,2,1,0:T(8,128)(2,1)S(1)} %copy-done.49, ...), custom_call_target="tpu_custom_call" | custom-call | flops 2147483648 | bytes 6291456 | tf_op jit(solution)/shard_map/query_rows/pallas_call | solution.py:394
  324.6 4.6 %collective-permute-done.56.g3 = bf16[2,4,128,128]{3,2,1,0:T(8,128)(2,1)S(1)} collective-permute-done((bf16[2,4,128,128]{3,2,1,0:T(8,128)(2,1)S(1)}, bf16[2,4,128,128]{3,2,1,0:T(8,128)(2,1)S(1)}, u32[]{:S(2)}, u32[]{:S(2)}) %collective-permute-start.56) | collective-permute-done | bytes 262176 | tf_op jit(solution)/shard_map/ppermute | solution.py:38
  341.9 9.5 %key_back.1 = (bf16[2,8,64,512]{3,2,1,0:T(8,128)(2,1)S(1)}, bf16[2,8,64,512]{3,2,1,0:T(8,128)(2,1)S(1)}, f32[8,64,1024]{2,1,0:T(8,128)}, bf16[8,64,1024]{2,1,0:T(8,128)(2,1)S(1)}) custom-call(s32[4,16,2]{2,1,0:T(8,128)S(1)} %copy-done.42, bf16[2,8,64,512]{3,2,1,0:T(8,128)(2,1)S(1)} %get-tuple-element.200.key_grad, ...), custom_call_target="tpu_custom_call" | custom-call | flops 2147483648 | bytes 16777216 | tf_op jit(solution)/shard_map/key_back/pallas_call | solution.py:394
  367.8 10.4 %collective-permute-done.62 = bf16[2,88,1024]{2,1,0:T(8,128)(2,1)S(1)} collective-permute-done((bf16[2,88,1024]{2,1,0:T(8,128)(2,1)S(1)}, bf16[2,88,1024]{2,1,0:T(8,128)(2,1)S(1)}, u32[]{:S(2)}, u32[]{:S(2)}) %collective-permute-start.62) | collective-permute-done | bytes 360480 | tf_op jit(solution)/shard_map/ppermute | solution.py:38
  378.1 6.9 %collective-permute-done.61 = bf16[8,1,128,256]{3,2,1,0:T(8,128)(2,1)S(1)} collective-permute-done((bf16[8,1,128,256]{3,2,1,0:T(8,128)(2,1)S(1)}, bf16[8,1,128,256]{3,2,1,0:T(8,128)(2,1)S(1)}, u32[]{:S(2)}, u32[]{:S(2)}) %collective-permute-start.61) | collective-permute-done | bytes 524320 | tf_op jit(solution)/shard_map/ppermute | solution.py:38
  (583 shorter events, 225.4 us)
Async XLA Ops:
  0.7 25.9 %collective-permute-start = (f32[2]{0:T(128)}, f32[2]{0:T(128)}, u32[]{:S(2)}, u32[]{:S(2)}) collective-permute-start(f32[2]{0:T(128)} %param.25), channel_id=1, source_target_pairs={{0,2},{1,3},{2,0},{3,1},{4,6},{5,7},{6,4},{7,5},{8,10},{9,11},{10,... | collective-permute-start | bytes 32 | tf_op jit(solution)/shard_map/ppermute | solution.py:38
  16.5 30.7 %collective-permute-start.1 = (bf16[8,64,1024]{2,1,0:T(8,128)(2,1)S(1)}, bf16[8,64,1024]{2,1,0:T(8,128)(2,1)S(1)}, u32[]{:S(2)}, u32[]{:S(2)}) collective-permute-start(bf16[8,64,1024]{2,1,0:T(8,128)(2,1)S(1)} %fusion.11.near), channel_id=1, source_target_pairs={{0,1},{1,0},{2,3},{3,2},{4,5},{5,4},{6,7},{7,6},{8,9},{9,8},{10,11... | collective-permute-start | bytes 3145736 | tf_op jit(solution)/shard_map/ppermute | solution.py:38
  79.3 22.7 %collective-permute-start.22 = (bf16[8,2,128,256]{3,2,1,0:T(8,128)(2,1)S(1)}, bf16[8,2,128,256]{3,2,1,0:T(8,128)(2,1)}, u32[]{:S(2)}, u32[]{:S(2)}) collective-permute-start(bf16[8,2,128,256]{3,2,1,0:T(8,128)(2,1)S(1)} %constant_dynamic-update-slice_fusion.3.w0), channel_id=1, source_target_pairs={{0,4},{1,5},{2,6},{3,7},{4,0},{5,1},{6,2},{7,3},{8,12},{9,13},{10,... | collective-permute-start | bytes 3145736 | tf_op jit(solution)/shard_map/ppermute | solution.py:38
  82.0 20.0 %collective-permute-start.24 = (bf16[2,2,88,1024]{3,2,1,0:T(8,128)(2,1)S(1)}, bf16[2,2,88,1024]{3,2,1,0:T(8,128)(2,1)S(1)}, u32[]{:S(2)}, u32[]{:S(2)}) collective-permute-start(bf16[2,2,88,1024]{3,2,1,0:T(8,128)(2,1)S(1)} %pad_maximum_fusion.5), channel_id=1, source_target_pairs={{0,8},{1,9},{2,10},{3,11},{4,12},{5,13},{6,14},{7,15},{8,0},{9,1},... | collective-permute-start | bytes 2162696 | tf_op jit(solution)/shard_map/ppermute | solution.py:38
  101.9 18.6 %collective-permute-start.29 = (bf16[2,88,1024]{2,1,0:T(8,128)(2,1)S(1)}, bf16[2,88,1024]{2,1,0:T(8,128)(2,1)S(1)}, u32[]{:S(2)}, u32[]{:S(2)}) collective-permute-start(bf16[2,88,1024]{2,1,0:T(8,128)(2,1)S(1)} %pad_maximum_fusion.11), channel_id=1, source_target_pairs={{0,16},{1,17},{2,18},{3,19},{4,20},{5,21},{6,22},{7,23},{8,24},{9,... | collective-permute-start | bytes 1081352 | tf_op jit(solution)/shard_map/ppermute | solution.py:38
  125.7 36.4 %collective-permute-start.31 = (bf16[8,64,1024]{2,1,0:T(8,128)(2,1)S(1)}, bf16[8,64,1024]{2,1,0:T(8,128)(2,1)S(1)}, u32[]{:S(2)}, u32[]{:S(2)}) collective-permute-start(bf16[8,64,1024]{2,1,0:T(8,128)(2,1)S(1)} %copy-done.62), channel_id=1, source_target_pairs={{0,1},{1,0},{2,3},{3,2},{4,5},{5,4},{6,7},{7,6},{8,9},{9,8},{10,11... | collective-permute-start | bytes 3145736 | tf_op jit(solution)/shard_map/ppermute | solution.py:38
  127.6 34.6 %collective-permute-start.32 = (bf16[8,64,1024]{2,1,0:T(8,128)(2,1)S(1)}, bf16[8,64,1024]{2,1,0:T(8,128)(2,1)S(1)}, u32[]{:S(2)}, u32[]{:S(2)}) collective-permute-start(bf16[8,64,1024]{2,1,0:T(8,128)(2,1)S(1)} %constant_dynamic-update-slice_fusion.7), channel_id=1, source_target_pairs={{0,1},{1,0},{2,3},{3,2},{4,5},{5,4},{6,7},{7,6},{8,9},{9,8},{10,11... | collective-permute-start | bytes 3145736 | tf_op jit(solution)/shard_map/ppermute | solution.py:38
  127.9 34.3 %collective-permute-start.35 = (bf16[4,2,88,1024]{3,2,0,1:T(8,128)(2,1)S(1)}, bf16[4,2,88,1024]{3,2,0,1:T(8,128)(2,1)S(1)}, u32[]{:S(2)}, u32[]{:S(2)}) collective-permute-start(bf16[4,2,88,1024]{3,2,0,1:T(8,128)(2,1)S(1)} %copy.72), channel_id=1, source_target_pairs={{0,4},{1,5},{2,6},{3,7},{4,0},{5,1},{6,2},{7,3},{8,12},{9,13},{10,... | collective-permute-start | bytes 4325384 | tf_op jit(solution)/shard_map/ppermute | solution.py:38
  130.6 31.6 %collective-permute-start.34 = (bf16[8,64,1024]{2,1,0:T(8,128)(2,1)S(1)}, bf16[8,64,1024]{2,1,0:T(8,128)(2,1)S(1)}, u32[]{:S(2)}, u32[]{:S(2)}) collective-permute-start(bf16[8,64,1024]{2,1,0:T(8,128)(2,1)S(1)} %multiply_convert_fusion.4), channel_id=1, source_target_pairs={{0,2},{1,3},{2,0},{3,1},{4,6},{5,7},{6,4},{7,5},{8,10},{9,11},{10,... | collective-permute-start | bytes 3145736 | tf_op jit(solution)/shard_map/ppermute | solution.py:38
  130.8 18.3 %collective-permute-start.33 = (bf16[4,88,1024]{2,1,0:T(8,128)(2,1)S(1)}, bf16[4,88,1024]{2,1,0:T(8,128)(2,1)S(1)}, u32[]{:S(2)}, u32[]{:S(2)}) collective-permute-start(bf16[4,88,1024]{2,1,0:T(8,128)(2,1)S(1)} %pad_maximum_fusion.6), channel_id=1, source_target_pairs={{0,8},{1,9},{2,10},{3,11},{4,12},{5,13},{6,14},{7,15},{8,0},{9,1},... | collective-permute-start | bytes 2162696 | tf_op jit(solution)/shard_map/ppermute | solution.py:38
  149.4 18.7 %collective-permute-start.36 = (bf16[8,64,1024]{2,1,0:T(8,128)(2,1)S(1)}, bf16[8,64,1024]{2,1,0:T(8,128)(2,1)S(1)}, u32[]{:S(2)}, u32[]{:S(2)}) collective-permute-start(bf16[8,64,1024]{2,1,0:T(8,128)(2,1)S(1)} %multiply_convert_fusion.4), channel_id=1, source_target_pairs={{0,1},{1,0},{2,3},{3,2},{4,5},{5,4},{6,7},{7,6},{8,9},{9,8},{10,11... | collective-permute-start | bytes 3145736 | tf_op jit(solution)/shard_map/ppermute | solution.py:38
  202.9 28.2 %collective-permute-start.39 = (bf16[8,64,1024]{2,1,0:T(8,128)(2,1)S(1)}, bf16[8,64,1024]{2,1,0:T(8,128)(2,1)S(1)}, u32[]{:S(2)}, u32[]{:S(2)}) collective-permute-start(bf16[8,64,1024]{2,1,0:T(8,128)(2,1)S(1)} %fusion.33), channel_id=1, source_target_pairs={{0,2},{1,3},{2,0},{3,1},{4,6},{5,7},{6,4},{7,5},{8,10},{9,11},{10,... | collective-permute-start | bytes 3145736 | tf_op jit(solution)/shard_map/ppermute | solution.py:38
  236.4 24.9 %collective-permute-start.43 = (bf16[2,2,88,1024]{3,2,0,1:T(8,128)(2,1)}, bf16[2,2,88,1024]{3,2,0,1:T(8,128)(2,1)}, u32[]{:S(2)}, u32[]{:S(2)}) collective-permute-start(bf16[2,2,88,1024]{3,2,0,1:T(8,128)(2,1)} %bitcast.202), channel_id=1, source_target_pairs={{0,8},{1,9},{2,10},{3,11},{4,12},{5,13},{6,14},{7,15},{8,0},{9,1},... | collective-permute-start | bytes 2162696 | tf_op jit(solution)/shard_map/ppermute | solution.py:38
  238.9 22.4 %collective-permute-start.42 = (bf16[4,88,1024]{2,1,0:T(8,128)(2,1)}, bf16[4,88,1024]{2,1,0:T(8,128)(2,1)}, u32[]{:S(2)}, u32[]{:S(2)}) collective-permute-start(bf16[4,88,1024]{2,1,0:T(8,128)(2,1)} %slice_bitcast_fusion.2), channel_id=1, source_target_pairs={{0,4},{1,5},{2,6},{3,7},{4,0},{5,1},{6,2},{7,3},{8,12},{9,13},{10,... | collective-permute-start | bytes 2162696 | tf_op jit(solution)/shard_map/ppermute | solution.py:38
  262.9 18.7 %collective-permute-start.47 = (bf16[2,88,1024]{2,1,0:T(8,128)(2,1)S(1)}, bf16[2,88,1024]{2,1,0:T(8,128)(2,1)S(1)}, u32[]{:S(2)}, u32[]{:S(2)}) collective-permute-start(bf16[2,88,1024]{2,1,0:T(8,128)(2,1)S(1)} %slice_bitcast_fusion.10), channel_id=1, source_target_pairs={{0,16},{1,17},{2,18},{3,19},{4,20},{5,21},{6,22},{7,23},{8,24},{9,... | collective-permute-start | bytes 1081352 | tf_op jit(solution)/shard_map/ppermute | solution.py:38
  285.5 31.5 %collective-permute-start.48 = (bf16[2,8,64,1024]{3,2,1,0:T(8,128)(2,1)S(1)}, bf16[2,8,64,1024]{3,2,1,0:T(8,128)(2,1)S(1)}, u32[]{:S(2)}, u32[]{:S(2)}) collective-permute-start(bf16[2,8,64,1024]{3,2,1,0:T(8,128)(2,1)S(1)} %slice.255), channel_id=1, source_target_pairs={{0,1},{1,0},{2,3},{3,2},{4,5},{5,4},{6,7},{7,6},{8,9},{9,8},{10,11... | collective-permute-start | bytes 6291464 | tf_op jit(solution)/shard_map/ppermute | solution.py:38
  292.0 19.5 %collective-permute-start.53 = (bf16[8,1,128,256]{3,2,1,0:T(8,128)(2,1)S(1)}, bf16[8,1,128,256]{3,2,1,0:T(8,128)(2,1)}, u32[]{:S(2)}, u32[]{:S(2)}) collective-permute-start(bf16[8,1,128,256]{3,2,1,0:T(8,128)(2,1)S(1)} %get-tuple-element.210), channel_id=1, source_target_pairs={{0,2},{1,3},{2,0},{3,1},{4,6},{5,7},{6,4},{7,5},{8,10},{9,11},{10,... | collective-permute-start | bytes 1572872 | tf_op jit(solution)/shard_map/ppermute | solution.py:38
  323.8 66.1 %collective-permute-start.65 = (bf16[88,1024]{1,0:T(8,128)(2,1)}, bf16[88,1024]{1,0:T(8,128)(2,1)}, u32[]{:S(2)}, u32[]{:S(2)}) collective-permute-start(bf16[88,1024]{1,0:T(8,128)(2,1)} %slice_bitcast_fusion.12), channel_id=1, source_target_pairs={{0,4},{1,5},{2,6},{3,7},{4,0},{5,1},{6,2},{7,3},{8,12},{9,13},{10,... | collective-permute-start | bytes 540680 | tf_op jit(solution)/shard_map/ppermute | solution.py:38
  334.8 22.4 %collective-permute-start.57 = (bf16[2,2,88,1024]{3,2,1,0:T(8,128)(2,1)}, bf16[2,2,88,1024]{3,2,1,0:T(8,128)(2,1)}, u32[]{:S(2)}, u32[]{:S(2)}) collective-permute-start(bf16[2,2,88,1024]{3,2,1,0:T(8,128)(2,1)} %slice.210), channel_id=1, source_target_pairs={{0,8},{1,9},{2,10},{3,11},{4,12},{5,13},{6,14},{7,15},{8,0},{9,1},... | collective-permute-start | bytes 2162696 | tf_op jit(solution)/shard_map/ppermute | solution.py:38
  337.3 19.9 %collective-permute-start.58 = (bf16[4,2,128,256]{3,2,1,0:T(8,128)(2,1)}, bf16[4,2,128,256]{3,2,1,0:T(8,128)(2,1)}, u32[]{:S(2)}, u32[]{:S(2)}) collective-permute-start(bf16[4,2,128,256]{3,2,1,0:T(8,128)(2,1)} %slice.260), channel_id=1, source_target_pairs={{0,2},{1,3},{2,0},{3,1},{4,6},{5,7},{6,4},{7,5},{8,10},{9,11},{10,... | collective-permute-start | bytes 1572872 | tf_op jit(solution)/shard_map/ppermute | solution.py:38
  341.5 48.4 %collective-permute-start.67 = (bf16[8,64,1024]{2,1,0:T(8,128)(2,1)}, bf16[8,64,1024]{2,1,0:T(8,128)(2,1)}, u32[]{:S(2)}, u32[]{:S(2)}) collective-permute-start(bf16[8,64,1024]{2,1,0:T(8,128)(2,1)} %fusion.34), channel_id=1, source_target_pairs={{0,2},{1,3},{2,0},{3,1},{4,6},{5,7},{6,4},{7,5},{8,10},{9,11},{10,... | collective-permute-start | bytes 3145736 | tf_op jit(solution)/shard_map/ppermute | solution.py:38
  358.6 19.5 %collective-permute-start.62 = (bf16[2,88,1024]{2,1,0:T(8,128)(2,1)S(1)}, bf16[2,88,1024]{2,1,0:T(8,128)(2,1)S(1)}, u32[]{:S(2)}, u32[]{:S(2)}) collective-permute-start(bf16[2,88,1024]{2,1,0:T(8,128)(2,1)S(1)} %slice_bitcast_fusion.9), channel_id=1, source_target_pairs={{0,16},{1,17},{2,18},{3,19},{4,20},{5,21},{6,22},{7,23},{8,24},{9,... | collective-permute-start | bytes 1081352 | tf_op jit(solution)/shard_map/ppermute | solution.py:38
  358.7 19.4 %collective-permute-start.60 = (bf16[8,1,128,256]{3,2,1,0:T(8,128)(2,1)S(1)}, bf16[8,1,128,256]{3,2,1,0:T(8,128)(2,1)S(1)}, u32[]{:S(2)}, u32[]{:S(2)}) collective-permute-start(bf16[8,1,128,256]{3,2,1,0:T(8,128)(2,1)S(1)} %get-tuple-element.234), channel_id=1, source_target_pairs={{0,4},{1,5},{2,6},{3,7},{4,0},{5,1},{6,2},{7,3},{8,12},{9,13},{10,... | collective-permute-start | bytes 1572872 | tf_op jit(solution)/shard_map/ppermute | solution.py:38
  362.4 22.6 %collective-permute-start.61 = (bf16[8,1,128,256]{3,2,1,0:T(8,128)(2,1)S(1)}, bf16[8,1,128,256]{3,2,1,0:T(8,128)(2,1)S(1)}, u32[]{:S(2)}, u32[]{:S(2)}) collective-permute-start(bf16[8,1,128,256]{3,2,1,0:T(8,128)(2,1)S(1)} %get-tuple-element.235), channel_id=1, source_target_pairs={{0,2},{1,3},{2,0},{3,1},{4,6},{5,7},{6,4},{7,5},{8,10},{9,11},{10,... | collective-permute-start | bytes 1572872 | tf_op jit(solution)/shard_map/ppermute | solution.py:38
  (194 other events, 1970.5 us)

commit v5 on v4

--- a/solution.py
+++ b/solution.py
@@ -353,6 +353,38 @@
     far_out[...] = out[count * size :].astype(BF16).reshape(far_out.shape)
 
 
+def hidden_kernel(
+    spots, n0, n1, n2, n3, branch_rows, gate_w, lift_w, down_w,
+    inner_out, gate_out, lift_out, keep, send, branch_keep, branch_send
+):
+    x, b = [], get(branch_rows)
+    for n in (n0, n1, n2, n3):
+        x.append(n[...].reshape(-1, n.shape[-1]))
+    x = jnp.concatenate(x, axis=0)
+    gate, lift, down = gate_w[...], lift_w[...], down_w[...]
+    parts = []
+    for r in range(0, x.shape[0], 256):
+        rows = slice(r, r + 256)
+        gate_pre = mm(x[rows], gate, NT)
+        lift_pre = mm(x[rows], lift, NT)
+        inner_grad = mm(b[rows], down, NT)
+        q = jax.nn.sigmoid(gate_pre)
+        act = gate_pre * q
+        gate_grad = (inner_grad * lift_pre * (q + act * (1.0 - q))).astype(BF16)
+        lift_grad = (inner_grad * act).astype(BF16)
+        inner = (act * lift_pre).astype(BF16)
+        total = (mm(gate_grad, gate) + mm(lift_grad, lift)).astype(BF16)
+        parts.append((inner, gate_grad, lift_grad, total, mm(inner, down).astype(BF16)))
+    inner, gate_grad, lift_grad, total, branch = (jnp.concatenate(p, axis=0) for p in zip(*parts))
+    put(inner_out, slice(None), inner)
+    put(gate_out, slice(None), gate_grad)
+    put(lift_out, slice(None), lift_grad)
+    half = total.shape[0] // 2
+    for near, far, value in ((keep, send, total), (branch_keep, branch_send, branch)):
+        near[...] = value[:half].reshape(near.shape)
+        far[...] = value[half:].reshape(far.shape)
+
+
 def outer_kernel(order, spots, near, far, *refs):
     count = (len(refs) - 4) // 1
     grads, (keep, send, whole, sems) = refs[:count], refs[count:]
@@ -385,7 +417,7 @@
         if kind == "pair":
             size = shape[1] // steps
             return pl.BlockSpec(
-                (2, size, *shape[2:]), lambda i, _: (0, i) + (0,) * (len(shape) - 2)
+                (shape[0], size, *shape[2:]), lambda i, _: (0, i) + (0,) * (len(shape) - 2)
             )
         return pl.BlockSpec(shape, lambda i, _: (0,) * len(shape))
 
@@ -401,7 +433,7 @@
             out_specs=[spec(s, kind) for s, _, kind in outputs],
             scratch_shapes=scratch,
         ),
-        compiler_params=pltpu.CompilerParams(vmem_limit_bytes=40 * 2**20),
+        compiler_params=pltpu.CompilerParams(vmem_limit_bytes=44 * 2**20),
         cost_estimate=pl.CostEstimate(flops=flops, bytes_accessed=moved, transcendentals=0),
         name=name,
     )(spots, *[a for a, _ in inputs])
@@ -667,42 +699,40 @@
     dn_z = swap(dn, z_near)
 
     def quarters(mine, got_x):
-        return jnp.stack([mine, got_x, swap(mine, 1), swap(got_x, 1)])
-
-    def core_part(parts):
-        parts = parts.astype(BF16)
-        got = swap(parts[2:], 1)
-        return fold(parts[0], got[0], F32), fold(parts[1], got[1])
-
-    normed_two = quarters(two, two_x)
+        return [mine, got_x, swap(mine, 1), swap(got_x, 1)]
+
+    def core_part(keep, send):
+        got = swap(send, 1)
+        return fold(keep[0], got[0], F32), fold(keep[1], got[1])
+
+    two_pieces = quarters(two, two_x)
+    normed_two = jnp.stack(two_pieces)
     row_starts = (narrow_index ^ jnp.array([0, x_mask, 1, 1 + x_mask], jnp.int32)) * quarter
     row_spots = wide_index * (quarter * narrow_count) + row_starts[:, None] + jnp.arange(quarter)
     row_mask = (row_spots[:, None, :] < valid_lengths[None, :, None]).astype(F32)[..., None]
-    branch_rows = quarters(output_cotangent, jnp.concatenate(cotangent_x))
+    branch_rows = jnp.stack(quarters(output_cotangent, jnp.concatenate(cotangent_x)))
     branch_rows = (row_mask * branch_rows.astype(F32)).astype(BF16)
     gate_t = join(gl[:, 0], gl_y[:, 0]).reshape(-1, width)
     lift_t = join(gl[:, 1], gl_y[:, 1]).reshape(-1, width)
     bulk = half // 2
     down_t = jnp.swapaxes(join(dn, dn_z).reshape(bulk, 2, -1, width), 0, 1).reshape(-1, width)
 
-    def hidden(rows_in, matrix):
-        return jnp.einsum("pbld,fd->pblf", rows_in, matrix, preferred_element_type=F32)
-
     def outer(a, b):
         return jnp.einsum("pblf,pbld->fd", a, b, preferred_element_type=F32).astype(BF16)
 
-    gate_pre = hidden(normed_two, gate_t)
-    lift_pre = hidden(normed_two, lift_t)
-    inner_grad = hidden(branch_rows, down_t)
-    gate_act = apply_swish(gate_pre)
-    inner = (gate_act * lift_pre).astype(BF16)
-    gate_grad = (inner_grad * lift_pre * swish_slope(gate_pre)).astype(BF16)
-    lift_grad = (inner_grad * gate_act).astype(BF16)
-    normed_grad = jnp.einsum("pblf,fd->pbld", gate_grad, gate_t, preferred_element_type=F32)
-    normed_grad = normed_grad + jnp.einsum(
-        "pblf,fd->pbld", lift_grad, lift_t, preferred_element_type=F32
-    )
-    row_mine, row_send = core_part(normed_grad)
+    hidden_shape = (4, slots, quarter, gate_t.shape[0])
+    sum_shape = (2, slots, quarter, width)
+    hidden_flops = 2 * 4 * slots * quarter * width * gate_t.shape[0]
+    inner, gate_grad, lift_grad, row_keep, row_send, branch_keep, branch_send = run(
+        hidden_kernel, "hidden", spots,
+        [
+            *[(p, "rows") for p in two_pieces], (branch_rows, "pair"), (gate_t, "whole"),
+            (lift_t, "whole"), (down_t, "whole"),
+        ],
+        [(hidden_shape, BF16, "pair")] * 3 + [(sum_shape, BF16, "pair")] * 4,
+        [], steps, 6 * hidden_flops,
+    )
+    row_mine, row_send = core_part(row_keep, row_send)
     row_got = swap(row_send, x_mask)
     gate_grad, lift_grad, inner, row_send = tie(gate_grad, lift_grad, inner, row_send)
     gate_g = outer(gate_grad, normed_two).reshape(2, bulk, -1, width)
@@ -710,9 +740,13 @@
     lift_grad, inner, gate_g = tie(lift_grad, inner, gate_g)
     lift_g = outer(lift_grad, normed_two).reshape(2, bulk, -1, width)
     down_g = outer(inner, branch_rows).reshape(2, 2, bulk // 2, -1, width)
-    down_z = swap(down_g[:, 1], z_near)
-    row_got, gate_y = tie(row_got, gate_y)
-    lift_y = swap(tie(lift_g, gate_y)[0][1], y_mask)
+    branch_mine, branch_send = core_part(branch_keep, branch_send)
+    row_got, gate_y, lift_g, down_z_send, branch_send = tie(
+        row_got, gate_y, lift_g, down_g[:, 1], branch_send
+    )
+    lift_y = swap(lift_g[1], y_mask)
+    branch_got = swap(branch_send, x_mask)
+    down_z = swap(down_z_send, z_near)
     middle_grad = cotangent + norm_backward(middle, row_mine + row_got.astype(F32))
 
     attended_grad = middle_grad.astype(BF16)
@@ -733,13 +767,8 @@
         [wide_scratch, held_scratch, dma((members,)), dma((4,))],
         steps, 2 * square_flops,
     )
-    state_grad, lift_y, down_z, gated = tie(state_grad, lift_y, down_z, gated)
+    state_grad, lift_y, branch_got, gated = tie(state_grad, lift_y, branch_got, gated)
     near = bulk // 2
-    down_g = jnp.moveaxis(fold(down_g[:, 0], down_z), 1, 0)
-    for m in z_far[:0:-1]:
-        size = down_g.shape[0] // 2
-        down_g = fold(down_g[:size], swap(down_g[size:], m))
-    down_far = swap(down_g[1], z_far[0])
     scan = Carry(state_grad, block_decay, True)
     scan.spread()
 
@@ -762,12 +791,14 @@
         [wide_scratch, wide_scratch, dma((2, members))],
         steps, 2 * square_flops,
     )
-    *scan.got, down_far, query_keep, query_send, output_keep, output_send, inner = tie(
-        *scan.got, down_far, query_keep, query_send, output_keep, output_send, inner
-    )
-    branch = jnp.einsum("pblf,fd->pbld", inner, down_t, preferred_element_type=F32)
-    branch_mine, branch_send = core_part(branch)
-    down_g = fold(down_g[0], down_far)
+    *scan.got, down_z, query_keep, query_send, output_keep, output_send = tie(
+        *scan.got, down_z, query_keep, query_send, output_keep, output_send
+    )
+    layer_output = (middle + mask_rows * (branch_mine + branch_got.astype(F32))).astype(BF16)
+    down_g = jnp.moveaxis(fold(down_g[:, 0], down_z), 1, 0)
+    for m in z_far[:0:-1]:
+        size = down_g.shape[0] // 2
+        down_g = fold(down_g[:size], swap(down_g[size:], m))
     gl_g = jnp.stack([fold(gate_g[0], gate_y), fold(lift_g[0], lift_y)], axis=1)
 
     query_y, output_x = swap(query_send[:, :1], y_mask), swap(output_send, x_mask)
@@ -782,16 +813,14 @@
 
     scan.along(backward_step)
     query_y = jnp.concatenate([held["y"], held["more"]], axis=1)
-    scan.before, query_rows, branch_send = tie(scan.before, query_rows, branch_send)
+    scan.before, query_rows, down_g, gl_g = tie(scan.before, query_rows, down_g, gl_g)
+    down_far = swap(down_g[1], z_far[0])
+    gl_z = swap(gl_g[near:], z_near)
     later_parts = list(tie(*scan.back()))
-    gl_g, query_keep, output_keep, branch_send = tie(
-        gl_g, query_keep, output_keep, branch_send, *later_parts
-    )[:4]
+    query_keep, output_keep = tie(query_keep, output_keep, *later_parts)[:2]
     query_g, output_g = fold(query_keep, query_y), fold(output_keep, held["x"])
     quad = half // 2
-    gl_z = swap(gl_g[near:], z_near)
     query_x, output_y = swap(query_g[quad:], x_mask), swap(output_g[quad:], y_mask)
-    branch_got = swap(branch_send, x_mask)
     later_inputs = [(p, "any") for p in later_parts]
     quad = half // 2
     def far_pairs(x):
@@ -825,9 +854,10 @@
     )
     key_keep, key_send = square("key_outer", 0, normed_pair, key_out)
     value_keep, value_send = square("value_outer", 2, normed_pair, value_out)
-    key_send, value_send, gl_z, query_x, output_y = tie(
-        key_send, value_send, gl_z, query_x, output_y
-    )
+    key_send, value_send, gl_z, down_far, query_x, output_y = tie(
+        key_send, value_send, gl_z, down_far, query_x, output_y
+    )
+    down_g = fold(down_g[0], down_far)
     gl_g = fold(gl_g[:near], gl_z)
     for m in z_far[:0:-1]:
         size = gl_g.shape[0] // 2
@@ -843,8 +873,7 @@
         [fold(query_g[:quad], query_x), fold(output_g[:quad], output_y)], axis=1
     )
     qmo_z = swap(qmo_g[near:], z_near)
-    key_x, value_z, down_y, qmo_z, branch_got = tie(key_x, value_z, down_y, qmo_z, branch_got)
-    layer_output = (middle + mask_rows * (branch_mine + branch_got.astype(F32))).astype(BF16)
+    key_x, value_z, down_y, qmo_z = tie(key_x, value_z, down_y, qmo_z)
     key_g, value_g = fold(key_g[:quad], key_x), fold(value_g[:quad], value_z)
     key_z, value_far = swap(key_g[near:], z_near), far_pairs(value_g)
     qmo_g = far_folds(fold(qmo_g[:near], qmo_z))[0]

time: 424 us -> 389 us (0.917)
  matrix products: 51.2 us -> 9.54 us
  Pallas kernels: 61.9 us -> 88.9 us
  local copies, waits for them, and re-layouts: 28 us -> 16.3 us
  other arithmetic: 44.8 us -> 38.6 us
    dot_general x6 -> x0, matrix products: 38.8 us -> none  [the longest x3 21.5 us: hidden(): jnp.einsum('pbld,fd->pblf', rows_in, matrix, preferred_element_type=F32)]
    pallas_call x10 -> x11, Pallas kernels: 61.9 us -> 88.9 us  [run(): pl.pallas_call(kernel, out_shape=[jax.ShapeDtypeStruct(s, d) for s, d, _...]
    unnamed x296 -> x258, local copies, waits for them, and re-layouts: 15.1 us -> 7.6 us
    convert_element_type x15, other arithmetic: 8.72 us -> 3.44 us  [fold(): return (mine.astype(F32) + got.astype(F32)).astype(dtype)]
    ppermute x4, waiting for transfers between devices: 22.3 us -> 17.1 us  [shift_z(): return lax.ppermute(x, AXES, pairs)]
  transfers between devices with their start and end apart: 74 -> 74, of which waited for: 31 -> 34; matrix products, arithmetic and copies ran while one was open for 17% -> 14% of each run, Pallas kernels for 14% -> 15%
where the time goes in v5:
time: 389 us; the launch traced here: 382 us
  waiting for transfers between devices  146 us (38%)
  Pallas kernels  88.9 us (23%)
  starting transfers between devices  79.3 us (20%)
  other arithmetic  38.6 us (10%)
  local copies, waits for them, and re-layouts  16.3 us (4%)
  matrix products  9.54 us (2%)
    ppermute x70, waiting for transfers between devices, exchange(): return lax.ppermute(x, AXES, [(i, i ^ mask) for i in range(count)])  129 us
    pallas_call x11, Pallas kernels, run(): pl.pallas_call(kernel, out_shape=[jax.ShapeDtypeStruct(s, d) for s, d, _...  88.9 us
    ppermute x70, starting transfers between devices, exchange(): return lax.ppermute(x, AXES, [(i, i ^ mask) for i in range(count)])  73.1 us
    ppermute x4, waiting for transfers between devices, shift_z(): return lax.ppermute(x, AXES, pairs)  17.1 us
    dot_general x3, matrix products, outer(): jnp.einsum('pblf,pbld->fd', a, b, preferred_element_type=F32).astype(BF16)  9.54 us
  transfers between devices with their start and end apart: 74, of which 34 were waited for; matrix products, arithmetic and copies ran while one was open for 14% of the time, Pallas kernels for 15%

profile of v5, /device:TPU:0, one launch (start us, length us, event | category | flops | bytes accessed | tf_op | source)
XLA Modules:
  0.0 382.0 jit_solution(17902699055801200172)
XLA Ops:
  26.5 3.4 collective-permute-done.8
  37.3 7.4 %collective-permute-done.12 = bf16[1,3,128,256]{3,2,1,0:T(8,128)(2,1)S(1)} collective-permute-done((bf16[1,3,128,256]{3,2,1,0:T(8,128)(2,1)S(1)}, bf16[1,3,128,256]{3,2,1,0:T(8,128)(2,1)S(1)}, u32[]{:S(2)}, u32[]{:S(2)}) %collective-permute-start.12) | collective-permute-done | bytes 196640 | tf_op jit(solution)/shard_map/ppermute | solution.py:38
  47.2 6.0 %key_value.1 = (bf16[2,8,64,512]{3,2,1,0:T(8,128)(2,1)S(1)}, bf16[2,8,64,512]{3,2,1,0:T(8,128)(2,1)S(1)}, bf16[2,8,64,512]{3,2,1,0:T(8,128)(2,1)S(1)}, bf16[8,4,128,128]{3,2,1,0:T(8,128)(2,1)S(1)}) custom-call(s32[4,16,2]{2,1,0:T(8,128)S(1)} %add_add_fusion.spots, bf16[8,64,1024]{2,1,0:T(8,128)(2,1)S(1)} %fusion.10.near, ...), custom_call_target="tpu_custom_call" | custom-call | flops 2147483648 | bytes 9437184 | tf_op jit(solution)/shard_map/key_value/pallas_call | solution.py:426
  75.1 5.5 %collective-permute-done.19 = bf16[4,1,128,256]{3,2,1,0:T(8,128)(2,1)S(1)} collective-permute-done((bf16[4,1,128,256]{3,2,1,0:T(8,128)(2,1)S(1)}, bf16[4,1,128,256]{3,2,1,0:T(8,128)(2,1)S(1)}, u32[]{:S(2)}, u32[]{:S(2)}) %collective-permute-start.19) | collective-permute-done | bytes 262176 | tf_op jit(solution)/shard_map/ppermute | solution.py:38
  89.9 7.3 %collective-permute-done.21 = bf16[2,4,128,128]{3,2,1,0:T(8,128)(2,1)S(1)} collective-permute-done((bf16[2,4,128,128]{3,2,1,0:T(8,128)(2,1)S(1)}, bf16[2,4,128,128]{3,2,1,0:T(8,128)(2,1)S(1)}, u32[]{:S(2)}, u32[]{:S(2)}) %collective-permute-start.21) | collective-permute-done | bytes 262176 | tf_op jit(solution)/shard_map/ppermute | solution.py:50
  97.2 4.7 %collective-permute-done.25 = bf16[4,64,1024]{2,1,0:T(8,128)(2,1)S(1)} collective-permute-done((bf16[4,64,1024]{2,1,0:T(8,128)(2,1)S(1)}, bf16[4,64,1024]{2,1,0:T(8,128)(2,1)S(1)}, u32[]{:S(2)}, u32[]{:S(2)}) %collective-permute-start.25) | collective-permute-done | bytes 524320 | tf_op jit(solution)/shard_map/ppermute | solution.py:38
  101.9 4.0 %collective-permute-start.29 = (bf16[2,88,1024]{2,1,0:T(8,128)(2,1)S(1)}, bf16[2,88,1024]{2,1,0:T(8,128)(2,1)S(1)}, u32[]{:S(2)}, u32[]{:S(2)}) collective-permute-start(bf16[2,88,1024]{2,1,0:T(8,128)(2,1)S(1)} %pad_maximum_fusion.11), channel_id=1, source_target_pairs={{0,16},{1,17},{2,18},{3,19},{4,20},{5,21},{6,22},{7,23},{8,24},{9,... | collective-permute-start | bytes 1081352 | tf_op jit(solution)/shard_map/ppermute | solution.py:38
  113.4 8.5 %query.1 = (bf16[2,8,64,512]{3,2,1,0:T(8,128)(2,1)S(1)}, bf16[2,8,64,512]{3,2,1,0:T(8,128)(2,1)S(1)}, bf16[2,8,64,512]{3,2,1,0:T(8,128)(2,1)S(1)}, bf16[2,8,64,512]{3,2,1,0:T(8,128)(2,1)S(1)}) custom-call(s32[4,16,2]{2,1,0:T(8,128)S(1)} %copy-done.35, bf16[8,64,1024]{2,1,0:T(8,128)(2,1)S(1)} %copy-done.23, bf16[8,64,1024]{2,1,0:T(8,128)(2,1)S(1)} %copy-done.44, ...), custom_call_target="tpu_custom_call" | custom-call | flops 2147483648 | bytes 12058624 | tf_op jit(solution)/shard_map/query/pallas_call | solution.py:426
  123.1 5.7 %mixed.1 = (bf16[2,8,64,512]{3,2,1,0:T(8,128)(2,1)S(1)}, bf16[2,8,64,512]{3,2,1,0:T(8,128)(2,1)S(1)}, f32[8,64,1024]{2,1,0:T(8,128)}, bf16[8,64,1024]{2,1,0:T(8,128)(2,1)S(1)}) custom-call(s32[4,16,2]{2,1,0:T(8,128)S(1)} %copy-done.35, bf16[2,8,64,512]{3,2,1,0:T(8,128)(2,1)S(1)} %get-tuple-element.170.queries, ...), custom_call_target="tpu_custom_call" | custom-call | flops 1073741824 | bytes 11010048 | tf_op jit(solution)/shard_map/mixed/pallas_call | solution.py:426
  138.0 26.5 %collective-permute-done.32 = bf16[4,2,88,1024]{3,2,0,1:T(8,128)(2,1)S(1)} collective-permute-done((bf16[4,2,88,1024]{3,2,0,1:T(8,128)(2,1)S(1)}, bf16[4,2,88,1024]{3,2,0,1:T(8,128)(2,1)S(1)}, u32[]{:S(2)}, u32[]{:S(2)}) %collective-permute-start.32) | collective-permute-done | bytes 1441824 | tf_op jit(solution)/shard_map/ppermute | solution.py:38
  168.6 26.1 %hidden.1 = (bf16[4,8,64,704]{3,2,1,0:T(8,128)(2,1)}, bf16[4,8,64,704]{3,2,1,0:T(8,128)(2,1)}, bf16[4,8,64,704]{3,2,1,0:T(8,128)(2,1)}, bf16[2,8,64,1024]{3,2,1,...) custom-call(s32[4,16,2]{2,1,0:T(8,128)S(1)} %copy-done.35, ...), custom_call_target="tpu_custom_call" | custom-call | flops 17716740096 | bytes 29753344 | tf_op jit(solution)/shard_map/hidden/pallas_call | solution.py:426
  195.6 3.6 collective-permute-done.39
  200.7 3.2 bitcast_convert_fusion.2
  215.9 9.3 %collective-permute-done.41 = bf16[4,88,1024]{2,1,0:T(8,128)(2,1)S(1)} collective-permute-done((bf16[4,88,1024]{2,1,0:T(8,128)(2,1)S(1)}, bf16[4,88,1024]{2,1,0:T(8,128)(2,1)S(1)}, u32[]{:S(2)}, u32[]{:S(2)}) %collective-permute-start.41) | collective-permute-done | bytes 720928 | tf_op jit(solution)/shard_map/ppermute | solution.py:38
  235.8 12.7 %mixed_back.1 = (bf16[2,8,64,512]{3,2,1,0:T(8,128)(2,1)S(1)}, bf16[2,8,64,512]{3,2,1,0:T(8,128)(2,1)S(1)}, bf16[2,8,64,512]{3,2,1,0:T(8,128)(2,1)S(1)}, bf16[2,8...) custom-call(s32[4,16,2]{2,1,0:T(8,128)S(1)} %copy-done.36, bf16[8,64,1024]{2,1,0:T(8,128)(2,1)S(1)} %get-tuple-element.270.near, ...), custom_call_target="tpu_custom_call" | custom-call | flops 2147483648 | bytes 18874368 | tf_op jit(solution)/shard_map/mixed_back/pallas_call | solution.py:426
  248.7 5.3 %collective-permute-done.44 = bf16[8,64,1024]{2,1,0:T(8,128)(2,1)} collective-permute-done((bf16[8,64,1024]{2,1,0:T(8,128)(2,1)}, bf16[8,64,1024]{2,1,0:T(8,128)(2,1)}, u32[]{:S(2)}, u32[]{:S(2)}) %collective-permute-start.44) | collective-permute-done | bytes 1048608 | tf_op jit(solution)/shard_map/ppermute | solution.py:38
  257.8 4.0 %output_outer.1 = (bf16[8,1,128,256]{3,2,1,0:T(8,128)(2,1)S(1)}, bf16[8,1,128,256]{3,2,1,0:T(8,128)(2,1)S(1)}) custom-call(s32[4,16,2]{2,1,0:T(8,128)S(1)} %copy-done.36, bf16[8,64,1024]{2,1,0:T(8,128)(2,1)S(1)} %get-tuple-element.270.near, bf16[8,64,1024]{2,1,0:T(8,128)(2,1)} %collective-permute-done.42.far, bf16[2,8,64,512]{3,2,1,0:T(8,128)(2,1)S(1)} %copy-done.47), custom_call_target="tpu_custom_call" | custom-call | flops 1073741824 | bytes 4194304 | tf_op jit(solution)/shard_map/output_outer/pallas_call | solution.py:426
  261.8 4.3 %query_outer.1 = (bf16[8,2,128,256]{3,2,1,0:T(8,128)(2,1)S(1)}, bf16[8,2,128,256]{3,2,1,0:T(8,128)(2,1)S(1)}) custom-call(s32[4,16,2]{2,1,0:T(8,128)S(1)} %copy-done.36, bf16[8,64,1024]{2,1,0:T(8,128)(2,1)S(1)} %copy-done.24, bf16[8,64,1024]{2,1,0:T(8,128)(2,1)S(1)} %copy-done.45, bf16[2,8,64,512]{3,2,1,0:T(8,128)(2,1)S(1)} %get-tuple-element.210.refs_0_.query_grad, ...), custom_call_target="tpu_custom_call" | custom-call | flops 2147483648 | bytes 6291456 | tf_op jit(solution)/shard_map/query_outer/pallas_call | solution.py:426
  272.6 6.0 %query_rows.1.rows_in = bf16[2,8,64,1024]{3,2,1,0:T(8,128)(2,1)S(1)} custom-call(s32[4,16,2]{2,1,0:T(8,128)S(1)} %copy-done.36, bf16[2,8,64,512]{3,2,1,0:T(8,128)(2,1)S(1)} %get-tuple-element.210.refs_0_.query_grad, bf16[2,8,64,512]{3,2,1,0:T(8,128)(2,1)S(1)} %get-tuple-element.211.refs_1_.modulate_grad, bf16[8,2,128,256]{3,2,1,0:T(8,128)(2,1)S(1)} %copy-done.42, ...), custom_call_target="tpu_custom_call" | custom-call | flops 2147483648 | bytes 6291456 | tf_op jit(solution)/shard_map/query_rows/pallas_call | solution.py:426
  284.6 5.7 %collective-permute-done.53 = bf16[8,1,128,256]{3,2,1,0:T(8,128)(2,1)S(1)} collective-permute-done((bf16[8,1,128,256]{3,2,1,0:T(8,128)(2,1)S(1)}, bf16[8,1,128,256]{3,2,1,0:T(8,128)(2,1)S(1)}, u32[]{:S(2)}, u32[]{:S(2)}) %collective-permute-start.53) | collective-permute-done | bytes 524320 | tf_op jit(solution)/shard_map/ppermute | solution.py:38
  290.3 6.4 %collective-permute-done.51 = bf16[2,4,128,128]{3,2,1,0:T(8,128)(2,1)S(1)} collective-permute-done((bf16[2,4,128,128]{3,2,1,0:T(8,128)(2,1)S(1)}, bf16[2,4,128,128]{3,2,1,0:T(8,128)(2,1)S(1)}, u32[]{:S(2)}, u32[]{:S(2)}) %collective-permute-start.51) | collective-permute-done | bytes 262176 | tf_op jit(solution)/shard_map/ppermute | solution.py:50
  315.1 10.0 %key_back.1 = (bf16[2,8,64,512]{3,2,1,0:T(8,128)(2,1)S(1)}, bf16[2,8,64,512]{3,2,1,0:T(8,128)(2,1)S(1)}, f32[8,64,1024]{2,1,0:T(8,128)}, bf16[8,64,1024]{2,1,0:T(8,128)(2,1)S(1)}) custom-call(s32[4,16,2]{2,1,0:T(8,128)S(1)} %copy-done.36, bf16[2,8,64,512]{3,2,1,0:T(8,128)(2,1)S(1)} %get-tuple-element.205.key_grad, ...), custom_call_target="tpu_custom_call" | custom-call | flops 2147483648 | bytes 16777216 | tf_op jit(solution)/shard_map/key_back/pallas_call | solution.py:426
  333.4 18.5 %collective-permute-done.64 = bf16[2,88,1024]{2,1,0:T(8,128)(2,1)S(1)} collective-permute-done((bf16[2,88,1024]{2,1,0:T(8,128)(2,1)S(1)}, bf16[2,88,1024]{2,1,0:T(8,128)(2,1)S(1)}, u32[]{:S(2)}, u32[]{:S(2)}) %collective-permute-start.64) | collective-permute-done | bytes 360480 | tf_op jit(solution)/shard_map/ppermute | solution.py:38
  366.3 7.9 %collective-permute-done.72 = bf16[1,2,1,128,256]{4,3,1,2,0:T(8,128)(2,1)S(1)} collective-permute-done((bf16[1,2,1,128,256]{4,3,1,2,0:T(8,128)(2,1)S(1)}, bf16[1,2,1,128,256]{4,3,1,2,0:T(8,128)(2,1)S(1)}, u32[]{:S(2)}, u32[]{:S(2)}) %collective-permute-start.72) | collective-permute-done | bytes 131104 | tf_op jit(solution)/shard_map/ppermute | solution.py:38
  (538 shorter events, 176.6 us)
Async XLA Ops:
  0.7 25.8 %collective-permute-start = (f32[2]{0:T(128)}, f32[2]{0:T(128)S(1)}, u32[]{:S(2)}, u32[]{:S(2)}) collective-permute-start(f32[2]{0:T(128)} %param.25), channel_id=1, source_target_pairs={{0,2},{1,3},{2,0},{3,1},{4,6},{5,7},{6,4},{7,5},{8,10},{9,11},{10,... | collective-permute-start | bytes 32 | tf_op jit(solution)/shard_map/ppermute | solution.py:38
  16.3 30.5 %collective-permute-start.1 = (bf16[8,64,1024]{2,1,0:T(8,128)(2,1)S(1)}, bf16[8,64,1024]{2,1,0:T(8,128)(2,1)S(1)}, u32[]{:S(2)}, u32[]{:S(2)}) collective-permute-start(bf16[8,64,1024]{2,1,0:T(8,128)(2,1)S(1)} %fusion.10.near), channel_id=1, source_target_pairs={{0,1},{1,0},{2,3},{3,2},{4,5},{5,4},{6,7},{7,6},{8,9},{9,8},{10,11... | collective-permute-start | bytes 3145736 | tf_op jit(solution)/shard_map/ppermute | solution.py:38
  80.7 21.2 %collective-permute-start.22 = (bf16[8,2,128,256]{3,2,1,0:T(8,128)(2,1)S(1)}, bf16[8,2,128,256]{3,2,1,0:T(8,128)(2,1)}, u32[]{:S(2)}, u32[]{:S(2)}) collective-permute-start(bf16[8,2,128,256]{3,2,1,0:T(8,128)(2,1)S(1)} %constant_dynamic-update-slice_fusion.3.w0), channel_id=1, source_target_pairs={{0,4},{1,5},{2,6},{3,7},{4,0},{5,1},{6,2},{7,3},{8,12},{9,13},{10,... | collective-permute-start | bytes 3145736 | tf_op jit(solution)/shard_map/ppermute | solution.py:38
  83.3 18.6 %collective-permute-start.24 = (bf16[2,2,88,1024]{3,2,1,0:T(8,128)(2,1)S(1)}, bf16[2,2,88,1024]{3,2,1,0:T(8,128)(2,1)S(1)}, u32[]{:S(2)}, u32[]{:S(2)}) collective-permute-start(bf16[2,2,88,1024]{3,2,1,0:T(8,128)(2,1)S(1)} %pad_maximum_fusion.5), channel_id=1, source_target_pairs={{0,8},{1,9},{2,10},{3,11},{4,12},{5,13},{6,14},{7,15},{8,0},{9,1},... | collective-permute-start | bytes 2162696 | tf_op jit(solution)/shard_map/ppermute | solution.py:38
  101.9 21.1 %collective-permute-start.29 = (bf16[2,88,1024]{2,1,0:T(8,128)(2,1)S(1)}, bf16[2,88,1024]{2,1,0:T(8,128)(2,1)S(1)}, u32[]{:S(2)}, u32[]{:S(2)}) collective-permute-start(bf16[2,88,1024]{2,1,0:T(8,128)(2,1)S(1)} %pad_maximum_fusion.11), channel_id=1, source_target_pairs={{0,16},{1,17},{2,18},{3,19},{4,20},{5,21},{6,22},{7,23},{8,24},{9,... | collective-permute-start | bytes 1081352 | tf_op jit(solution)/shard_map/ppermute | solution.py:38
  128.9 36.1 %collective-permute-start.35 = (bf16[8,64,1024]{2,1,0:T(8,128)(2,1)S(1)}, bf16[8,64,1024]{2,1,0:T(8,128)(2,1)S(1)}, u32[]{:S(2)}, u32[]{:S(2)}) collective-permute-start(bf16[8,64,1024]{2,1,0:T(8,128)(2,1)S(1)} %copy-done.53), channel_id=1, source_target_pairs={{0,1},{1,0},{2,3},{3,2},{4,5},{5,4},{6,7},{7,6},{8,9},{9,8},{10,11... | collective-permute-start | bytes 3145736 | tf_op jit(solution)/shard_map/ppermute | solution.py:38
  131.0 33.5 %collective-permute-start.32 = (bf16[4,2,88,1024]{3,2,0,1:T(8,128)(2,1)S(1)}, bf16[4,2,88,1024]{3,2,0,1:T(8,128)(2,1)S(1)}, u32[]{:S(2)}, u32[]{:S(2)}) collective-permute-start(bf16[4,2,88,1024]{3,2,0,1:T(8,128)(2,1)S(1)} %copy.72), channel_id=1, source_target_pairs={{0,4},{1,5},{2,6},{3,7},{4,0},{5,1},{6,2},{7,3},{8,12},{9,13},{10,... | collective-permute-start | bytes 4325384 | tf_op jit(solution)/shard_map/ppermute | solution.py:38
  132.4 32.6 %collective-permute-start.36 = (bf16[8,64,1024]{2,1,0:T(8,128)(2,1)S(1)}, bf16[8,64,1024]{2,1,0:T(8,128)(2,1)S(1)}, u32[]{:S(2)}, u32[]{:S(2)}) collective-permute-start(bf16[8,64,1024]{2,1,0:T(8,128)(2,1)S(1)} %constant_dynamic-update-slice_fusion.10), channel_id=1, source_target_pairs={{0,1},{1,0},{2,3},{3,2},{4,5},{5,4},{6,7},{7,6},{8,9},{9,8},{10,11... | collective-permute-start | bytes 3145736 | tf_op jit(solution)/shard_map/ppermute | solution.py:38
  133.5 30.9 %collective-permute-start.31 = (bf16[8,64,1024]{2,1,0:T(8,128)(2,1)S(1)}, bf16[8,64,1024]{2,1,0:T(8,128)(2,1)S(1)}, u32[]{:S(2)}, u32[]{:S(2)}) collective-permute-start(bf16[8,64,1024]{2,1,0:T(8,128)(2,1)S(1)} %multiply_convert_fusion.1.n0), channel_id=1, source_target_pairs={{0,2},{1,3},{2,0},{3,1},{4,6},{5,7},{6,4},{7,5},{8,10},{9,11},{10,... | collective-permute-start | bytes 3145736 | tf_op jit(solution)/shard_map/ppermute | solution.py:38
  134.9 32.7 %collective-permute-start.37 = (bf16[4,88,1024]{2,1,0:T(8,128)(2,1)S(1)}, bf16[4,88,1024]{2,1,0:T(8,128)(2,1)S(1)}, u32[]{:S(2)}, u32[]{:S(2)}) collective-permute-start(bf16[4,88,1024]{2,1,0:T(8,128)(2,1)S(1)} %pad_maximum_fusion.6), channel_id=1, source_target_pairs={{0,8},{1,9},{2,10},{3,11},{4,12},{5,13},{6,14},{7,15},{8,0},{9,1},... | collective-permute-start | bytes 2162696 | tf_op jit(solution)/shard_map/ppermute | solution.py:38
  195.2 18.6 %collective-permute-start.38 = (bf16[2,8,64,1024]{3,2,1,0:T(8,128)(2,1)}, bf16[2,8,64,1024]{3,2,1,0:T(8,128)(2,1)S(1)}, u32[]{:S(2)}, u32[]{:S(2)}) collective-permute-start(bf16[2,8,64,1024]{3,2,1,0:T(8,128)(2,1)} %get-tuple-element.186), channel_id=1, source_target_pairs={{0,1},{1,0},{2,3},{3,2},{4,5},{5,4},{6,7},{7,6},{8,9},{9,8},{10,11... | collective-permute-start | bytes 6291464 | tf_op jit(solution)/shard_map/ppermute | solution.py:38
  199.6 25.5 %collective-permute-start.40 = (bf16[8,64,1024]{2,1,0:T(8,128)(2,1)S(1)}, bf16[8,64,1024]{2,1,0:T(8,128)(2,1)S(1)}, u32[]{:S(2)}, u32[]{:S(2)}) collective-permute-start(bf16[8,64,1024]{2,1,0:T(8,128)(2,1)S(1)} %fusion.32), channel_id=1, source_target_pairs={{0,2},{1,3},{2,0},{3,1},{4,6},{5,7},{6,4},{7,5},{8,10},{9,11},{10,... | collective-permute-start | bytes 3145736 | tf_op jit(solution)/shard_map/ppermute | solution.py:38
  207.2 18.0 %collective-permute-start.41 = (bf16[4,88,1024]{2,1,0:T(8,128)(2,1)S(1)}, bf16[4,88,1024]{2,1,0:T(8,128)(2,1)S(1)}, u32[]{:S(2)}, u32[]{:S(2)}) collective-permute-start(bf16[4,88,1024]{2,1,0:T(8,128)(2,1)S(1)} %bitcast.212), channel_id=1, source_target_pairs={{0,4},{1,5},{2,6},{3,7},{4,0},{5,1},{6,2},{7,3},{8,12},{9,13},{10,... | collective-permute-start | bytes 2162696 | tf_op jit(solution)/shard_map/ppermute | solution.py:38
  228.2 25.9 %collective-permute-start.44 = (bf16[8,64,1024]{2,1,0:T(8,128)(2,1)}, bf16[8,64,1024]{2,1,0:T(8,128)(2,1)}, u32[]{:S(2)}, u32[]{:S(2)}) collective-permute-start(bf16[8,64,1024]{2,1,0:T(8,128)(2,1)} %fusion.33), channel_id=1, source_target_pairs={{0,2},{1,3},{2,0},{3,1},{4,6},{5,7},{6,4},{7,5},{8,10},{9,11},{10,... | collective-permute-start | bytes 3145736 | tf_op jit(solution)/shard_map/ppermute | solution.py:38
  230.2 18.5 %collective-permute-start.43 = (bf16[4,88,1024]{2,1,0:T(8,128)(2,1)}, bf16[4,88,1024]{2,1,0:T(8,128)(2,1)}, u32[]{:S(2)}, u32[]{:S(2)}) collective-permute-start(bf16[4,88,1024]{2,1,0:T(8,128)(2,1)} %slice_bitcast_fusion.2), channel_id=1, source_target_pairs={{0,4},{1,5},{2,6},{3,7},{4,0},{5,1},{6,2},{7,3},{8,12},{9,13},{10,... | collective-permute-start | bytes 2162696 | tf_op jit(solution)/shard_map/ppermute | solution.py:38
  231.7 35.9 %collective-permute-start.48 = (bf16[2,2,88,1024]{3,2,0,1:T(8,128)(2,1)}, bf16[2,2,88,1024]{3,2,0,1:T(8,128)(2,1)S(1)}, u32[]{:S(2)}, u32[]{:S(2)}) collective-permute-start(bf16[2,2,88,1024]{3,2,0,1:T(8,128)(2,1)} %bitcast.211), channel_id=1, source_target_pairs={{0,8},{1,9},{2,10},{3,11},{4,12},{5,13},{6,14},{7,15},{8,0},{9,1},... | collective-permute-start | bytes 2162696 | tf_op jit(solution)/shard_map/ppermute | solution.py:38
  304.3 26.5 %collective-permute-start.58 = (bf16[2,2,88,1024]{3,2,1,0:T(8,128)(2,1)S(1)}, bf16[2,2,88,1024]{3,2,1,0:T(8,128)(2,1)S(1)}, u32[]{:S(2)}, u32[]{:S(2)}) collective-permute-start(bf16[2,2,88,1024]{3,2,1,0:T(8,128)(2,1)S(1)} %slice.201), channel_id=1, source_target_pairs={{0,8},{1,9},{2,10},{3,11},{4,12},{5,13},{6,14},{7,15},{8,0},{9,1},... | collective-permute-start | bytes 2162696 | tf_op jit(solution)/shard_map/ppermute | solution.py:38
  304.7 26.1 %collective-permute-start.59 = (bf16[2,88,1024]{2,1,0:T(8,128)(2,1)S(1)}, bf16[2,88,1024]{2,1,0:T(8,128)(2,1)S(1)}, u32[]{:S(2)}, u32[]{:S(2)}) collective-permute-start(bf16[2,88,1024]{2,1,0:T(8,128)(2,1)S(1)} %slice_bitcast_fusion.9), channel_id=1, source_target_pairs={{0,16},{1,17},{2,18},{3,19},{4,20},{5,21},{6,22},{7,23},{8,24},{9,... | collective-permute-start | bytes 1081352 | tf_op jit(solution)/shard_map/ppermute | solution.py:38
  311.2 19.6 %collective-permute-start.60 = (bf16[4,2,128,256]{3,2,1,0:T(8,128)(2,1)S(1)}, bf16[4,2,128,256]{3,2,1,0:T(8,128)(2,1)S(1)}, u32[]{:S(2)}, u32[]{:S(2)}) collective-permute-start(bf16[4,2,128,256]{3,2,1,0:T(8,128)(2,1)S(1)} %slice.244), channel_id=1, source_target_pairs={{0,2},{1,3},{2,0},{3,1},{4,6},{5,7},{6,4},{7,5},{8,10},{9,11},{10,... | collective-permute-start | bytes 1572872 | tf_op jit(solution)/shard_map/ppermute | solution.py:38
  325.1 30.0 %collective-permute-start.57 = (bf16[8,64,1024]{2,1,0:T(8,128)(2,1)S(1)}, bf16[8,64,1024]{2,1,0:T(8,128)(2,1)S(1)}, u32[]{:S(2)}, u32[]{:S(2)}) collective-permute-start(bf16[8,64,1024]{2,1,0:T(8,128)(2,1)S(1)} %get-tuple-element.237), channel_id=1, source_target_pairs={{0,1},{1,0},{2,3},{3,2},{4,5},{5,4},{6,7},{7,6},{8,9},{9,8},{10,11... | collective-permute-start | bytes 3145736 | tf_op jit(solution)/shard_map/ppermute | solution.py:38
  331.1 28.5 %collective-permute-start.68 = (bf16[2,3,128,256]{3,2,1,0:T(8,128)(2,1)S(1)}, bf16[2,3,128,256]{3,2,1,0:T(8,128)(2,1)S(1)}, u32[]{:S(2)}, u32[]{:S(2)}) collective-permute-start(bf16[2,3,128,256]{3,2,1,0:T(8,128)(2,1)S(1)} %pad_maximum_fusion.9), channel_id=1, source_target_pairs={{0,8},{1,9},{2,10},{3,11},{4,12},{5,13},{6,14},{7,15},{8,0},{9,1},... | collective-permute-start | bytes 1179656 | tf_op jit(solution)/shard_map/ppermute | solution.py:38
  331.4 21.4 %collective-permute-start.62 = (bf16[8,1,128,256]{3,2,1,0:T(8,128)(2,1)S(1)}, bf16[8,1,128,256]{3,2,1,0:T(8,128)(2,1)S(1)}, u32[]{:S(2)}, u32[]{:S(2)}) collective-permute-start(bf16[8,1,128,256]{3,2,1,0:T(8,128)(2,1)S(1)} %get-tuple-element.254), channel_id=1, source_target_pairs={{0,4},{1,5},{2,6},{3,7},{4,0},{5,1},{6,2},{7,3},{8,12},{9,13},{10,... | collective-permute-start | bytes 1572872 | tf_op jit(solution)/shard_map/ppermute | solution.py:38
  331.6 21.2 %collective-permute-start.63 = (bf16[8,1,128,256]{3,2,1,0:T(8,128)(2,1)S(1)}, bf16[8,1,128,256]{3,2,1,0:T(8,128)(2,1)S(1)}, u32[]{:S(2)}, u32[]{:S(2)}) collective-permute-start(bf16[8,1,128,256]{3,2,1,0:T(8,128)(2,1)S(1)} %get-tuple-element.255), channel_id=1, source_target_pairs={{0,2},{1,3},{2,0},{3,1},{4,6},{5,7},{6,4},{7,5},{8,10},{9,11},{10,... | collective-permute-start | bytes 1572872 | tf_op jit(solution)/shard_map/ppermute | solution.py:38
  333.1 18.7 %collective-permute-start.64 = (bf16[2,88,1024]{2,1,0:T(8,128)(2,1)S(1)}, bf16[2,88,1024]{2,1,0:T(8,128)(2,1)S(1)}, u32[]{:S(2)}, u32[]{:S(2)}) collective-permute-start(bf16[2,88,1024]{2,1,0:T(8,128)(2,1)S(1)} %slice_bitcast_fusion.8), channel_id=1, source_target_pairs={{0,16},{1,17},{2,18},{3,19},{4,20},{5,21},{6,22},{7,23},{8,24},{9,... | collective-permute-start | bytes 1081352 | tf_op jit(solution)/shard_map/ppermute | solution.py:38
  (175 other events, 1736.7 us)

commit v6 on v5

--- a/solution.py
+++ b/solution.py
@@ -307,30 +307,40 @@
         put(query_grad, lanes, turn(gq, cosine[...], -sine[...]) * slope)
 
 
-def rows_kernel(spots, query_grad, modulate_grad, w0, w1, out, wq, wm, sems):
+def rows_kernel(
+    spots, query_grad, modulate_grad, key_grad, value_grad, w0, w1, kw0, kw1, vw0, vw1,
+    near_out, far_out, wq, wm, wk, wv, sems
+):
     @pl.when(pl.program_id(0) == 0)
     def _():
-        each_block(spots, [(0, 0, w0, w1, wq, sems.at[0]), (0, 1, w0, w1, wm, sems.at[1])])
-
-    put(out, slice(None), mm(get(query_grad), wq[...], NT) + mm(get(modulate_grad), wm[...], NT))
+        each_block(
+            spots,
+            [
+                (0, 0, w0, w1, wq, sems.at[0]), (0, 1, w0, w1, wm, sems.at[1]),
+                (0, 0, kw0, kw1, wk, sems.at[2]), (2, 0, vw0, vw1, wv, sems.at[3]),
+            ],
+        )
+
+    out = mm(get(query_grad), wq[...], NT) + mm(get(modulate_grad), wm[...], NT)
+    out = out + mm(get(key_grad), wk[...], NT) + mm(get(value_grad), wv[...], NT)
+    half = out.shape[0] // 2
+    near_out[...] = out[:half].reshape(near_out.shape)
+    far_out[...] = out[half:].astype(BF16).reshape(far_out.shape)
 
 
 def key_back_kernel(
-    spots, key_grad, value_grad, keys, values, key_pre, mask, cosine, sine, key_decay, rows_in,
-    g0, g1, g2, g3, kw0, kw1, vw0, vw1,
-    key_out, value_out, near_out, far_out, wk, wv, held, sems, state_sems
+    spots, key_grad, value_grad, keys, values, key_pre, mask, cosine, sine, key_decay,
+    g0, g1, g2, g3, key_out, value_out, held, state_sems
 ):
     @pl.when(pl.program_id(0) == 0)
     def _():
         load_states(spots, (g0, g1, g2, g3), held, state_sems)
-        each_block(spots, [(0, 0, kw0, kw1, wk, sems.at[0]), (2, 0, vw0, vw1, wv, sems.at[1])])
 
     step = pl.program_id(0)
     _, count, size, width = keys.shape
     heads = held.shape[2]
     head = width // heads
     valid = get(mask).astype(F32)
-    gks, gvs = [], []
     for h in range(heads):
         lanes = slice(h * head, (h + 1) * head)
         decay = key_decay[:, lanes]
@@ -343,31 +353,24 @@
         kp = get(key_pre, lanes).astype(F32)
         sg = jax.nn.sigmoid(kp)
         slope = sg + kp * sg * (1.0 - sg)
-        gks.append((turn(gk * valid, cosine[...], -sine[...]) * slope).astype(BF16))
-        gvs.append((gv * valid).astype(BF16))
-    gk, gv = jnp.concatenate(gks, axis=1), jnp.concatenate(gvs, axis=1)
-    put(key_out, slice(None), gk)
-    put(value_out, slice(None), gv)
-    out = get(rows_in).astype(F32) + mm(gk, wk[...], NT) + mm(gv, wv[...], NT)
-    near_out[...] = out[: count * size].reshape(near_out.shape)
-    far_out[...] = out[count * size :].astype(BF16).reshape(far_out.shape)
+        put(key_out, lanes, turn(gk * valid, cosine[...], -sine[...]) * slope)
+        put(value_out, lanes, gv * valid)
 
 
 def hidden_kernel(
-    spots, n0, n1, n2, n3, branch_rows, gate_w, lift_w, down_w,
+    spots, n0, n1, n2, n3, b0, b1, b2, b3, mask, gate_w, lift_w, down_w,
     inner_out, gate_out, lift_out, keep, send, branch_keep, branch_send
 ):
-    x, b = [], get(branch_rows)
-    for n in (n0, n1, n2, n3):
-        x.append(n[...].reshape(-1, n.shape[-1]))
-    x = jnp.concatenate(x, axis=0)
+    flat = lambda refs: jnp.concatenate([r[...].reshape(-1, r.shape[-1]) for r in refs], axis=0)
+    x, b = flat((n0, n1, n2, n3)), flat((b0, b1, b2, b3))
+    valid = get(mask)[:, :1].astype(F32)
     gate, lift, down = gate_w[...], lift_w[...], down_w[...]
     parts = []
     for r in range(0, x.shape[0], 256):
         rows = slice(r, r + 256)
         gate_pre = mm(x[rows], gate, NT)
         lift_pre = mm(x[rows], lift, NT)
-        inner_grad = mm(b[rows], down, NT)
+        inner_grad = mm(b[rows], down, NT) * valid[rows]
         q = jax.nn.sigmoid(gate_pre)
         act = gate_pre * q
         gate_grad = (inner_grad * lift_pre * (q + act * (1.0 - q))).astype(BF16)
@@ -433,8 +436,8 @@
             out_specs=[spec(s, kind) for s, _, kind in outputs],
             scratch_shapes=scratch,
         ),
-        compiler_params=pltpu.CompilerParams(vmem_limit_bytes=44 * 2**20),
-        cost_estimate=pl.CostEstimate(flops=flops, bytes_accessed=moved, transcendentals=0),
+        compiler_params=pltpu.CompilerParams(vmem_limit_bytes=40 * 2**20),
+        cost_estimate=pl.CostEstimate(flops=int(flops * 2), bytes_accessed=int(moved * 2), transcendentals=0),
         name=name,
     )(spots, *[a for a, _ in inputs])
 
@@ -710,8 +713,8 @@
     row_starts = (narrow_index ^ jnp.array([0, x_mask, 1, 1 + x_mask], jnp.int32)) * quarter
     row_spots = wide_index * (quarter * narrow_count) + row_starts[:, None] + jnp.arange(quarter)
     row_mask = (row_spots[:, None, :] < valid_lengths[None, :, None]).astype(F32)[..., None]
-    branch_rows = jnp.stack(quarters(output_cotangent, jnp.concatenate(cotangent_x)))
-    branch_rows = (row_mask * branch_rows.astype(F32)).astype(BF16)
+    branch_pieces = quarters(output_cotangent, jnp.concatenate(cotangent_x))
+    row_mask_wide = jnp.broadcast_to(row_mask, (4, slots, quarter, head_size)).astype(BF16)
     gate_t = join(gl[:, 0], gl_y[:, 0]).reshape(-1, width)
     lift_t = join(gl[:, 1], gl_y[:, 1]).reshape(-1, width)
     bulk = half // 2
@@ -726,7 +729,8 @@
     inner, gate_grad, lift_grad, row_keep, row_send, branch_keep, branch_send = run(
         hidden_kernel, "hidden", spots,
         [
-            *[(p, "rows") for p in two_pieces], (branch_rows, "pair"), (gate_t, "whole"),
+            *[(p, "rows") for p in two_pieces], *[(p, "rows") for p in branch_pieces],
+            (row_mask_wide, "pair"), (gate_t, "whole"),
             (lift_t, "whole"), (down_t, "whole"),
         ],
         [(hidden_shape, BF16, "pair")] * 3 + [(sum_shape, BF16, "pair")] * 4,
@@ -734,6 +738,8 @@
     )
     row_mine, row_send = core_part(row_keep, row_send)
     row_got = swap(row_send, x_mask)
+    branch_rows = jnp.stack(branch_pieces).astype(F32)
+    branch_rows = (tie(row_mask, row_send)[0] * branch_rows).astype(BF16)
     gate_grad, lift_grad, inner, row_send = tie(gate_grad, lift_grad, inner, row_send)
     gate_g = outer(gate_grad, normed_two).reshape(2, bulk, -1, width)
     gate_y = swap(gate_g[1], y_mask)
@@ -767,7 +773,7 @@
         [wide_scratch, held_scratch, dma((members,)), dma((4,))],
         steps, 2 * square_flops,
     )
-    state_grad, lift_y, branch_got, gated = tie(state_grad, lift_y, branch_got, gated)
+    state_grad, lift_y, gated = tie(state_grad, lift_y, gated)
     near = bulk // 2
     scan = Carry(state_grad, block_decay, True)
     scan.spread()
@@ -784,15 +790,8 @@
 
     output_keep, output_send = square("output_outer", 1, attended_pair, gated)
     query_keep, query_send = square("query_outer", 0, normed_pair, query_grad, modulate_grad)
-    (query_rows,) = run(
-        rows_kernel, "query_rows", spots,
-        [(query_grad, "pair"), (modulate_grad, "pair"), (query_parts[0], "any"), (query_parts[1], "any")],
-        [((2, *row_shape), BF16, "pair")],
-        [wide_scratch, wide_scratch, dma((2, members))],
-        steps, 2 * square_flops,
-    )
-    *scan.got, down_z, query_keep, query_send, output_keep, output_send = tie(
-        *scan.got, down_z, query_keep, query_send, output_keep, output_send
+    *scan.got, down_z, branch_got, query_keep, query_send, output_keep, output_send = tie(
+        *scan.got, down_z, branch_got, query_keep, query_send, output_keep, output_send
     )
     layer_output = (middle + mask_rows * (branch_mine + branch_got.astype(F32))).astype(BF16)
     down_g = jnp.moveaxis(fold(down_g[:, 0], down_z), 1, 0)
@@ -813,7 +812,7 @@
 
     scan.along(backward_step)
     query_y = jnp.concatenate([held["y"], held["more"]], axis=1)
-    scan.before, query_rows, down_g, gl_g = tie(scan.before, query_rows, down_g, gl_g)
+    scan.before, down_g, gl_g = tie(scan.before, down_g, gl_g)
     down_far = swap(down_g[1], z_far[0])
     gl_z = swap(gl_g[near:], z_near)
     later_parts = list(tie(*scan.back()))
@@ -836,21 +835,16 @@
             x = (fold if size > 1 else final)(x[:size], swap(x[size:], m))
         return x
 
-    key_out, value_out, near_rows, far_rows = run(
+    key_out, value_out = run(
         key_back_kernel, "key_back", spots,
         [
             (key_grad, "pair"), (value_grad, "pair"), (keys, "pair"), (values, "pair"),
             (key_pre, "pair"), (mask_wide, "pair"), (cosine, "whole"), (sine, "whole"),
-            (key_decay, "whole"), (query_rows, "pair"), *later_inputs,
-            (key_parts[0], "any"), (key_parts[1], "any"),
-            (value_parts[0], "any"), (value_parts[1], "any"),
-        ],
-        [
-            (chip_shape, BF16, "pair"), (chip_shape, BF16, "pair"), (row_shape, F32, "rows"),
-            (row_shape, BF16, "rows"),
-        ],
-        [wide_scratch, wide_scratch, held_scratch, dma((2, members)), dma((4,))],
-        steps, 2 * square_flops,
+            (key_decay, "whole"), *later_inputs,
+        ],
+        [(chip_shape, BF16, "pair"), (chip_shape, BF16, "pair")],
+        [held_scratch, dma((4,))],
+        steps, square_flops // 2,
     )
     key_keep, key_send = square("key_outer", 0, normed_pair, key_out)
     value_keep, value_send = square("value_outer", 2, normed_pair, value_out)
@@ -864,16 +858,29 @@
         gl_g = fold(gl_g[:size], swap(gl_g[size:], m))
     gl_far = swap(gl_g[1], z_far[0])
     key_y, value_x = swap(key_send, y_mask), swap(value_send, x_mask)
-    key_y, value_x, gl_far = tie(key_y, value_x, gl_far)
+    key_out, value_out = tie(key_out, value_out, key_send, value_send)[:2]
+    near_rows, far_rows = run(
+        rows_kernel, "rows", spots,
+        [
+            (query_grad, "pair"), (modulate_grad, "pair"), (key_out, "pair"),
+            (value_out, "pair"), (query_parts[0], "any"), (query_parts[1], "any"),
+            (key_parts[0], "any"), (key_parts[1], "any"),
+            (value_parts[0], "any"), (value_parts[1], "any"),
+        ],
+        [(row_shape, F32, "rows"), (row_shape, BF16, "rows")],
+        [wide_scratch] * 4 + [dma((4, members))],
+        steps, 4 * square_flops,
+    )
+    key_y, value_x, near_rows = tie(key_y, value_x, near_rows)
     down_y = swap(down_g[1], y_mask)
-    gate_lift = final(gl_g[0], gl_far)
     key_g, value_g = fold(key_keep, key_y), fold(value_keep, value_x)
     key_x, value_z = swap(key_g[quad:], x_mask), swap(value_g[quad:], z_near)
     qmo_g = jnp.concatenate(
         [fold(query_g[:quad], query_x), fold(output_g[:quad], output_y)], axis=1
     )
     qmo_z = swap(qmo_g[near:], z_near)
-    key_x, value_z, down_y, qmo_z = tie(key_x, value_z, down_y, qmo_z)
+    key_x, value_z, down_y, qmo_z, gl_far = tie(key_x, value_z, down_y, qmo_z, gl_far)
+    gate_lift = final(gl_g[0], gl_far)
     key_g, value_g = fold(key_g[:quad], key_x), fold(value_g[:quad], value_z)
     key_z, value_far = swap(key_g[near:], z_near), far_pairs(value_g)
     qmo_g = far_folds(fold(qmo_g[:near], qmo_z))[0]

time: 389 us -> 374 us (0.961)
  other arithmetic: 38.6 us -> 28.2 us
  starting transfers between devices: 79.3 us -> 69.7 us
  waiting for transfers between devices: 146 us -> 153 us
  Pallas kernels: 88.9 us -> 82.8 us
  local copies, waits for them, and re-layouts: 16.3 us -> 20.7 us
    ppermute x4, waiting for transfers between devices: 17.1 us -> 31.9 us  [shift_z(): return lax.ppermute(x, AXES, pairs)]
    ppermute x70, starting transfers between devices: 73.1 us -> 62.5 us  [exchange(): return lax.ppermute(x, AXES, [(i, i ^ mask) for i in range(count)])]
    ppermute x70, waiting for transfers between devices: 129 us -> 121 us  [exchange(): return lax.ppermute(x, AXES, [(i, i ^ mask) for i in range(count)])]
    pallas_call x11, Pallas kernels: 88.9 us -> 82.8 us  [run(): pl.pallas_call(kernel, out_shape=[jax.ShapeDtypeStruct(s, d) for s, d, _...]
    unnamed x258 -> x178, local copies, waits for them, and re-layouts: 7.6 us -> 9.39 us
  transfers between devices with their start and end apart: 74 -> 74, of which waited for: 34 -> 40; matrix products, arithmetic and copies ran while one was open for 14% -> 13% of each run, Pallas kernels for 15% -> 14%
where the time goes in v6:
time: 374 us; the launch traced here: 368 us
  waiting for transfers between devices  153 us (41%)
  Pallas kernels  82.8 us (22%)
  starting transfers between devices  69.7 us (19%)
  other arithmetic  28.2 us (8%)
  local copies, waits for them, and re-layouts  20.7 us (6%)
  matrix products  11 us (3%)
    ppermute x70, waiting for transfers between devices, exchange(): return lax.ppermute(x, AXES, [(i, i ^ mask) for i in range(count)])  121 us
    pallas_call x11, Pallas kernels, run(): pl.pallas_call(kernel, out_shape=[jax.ShapeDtypeStruct(s, d) for s, d, _...  82.8 us
    ppermute x70, starting transfers between devices, exchange(): return lax.ppermute(x, AXES, [(i, i ^ mask) for i in range(count)])  62.5 us
    ppermute x4, waiting for transfers between devices, shift_z(): return lax.ppermute(x, AXES, pairs)  31.9 us
    dot_general x3, matrix products, outer(): jnp.einsum('pblf,pbld->fd', a, b, preferred_element_type=F32).astype(BF16)  11 us
    unnamed x178, local copies, waits for them, and re-layouts  9.39 us
  transfers between devices with their start and end apart: 74, of which 40 were waited for; matrix products, arithmetic and copies ran while one was open for 13% of the time, Pallas kernels for 14%

profile of v6, /device:TPU:0, one launch (start us, length us, event | category | flops | bytes accessed | tf_op | source)
XLA Modules:
  0.0 368.4 jit_solution(16594548123054276845)
XLA Ops:
  29.4 4.3 %collective-permute-done.8 = bf16[4,1,128,256]{3,2,1,0:T(8,128)(2,1)S(1)} collective-permute-done((bf16[4,1,128,256]{3,2,1,0:T(8,128)(2,1)S(1)}, bf16[4,1,128,256]{3,2,1,0:T(8,128)(2,1)S(1)}, u32[]{:S(2)}, u32[]{:S(2)}) %collective-permute-start.8) | collective-permute-done | bytes 262176 | tf_op jit(solution)/shard_map/ppermute | solution.py:38
  37.9 7.9 %collective-permute-done.12 = bf16[1,3,128,256]{3,2,1,0:T(8,128)(2,1)S(1)} collective-permute-done((bf16[1,3,128,256]{3,2,1,0:T(8,128)(2,1)S(1)}, bf16[1,3,128,256]{3,2,1,0:T(8,128)(2,1)S(1)}, u32[]{:S(2)}, u32[]{:S(2)}) %collective-permute-start.12) | collective-permute-done | bytes 196640 | tf_op jit(solution)/shard_map/ppermute | solution.py:38
  47.0 6.0 %key_value.1 = (bf16[2,8,64,512]{3,2,1,0:T(8,128)(2,1)S(1)}, bf16[2,8,64,512]{3,2,1,0:T(8,128)(2,1)S(1)}, bf16[2,8,64,512]{3,2,1,0:T(8,128)(2,1)S(1)}, bf16[8,4,128,128]{3,2,1,0:T(8,128)(2,1)S(1)}) custom-call(s32[4,16,2]{2,1,0:T(8,128)S(1)} %add_add_fusion.spots, bf16[8,64,1024]{2,1,0:T(8,128)(2,1)S(1)} %copy-done.6, ...), custom_call_target="tpu_custom_call" | custom-call | flops 4294967296 | bytes 18874368 | tf_op jit(solution)/shard_map/key_value/pallas_call | solution.py:429
  64.2 4.0 %collective-permute-done.16 = bf16[2,4,128,128]{3,2,1,0:T(8,128)(2,1)S(1)} collective-permute-done((bf16[2,4,128,128]{3,2,1,0:T(8,128)(2,1)S(1)}, bf16[2,4,128,128]{3,2,1,0:T(8,128)(2,1)S(1)}, u32[]{:S(2)}, u32[]{:S(2)}) %collective-permute-start.16) | collective-permute-done | bytes 262176 | tf_op jit(solution)/shard_map/ppermute | solution.py:38
  87.4 11.2 %collective-permute-done.21 = bf16[2,4,128,128]{3,2,1,0:T(8,128)(2,1)S(1)} collective-permute-done((bf16[2,4,128,128]{3,2,1,0:T(8,128)(2,1)S(1)}, bf16[2,4,128,128]{3,2,1,0:T(8,128)(2,1)S(1)}, u32[]{:S(2)}, u32[]{:S(2)}) %collective-permute-start.21) | collective-permute-done | bytes 262176 | tf_op jit(solution)/shard_map/ppermute | solution.py:50
  98.6 3.7 %collective-permute-done.25 = bf16[4,64,1024]{2,1,0:T(8,128)(2,1)S(1)} collective-permute-done((bf16[4,64,1024]{2,1,0:T(8,128)(2,1)S(1)}, bf16[4,64,1024]{2,1,0:T(8,128)(2,1)S(1)}, u32[]{:S(2)}, u32[]{:S(2)}) %collective-permute-start.25) | collective-permute-done | bytes 524320 | tf_op jit(solution)/shard_map/ppermute | solution.py:38
  109.4 7.1 %query.1 = (bf16[2,8,64,512]{3,2,1,0:T(8,128)(2,1)S(1)}, bf16[2,8,64,512]{3,2,1,0:T(8,128)(2,1)S(1)}, bf16[2,8,64,512]{3,2,1,0:T(8,128)(2,1)S(1)}, bf16[2,8,64,512]{3,2,1,0:T(8,128)(2,1)S(1)}) custom-call(s32[4,16,2]{2,1,0:T(8,128)S(1)} %add_add_fusion.spots, bf16[8,64,1024]{2,1,0:T(8,128)(2,1)S(1)} %copy-done.6, ...), custom_call_target="tpu_custom_call" | custom-call | flops 4294967296 | bytes 24117248 | tf_op jit(solution)/shard_map/query/pallas_call | solution.py:429
  117.9 4.9 %mixed.1 = (bf16[2,8,64,512]{3,2,1,0:T(8,128)(2,1)S(1)}, bf16[2,8,64,512]{3,2,1,0:T(8,128)(2,1)S(1)}, f32[8,64,1024]{2,1,0:T(8,128)S(1)}, bf16[8,64,1024]{2,1,0:T(8,128)(2,1)S(1)}) custom-call(s32[4,16,2]{2,1,0:T(8,128)S(1)} %add_add_fusion.spots, bf16[2,8,64,512]{3,2,1,0:T(8,128)(2,1)S(1)} %get-tuple-element.173.queries, ...), custom_call_target="tpu_custom_call" | custom-call | flops 2147483648 | bytes 22020096 | tf_op jit(solution)/shard_map/mixed/pallas_call | solution.py:429
  130.6 27.6 %collective-permute-done.32 = bf16[4,2,88,1024]{3,2,0,1:T(8,128)(2,1)S(1)} collective-permute-done((bf16[4,2,88,1024]{3,2,0,1:T(8,128)(2,1)S(1)}, bf16[4,2,88,1024]{3,2,0,1:T(8,128)(2,1)S(1)}, u32[]{:S(2)}, u32[]{:S(2)}) %collective-permute-start.32) | collective-permute-done | bytes 1441824 | tf_op jit(solution)/shard_map/ppermute | solution.py:38
  162.8 25.1 %hidden.1 = (bf16[4,8,64,704]{3,2,1,0:T(8,128)(2,1)}, bf16[4,8,64,704]{3,2,1,0:T(8,128)(2,1)}, bf16[4,8,64,704]{3,2,1,0:T(8,128)(2,1)}, bf16[2,8,64,1024]{3,2,1,...) custom-call(s32[4,16,2]{2,1,0:T(8,128)S(1)} %add_add_fusion.spots, ...), custom_call_target="tpu_custom_call" | custom-call | flops 35433480192 | bytes 60555264 | tf_op jit(solution)/shard_map/hidden/pallas_call | solution.py:429
  200.2 4.4 %bitcast_convert_fusion.1 = bf16[704,1024]{1,0:T(8,128)(2,1)} fusion(bf16[4,8,64,704]{3,2,1,0:T(8,128)(2,1)S(1)} %copy-done.82, bf16[1,8,64,1024]{3,2,1,0:T(8,128)(2,1)S(1)} %bitcast.205, bf16[1,8,64,1024]{3,2,1,0:T(8,128)(2,1)S(1)} %bitcast.203, bf16[1,8,64,1024]{3,2,1,0:T(8,128)(2,1)S(1)} %bitcast.200, bf16[1,8,64,1024]{3,2,1,0:T(8,128)(2,1)S(1)} %fusion.116), kind=kOutput, calls=%fused_computation.17 | convolution fusion | flops 2959802368 | bytes 8519680 | tf_op jit(solution)/shard_map/pblf,pbld->fd/dot_general | solution.py:724
  208.2 6.2 %collective-permute-done.41 = bf16[4,88,1024]{2,1,0:T(8,128)(2,1)S(1)} collective-permute-done((bf16[4,88,1024]{2,1,0:T(8,128)(2,1)S(1)}, bf16[4,88,1024]{2,1,0:T(8,128)(2,1)S(1)}, u32[]{:S(2)}, u32[]{:S(2)}) %collective-permute-start.41) | collective-permute-done | bytes 720928 | tf_op jit(solution)/shard_map/ppermute | solution.py:38
  229.1 12.6 %mixed_back.1 = (bf16[2,8,64,512]{3,2,1,0:T(8,128)(2,1)S(1)}, bf16[2,8,64,512]{3,2,1,0:T(8,128)(2,1)S(1)}, bf16[2,8,64,512]{3,2,1,0:T(8,128)(2,1)S(1)}, bf16[2,8...) custom-call(s32[4,16,2]{2,1,0:T(8,128)S(1)} %add_add_fusion.spots, ...), custom_call_target="tpu_custom_call" | custom-call | flops 4294967296 | bytes 37748736 | tf_op jit(solution)/shard_map/mixed_back/pallas_call | solution.py:429
  245.4 4.3 %query_outer.1 = (bf16[8,2,128,256]{3,2,1,0:T(8,128)(2,1)S(1)}, bf16[8,2,128,256]{3,2,1,0:T(8,128)(2,1)S(1)}) custom-call(s32[4,16,2]{2,1,0:T(8,128)S(1)} %add_add_fusion.spots, bf16[8,64,1024]{2,1,0:T(8,128)(2,1)S(1)} %copy-done.7, bf16[8,64,1024]{2,1,0:T(8,128)(2,1)S(1)} %copy-done.22, bf16[2,8,64,512]{3,2,1,0:T(8,128)(2,1)S(1)} %get-tuple-element.210.refs_0_.query_grad, ...), custom_call_target="tpu_custom_call" | custom-call | flops 4294967296 | bytes 12582912 | tf_op jit(solution)/shard_map/query_outer/pallas_call | solution.py:429
  249.8 4.0 %output_outer.1 = (bf16[8,1,128,256]{3,2,1,0:T(8,128)(2,1)S(1)}, bf16[8,1,128,256]{3,2,1,0:T(8,128)(2,1)S(1)}) custom-call(s32[4,16,2]{2,1,0:T(8,128)S(1)} %add_add_fusion.spots, bf16[8,64,1024]{2,1,0:T(8,128)(2,1)S(1)} %copy-done.10, bf16[8,64,1024]{2,1,0:T(8,128)(2,1)} %collective-permute-done.42.far, bf16[2,8,64,512]{3,2,1,0:T(8,128)(2,1)S(1)} %copy-done.38), custom_call_target="tpu_custom_call" | custom-call | flops 2147483648 | bytes 8388608 | tf_op jit(solution)/shard_map/output_outer/pallas_call | solution.py:429
  255.0 5.5 %collective-permute-done.46 = bf16[2,4,128,128]{3,2,1,0:T(8,128)(2,1)S(1)} collective-permute-done((bf16[2,4,128,128]{3,2,1,0:T(8,128)(2,1)S(1)}, bf16[2,4,128,128]{3,2,1,0:T(8,128)(2,1)S(1)}, u32[]{:S(2)}, u32[]{:S(2)}) %collective-permute-start.46) | collective-permute-done | bytes 262176 | tf_op jit(solution)/shard_map/ppermute | solution.py:38
  263.6 6.8 %collective-permute-done.49 = bf16[2,4,128,128]{3,2,1,0:T(8,128)(2,1)S(1)} collective-permute-done((bf16[2,4,128,128]{3,2,1,0:T(8,128)(2,1)S(1)}, bf16[2,4,128,128]{3,2,1,0:T(8,128)(2,1)S(1)}, u32[]{:S(2)}, u32[]{:S(2)}) %collective-permute-start.49) | collective-permute-done | bytes 262176 | tf_op jit(solution)/shard_map/ppermute | solution.py:50
  275.9 12.9 %collective-permute-done.51 = bf16[2,4,128,128]{3,2,1,0:T(8,128)(2,1)S(1)} collective-permute-done((bf16[2,4,128,128]{3,2,1,0:T(8,128)(2,1)S(1)}, bf16[2,4,128,128]{3,2,1,0:T(8,128)(2,1)S(1)}, u32[]{:S(2)}, u32[]{:S(2)}) %collective-permute-start.51) | collective-permute-done | bytes 262176 | tf_op jit(solution)/shard_map/ppermute | solution.py:50
  297.0 3.8 %collective-permute-done.54.g1 = bf16[2,4,128,128]{3,2,1,0:T(8,128)(2,1)S(1)} collective-permute-done((bf16[2,4,128,128]{3,2,1,0:T(8,128)(2,1)S(1)}, bf16[2,4,128,128]{3,2,1,0:T(8,128)(2,1)S(1)}, u32[]{:S(2)}, u32[]{:S(2)}) %collective-permute-start.54) | collective-permute-done | bytes 262176 | tf_op jit(solution)/shard_map/ppermute | solution.py:38
  300.7 3.7 collective-permute-done.56.g3
  306.6 4.7 %key_back.1 = (bf16[2,8,64,512]{3,2,1,0:T(8,128)(2,1)S(1)}, bf16[2,8,64,512]{3,2,1,0:T(8,128)(2,1)S(1)}) custom-call(s32[4,16,2]{2,1,0:T(8,128)S(1)} %add_add_fusion.spots, bf16[2,8,64,512]{3,2,1,0:T(8,128)(2,1)S(1)} %get-tuple-element.218.key_grad, bf16[2,8,64,512]{3,2,1,0:T(8,128)(2,1)S(1)} %get-tuple-element.219.value_grad, ...), custom_call_target="tpu_custom_call" | custom-call | flops 1073741824 | bytes 18874368 | tf_op jit(solution)/shard_map/key_back/pallas_call | solution.py:429
  323.3 8.5 %rows.1 = (f32[8,64,1024]{2,1,0:T(8,128)S(1)}, bf16[8,64,1024]{2,1,0:T(8,128)(2,1)S(1)}) custom-call(s32[4,16,2]{2,1,0:T(8,128)S(1)} %add_add_fusion.spots, bf16[2,8,64,512]{3,2,1,0:T(8,128)(2,1)S(1)} %get-tuple-element.210.refs_0_.query_grad, bf16[2,8,64,512]{3,2,1,0:T(8,128)(2,1)S(1)} %get-tuple-element.211.refs_1_.modulate_grad, ...), custom_call_target="tpu_custom_call" | custom-call | flops 8589934592 | bytes 23068672 | tf_op jit(solution)/shard_map/rows/pallas_call | solution.py:429
  338.4 4.6 %collective-permute-done.65 = bf16[4,1,128,256]{3,2,1,0:T(8,128)(2,1)S(1)} collective-permute-done((bf16[4,1,128,256]{3,2,1,0:T(8,128)(2,1)S(1)}, bf16[4,1,128,256]{3,2,1,0:T(8,128)(2,1)S(1)}, u32[]{:S(2)}, u32[]{:S(2)}) %collective-permute-start.65) | collective-permute-done | bytes 262176 | tf_op jit(solution)/shard_map/ppermute | solution.py:38
  358.4 4.1 %collective-permute-done.71 = bf16[1,1,128,256]{3,2,1,0:T(8,128)(2,1)S(1)} collective-permute-done((bf16[1,1,128,256]{3,2,1,0:T(8,128)(2,1)S(1)}, bf16[1,1,128,256]{3,2,1,0:T(8,128)(2,1)S(1)}, u32[]{:S(2)}, u32[]{:S(2)}) %collective-permute-start.71) | collective-permute-done | bytes 65568 | tf_op jit(solution)/shard_map/ppermute | solution.py:38
  (459 shorter events, 177.7 us)
Async XLA Ops:
  0.7 27.9 %collective-permute-start = (f32[2]{0:T(128)}, f32[2]{0:T(128)}, u32[]{:S(2)}, u32[]{:S(2)}) collective-permute-start(f32[2]{0:T(128)} %param.25), channel_id=1, source_target_pairs={{0,2},{1,3},{2,0},{3,1},{4,6},{5,7},{6,4},{7,5},{8,10},{9,11},{10,... | collective-permute-start | bytes 32 | tf_op jit(solution)/shard_map/ppermute | solution.py:38
  10.1 16.9 %collective-permute-start.7 = (bf16[4,64,1024]{2,1,0:T(8,128)(2,1)}, bf16[4,64,1024]{2,1,0:T(8,128)(2,1)}, u32[]{:S(2)}, u32[]{:S(2)}) collective-permute-start(bf16[4,64,1024]{2,1,0:T(8,128)(2,1)} %get-tuple-element.308), channel_id=1, source_target_pairs={{0,2},{1,3},{2,0},{3,1},{4,6},{5,7},{6,4},{7,5},{8,10},{9,11},{10,... | collective-permute-start | bytes 1572872 | tf_op jit(solution)/shard_map/ppermute | solution.py:38
  21.9 24.8 %collective-permute-start.1 = (bf16[8,64,1024]{2,1,0:T(8,128)(2,1)S(1)}, bf16[8,64,1024]{2,1,0:T(8,128)(2,1)S(1)}, u32[]{:S(2)}, u32[]{:S(2)}) collective-permute-start(bf16[8,64,1024]{2,1,0:T(8,128)(2,1)S(1)} %fusion.10.near), channel_id=1, source_target_pairs={{0,1},{1,0},{2,3},{3,2},{4,5},{5,4},{6,7},{7,6},{8,9},{9,8},{10,11... | collective-permute-start | bytes 3145736 | tf_op jit(solution)/shard_map/ppermute | solution.py:38
  77.4 24.9 %collective-permute-start.22 = (bf16[8,2,128,256]{3,2,1,0:T(8,128)(2,1)S(1)}, bf16[8,2,128,256]{3,2,1,0:T(8,128)(2,1)S(1)}, u32[]{:S(2)}, u32[]{:S(2)}) collective-permute-start(bf16[8,2,128,256]{3,2,1,0:T(8,128)(2,1)S(1)} %constant_dynamic-update-slice_fusion.3.w0), channel_id=1, source_target_pairs={{0,4},{1,5},{2,6},{3,7},{4,0},{5,1},{6,2},{7,3},{8,12},{9,13},{10,... | collective-permute-start | bytes 3145736 | tf_op jit(solution)/shard_map/ppermute | solution.py:38
  79.4 23.0 %collective-permute-start.24 = (bf16[2,2,88,1024]{3,2,1,0:T(8,128)(2,1)S(1)}, bf16[2,2,88,1024]{3,2,1,0:T(8,128)(2,1)S(1)}, u32[]{:S(2)}, u32[]{:S(2)}) collective-permute-start(bf16[2,2,88,1024]{3,2,1,0:T(8,128)(2,1)S(1)} %pad_maximum_fusion.5), channel_id=1, source_target_pairs={{0,8},{1,9},{2,10},{3,11},{4,12},{5,13},{6,14},{7,15},{8,0},{9,1},... | collective-permute-start | bytes 2162696 | tf_op jit(solution)/shard_map/ppermute | solution.py:38
  80.5 18.1 %collective-permute-start.23 = (bf16[8,1,128,256]{3,2,1,0:T(8,128)(2,1)S(1)}, bf16[8,1,128,256]{3,2,1,0:T(8,128)(2,1)S(1)}, u32[]{:S(2)}, u32[]{:S(2)}) collective-permute-start(bf16[8,1,128,256]{3,2,1,0:T(8,128)(2,1)S(1)} %constant_dynamic-update-slice_fusion.5.w0), channel_id=1, source_target_pairs={{0,2},{1,3},{2,0},{3,1},{4,6},{5,7},{6,4},{7,5},{8,10},{9,11},{10,... | collective-permute-start | bytes 1572872 | tf_op jit(solution)/shard_map/ppermute | solution.py:38
  82.8 19.5 %collective-permute-start.25 = (bf16[4,64,1024]{2,1,0:T(8,128)(2,1)S(1)}, bf16[4,64,1024]{2,1,0:T(8,128)(2,1)S(1)}, u32[]{:S(2)}, u32[]{:S(2)}) collective-permute-start(bf16[4,64,1024]{2,1,0:T(8,128)(2,1)S(1)} %copy-done.63), channel_id=1, source_target_pairs={{0,2},{1,3},{2,0},{3,1},{4,6},{5,7},{6,4},{7,5},{8,10},{9,11},{10,... | collective-permute-start | bytes 1572872 | tf_op jit(solution)/shard_map/ppermute | solution.py:38
  123.9 35.7 %collective-permute-start.35 = (bf16[8,64,1024]{2,1,0:T(8,128)(2,1)S(1)}, bf16[8,64,1024]{2,1,0:T(8,128)(2,1)S(1)}, u32[]{:S(2)}, u32[]{:S(2)}) collective-permute-start(bf16[8,64,1024]{2,1,0:T(8,128)(2,1)S(1)} %copy-done), channel_id=1, source_target_pairs={{0,1},{1,0},{2,3},{3,2},{4,5},{5,4},{6,7},{7,6},{8,9},{9,8},{10,11... | collective-permute-start | bytes 3145736 | tf_op jit(solution)/shard_map/ppermute | solution.py:38
  124.9 33.4 %collective-permute-start.32 = (bf16[4,2,88,1024]{3,2,0,1:T(8,128)(2,1)S(1)}, bf16[4,2,88,1024]{3,2,0,1:T(8,128)(2,1)S(1)}, u32[]{:S(2)}, u32[]{:S(2)}) collective-permute-start(bf16[4,2,88,1024]{3,2,0,1:T(8,128)(2,1)S(1)} %copy.72), channel_id=1, source_target_pairs={{0,4},{1,5},{2,6},{3,7},{4,0},{5,1},{6,2},{7,3},{8,12},{9,13},{10,... | collective-permute-start | bytes 4325384 | tf_op jit(solution)/shard_map/ppermute | solution.py:38
  127.2 31.1 %collective-permute-start.31 = (bf16[8,64,1024]{2,1,0:T(8,128)(2,1)S(1)}, bf16[8,64,1024]{2,1,0:T(8,128)(2,1)S(1)}, u32[]{:S(2)}, u32[]{:S(2)}) collective-permute-start(bf16[8,64,1024]{2,1,0:T(8,128)(2,1)S(1)} %multiply_convert_fusion.1.n0), channel_id=1, source_target_pairs={{0,2},{1,3},{2,0},{3,1},{4,6},{5,7},{6,4},{7,5},{8,10},{9,11},{10,... | collective-permute-start | bytes 3145736 | tf_op jit(solution)/shard_map/ppermute | solution.py:38
  127.9 31.0 %collective-permute-start.37 = (bf16[4,88,1024]{2,1,0:T(8,128)(2,1)S(1)}, bf16[4,88,1024]{2,1,0:T(8,128)(2,1)S(1)}, u32[]{:S(2)}, u32[]{:S(2)}) collective-permute-start(bf16[4,88,1024]{2,1,0:T(8,128)(2,1)S(1)} %pad_maximum_fusion.6), channel_id=1, source_target_pairs={{0,8},{1,9},{2,10},{3,11},{4,12},{5,13},{6,14},{7,15},{8,0},{9,1},... | collective-permute-start | bytes 2162696 | tf_op jit(solution)/shard_map/ppermute | solution.py:38
  130.6 29.1 %collective-permute-start.36 = (bf16[8,64,1024]{2,1,0:T(8,128)(2,1)S(1)}, bf16[8,64,1024]{2,1,0:T(8,128)(2,1)S(1)}, u32[]{:S(2)}, u32[]{:S(2)}) collective-permute-start(bf16[8,64,1024]{2,1,0:T(8,128)(2,1)S(1)} %constant_dynamic-update-slice_fusion.10.b1), channel_id=1, source_target_pairs={{0,1},{1,0},{2,3},{3,2},{4,5},{5,4},{6,7},{7,6},{8,9},{9,8},{10,11... | collective-permute-start | bytes 3145736 | tf_op jit(solution)/shard_map/ppermute | solution.py:38
  188.4 18.2 %collective-permute-start.38 = (bf16[2,8,64,1024]{3,2,1,0:T(8,128)(2,1)}, bf16[2,8,64,1024]{3,2,1,0:T(8,128)(2,1)S(1)}, u32[]{:S(2)}, u32[]{:S(2)}) collective-permute-start(bf16[2,8,64,1024]{3,2,1,0:T(8,128)(2,1)} %get-tuple-element.189), channel_id=1, source_target_pairs={{0,1},{1,0},{2,3},{3,2},{4,5},{5,4},{6,7},{7,6},{8,9},{9,8},{10,11... | collective-permute-start | bytes 6291464 | tf_op jit(solution)/shard_map/ppermute | solution.py:38
  192.8 25.3 %collective-permute-start.40 = (bf16[8,64,1024]{2,1,0:T(8,128)(2,1)S(1)}, bf16[8,64,1024]{2,1,0:T(8,128)(2,1)S(1)}, u32[]{:S(2)}, u32[]{:S(2)}) collective-permute-start(bf16[8,64,1024]{2,1,0:T(8,128)(2,1)S(1)} %fusion.32), channel_id=1, source_target_pairs={{0,2},{1,3},{2,0},{3,1},{4,6},{5,7},{6,4},{7,5},{8,10},{9,11},{10,... | collective-permute-start | bytes 3145736 | tf_op jit(solution)/shard_map/ppermute | solution.py:38
  196.5 18.0 %collective-permute-start.41 = (bf16[4,88,1024]{2,1,0:T(8,128)(2,1)S(1)}, bf16[4,88,1024]{2,1,0:T(8,128)(2,1)S(1)}, u32[]{:S(2)}, u32[]{:S(2)}) collective-permute-start(bf16[4,88,1024]{2,1,0:T(8,128)(2,1)S(1)} %bitcast.213), channel_id=1, source_target_pairs={{0,4},{1,5},{2,6},{3,7},{4,0},{5,1},{6,2},{7,3},{8,12},{9,13},{10,... | collective-permute-start | bytes 2162696 | tf_op jit(solution)/shard_map/ppermute | solution.py:38
  222.4 19.3 %collective-permute-start.43 = (bf16[4,88,1024]{2,1,0:T(8,128)(2,1)S(1)}, bf16[4,88,1024]{2,1,0:T(8,128)(2,1)S(1)}, u32[]{:S(2)}, u32[]{:S(2)}) collective-permute-start(bf16[4,88,1024]{2,1,0:T(8,128)(2,1)S(1)} %slice_bitcast_fusion.2), channel_id=1, source_target_pairs={{0,4},{1,5},{2,6},{3,7},{4,0},{5,1},{6,2},{7,3},{8,12},{9,13},{10,... | collective-permute-start | bytes 2162696 | tf_op jit(solution)/shard_map/ppermute | solution.py:38
  223.1 30.7 %collective-permute-start.48 = (bf16[8,64,1024]{2,1,0:T(8,128)(2,1)}, bf16[8,64,1024]{2,1,0:T(8,128)(2,1)S(1)}, u32[]{:S(2)}, u32[]{:S(2)}) collective-permute-start(bf16[8,64,1024]{2,1,0:T(8,128)(2,1)} %fusion.33), channel_id=1, source_target_pairs={{0,2},{1,3},{2,0},{3,1},{4,6},{5,7},{6,4},{7,5},{8,10},{9,11},{10,... | collective-permute-start | bytes 3145736 | tf_op jit(solution)/shard_map/ppermute | solution.py:38
  223.4 30.4 %collective-permute-start.47 = (bf16[2,2,88,1024]{3,2,0,1:T(8,128)(2,1)}, bf16[2,2,88,1024]{3,2,0,1:T(8,128)(2,1)S(1)}, u32[]{:S(2)}, u32[]{:S(2)}) collective-permute-start(bf16[2,2,88,1024]{3,2,0,1:T(8,128)(2,1)} %bitcast.212), channel_id=1, source_target_pairs={{0,8},{1,9},{2,10},{3,11},{4,12},{5,13},{6,14},{7,15},{8,0},{9,1},... | collective-permute-start | bytes 2162696 | tf_op jit(solution)/shard_map/ppermute | solution.py:38
  293.6 24.3 %collective-permute-start.57 = (bf16[2,2,88,1024]{3,2,1,0:T(8,128)(2,1)S(1)}, bf16[2,2,88,1024]{3,2,1,0:T(8,128)(2,1)S(1)}, u32[]{:S(2)}, u32[]{:S(2)}) collective-permute-start(bf16[2,2,88,1024]{3,2,1,0:T(8,128)(2,1)S(1)} %slice.200), channel_id=1, source_target_pairs={{0,8},{1,9},{2,10},{3,11},{4,12},{5,13},{6,14},{7,15},{8,0},{9,1},... | collective-permute-start | bytes 2162696 | tf_op jit(solution)/shard_map/ppermute | solution.py:38
  293.7 23.3 %collective-permute-start.58 = (bf16[2,88,1024]{2,1,0:T(8,128)(2,1)S(1)}, bf16[2,88,1024]{2,1,0:T(8,128)(2,1)S(1)}, u32[]{:S(2)}, u32[]{:S(2)}) collective-permute-start(bf16[2,88,1024]{2,1,0:T(8,128)(2,1)S(1)} %slice_bitcast_fusion.9), channel_id=1, source_target_pairs={{0,16},{1,17},{2,18},{3,19},{4,20},{5,21},{6,22},{7,23},{8,24},{9,... | collective-permute-start | bytes 1081352 | tf_op jit(solution)/shard_map/ppermute | solution.py:38
  319.9 16.8 %collective-permute-start.68 = (bf16[2,88,1024]{2,1,0:T(8,128)(2,1)S(1)}, bf16[2,88,1024]{2,1,0:T(8,128)(2,1)S(1)}, u32[]{:S(2)}, u32[]{:S(2)}) collective-permute-start(bf16[2,88,1024]{2,1,0:T(8,128)(2,1)S(1)} %slice_bitcast_fusion.8), channel_id=1, source_target_pairs={{0,16},{1,17},{2,18},{3,19},{4,20},{5,21},{6,22},{7,23},{8,24},{9,... | collective-permute-start | bytes 1081352 | tf_op jit(solution)/shard_map/ppermute | solution.py:38
  321.4 17.0 %collective-permute-start.67 = (bf16[2,3,128,256]{3,2,1,0:T(8,128)(2,1)S(1)}, bf16[2,3,128,256]{3,2,1,0:T(8,128)(2,1)S(1)}, u32[]{:S(2)}, u32[]{:S(2)}) collective-permute-start(bf16[2,3,128,256]{3,2,1,0:T(8,128)(2,1)S(1)} %pad_maximum_fusion.9), channel_id=1, source_target_pairs={{0,8},{1,9},{2,10},{3,11},{4,12},{5,13},{6,14},{7,15},{8,0},{9,1},... | collective-permute-start | bytes 1179656 | tf_op jit(solution)/shard_map/ppermute | solution.py:38
  336.7 28.0 %collective-permute-start.63 = (bf16[8,64,1024]{2,1,0:T(8,128)(2,1)S(1)}, bf16[8,64,1024]{2,1,0:T(8,128)(2,1)S(1)}, u32[]{:S(2)}, u32[]{:S(2)}) collective-permute-start(bf16[8,64,1024]{2,1,0:T(8,128)(2,1)S(1)} %get-tuple-element.258), channel_id=1, source_target_pairs={{0,1},{1,0},{2,3},{3,2},{4,5},{5,4},{6,7},{7,6},{8,9},{9,8},{10,11... | collective-permute-start | bytes 3145736 | tf_op jit(solution)/shard_map/ppermute | solution.py:38
  345.3 18.6 %collective-permute-start.69 = (bf16[1,3,128,256]{3,2,1,0:T(8,128)(2,1)S(1)}, bf16[1,3,128,256]{3,2,1,0:T(8,128)(2,1)S(1)}, u32[]{:S(2)}, u32[]{:S(2)}) collective-permute-start(bf16[1,3,128,256]{3,2,1,0:T(8,128)(2,1)S(1)} %slice.254), channel_id=1, source_target_pairs={{0,16},{1,17},{2,18},{3,19},{4,20},{5,21},{6,22},{7,23},{8,24},{9,... | collective-permute-start | bytes 589832 | tf_op jit(solution)/shard_map/ppermute | solution.py:38
  (135 other events, 1339.2 us)

commit v7 on v6

--- a/solution.py
+++ b/solution.py
@@ -437,7 +437,7 @@
             scratch_shapes=scratch,
         ),
         compiler_params=pltpu.CompilerParams(vmem_limit_bytes=40 * 2**20),
-        cost_estimate=pl.CostEstimate(flops=int(flops * 2), bytes_accessed=int(moved * 2), transcendentals=0),
+        cost_estimate=pl.CostEstimate(flops=int(flops * 2.4), bytes_accessed=int(moved * 2.4), transcendentals=0),
         name=name,
     )(spots, *[a for a, _ in inputs])
 
@@ -822,13 +822,6 @@
     query_x, output_y = swap(query_g[quad:], x_mask), swap(output_g[quad:], y_mask)
     later_inputs = [(p, "any") for p in later_parts]
     quad = half // 2
-    def far_pairs(x):
-        x = x.reshape(-1, 2, *x.shape[1:])
-        for m in reversed(z_far):
-            size = x.shape[0] // 2
-            x = fold(x[:size], swap(x[size:], m))
-        return x[0]
-
     def far_folds(x):
         for m in reversed(z_far):
             size = x.shape[0] // 2
@@ -847,7 +840,7 @@
         steps, square_flops // 2,
     )
     key_keep, key_send = square("key_outer", 0, normed_pair, key_out)
-    value_keep, value_send = square("value_outer", 2, normed_pair, value_out)
+    value_keep, value_send = square("value_outer", 1, normed_pair, value_out)
     key_send, value_send, gl_z, down_far, query_x, output_y = tie(
         key_send, value_send, gl_z, down_far, query_x, output_y
     )
@@ -871,22 +864,20 @@
         [wide_scratch] * 4 + [dma((4, members))],
         steps, 4 * square_flops,
     )
+    qmo_g = jnp.concatenate(
+        [fold(query_g[:quad], query_x), fold(output_g[:quad], output_y)], axis=1
+    )
+    qmo_z = swap(qmo_g[near:], z_near)
     key_y, value_x, near_rows = tie(key_y, value_x, near_rows)
     down_y = swap(down_g[1], y_mask)
     key_g, value_g = fold(key_keep, key_y), fold(value_keep, value_x)
-    key_x, value_z = swap(key_g[quad:], x_mask), swap(value_g[quad:], z_near)
-    qmo_g = jnp.concatenate(
-        [fold(query_g[:quad], query_x), fold(output_g[:quad], output_y)], axis=1
-    )
-    qmo_z = swap(qmo_g[near:], z_near)
-    key_x, value_z, down_y, qmo_z, gl_far = tie(key_x, value_z, down_y, qmo_z, gl_far)
+    key_x, value_y = swap(key_g[quad:], x_mask), swap(value_g[quad:], y_mask)
+    key_x, value_y, down_y, qmo_z, gl_far = tie(key_x, value_y, down_y, qmo_z, gl_far)
     gate_lift = final(gl_g[0], gl_far)
-    key_g, value_g = fold(key_g[:quad], key_x), fold(value_g[:quad], value_z)
-    key_z, value_far = swap(key_g[near:], z_near), far_pairs(value_g)
+    kv_g = jnp.concatenate([fold(key_g[:quad], key_x), fold(value_g[:quad], value_y)], axis=1)
+    kv_z = swap(kv_g[near:], z_near)
     qmo_g = far_folds(fold(qmo_g[:near], qmo_z))[0]
-    key_gradient = far_folds(fold(key_g[:near], key_z))[0][0]
-    value_y = swap(value_far[1], y_mask)
-    value_gradient = final(value_far[0], value_y)[0]
+    key_gradient, value_gradient = far_folds(fold(kv_g[:near], kv_z))[0]
     query_gradient, modulate_gradient, output_gradient = qmo_g
     down_gradient = final(down_g[0], down_y).T
     gate_gradient, lift_gradient = gate_lift[0].T, gate_lift[1].T

time: 374 us -> 366 us (0.979)
  waiting for transfers between devices: 153 us -> 149 us
    ppermute x70 -> x68, waiting for transfers between devices: 121 us -> 117 us  [exchange(): return lax.ppermute(x, AXES, [(i, i ^ mask) for i in range(count)])]
    ppermute x70 -> x68, starting transfers between devices: 62.5 us -> 59.5 us  [exchange(): return lax.ppermute(x, AXES, [(i, i ^ mask) for i in range(count)])]
  transfers between devices with their start and end apart: 74 -> 72, of which waited for: 40 -> 42; matrix products, arithmetic and copies ran while one was open for 13% -> 13% of each run, Pallas kernels for 14% -> 15%
where the time goes in v7:
time: 366 us; the launch traced here: 360 us
  waiting for transfers between devices  149 us (41%)
  Pallas kernels  82.8 us (23%)
  starting transfers between devices  66.6 us (18%)
  other arithmetic  27 us (7%)
  local copies, waits for them, and re-layouts  20.3 us (6%)
  matrix products  11 us (3%)
    ppermute x68, waiting for transfers between devices, exchange(): return lax.ppermute(x, AXES, [(i, i ^ mask) for i in range(count)])  117 us
    pallas_call x11, Pallas kernels, run(): pl.pallas_call(kernel, out_shape=[jax.ShapeDtypeStruct(s, d) for s, d, _...  82.8 us
    ppermute x68, starting transfers between devices, exchange(): return lax.ppermute(x, AXES, [(i, i ^ mask) for i in range(count)])  59.5 us
    ppermute x4, waiting for transfers between devices, shift_z(): return lax.ppermute(x, AXES, pairs)  31.9 us
    dot_general x3, matrix products, outer(): jnp.einsum('pblf,pbld->fd', a, b, preferred_element_type=F32).astype(BF16)  11 us
    unnamed x178, local copies, waits for them, and re-layouts  8.35 us
  transfers between devices with their start and end apart: 72, of which 42 were waited for; matrix products, arithmetic and copies ran while one was open for 13% of the time, Pallas kernels for 15%

profile of v7, /device:TPU:0, one launch (start us, length us, event | category | flops | bytes accessed | tf_op | source)
XLA Modules:
  0.0 359.8 jit_solution(15221265821225295590)
XLA Ops:
  29.1 4.3 %collective-permute-done.8 = bf16[4,1,128,256]{3,2,1,0:T(8,128)(2,1)S(1)} collective-permute-done((bf16[4,1,128,256]{3,2,1,0:T(8,128)(2,1)S(1)}, bf16[4,1,128,256]{3,2,1,0:T(8,128)(2,1)S(1)}, u32[]{:S(2)}, u32[]{:S(2)}) %collective-permute-start.8) | collective-permute-done | bytes 262176 | tf_op jit(solution)/shard_map/ppermute | solution.py:38
  37.7 7.9 %collective-permute-done.12 = bf16[1,3,128,256]{3,2,1,0:T(8,128)(2,1)S(1)} collective-permute-done((bf16[1,3,128,256]{3,2,1,0:T(8,128)(2,1)S(1)}, bf16[1,3,128,256]{3,2,1,0:T(8,128)(2,1)S(1)}, u32[]{:S(2)}, u32[]{:S(2)}) %collective-permute-start.12) | collective-permute-done | bytes 196640 | tf_op jit(solution)/shard_map/ppermute | solution.py:38
  46.8 6.0 %key_value.1 = (bf16[2,8,64,512]{3,2,1,0:T(8,128)(2,1)S(1)}, bf16[2,8,64,512]{3,2,1,0:T(8,128)(2,1)S(1)}, bf16[2,8,64,512]{3,2,1,0:T(8,128)(2,1)S(1)}, bf16[8,4,128,128]{3,2,1,0:T(8,128)(2,1)S(1)}) custom-call(s32[4,16,2]{2,1,0:T(8,128)S(1)} %add_add_fusion.spots, bf16[8,64,1024]{2,1,0:T(8,128)(2,1)S(1)} %copy-done.6, ...), custom_call_target="tpu_custom_call" | custom-call | flops 5153960960 | bytes 22649240 | tf_op jit(solution)/shard_map/key_value/pallas_call | solution.py:429
  64.0 4.0 %collective-permute-done.16 = bf16[2,4,128,128]{3,2,1,0:T(8,128)(2,1)S(1)} collective-permute-done((bf16[2,4,128,128]{3,2,1,0:T(8,128)(2,1)S(1)}, bf16[2,4,128,128]{3,2,1,0:T(8,128)(2,1)S(1)}, u32[]{:S(2)}, u32[]{:S(2)}) %collective-permute-start.16) | collective-permute-done | bytes 262176 | tf_op jit(solution)/shard_map/ppermute | solution.py:38
  73.4 3.6 collective-permute-done.19
  87.2 11.2 %collective-permute-done.21 = bf16[2,4,128,128]{3,2,1,0:T(8,128)(2,1)S(1)} collective-permute-done((bf16[2,4,128,128]{3,2,1,0:T(8,128)(2,1)S(1)}, bf16[2,4,128,128]{3,2,1,0:T(8,128)(2,1)S(1)}, u32[]{:S(2)}, u32[]{:S(2)}) %collective-permute-start.21) | collective-permute-done | bytes 262176 | tf_op jit(solution)/shard_map/ppermute | solution.py:50
  98.4 3.7 %collective-permute-done.25 = bf16[4,64,1024]{2,1,0:T(8,128)(2,1)S(1)} collective-permute-done((bf16[4,64,1024]{2,1,0:T(8,128)(2,1)S(1)}, bf16[4,64,1024]{2,1,0:T(8,128)(2,1)S(1)}, u32[]{:S(2)}, u32[]{:S(2)}) %collective-permute-start.25) | collective-permute-done | bytes 524320 | tf_op jit(solution)/shard_map/ppermute | solution.py:38
  109.2 7.1 %query.1 = (bf16[2,8,64,512]{3,2,1,0:T(8,128)(2,1)S(1)}, bf16[2,8,64,512]{3,2,1,0:T(8,128)(2,1)S(1)}, bf16[2,8,64,512]{3,2,1,0:T(8,128)(2,1)S(1)}, bf16[2,8,64,512]{3,2,1,0:T(8,128)(2,1)S(1)}) custom-call(s32[4,16,2]{2,1,0:T(8,128)S(1)} %add_add_fusion.spots, bf16[8,64,1024]{2,1,0:T(8,128)(2,1)S(1)} %copy-done.6, ...), custom_call_target="tpu_custom_call" | custom-call | flops 5153960960 | bytes 28940696 | tf_op jit(solution)/shard_map/query/pallas_call | solution.py:429
  117.7 4.9 %mixed.1 = (bf16[2,8,64,512]{3,2,1,0:T(8,128)(2,1)S(1)}, bf16[2,8,64,512]{3,2,1,0:T(8,128)(2,1)S(1)}, f32[8,64,1024]{2,1,0:T(8,128)S(1)}, bf16[8,64,1024]{2,1,0:T(8,128)(2,1)S(1)}) custom-call(s32[4,16,2]{2,1,0:T(8,128)S(1)} %add_add_fusion.spots, bf16[2,8,64,512]{3,2,1,0:T(8,128)(2,1)S(1)} %get-tuple-element.173.queries, ...), custom_call_target="tpu_custom_call" | custom-call | flops 2576980480 | bytes 26424116 | tf_op jit(solution)/shard_map/mixed/pallas_call | solution.py:429
  130.4 27.7 %collective-permute-done.32 = bf16[4,2,88,1024]{3,2,0,1:T(8,128)(2,1)S(1)} collective-permute-done((bf16[4,2,88,1024]{3,2,0,1:T(8,128)(2,1)S(1)}, bf16[4,2,88,1024]{3,2,0,1:T(8,128)(2,1)S(1)}, u32[]{:S(2)}, u32[]{:S(2)}) %collective-permute-start.32) | collective-permute-done | bytes 1441824 | tf_op jit(solution)/shard_map/ppermute | solution.py:38
  162.6 25.1 %hidden.1 = (bf16[4,8,64,704]{3,2,1,0:T(8,128)(2,1)}, bf16[4,8,64,704]{3,2,1,0:T(8,128)(2,1)}, bf16[4,8,64,704]{3,2,1,0:T(8,128)(2,1)}, bf16[2,8,64,1024]{3,2,1,...) custom-call(s32[4,16,2]{2,1,0:T(8,128)S(1)} %add_add_fusion.spots, ...), custom_call_target="tpu_custom_call" | custom-call | flops 42520174592 | bytes 72666320 | tf_op jit(solution)/shard_map/hidden/pallas_call | solution.py:429
  200.0 4.4 %bitcast_convert_fusion.1 = bf16[704,1024]{1,0:T(8,128)(2,1)} fusion(bf16[4,8,64,704]{3,2,1,0:T(8,128)(2,1)S(1)} %copy-done.82, bf16[1,8,64,1024]{3,2,1,0:T(8,128)(2,1)S(1)} %bitcast.189, bf16[1,8,64,1024]{3,2,1,0:T(8,128)(2,1)S(1)} %bitcast.187, bf16[1,8,64,1024]{3,2,1,0:T(8,128)(2,1)S(1)} %bitcast.184, bf16[1,8,64,1024]{3,2,1,0:T(8,128)(2,1)S(1)} %fusion.115), kind=kOutput, calls=%fused_computation.17 | convolution fusion | flops 2959802368 | bytes 8519680 | tf_op jit(solution)/shard_map/pblf,pbld->fd/dot_general | solution.py:724
  208.0 6.2 %collective-permute-done.41 = bf16[4,88,1024]{2,1,0:T(8,128)(2,1)S(1)} collective-permute-done((bf16[4,88,1024]{2,1,0:T(8,128)(2,1)S(1)}, bf16[4,88,1024]{2,1,0:T(8,128)(2,1)S(1)}, u32[]{:S(2)}, u32[]{:S(2)}) %collective-permute-start.41) | collective-permute-done | bytes 720928 | tf_op jit(solution)/shard_map/ppermute | solution.py:38
  214.2 3.7 %collective-permute-done.40 = bf16[8,64,1024]{2,1,0:T(8,128)(2,1)S(1)} collective-permute-done((bf16[8,64,1024]{2,1,0:T(8,128)(2,1)S(1)}, bf16[8,64,1024]{2,1,0:T(8,128)(2,1)S(1)}, u32[]{:S(2)}, u32[]{:S(2)}) %collective-permute-start.40) | collective-permute-done | bytes 1048608 | tf_op jit(solution)/shard_map/ppermute | solution.py:38
  228.8 12.6 %mixed_back.1 = (bf16[2,8,64,512]{3,2,1,0:T(8,128)(2,1)S(1)}, bf16[2,8,64,512]{3,2,1,0:T(8,128)(2,1)S(1)}, bf16[2,8,64,512]{3,2,1,0:T(8,128)(2,1)S(1)}, bf16[2,8...) custom-call(s32[4,16,2]{2,1,0:T(8,128)S(1)} %add_add_fusion.spots, ...), custom_call_target="tpu_custom_call" | custom-call | flops 5153960960 | bytes 45298484 | tf_op jit(solution)/shard_map/mixed_back/pallas_call | solution.py:429
  245.1 4.3 %query_outer.1 = (bf16[8,2,128,256]{3,2,1,0:T(8,128)(2,1)S(1)}, bf16[8,2,128,256]{3,2,1,0:T(8,128)(2,1)S(1)}) custom-call(s32[4,16,2]{2,1,0:T(8,128)S(1)} %add_add_fusion.spots, bf16[8,64,1024]{2,1,0:T(8,128)(2,1)S(1)} %copy-done.7, bf16[8,64,1024]{2,1,0:T(8,128)(2,1)S(1)} %copy-done.22, bf16[2,8,64,512]{3,2,1,0:T(8,128)(2,1)S(1)} %get-tuple-element.210.refs_0_.query_grad, ...), custom_call_target="tpu_custom_call" | custom-call | flops 5153960960 | bytes 15099494 | tf_op jit(solution)/shard_map/query_outer/pallas_call | solution.py:429
  249.5 4.0 %output_outer.1 = (bf16[8,1,128,256]{3,2,1,0:T(8,128)(2,1)S(1)}, bf16[8,1,128,256]{3,2,1,0:T(8,128)(2,1)S(1)}) custom-call(s32[4,16,2]{2,1,0:T(8,128)S(1)} %add_add_fusion.spots, bf16[8,64,1024]{2,1,0:T(8,128)(2,1)S(1)} %copy-done.10, bf16[8,64,1024]{2,1,0:T(8,128)(2,1)} %collective-permute-done.42.far, bf16[2,8,64,512]{3,2,1,0:T(8,128)(2,1)S(1)} %copy-done.38), custom_call_target="tpu_custom_call" | custom-call | flops 2576980480 | bytes 10066329 | tf_op jit(solution)/shard_map/output_outer/pallas_call | solution.py:429
  254.8 5.5 %collective-permute-done.46 = bf16[2,4,128,128]{3,2,1,0:T(8,128)(2,1)S(1)} collective-permute-done((bf16[2,4,128,128]{3,2,1,0:T(8,128)(2,1)S(1)}, bf16[2,4,128,128]{3,2,1,0:T(8,128)(2,1)S(1)}, u32[]{:S(2)}, u32[]{:S(2)}) %collective-permute-start.46) | collective-permute-done | bytes 262176 | tf_op jit(solution)/shard_map/ppermute | solution.py:38
  263.3 6.8 %collective-permute-done.49 = bf16[2,4,128,128]{3,2,1,0:T(8,128)(2,1)S(1)} collective-permute-done((bf16[2,4,128,128]{3,2,1,0:T(8,128)(2,1)S(1)}, bf16[2,4,128,128]{3,2,1,0:T(8,128)(2,1)S(1)}, u32[]{:S(2)}, u32[]{:S(2)}) %collective-permute-start.49) | collective-permute-done | bytes 262176 | tf_op jit(solution)/shard_map/ppermute | solution.py:50
  275.7 12.8 %collective-permute-done.51 = bf16[2,4,128,128]{3,2,1,0:T(8,128)(2,1)S(1)} collective-permute-done((bf16[2,4,128,128]{3,2,1,0:T(8,128)(2,1)S(1)}, bf16[2,4,128,128]{3,2,1,0:T(8,128)(2,1)S(1)}, u32[]{:S(2)}, u32[]{:S(2)}) %collective-permute-start.51) | collective-permute-done | bytes 262176 | tf_op jit(solution)/shard_map/ppermute | solution.py:50
  296.6 3.8 %collective-permute-done.54.g1 = bf16[2,4,128,128]{3,2,1,0:T(8,128)(2,1)S(1)} collective-permute-done((bf16[2,4,128,128]{3,2,1,0:T(8,128)(2,1)S(1)}, bf16[2,4,128,128]{3,2,1,0:T(8,128)(2,1)S(1)}, u32[]{:S(2)}, u32[]{:S(2)}) %collective-permute-start.54) | collective-permute-done | bytes 262176 | tf_op jit(solution)/shard_map/ppermute | solution.py:38
  306.3 4.7 %key_back.1 = (bf16[2,8,64,512]{3,2,1,0:T(8,128)(2,1)S(1)}, bf16[2,8,64,512]{3,2,1,0:T(8,128)(2,1)S(1)}) custom-call(s32[4,16,2]{2,1,0:T(8,128)S(1)} %add_add_fusion.spots, bf16[2,8,64,512]{3,2,1,0:T(8,128)(2,1)S(1)} %get-tuple-element.218.key_grad, bf16[2,8,64,512]{3,2,1,0:T(8,128)(2,1)S(1)} %get-tuple-element.219.value_grad, ...), custom_call_target="tpu_custom_call" | custom-call | flops 1288490240 | bytes 22649240 | tf_op jit(solution)/shard_map/key_back/pallas_call | solution.py:429
  323.0 8.5 %rows.1 = (f32[8,64,1024]{2,1,0:T(8,128)S(1)}, bf16[8,64,1024]{2,1,0:T(8,128)(2,1)S(1)}) custom-call(s32[4,16,2]{2,1,0:T(8,128)S(1)} %add_add_fusion.spots, bf16[2,8,64,512]{3,2,1,0:T(8,128)(2,1)S(1)} %get-tuple-element.210.refs_0_.query_grad, bf16[2,8,64,512]{3,2,1,0:T(8,128)(2,1)S(1)} %get-tuple-element.211.refs_1_.modulate_grad, ...), custom_call_target="tpu_custom_call" | custom-call | flops 10307921920 | bytes 27682406 | tf_op jit(solution)/shard_map/rows/pallas_call | solution.py:429
  344.7 4.6 %collective-permute-done.69 = bf16[1,3,128,256]{3,2,1,0:T(8,128)(2,1)S(1)} collective-permute-done((bf16[1,3,128,256]{3,2,1,0:T(8,128)(2,1)S(1)}, bf16[1,3,128,256]{3,2,1,0:T(8,128)(2,1)S(1)}, u32[]{:S(2)}, u32[]{:S(2)}) %collective-permute-start.69) | collective-permute-done | bytes 196640 | tf_op jit(solution)/shard_map/ppermute | solution.py:38
  (452 shorter events, 169.6 us)
Async XLA Ops:
  0.7 27.7 %collective-permute-start = (f32[2]{0:T(128)}, f32[2]{0:T(128)}, u32[]{:S(2)}, u32[]{:S(2)}) collective-permute-start(f32[2]{0:T(128)} %param.25), channel_id=1, source_target_pairs={{0,2},{1,3},{2,0},{3,1},{4,6},{5,7},{6,4},{7,5},{8,10},{9,11},{10,... | collective-permute-start | bytes 32 | tf_op jit(solution)/shard_map/ppermute | solution.py:38
  10.1 16.7 %collective-permute-start.7 = (bf16[4,64,1024]{2,1,0:T(8,128)(2,1)}, bf16[4,64,1024]{2,1,0:T(8,128)(2,1)}, u32[]{:S(2)}, u32[]{:S(2)}) collective-permute-start(bf16[4,64,1024]{2,1,0:T(8,128)(2,1)} %get-tuple-element.308), channel_id=1, source_target_pairs={{0,2},{1,3},{2,0},{3,1},{4,6},{5,7},{6,4},{7,5},{8,10},{9,11},{10,... | collective-permute-start | bytes 1572872 | tf_op jit(solution)/shard_map/ppermute | solution.py:38
  21.7 24.8 %collective-permute-start.1 = (bf16[8,64,1024]{2,1,0:T(8,128)(2,1)S(1)}, bf16[8,64,1024]{2,1,0:T(8,128)(2,1)S(1)}, u32[]{:S(2)}, u32[]{:S(2)}) collective-permute-start(bf16[8,64,1024]{2,1,0:T(8,128)(2,1)S(1)} %fusion.10.near), channel_id=1, source_target_pairs={{0,1},{1,0},{2,3},{3,2},{4,5},{5,4},{6,7},{7,6},{8,9},{9,8},{10,11... | collective-permute-start | bytes 3145736 | tf_op jit(solution)/shard_map/ppermute | solution.py:38
  77.2 24.9 %collective-permute-start.22 = (bf16[8,2,128,256]{3,2,1,0:T(8,128)(2,1)S(1)}, bf16[8,2,128,256]{3,2,1,0:T(8,128)(2,1)S(1)}, u32[]{:S(2)}, u32[]{:S(2)}) collective-permute-start(bf16[8,2,128,256]{3,2,1,0:T(8,128)(2,1)S(1)} %constant_dynamic-update-slice_fusion.3.w0), channel_id=1, source_target_pairs={{0,4},{1,5},{2,6},{3,7},{4,0},{5,1},{6,2},{7,3},{8,12},{9,13},{10,... | collective-permute-start | bytes 3145736 | tf_op jit(solution)/shard_map/ppermute | solution.py:38
  79.1 23.0 %collective-permute-start.24 = (bf16[2,2,88,1024]{3,2,1,0:T(8,128)(2,1)S(1)}, bf16[2,2,88,1024]{3,2,1,0:T(8,128)(2,1)S(1)}, u32[]{:S(2)}, u32[]{:S(2)}) collective-permute-start(bf16[2,2,88,1024]{3,2,1,0:T(8,128)(2,1)S(1)} %pad_maximum_fusion.5), channel_id=1, source_target_pairs={{0,8},{1,9},{2,10},{3,11},{4,12},{5,13},{6,14},{7,15},{8,0},{9,1},... | collective-permute-start | bytes 2162696 | tf_op jit(solution)/shard_map/ppermute | solution.py:38
  80.3 18.1 %collective-permute-start.23 = (bf16[8,1,128,256]{3,2,1,0:T(8,128)(2,1)S(1)}, bf16[8,1,128,256]{3,2,1,0:T(8,128)(2,1)S(1)}, u32[]{:S(2)}, u32[]{:S(2)}) collective-permute-start(bf16[8,1,128,256]{3,2,1,0:T(8,128)(2,1)S(1)} %constant_dynamic-update-slice_fusion.5.w0), channel_id=1, source_target_pairs={{0,2},{1,3},{2,0},{3,1},{4,6},{5,7},{6,4},{7,5},{8,10},{9,11},{10,... | collective-permute-start | bytes 1572872 | tf_op jit(solution)/shard_map/ppermute | solution.py:38
  82.6 19.5 %collective-permute-start.25 = (bf16[4,64,1024]{2,1,0:T(8,128)(2,1)S(1)}, bf16[4,64,1024]{2,1,0:T(8,128)(2,1)S(1)}, u32[]{:S(2)}, u32[]{:S(2)}) collective-permute-start(bf16[4,64,1024]{2,1,0:T(8,128)(2,1)S(1)} %copy-done.63), channel_id=1, source_target_pairs={{0,2},{1,3},{2,0},{3,1},{4,6},{5,7},{6,4},{7,5},{8,10},{9,11},{10,... | collective-permute-start | bytes 1572872 | tf_op jit(solution)/shard_map/ppermute | solution.py:38
  82.8 15.5 %collective-permute-start.21 = (bf16[2,4,128,128]{3,2,1,0:T(8,128)(2,1)S(1)}, bf16[2,4,128,128]{3,2,1,0:T(8,128)(2,1)S(1)}, u32[]{:S(2)}, u32[]{:S(2)}) collective-permute-start(bf16[2,4,128,128]{3,2,1,0:T(8,128)(2,1)S(1)} %fusion.40), channel_id=1, source_target_pairs={{0,16},{1,17},{2,18},{3,19},{4,20},{5,21},{6,22},{7,23},{8,24},{9,... | collective-permute-start | bytes 786440 | tf_op jit(solution)/shard_map/ppermute | solution.py:50
  123.7 35.7 %collective-permute-start.35 = (bf16[8,64,1024]{2,1,0:T(8,128)(2,1)S(1)}, bf16[8,64,1024]{2,1,0:T(8,128)(2,1)S(1)}, u32[]{:S(2)}, u32[]{:S(2)}) collective-permute-start(bf16[8,64,1024]{2,1,0:T(8,128)(2,1)S(1)} %copy-done), channel_id=1, source_target_pairs={{0,1},{1,0},{2,3},{3,2},{4,5},{5,4},{6,7},{7,6},{8,9},{9,8},{10,11... | collective-permute-start | bytes 3145736 | tf_op jit(solution)/shard_map/ppermute | solution.py:38
  124.7 33.4 %collective-permute-start.32 = (bf16[4,2,88,1024]{3,2,0,1:T(8,128)(2,1)S(1)}, bf16[4,2,88,1024]{3,2,0,1:T(8,128)(2,1)S(1)}, u32[]{:S(2)}, u32[]{:S(2)}) collective-permute-start(bf16[4,2,88,1024]{3,2,0,1:T(8,128)(2,1)S(1)} %copy.68), channel_id=1, source_target_pairs={{0,4},{1,5},{2,6},{3,7},{4,0},{5,1},{6,2},{7,3},{8,12},{9,13},{10,... | collective-permute-start | bytes 4325384 | tf_op jit(solution)/shard_map/ppermute | solution.py:38
  127.0 31.1 %collective-permute-start.31 = (bf16[8,64,1024]{2,1,0:T(8,128)(2,1)S(1)}, bf16[8,64,1024]{2,1,0:T(8,128)(2,1)S(1)}, u32[]{:S(2)}, u32[]{:S(2)}) collective-permute-start(bf16[8,64,1024]{2,1,0:T(8,128)(2,1)S(1)} %multiply_convert_fusion.1.n0), channel_id=1, source_target_pairs={{0,2},{1,3},{2,0},{3,1},{4,6},{5,7},{6,4},{7,5},{8,10},{9,11},{10,... | collective-permute-start | bytes 3145736 | tf_op jit(solution)/shard_map/ppermute | solution.py:38
  127.7 31.0 %collective-permute-start.37 = (bf16[4,88,1024]{2,1,0:T(8,128)(2,1)S(1)}, bf16[4,88,1024]{2,1,0:T(8,128)(2,1)S(1)}, u32[]{:S(2)}, u32[]{:S(2)}) collective-permute-start(bf16[4,88,1024]{2,1,0:T(8,128)(2,1)S(1)} %pad_maximum_fusion.6), channel_id=1, source_target_pairs={{0,8},{1,9},{2,10},{3,11},{4,12},{5,13},{6,14},{7,15},{8,0},{9,1},... | collective-permute-start | bytes 2162696 | tf_op jit(solution)/shard_map/ppermute | solution.py:38
  130.4 29.1 %collective-permute-start.36 = (bf16[8,64,1024]{2,1,0:T(8,128)(2,1)S(1)}, bf16[8,64,1024]{2,1,0:T(8,128)(2,1)S(1)}, u32[]{:S(2)}, u32[]{:S(2)}) collective-permute-start(bf16[8,64,1024]{2,1,0:T(8,128)(2,1)S(1)} %constant_dynamic-update-slice_fusion.10.b1), channel_id=1, source_target_pairs={{0,1},{1,0},{2,3},{3,2},{4,5},{5,4},{6,7},{7,6},{8,9},{9,8},{10,11... | collective-permute-start | bytes 3145736 | tf_op jit(solution)/shard_map/ppermute | solution.py:38
  188.2 18.1 %collective-permute-start.38 = (bf16[2,8,64,1024]{3,2,1,0:T(8,128)(2,1)}, bf16[2,8,64,1024]{3,2,1,0:T(8,128)(2,1)S(1)}, u32[]{:S(2)}, u32[]{:S(2)}) collective-permute-start(bf16[2,8,64,1024]{3,2,1,0:T(8,128)(2,1)} %get-tuple-element.189), channel_id=1, source_target_pairs={{0,1},{1,0},{2,3},{3,2},{4,5},{5,4},{6,7},{7,6},{8,9},{9,8},{10,11... | collective-permute-start | bytes 6291464 | tf_op jit(solution)/shard_map/ppermute | solution.py:38
  192.6 25.3 %collective-permute-start.40 = (bf16[8,64,1024]{2,1,0:T(8,128)(2,1)S(1)}, bf16[8,64,1024]{2,1,0:T(8,128)(2,1)S(1)}, u32[]{:S(2)}, u32[]{:S(2)}) collective-permute-start(bf16[8,64,1024]{2,1,0:T(8,128)(2,1)S(1)} %fusion.32), channel_id=1, source_target_pairs={{0,2},{1,3},{2,0},{3,1},{4,6},{5,7},{6,4},{7,5},{8,10},{9,11},{10,... | collective-permute-start | bytes 3145736 | tf_op jit(solution)/shard_map/ppermute | solution.py:38
  196.2 18.0 %collective-permute-start.41 = (bf16[4,88,1024]{2,1,0:T(8,128)(2,1)S(1)}, bf16[4,88,1024]{2,1,0:T(8,128)(2,1)S(1)}, u32[]{:S(2)}, u32[]{:S(2)}) collective-permute-start(bf16[4,88,1024]{2,1,0:T(8,128)(2,1)S(1)} %bitcast.196), channel_id=1, source_target_pairs={{0,4},{1,5},{2,6},{3,7},{4,0},{5,1},{6,2},{7,3},{8,12},{9,13},{10,... | collective-permute-start | bytes 2162696 | tf_op jit(solution)/shard_map/ppermute | solution.py:38
  222.2 19.2 %collective-permute-start.43 = (bf16[4,88,1024]{2,1,0:T(8,128)(2,1)S(1)}, bf16[4,88,1024]{2,1,0:T(8,128)(2,1)S(1)}, u32[]{:S(2)}, u32[]{:S(2)}) collective-permute-start(bf16[4,88,1024]{2,1,0:T(8,128)(2,1)S(1)} %slice_bitcast_fusion.2), channel_id=1, source_target_pairs={{0,4},{1,5},{2,6},{3,7},{4,0},{5,1},{6,2},{7,3},{8,12},{9,13},{10,... | collective-permute-start | bytes 2162696 | tf_op jit(solution)/shard_map/ppermute | solution.py:38
  222.9 30.7 %collective-permute-start.48 = (bf16[8,64,1024]{2,1,0:T(8,128)(2,1)}, bf16[8,64,1024]{2,1,0:T(8,128)(2,1)S(1)}, u32[]{:S(2)}, u32[]{:S(2)}) collective-permute-start(bf16[8,64,1024]{2,1,0:T(8,128)(2,1)} %fusion.33), channel_id=1, source_target_pairs={{0,2},{1,3},{2,0},{3,1},{4,6},{5,7},{6,4},{7,5},{8,10},{9,11},{10,... | collective-permute-start | bytes 3145736 | tf_op jit(solution)/shard_map/ppermute | solution.py:38
  223.2 30.4 %collective-permute-start.47 = (bf16[2,2,88,1024]{3,2,0,1:T(8,128)(2,1)}, bf16[2,2,88,1024]{3,2,0,1:T(8,128)(2,1)S(1)}, u32[]{:S(2)}, u32[]{:S(2)}) collective-permute-start(bf16[2,2,88,1024]{3,2,0,1:T(8,128)(2,1)} %bitcast.195), channel_id=1, source_target_pairs={{0,8},{1,9},{2,10},{3,11},{4,12},{5,13},{6,14},{7,15},{8,0},{9,1},... | collective-permute-start | bytes 2162696 | tf_op jit(solution)/shard_map/ppermute | solution.py:38
  293.3 24.1 %collective-permute-start.57 = (bf16[2,2,88,1024]{3,2,1,0:T(8,128)(2,1)S(1)}, bf16[2,2,88,1024]{3,2,1,0:T(8,128)(2,1)S(1)}, u32[]{:S(2)}, u32[]{:S(2)}) collective-permute-start(bf16[2,2,88,1024]{3,2,1,0:T(8,128)(2,1)S(1)} %slice.184), channel_id=1, source_target_pairs={{0,8},{1,9},{2,10},{3,11},{4,12},{5,13},{6,14},{7,15},{8,0},{9,1},... | collective-permute-start | bytes 2162696 | tf_op jit(solution)/shard_map/ppermute | solution.py:38
  293.4 23.2 %collective-permute-start.58 = (bf16[2,88,1024]{2,1,0:T(8,128)(2,1)S(1)}, bf16[2,88,1024]{2,1,0:T(8,128)(2,1)S(1)}, u32[]{:S(2)}, u32[]{:S(2)}) collective-permute-start(bf16[2,88,1024]{2,1,0:T(8,128)(2,1)S(1)} %slice_bitcast_fusion.9), channel_id=1, source_target_pairs={{0,16},{1,17},{2,18},{3,19},{4,20},{5,21},{6,22},{7,23},{8,24},{9,... | collective-permute-start | bytes 1081352 | tf_op jit(solution)/shard_map/ppermute | solution.py:38
  319.4 16.7 %collective-permute-start.68 = (bf16[2,88,1024]{2,1,0:T(8,128)(2,1)S(1)}, bf16[2,88,1024]{2,1,0:T(8,128)(2,1)S(1)}, u32[]{:S(2)}, u32[]{:S(2)}) collective-permute-start(bf16[2,88,1024]{2,1,0:T(8,128)(2,1)S(1)} %slice_bitcast_fusion.8), channel_id=1, source_target_pairs={{0,16},{1,17},{2,18},{3,19},{4,20},{5,21},{6,22},{7,23},{8,24},{9,... | collective-permute-start | bytes 1081352 | tf_op jit(solution)/shard_map/ppermute | solution.py:38
  321.1 16.0 %collective-permute-start.67 = (bf16[2,3,128,256]{3,2,1,0:T(8,128)(2,1)S(1)}, bf16[2,3,128,256]{3,2,1,0:T(8,128)(2,1)S(1)}, u32[]{:S(2)}, u32[]{:S(2)}) collective-permute-start(bf16[2,3,128,256]{3,2,1,0:T(8,128)(2,1)S(1)} %pad_maximum_fusion.9), channel_id=1, source_target_pairs={{0,8},{1,9},{2,10},{3,11},{4,12},{5,13},{6,14},{7,15},{8,0},{9,1},... | collective-permute-start | bytes 1179656 | tf_op jit(solution)/shard_map/ppermute | solution.py:38
  336.2 17.5 %collective-permute-start.63 = (bf16[8,64,1024]{2,1,0:T(8,128)(2,1)S(1)}, bf16[8,64,1024]{2,1,0:T(8,128)(2,1)S(1)}, u32[]{:S(2)}, u32[]{:S(2)}) collective-permute-start(bf16[8,64,1024]{2,1,0:T(8,128)(2,1)S(1)} %get-tuple-element.258), channel_id=1, source_target_pairs={{0,1},{1,0},{2,3},{3,2},{4,5},{5,4},{6,7},{7,6},{8,9},{9,8},{10,11... | collective-permute-start | bytes 3145736 | tf_op jit(solution)/shard_map/ppermute | solution.py:38
  (133 other events, 1299.0 us)

commit v8 on v7

--- a/solution.py
+++ b/solution.py
@@ -436,7 +436,7 @@
             out_specs=[spec(s, kind) for s, _, kind in outputs],
             scratch_shapes=scratch,
         ),
-        compiler_params=pltpu.CompilerParams(vmem_limit_bytes=40 * 2**20),
+        compiler_params=pltpu.CompilerParams(vmem_limit_bytes=(48 if name == "mixed_back" else 40) * 2**20),
         cost_estimate=pl.CostEstimate(flops=int(flops * 2.4), bytes_accessed=int(moved * 2.4), transcendentals=0),
         name=name,
     )(spots, *[a for a, _ in inputs])
@@ -747,10 +747,10 @@
     lift_g = outer(lift_grad, normed_two).reshape(2, bulk, -1, width)
     down_g = outer(inner, branch_rows).reshape(2, 2, bulk // 2, -1, width)
     branch_mine, branch_send = core_part(branch_keep, branch_send)
-    row_got, gate_y, lift_g, down_z_send, branch_send = tie(
-        row_got, gate_y, lift_g, down_g[:, 1], branch_send
-    )
-    lift_y = swap(lift_g[1], y_mask)
+    row_got, gate_y, lift_send, down_z_send, branch_send = tie(
+        row_got, gate_y, lift_g[1], down_g[:, 1], branch_send
+    )
+    lift_y = swap(lift_send, y_mask)
     branch_got = swap(branch_send, x_mask)
     down_z = swap(down_z_send, z_near)
     middle_grad = cotangent + norm_backward(middle, row_mine + row_got.astype(F32))
@@ -790,8 +790,8 @@
 
     output_keep, output_send = square("output_outer", 1, attended_pair, gated)
     query_keep, query_send = square("query_outer", 0, normed_pair, query_grad, modulate_grad)
-    *scan.got, down_z, branch_got, query_keep, query_send, output_keep, output_send = tie(
-        *scan.got, down_z, branch_got, query_keep, query_send, output_keep, output_send
+    *scan.got, gate_y, down_z, branch_got, query_keep, query_send, output_keep, output_send = tie(
+        *scan.got, gate_y, down_z, branch_got, query_keep, query_send, output_keep, output_send
     )
     layer_output = (middle + mask_rows * (branch_mine + branch_got.astype(F32))).astype(BF16)
     down_g = jnp.moveaxis(fold(down_g[:, 0], down_z), 1, 0)

time: 366 us -> 361 us (0.986)
  waiting for transfers between devices: 149 us -> 139 us
  starting transfers between devices: 66.6 us -> 73 us
  other arithmetic: 27 us -> 23.3 us
    ppermute x68, waiting for transfers between devices: 117 us -> 107 us  [exchange(): return lax.ppermute(x, AXES, [(i, i ^ mask) for i in range(count)])]
    ppermute x68, starting transfers between devices: 59.5 us -> 64.6 us  [exchange(): return lax.ppermute(x, AXES, [(i, i ^ mask) for i in range(count)])]
  transfers between devices with their start and end apart: 72 -> 72, of which waited for: 42 -> 34; matrix products, arithmetic and copies ran while one was open for 13% -> 12% of each run, Pallas kernels for 15% -> 15%
where the time goes in v8:
time: 361 us; the launch traced here: 355 us
  waiting for transfers between devices  139 us (39%)
  Pallas kernels  83.8 us (23%)
  starting transfers between devices  73 us (20%)
  other arithmetic  23.3 us (6%)
  local copies, waits for them, and re-layouts  22.7 us (6%)
  matrix products  9.68 us (3%)
    ppermute x68, waiting for transfers between devices, exchange(): return lax.ppermute(x, AXES, [(i, i ^ mask) for i in range(count)])  107 us
    pallas_call x11, Pallas kernels, run(): pl.pallas_call(kernel, out_shape=[jax.ShapeDtypeStruct(s, d) for s, d, _...  83.8 us
    ppermute x68, starting transfers between devices, exchange(): return lax.ppermute(x, AXES, [(i, i ^ mask) for i in range(count)])  64.6 us
    ppermute x4, waiting for transfers between devices, shift_z(): return lax.ppermute(x, AXES, pairs)  32.3 us
    unnamed x178, local copies, waits for them, and re-layouts  11.5 us
    dot_general x3, matrix products, outer(): jnp.einsum('pblf,pbld->fd', a, b, preferred_element_type=F32).astype(BF16)  9.68 us
    ppermute x4, starting transfers between devices, shift_z(): return lax.ppermute(x, AXES, pairs)  8.47 us
  transfers between devices with their start and end apart: 72, of which 34 were waited for; matrix products, arithmetic and copies ran while one was open for 12% of the time, Pallas kernels for 15%

profile of v8, /device:TPU:0, one launch (start us, length us, event | category | flops | bytes accessed | tf_op | source)
XLA Modules:
  0.0 354.7 jit_solution(14713875803814729829)
XLA Ops:
  26.2 3.9 %collective-permute-done.8 = bf16[4,1,128,256]{3,2,1,0:T(8,128)(2,1)S(1)} collective-permute-done((bf16[4,1,128,256]{3,2,1,0:T(8,128)(2,1)S(1)}, bf16[4,1,128,256]{3,2,1,0:T(8,128)(2,1)S(1)}, u32[]{:S(2)}, u32[]{:S(2)}) %collective-permute-start.8) | collective-permute-done | bytes 262176 | tf_op jit(solution)/shard_map/ppermute | solution.py:38
  34.3 8.3 %collective-permute-done.12 = bf16[1,3,128,256]{3,2,1,0:T(8,128)(2,1)S(1)} collective-permute-done((bf16[1,3,128,256]{3,2,1,0:T(8,128)(2,1)S(1)}, bf16[1,3,128,256]{3,2,1,0:T(8,128)(2,1)S(1)}, u32[]{:S(2)}, u32[]{:S(2)}) %collective-permute-start.12) | collective-permute-done | bytes 196640 | tf_op jit(solution)/shard_map/ppermute | solution.py:38
  43.6 6.0 %key_value.1 = (bf16[2,8,64,512]{3,2,1,0:T(8,128)(2,1)S(1)}, bf16[2,8,64,512]{3,2,1,0:T(8,128)(2,1)S(1)}, bf16[2,8,64,512]{3,2,1,0:T(8,128)(2,1)S(1)}, bf16[8,4,128,128]{3,2,1,0:T(8,128)(2,1)S(1)}) custom-call(s32[4,16,2]{2,1,0:T(8,128)S(1)} %add_add_fusion.spots, bf16[8,64,1024]{2,1,0:T(8,128)(2,1)S(1)} %copy-done.8, ...), custom_call_target="tpu_custom_call" | custom-call | flops 5153960960 | bytes 22649240 | tf_op jit(solution)/shard_map/key_value/pallas_call | solution.py:429
  57.7 4.5 %collective-permute-done.15 = bf16[2,4,128,128]{3,2,1,0:T(8,128)(2,1)S(1)} collective-permute-done((bf16[2,4,128,128]{3,2,1,0:T(8,128)(2,1)S(1)}, bf16[2,4,128,128]{3,2,1,0:T(8,128)(2,1)S(1)}, u32[]{:S(2)}, u32[]{:S(2)}) %collective-permute-start.15) | collective-permute-done | bytes 262176 | tf_op jit(solution)/shard_map/ppermute | solution.py:38
  63.7 4.1 %collective-permute-start.17 = (bf16[2,4,128,128]{3,2,1,0:T(8,128)(2,1)S(1)}, bf16[2,4,128,128]{3,2,1,0:T(8,128)(2,1)S(1)}, u32[]{:S(2)}, u32[]{:S(2)}) collective-permute-start(bf16[2,4,128,128]{3,2,1,0:T(8,128)(2,1)S(1)} %get-tuple-element.282), channel_id=1, source_target_pairs={{0,8},{1,9},{2,10},{3,11},{4,12},{5,13},{6,14},{7,15},{8,16},{9,17... | collective-permute-start | bytes 786440 | tf_op jit(solution)/shard_map/ppermute | solution.py:50
  68.1 3.5 collective-permute-done.17
  71.7 5.5 %collective-permute-done.19 = bf16[4,1,128,256]{3,2,1,0:T(8,128)(2,1)S(1)} collective-permute-done((bf16[4,1,128,256]{3,2,1,0:T(8,128)(2,1)S(1)}, bf16[4,1,128,256]{3,2,1,0:T(8,128)(2,1)S(1)}, u32[]{:S(2)}, u32[]{:S(2)}) %collective-permute-start.19) | collective-permute-done | bytes 262176 | tf_op jit(solution)/shard_map/ppermute | solution.py:38
  83.0 10.4 %collective-permute-done.21 = bf16[2,4,128,128]{3,2,1,0:T(8,128)(2,1)S(1)} collective-permute-done((bf16[2,4,128,128]{3,2,1,0:T(8,128)(2,1)S(1)}, bf16[2,4,128,128]{3,2,1,0:T(8,128)(2,1)S(1)}, u32[]{:S(2)}, u32[]{:S(2)}) %collective-permute-start.21) | collective-permute-done | bytes 262176 | tf_op jit(solution)/shard_map/ppermute | solution.py:50
  93.4 3.7 %collective-permute-done.25 = bf16[4,64,1024]{2,1,0:T(8,128)(2,1)S(1)} collective-permute-done((bf16[4,64,1024]{2,1,0:T(8,128)(2,1)S(1)}, bf16[4,64,1024]{2,1,0:T(8,128)(2,1)S(1)}, u32[]{:S(2)}, u32[]{:S(2)}) %collective-permute-start.25) | collective-permute-done | bytes 524320 | tf_op jit(solution)/shard_map/ppermute | solution.py:38
  105.2 7.1 %query.1 = (bf16[2,8,64,512]{3,2,1,0:T(8,128)(2,1)S(1)}, bf16[2,8,64,512]{3,2,1,0:T(8,128)(2,1)S(1)}, bf16[2,8,64,512]{3,2,1,0:T(8,128)(2,1)S(1)}, bf16[2,8,64,512]{3,2,1,0:T(8,128)(2,1)S(1)}) custom-call(s32[4,16,2]{2,1,0:T(8,128)S(1)} %add_add_fusion.spots, bf16[8,64,1024]{2,1,0:T(8,128)(2,1)S(1)} %copy-done.8, ...), custom_call_target="tpu_custom_call" | custom-call | flops 5153960960 | bytes 28940696 | tf_op jit(solution)/shard_map/query/pallas_call | solution.py:429
  113.5 4.9 %mixed.1 = (bf16[2,8,64,512]{3,2,1,0:T(8,128)(2,1)S(1)}, bf16[2,8,64,512]{3,2,1,0:T(8,128)(2,1)S(1)}, f32[8,64,1024]{2,1,0:T(8,128)S(1)}, bf16[8,64,1024]{2,1,0:T(8,128)(2,1)S(1)}) custom-call(s32[4,16,2]{2,1,0:T(8,128)S(1)} %add_add_fusion.spots, bf16[2,8,64,512]{3,2,1,0:T(8,128)(2,1)S(1)} %get-tuple-element.174.queries, ...), custom_call_target="tpu_custom_call" | custom-call | flops 2576980480 | bytes 26424116 | tf_op jit(solution)/shard_map/mixed/pallas_call | solution.py:429
  127.2 26.6 %collective-permute-done.32 = bf16[4,2,88,1024]{3,2,0,1:T(8,128)(2,1)S(1)} collective-permute-done((bf16[4,2,88,1024]{3,2,0,1:T(8,128)(2,1)S(1)}, bf16[4,2,88,1024]{3,2,0,1:T(8,128)(2,1)S(1)}, u32[]{:S(2)}, u32[]{:S(2)}) %collective-permute-start.32) | collective-permute-done | bytes 1441824 | tf_op jit(solution)/shard_map/ppermute | solution.py:38
  158.4 25.1 %hidden.1 = (bf16[4,8,64,704]{3,2,1,0:T(8,128)(2,1)}, bf16[4,8,64,704]{3,2,1,0:T(8,128)(2,1)}, bf16[4,8,64,704]{3,2,1,0:T(8,128)(2,1)}, bf16[2,8,64,1024]{3,2,1,...) custom-call(s32[4,16,2]{2,1,0:T(8,128)S(1)} %add_add_fusion.spots, ...), custom_call_target="tpu_custom_call" | custom-call | flops 42520174592 | bytes 72666320 | tf_op jit(solution)/shard_map/hidden/pallas_call | solution.py:429
  184.4 3.5 collective-permute-done.39
  204.6 8.6 %collective-permute-done.41 = bf16[4,88,1024]{2,1,0:T(8,128)(2,1)S(1)} collective-permute-done((bf16[4,88,1024]{2,1,0:T(8,128)(2,1)S(1)}, bf16[4,88,1024]{2,1,0:T(8,128)(2,1)S(1)}, u32[]{:S(2)}, u32[]{:S(2)}) %collective-permute-start.41) | collective-permute-done | bytes 720928 | tf_op jit(solution)/shard_map/ppermute | solution.py:38
  227.0 13.5 %mixed_back.1 = (bf16[2,8,64,512]{3,2,1,0:T(8,128)(2,1)S(1)}, bf16[2,8,64,512]{3,2,1,0:T(8,128)(2,1)S(1)}, bf16[2,8,64,512]{3,2,1,0:T(8,128)(2,1)}, bf16[2,8,64,...) custom-call(s32[4,16,2]{2,1,0:T(8,128)S(1)} %add_add_fusion.spots, bf16[8,64,1024]{2,1,0:T(8,128)(2,1)} %copy-done.11, ...), custom_call_target="tpu_custom_call" | custom-call | flops 5153960960 | bytes 45298484 | tf_op jit(solution)/shard_map/mixed_back/pallas_call | solution.py:429
  245.6 4.0 %output_outer.1 = (bf16[8,1,128,256]{3,2,1,0:T(8,128)(2,1)S(1)}, bf16[8,1,128,256]{3,2,1,0:T(8,128)(2,1)S(1)}) custom-call(s32[4,16,2]{2,1,0:T(8,128)S(1)} %add_add_fusion.spots, bf16[8,64,1024]{2,1,0:T(8,128)(2,1)S(1)} %copy-done.12, bf16[8,64,1024]{2,1,0:T(8,128)(2,1)} %collective-permute-done.42.far, bf16[2,8,64,512]{3,2,1,0:T(8,128)(2,1)S(1)} %copy-done.40), custom_call_target="tpu_custom_call" | custom-call | flops 2576980480 | bytes 10066329 | tf_op jit(solution)/shard_map/output_outer/pallas_call | solution.py:429
  249.6 4.3 %query_outer.1 = (bf16[8,2,128,256]{3,2,1,0:T(8,128)(2,1)S(1)}, bf16[8,2,128,256]{3,2,1,0:T(8,128)(2,1)S(1)}) custom-call(s32[4,16,2]{2,1,0:T(8,128)S(1)} %add_add_fusion.spots, bf16[8,64,1024]{2,1,0:T(8,128)(2,1)S(1)} %copy-done.9, bf16[8,64,1024]{2,1,0:T(8,128)(2,1)S(1)} %copy-done.24, bf16[2,8,64,512]{3,2,1,0:T(8,128)(2,1)S(1)} %get-tuple-element.212.refs_0_.query_grad, ...), custom_call_target="tpu_custom_call" | custom-call | flops 5153960960 | bytes 15099494 | tf_op jit(solution)/shard_map/query_outer/pallas_call | solution.py:429
  260.2 5.9 %collective-permute-done.49 = bf16[2,4,128,128]{3,2,1,0:T(8,128)(2,1)S(1)} collective-permute-done((bf16[2,4,128,128]{3,2,1,0:T(8,128)(2,1)S(1)}, bf16[2,4,128,128]{3,2,1,0:T(8,128)(2,1)S(1)}, u32[]{:S(2)}, u32[]{:S(2)}) %collective-permute-start.49) | collective-permute-done | bytes 262176 | tf_op jit(solution)/shard_map/ppermute | solution.py:50
  271.5 12.4 %collective-permute-done.51 = bf16[2,4,128,128]{3,2,1,0:T(8,128)(2,1)S(1)} collective-permute-done((bf16[2,4,128,128]{3,2,1,0:T(8,128)(2,1)S(1)}, bf16[2,4,128,128]{3,2,1,0:T(8,128)(2,1)S(1)}, u32[]{:S(2)}, u32[]{:S(2)}) %collective-permute-start.51) | collective-permute-done | bytes 262176 | tf_op jit(solution)/shard_map/ppermute | solution.py:50
  294.6 4.0 %collective-permute-done.56.g3 = bf16[2,4,128,128]{3,2,1,0:T(8,128)(2,1)S(1)} collective-permute-done((bf16[2,4,128,128]{3,2,1,0:T(8,128)(2,1)S(1)}, bf16[2,4,128,128]{3,2,1,0:T(8,128)(2,1)S(1)}, u32[]{:S(2)}, u32[]{:S(2)}) %collective-permute-start.56) | collective-permute-done | bytes 262176 | tf_op jit(solution)/shard_map/ppermute | solution.py:38
  300.9 4.7 %key_back.1 = (bf16[2,8,64,512]{3,2,1,0:T(8,128)(2,1)S(1)}, bf16[2,8,64,512]{3,2,1,0:T(8,128)(2,1)S(1)}) custom-call(s32[4,16,2]{2,1,0:T(8,128)S(1)} %add_add_fusion.spots, bf16[2,8,64,512]{3,2,1,0:T(8,128)(2,1)S(1)} %copy-done.5, bf16[2,8,64,512]{3,2,1,0:T(8,128)(2,1)S(1)} %copy-done.6, bf16[2,8,64,512]{3,2,1,0:T(8,128)(2,1)S(1)} %copy-done.2, ...), custom_call_target="tpu_custom_call" | custom-call | flops 1288490240 | bytes 22649240 | tf_op jit(solution)/shard_map/key_back/pallas_call | solution.py:429
  317.3 8.5 %rows.1 = (f32[8,64,1024]{2,1,0:T(8,128)S(1)}, bf16[8,64,1024]{2,1,0:T(8,128)(2,1)S(1)}) custom-call(s32[4,16,2]{2,1,0:T(8,128)S(1)} %add_add_fusion.spots, bf16[2,8,64,512]{3,2,1,0:T(8,128)(2,1)S(1)} %get-tuple-element.212.refs_0_.query_grad, bf16[2,8,64,512]{3,2,1,0:T(8,128)(2,1)S(1)} %get-tuple-element.213.refs_1_.modulate_grad, ...), custom_call_target="tpu_custom_call" | custom-call | flops 10307921920 | bytes 27682406 | tf_op jit(solution)/shard_map/rows/pallas_call | solution.py:429
  339.3 4.5 %collective-permute-done.69 = bf16[1,3,128,256]{3,2,1,0:T(8,128)(2,1)S(1)} collective-permute-done((bf16[1,3,128,256]{3,2,1,0:T(8,128)(2,1)S(1)}, bf16[1,3,128,256]{3,2,1,0:T(8,128)(2,1)S(1)}, u32[]{:S(2)}, u32[]{:S(2)}) %collective-permute-start.69) | collective-permute-done | bytes 196640 | tf_op jit(solution)/shard_map/ppermute | solution.py:38
  (452 shorter events, 164.0 us)
Async XLA Ops:
  0.7 24.8 %collective-permute-start = (f32[2]{0:T(128)}, f32[2]{0:T(128)}, u32[]{:S(2)}, u32[]{:S(2)}) collective-permute-start(f32[2]{0:T(128)} %param.25), channel_id=1, source_target_pairs={{0,2},{1,3},{2,0},{3,1},{4,6},{5,7},{6,4},{7,5},{8,10},{9,11},{10,... | collective-permute-start | bytes 32 | tf_op jit(solution)/shard_map/ppermute | solution.py:38
  17.3 25.9 %collective-permute-start.1 = (bf16[8,64,1024]{2,1,0:T(8,128)(2,1)S(1)}, bf16[8,64,1024]{2,1,0:T(8,128)(2,1)S(1)}, u32[]{:S(2)}, u32[]{:S(2)}) collective-permute-start(bf16[8,64,1024]{2,1,0:T(8,128)(2,1)S(1)} %fusion.10.near), channel_id=1, source_target_pairs={{0,1},{1,0},{2,3},{3,2},{4,5},{5,4},{6,7},{7,6},{8,9},{9,8},{10,11... | collective-permute-start | bytes 3145736 | tf_op jit(solution)/shard_map/ppermute | solution.py:38
  77.2 20.0 %collective-permute-start.22 = (bf16[8,2,128,256]{3,2,1,0:T(8,128)(2,1)S(1)}, bf16[8,2,128,256]{3,2,1,0:T(8,128)(2,1)S(1)}, u32[]{:S(2)}, u32[]{:S(2)}) collective-permute-start(bf16[8,2,128,256]{3,2,1,0:T(8,128)(2,1)S(1)} %constant_dynamic-update-slice_fusion.3.w0), channel_id=1, source_target_pairs={{0,4},{1,5},{2,6},{3,7},{4,0},{5,1},{6,2},{7,3},{8,12},{9,13},{10,... | collective-permute-start | bytes 3145736 | tf_op jit(solution)/shard_map/ppermute | solution.py:38
  78.8 18.4 %collective-permute-start.24 = (bf16[2,2,88,1024]{3,2,1,0:T(8,128)(2,1)S(1)}, bf16[2,2,88,1024]{3,2,1,0:T(8,128)(2,1)S(1)}, u32[]{:S(2)}, u32[]{:S(2)}) collective-permute-start(bf16[2,2,88,1024]{3,2,1,0:T(8,128)(2,1)S(1)} %pad_maximum_fusion.5), channel_id=1, source_target_pairs={{0,8},{1,9},{2,10},{3,11},{4,12},{5,13},{6,14},{7,15},{8,0},{9,1},... | collective-permute-start | bytes 2162696 | tf_op jit(solution)/shard_map/ppermute | solution.py:38
  79.2 17.9 %collective-permute-start.25 = (bf16[4,64,1024]{2,1,0:T(8,128)(2,1)S(1)}, bf16[4,64,1024]{2,1,0:T(8,128)(2,1)S(1)}, u32[]{:S(2)}, u32[]{:S(2)}) collective-permute-start(bf16[4,64,1024]{2,1,0:T(8,128)(2,1)S(1)} %copy-done.64), channel_id=1, source_target_pairs={{0,2},{1,3},{2,0},{3,1},{4,6},{5,7},{6,4},{7,5},{8,10},{9,11},{10,... | collective-permute-start | bytes 1572872 | tf_op jit(solution)/shard_map/ppermute | solution.py:38
  97.2 16.2 %collective-permute-start.29 = (bf16[2,88,1024]{2,1,0:T(8,128)(2,1)S(1)}, bf16[2,88,1024]{2,1,0:T(8,128)(2,1)S(1)}, u32[]{:S(2)}, u32[]{:S(2)}) collective-permute-start(bf16[2,88,1024]{2,1,0:T(8,128)(2,1)S(1)} %pad_maximum_fusion.11), channel_id=1, source_target_pairs={{0,16},{1,17},{2,18},{3,19},{4,20},{5,21},{6,22},{7,23},{8,24},{9,... | collective-permute-start | bytes 1081352 | tf_op jit(solution)/shard_map/ppermute | solution.py:38
  119.5 35.7 %collective-permute-start.35 = (bf16[8,64,1024]{2,1,0:T(8,128)(2,1)S(1)}, bf16[8,64,1024]{2,1,0:T(8,128)(2,1)S(1)}, u32[]{:S(2)}, u32[]{:S(2)}) collective-permute-start(bf16[8,64,1024]{2,1,0:T(8,128)(2,1)S(1)} %copy-done), channel_id=1, source_target_pairs={{0,1},{1,0},{2,3},{3,2},{4,5},{5,4},{6,7},{7,6},{8,9},{9,8},{10,11... | collective-permute-start | bytes 3145736 | tf_op jit(solution)/shard_map/ppermute | solution.py:38
  120.4 33.4 %collective-permute-start.32 = (bf16[4,2,88,1024]{3,2,0,1:T(8,128)(2,1)S(1)}, bf16[4,2,88,1024]{3,2,0,1:T(8,128)(2,1)S(1)}, u32[]{:S(2)}, u32[]{:S(2)}) collective-permute-start(bf16[4,2,88,1024]{3,2,0,1:T(8,128)(2,1)S(1)} %copy.68), channel_id=1, source_target_pairs={{0,4},{1,5},{2,6},{3,7},{4,0},{5,1},{6,2},{7,3},{8,12},{9,13},{10,... | collective-permute-start | bytes 4325384 | tf_op jit(solution)/shard_map/ppermute | solution.py:38
  122.8 31.1 %collective-permute-start.31 = (bf16[8,64,1024]{2,1,0:T(8,128)(2,1)S(1)}, bf16[8,64,1024]{2,1,0:T(8,128)(2,1)S(1)}, u32[]{:S(2)}, u32[]{:S(2)}) collective-permute-start(bf16[8,64,1024]{2,1,0:T(8,128)(2,1)S(1)} %multiply_convert_fusion.1.n0), channel_id=1, source_target_pairs={{0,2},{1,3},{2,0},{3,1},{4,6},{5,7},{6,4},{7,5},{8,10},{9,11},{10,... | collective-permute-start | bytes 3145736 | tf_op jit(solution)/shard_map/ppermute | solution.py:38
  123.5 31.0 %collective-permute-start.37 = (bf16[4,88,1024]{2,1,0:T(8,128)(2,1)S(1)}, bf16[4,88,1024]{2,1,0:T(8,128)(2,1)S(1)}, u32[]{:S(2)}, u32[]{:S(2)}) collective-permute-start(bf16[4,88,1024]{2,1,0:T(8,128)(2,1)S(1)} %pad_maximum_fusion.6), channel_id=1, source_target_pairs={{0,8},{1,9},{2,10},{3,11},{4,12},{5,13},{6,14},{7,15},{8,0},{9,1},... | collective-permute-start | bytes 2162696 | tf_op jit(solution)/shard_map/ppermute | solution.py:38
  127.2 28.1 %collective-permute-start.36 = (bf16[8,64,1024]{2,1,0:T(8,128)(2,1)S(1)}, bf16[8,64,1024]{2,1,0:T(8,128)(2,1)S(1)}, u32[]{:S(2)}, u32[]{:S(2)}) collective-permute-start(bf16[8,64,1024]{2,1,0:T(8,128)(2,1)S(1)} %constant_dynamic-update-slice_fusion.10.b1), channel_id=1, source_target_pairs={{0,1},{1,0},{2,3},{3,2},{4,5},{5,4},{6,7},{7,6},{8,9},{9,8},{10,11... | collective-permute-start | bytes 3145736 | tf_op jit(solution)/shard_map/ppermute | solution.py:38
  184.0 18.9 %collective-permute-start.38 = (bf16[2,8,64,1024]{3,2,1,0:T(8,128)(2,1)}, bf16[2,8,64,1024]{3,2,1,0:T(8,128)(2,1)S(1)}, u32[]{:S(2)}, u32[]{:S(2)}) collective-permute-start(bf16[2,8,64,1024]{3,2,1,0:T(8,128)(2,1)} %get-tuple-element.190), channel_id=1, source_target_pairs={{0,1},{1,0},{2,3},{3,2},{4,5},{5,4},{6,7},{7,6},{8,9},{9,8},{10,11... | collective-permute-start | bytes 6291464 | tf_op jit(solution)/shard_map/ppermute | solution.py:38
  188.4 25.3 %collective-permute-start.40 = (bf16[8,64,1024]{2,1,0:T(8,128)(2,1)S(1)}, bf16[8,64,1024]{2,1,0:T(8,128)(2,1)S(1)}, u32[]{:S(2)}, u32[]{:S(2)}) collective-permute-start(bf16[8,64,1024]{2,1,0:T(8,128)(2,1)S(1)} %fusion.32), channel_id=1, source_target_pairs={{0,2},{1,3},{2,0},{3,1},{4,6},{5,7},{6,4},{7,5},{8,10},{9,11},{10,... | collective-permute-start | bytes 3145736 | tf_op jit(solution)/shard_map/ppermute | solution.py:38
  195.2 18.0 %collective-permute-start.41 = (bf16[4,88,1024]{2,1,0:T(8,128)(2,1)S(1)}, bf16[4,88,1024]{2,1,0:T(8,128)(2,1)S(1)}, u32[]{:S(2)}, u32[]{:S(2)}) collective-permute-start(bf16[4,88,1024]{2,1,0:T(8,128)(2,1)S(1)} %bitcast.192), channel_id=1, source_target_pairs={{0,4},{1,5},{2,6},{3,7},{4,0},{5,1},{6,2},{7,3},{8,12},{9,13},{10,... | collective-permute-start | bytes 2162696 | tf_op jit(solution)/shard_map/ppermute | solution.py:38
  216.4 24.1 %collective-permute-start.43 = (bf16[4,88,1024]{2,1,0:T(8,128)(2,1)}, bf16[4,88,1024]{2,1,0:T(8,128)(2,1)}, u32[]{:S(2)}, u32[]{:S(2)}) collective-permute-start(bf16[4,88,1024]{2,1,0:T(8,128)(2,1)} %bitcast.51), channel_id=1, source_target_pairs={{0,4},{1,5},{2,6},{3,7},{4,0},{5,1},{6,2},{7,3},{8,12},{9,13},{10,... | collective-permute-start | bytes 2162696 | tf_op jit(solution)/shard_map/ppermute | solution.py:38
  217.4 38.0 %collective-permute-start.48 = (bf16[8,64,1024]{2,1,0:T(8,128)(2,1)}, bf16[8,64,1024]{2,1,0:T(8,128)(2,1)S(1)}, u32[]{:S(2)}, u32[]{:S(2)}) collective-permute-start(bf16[8,64,1024]{2,1,0:T(8,128)(2,1)} %fusion.33), channel_id=1, source_target_pairs={{0,2},{1,3},{2,0},{3,1},{4,6},{5,7},{6,4},{7,5},{8,10},{9,11},{10,... | collective-permute-start | bytes 3145736 | tf_op jit(solution)/shard_map/ppermute | solution.py:38
  219.0 36.4 %collective-permute-start.47 = (bf16[2,2,88,1024]{3,2,0,1:T(8,128)(2,1)}, bf16[2,2,88,1024]{3,2,0,1:T(8,128)(2,1)S(1)}, u32[]{:S(2)}, u32[]{:S(2)}) collective-permute-start(bf16[2,2,88,1024]{3,2,0,1:T(8,128)(2,1)} %bitcast.191), channel_id=1, source_target_pairs={{0,8},{1,9},{2,10},{3,11},{4,12},{5,13},{6,14},{7,15},{8,0},{9,1},... | collective-permute-start | bytes 2162696 | tf_op jit(solution)/shard_map/ppermute | solution.py:38
  268.2 15.7 %collective-permute-start.52 = (bf16[8,1,128,256]{3,2,1,0:T(8,128)(2,1)S(1)}, bf16[8,1,128,256]{3,2,1,0:T(8,128)(2,1)S(1)}, u32[]{:S(2)}, u32[]{:S(2)}) collective-permute-start(bf16[8,1,128,256]{3,2,1,0:T(8,128)(2,1)S(1)} %get-tuple-element.229), channel_id=1, source_target_pairs={{0,4},{1,5},{2,6},{3,7},{4,0},{5,1},{6,2},{7,3},{8,12},{9,13},{10,... | collective-permute-start | bytes 1572872 | tf_op jit(solution)/shard_map/ppermute | solution.py:38
  288.8 23.3 %collective-permute-start.57 = (bf16[2,2,88,1024]{3,2,1,0:T(8,128)(2,1)S(1)}, bf16[2,2,88,1024]{3,2,1,0:T(8,128)(2,1)S(1)}, u32[]{:S(2)}, u32[]{:S(2)}) collective-permute-start(bf16[2,2,88,1024]{3,2,1,0:T(8,128)(2,1)S(1)} %slice.186), channel_id=1, source_target_pairs={{0,8},{1,9},{2,10},{3,11},{4,12},{5,13},{6,14},{7,15},{8,0},{9,1},... | collective-permute-start | bytes 2162696 | tf_op jit(solution)/shard_map/ppermute | solution.py:38
  288.9 22.4 %collective-permute-start.58 = (bf16[2,88,1024]{2,1,0:T(8,128)(2,1)S(1)}, bf16[2,88,1024]{2,1,0:T(8,128)(2,1)S(1)}, u32[]{:S(2)}, u32[]{:S(2)}) collective-permute-start(bf16[2,88,1024]{2,1,0:T(8,128)(2,1)S(1)} %slice_bitcast_fusion.8), channel_id=1, source_target_pairs={{0,16},{1,17},{2,18},{3,19},{4,20},{5,21},{6,22},{7,23},{8,24},{9,... | collective-permute-start | bytes 1081352 | tf_op jit(solution)/shard_map/ppermute | solution.py:38
  314.1 16.7 %collective-permute-start.68 = (bf16[2,88,1024]{2,1,0:T(8,128)(2,1)S(1)}, bf16[2,88,1024]{2,1,0:T(8,128)(2,1)S(1)}, u32[]{:S(2)}, u32[]{:S(2)}) collective-permute-start(bf16[2,88,1024]{2,1,0:T(8,128)(2,1)S(1)} %slice_bitcast_fusion.7), channel_id=1, source_target_pairs={{0,16},{1,17},{2,18},{3,19},{4,20},{5,21},{6,22},{7,23},{8,24},{9,... | collective-permute-start | bytes 1081352 | tf_op jit(solution)/shard_map/ppermute | solution.py:38
  315.4 16.0 %collective-permute-start.67 = (bf16[2,3,128,256]{3,2,1,0:T(8,128)(2,1)S(1)}, bf16[2,3,128,256]{3,2,1,0:T(8,128)(2,1)S(1)}, u32[]{:S(2)}, u32[]{:S(2)}) collective-permute-start(bf16[2,3,128,256]{3,2,1,0:T(8,128)(2,1)S(1)} %pad_maximum_fusion.9), channel_id=1, source_target_pairs={{0,8},{1,9},{2,10},{3,11},{4,12},{5,13},{6,14},{7,15},{8,0},{9,1},... | collective-permute-start | bytes 1179656 | tf_op jit(solution)/shard_map/ppermute | solution.py:38
  315.6 15.2 %collective-permute-start.66 = (bf16[88,1024]{1,0:T(8,128)(2,1)S(1)}, bf16[88,1024]{1,0:T(8,128)(2,1)S(1)}, u32[]{:S(2)}, u32[]{:S(2)}) collective-permute-start(bf16[88,1024]{1,0:T(8,128)(2,1)S(1)} %slice_bitcast_fusion.10), channel_id=1, source_target_pairs={{0,4},{1,5},{2,6},{3,7},{4,0},{5,1},{6,2},{7,3},{8,12},{9,13},{10,... | collective-permute-start | bytes 540680 | tf_op jit(solution)/shard_map/ppermute | solution.py:38
  330.8 17.5 %collective-permute-start.63 = (bf16[8,64,1024]{2,1,0:T(8,128)(2,1)S(1)}, bf16[8,64,1024]{2,1,0:T(8,128)(2,1)S(1)}, u32[]{:S(2)}, u32[]{:S(2)}) collective-permute-start(bf16[8,64,1024]{2,1,0:T(8,128)(2,1)S(1)} %get-tuple-element.260), channel_id=1, source_target_pairs={{0,1},{1,0},{2,3},{3,2},{4,5},{5,4},{6,7},{7,6},{8,9},{9,8},{10,11... | collective-permute-start | bytes 3145736 | tf_op jit(solution)/shard_map/ppermute | solution.py:38
  (133 other events, 1209.0 us)

commit v9 on v8

--- a/solution.py
+++ b/solution.py
@@ -406,6 +406,28 @@
     )
 
 
+def outer_pair_kernel(
+    orders, spots, near, far, g0, g1, keep0, send0, keep1, send1, whole, sems
+):
+    rows = near.shape[0] * near.shape[1]
+    width = near.shape[2]
+    tile = 256
+    for c in range(0, width, tile):
+        a = near[:, :, c : c + tile].reshape(rows, tile)
+        b = far[:, :, c : c + tile].reshape(rows, tile)
+        for k, g in enumerate((g0, g1)):
+            first, second = g[0].reshape(rows, -1), g[1].reshape(rows, -1)
+            whole[k, c : c + tile, :] = (mm(a, first, TN) + mm(b, second, TN)).astype(BF16)
+    each_block(
+        spots,
+        [
+            (orders[0], 0, keep0, send0, whole.at[0], sems.at[0]),
+            (orders[1], 0, keep1, send1, whole.at[1], sems.at[1]),
+        ],
+        out=True,
+    )
+
+
 ANY = pl.BlockSpec(memory_space=pltpu.HBM)
 VMEM = pl.BlockSpec(memory_space=pltpu.VMEM)
 
@@ -436,7 +458,7 @@
             out_specs=[spec(s, kind) for s, _, kind in outputs],
             scratch_shapes=scratch,
         ),
-        compiler_params=pltpu.CompilerParams(vmem_limit_bytes=(48 if name == "mixed_back" else 40) * 2**20),
+        compiler_params=pltpu.CompilerParams(vmem_limit_bytes=(46 if name == "mixed_back" else 40) * 2**20),
         cost_estimate=pl.CostEstimate(flops=int(flops * 2.4), bytes_accessed=int(moved * 2.4), transcendentals=0),
         name=name,
     )(spots, *[a for a, _ in inputs])
@@ -804,10 +826,10 @@
 
     def backward_step(step, got):
         if step == 1:
-            got, held["y"], mod_send = tie(got, query_y, query_send[:, 1:])
+            got, mod_send = tie(got, query_send[:, 1:])
             held["more"] = swap(mod_send, y_mask)
         if step == 2:
-            got, held["more"], held["x"] = tie(got, held["more"], output_x)
+            got, held["y"], held["more"], held["x"] = tie(got, query_y, held["more"], output_x)
         return got
 
     scan.along(backward_step)
@@ -839,8 +861,17 @@
         [held_scratch, dma((4,))],
         steps, square_flops // 2,
     )
-    key_keep, key_send = square("key_outer", 0, normed_pair, key_out)
-    value_keep, value_send = square("value_outer", 1, normed_pair, value_out)
+    part_shape = (half, 1, rows, cols)
+    key_keep, key_send, value_keep, value_send = run(
+        functools.partial(outer_pair_kernel, (0, 1)), "key_value_outer", spots,
+        [
+            (normed_pair[0], "whole"), (normed_pair[1], "whole"), (key_out, "whole"),
+            (value_out, "whole"),
+        ],
+        [(part_shape, BF16, "any")] * 4,
+        [pltpu.VMEM((2, width, inner_width), BF16), dma((2, members))],
+        1, 2 * square_flops,
+    )
     key_send, value_send, gl_z, down_far, query_x, output_y = tie(
         key_send, value_send, gl_z, down_far, query_x, output_y
     )

time: 361 us -> 360 us (level)
  the two profiles are of different devices: /device:TPU:0 before, /device:TPU:24 now
where the time goes in v9:
time: 360 us; the launch traced here: 354 us
  waiting for transfers between devices  140 us (39%)
  Pallas kernels  82.4 us (23%)
  starting transfers between devices  71.6 us (20%)
  local copies, waits for them, and re-layouts  24.6 us (7%)
  other arithmetic  23.4 us (6%)
  matrix products  9.69 us (3%)
    ppermute x68, waiting for transfers between devices, exchange(): return lax.ppermute(x, AXES, [(i, i ^ mask) for i in range(count)])  122 us
    pallas_call x10, Pallas kernels, run(): pl.pallas_call(kernel, out_shape=[jax.ShapeDtypeStruct(s, d) for s, d, _...  82.4 us
    ppermute x68, starting transfers between devices, exchange(): return lax.ppermute(x, AXES, [(i, i ^ mask) for i in range(count)])  59.6 us
    ppermute x4, waiting for transfers between devices, shift_z(): return lax.ppermute(x, AXES, pairs)  17.5 us
    unnamed x174, local copies, waits for them, and re-layouts  13.4 us
    ppermute x4, starting transfers between devices, shift_z(): return lax.ppermute(x, AXES, pairs)  12 us
    dot_general x3, matrix products, outer(): jnp.einsum('pblf,pbld->fd', a, b, preferred_element_type=F32).astype(BF16)  9.69 us
  transfers between devices with their start and end apart: 72, of which 38 were waited for; matrix products, arithmetic and copies ran while one was open for 12% of the time, Pallas kernels for 15%

profile of v9, /device:TPU:24, one launch (start us, length us, event | category | flops | bytes accessed | tf_op | source)
XLA Modules:
  0.0 353.9 jit_solution(12441961520914356670)
XLA Ops:
  22.5 3.5 collective-permute-done.8
  31.8 6.2 %collective-permute-done.12 = bf16[1,3,128,256]{3,2,1,0:T(8,128)(2,1)S(1)} collective-permute-done((bf16[1,3,128,256]{3,2,1,0:T(8,128)(2,1)S(1)}, bf16[1,3,128,256]{3,2,1,0:T(8,128)(2,1)S(1)}, u32[]{:S(2)}, u32[]{:S(2)}) %collective-permute-start.12) | collective-permute-done | bytes 196640 | tf_op jit(solution)/shard_map/ppermute | solution.py:38
  40.0 6.0 %key_value.1 = (bf16[2,8,64,512]{3,2,1,0:T(8,128)(2,1)S(1)}, bf16[2,8,64,512]{3,2,1,0:T(8,128)(2,1)S(1)}, bf16[2,8,64,512]{3,2,1,0:T(8,128)(2,1)S(1)}, bf16[8,4,128,128]{3,2,1,0:T(8,128)(2,1)S(1)}) custom-call(s32[4,16,2]{2,1,0:T(8,128)S(1)} %add_add_fusion.spots, bf16[8,64,1024]{2,1,0:T(8,128)(2,1)S(1)} %copy-done.6, ...), custom_call_target="tpu_custom_call" | custom-call | flops 5153960960 | bytes 22649240 | tf_op jit(solution)/shard_map/key_value/pallas_call | solution.py:451
  55.6 4.1 %collective-permute-done.16 = bf16[2,4,128,128]{3,2,1,0:T(8,128)(2,1)S(1)} collective-permute-done((bf16[2,4,128,128]{3,2,1,0:T(8,128)(2,1)S(1)}, bf16[2,4,128,128]{3,2,1,0:T(8,128)(2,1)S(1)}, u32[]{:S(2)}, u32[]{:S(2)}) %collective-permute-start.16) | collective-permute-done | bytes 262176 | tf_op jit(solution)/shard_map/ppermute | solution.py:38
  62.1 3.9 %collective-permute-done.20 = bf16[1,2,88,1024]{3,2,1,0:T(8,128)(2,1)S(1)} collective-permute-done((bf16[1,2,88,1024]{3,2,1,0:T(8,128)(2,1)S(1)}, bf16[1,2,88,1024]{3,2,1,0:T(8,128)(2,1)S(1)}, u32[]{:S(2)}, u32[]{:S(2)}) %collective-permute-start.20) | collective-permute-done | bytes 360480 | tf_op jit(solution)/shard_map/ppermute | solution.py:38
  77.2 9.8 %collective-permute-done.21 = bf16[2,4,128,128]{3,2,1,0:T(8,128)(2,1)S(1)} collective-permute-done((bf16[2,4,128,128]{3,2,1,0:T(8,128)(2,1)S(1)}, bf16[2,4,128,128]{3,2,1,0:T(8,128)(2,1)S(1)}, u32[]{:S(2)}, u32[]{:S(2)}) %collective-permute-start.21) | collective-permute-done | bytes 262176 | tf_op jit(solution)/shard_map/ppermute | solution.py:50
  88.0 7.7 %collective-permute-done.25 = bf16[4,64,1024]{2,1,0:T(8,128)(2,1)S(1)} collective-permute-done((bf16[4,64,1024]{2,1,0:T(8,128)(2,1)S(1)}, bf16[4,64,1024]{2,1,0:T(8,128)(2,1)S(1)}, u32[]{:S(2)}, u32[]{:S(2)}) %collective-permute-start.25) | collective-permute-done | bytes 524320 | tf_op jit(solution)/shard_map/ppermute | solution.py:38
  100.6 7.1 %query.1 = (bf16[2,8,64,512]{3,2,1,0:T(8,128)(2,1)S(1)}, bf16[2,8,64,512]{3,2,1,0:T(8,128)(2,1)S(1)}, bf16[2,8,64,512]{3,2,1,0:T(8,128)(2,1)S(1)}, bf16[2,8,64,512]{3,2,1,0:T(8,128)(2,1)S(1)}) custom-call(s32[4,16,2]{2,1,0:T(8,128)S(1)} %add_add_fusion.spots, bf16[8,64,1024]{2,1,0:T(8,128)(2,1)S(1)} %copy-done.6, ...), custom_call_target="tpu_custom_call" | custom-call | flops 5153960960 | bytes 28940696 | tf_op jit(solution)/shard_map/query/pallas_call | solution.py:451
  110.8 4.9 %mixed.1 = (bf16[2,8,64,512]{3,2,1,0:T(8,128)(2,1)S(1)}, bf16[2,8,64,512]{3,2,1,0:T(8,128)(2,1)S(1)}, f32[8,64,1024]{2,1,0:T(8,128)S(1)}, bf16[8,64,1024]{2,1,0:T(8,128)(2,1)S(1)}) custom-call(s32[4,16,2]{2,1,0:T(8,128)S(1)} %add_add_fusion.spots, bf16[2,8,64,512]{3,2,1,0:T(8,128)(2,1)S(1)} %get-tuple-element.174.queries, ...), custom_call_target="tpu_custom_call" | custom-call | flops 2576980480 | bytes 26424116 | tf_op jit(solution)/shard_map/mixed/pallas_call | solution.py:451
  122.2 29.0 %collective-permute-done.32 = bf16[4,2,88,1024]{3,2,0,1:T(8,128)(2,1)S(1)} collective-permute-done((bf16[4,2,88,1024]{3,2,0,1:T(8,128)(2,1)S(1)}, bf16[4,2,88,1024]{3,2,0,1:T(8,128)(2,1)S(1)}, u32[]{:S(2)}, u32[]{:S(2)}) %collective-permute-start.32) | collective-permute-done | bytes 1441824 | tf_op jit(solution)/shard_map/ppermute | solution.py:38
  155.7 25.1 %hidden.1 = (bf16[4,8,64,704]{3,2,1,0:T(8,128)(2,1)}, bf16[4,8,64,704]{3,2,1,0:T(8,128)(2,1)}, bf16[4,8,64,704]{3,2,1,0:T(8,128)(2,1)}, bf16[2,8,64,1024]{3,2,1,...) custom-call(s32[4,16,2]{2,1,0:T(8,128)S(1)} %add_add_fusion.spots, ...), custom_call_target="tpu_custom_call" | custom-call | flops 42520174592 | bytes 72666320 | tf_op jit(solution)/shard_map/hidden/pallas_call | solution.py:451
  181.7 3.5 collective-permute-done.39
  201.3 9.2 %collective-permute-done.41 = bf16[4,88,1024]{2,1,0:T(8,128)(2,1)S(1)} collective-permute-done((bf16[4,88,1024]{2,1,0:T(8,128)(2,1)S(1)}, bf16[4,88,1024]{2,1,0:T(8,128)(2,1)S(1)}, u32[]{:S(2)}, u32[]{:S(2)}) %collective-permute-start.41) | collective-permute-done | bytes 720928 | tf_op jit(solution)/shard_map/ppermute | solution.py:38
  222.5 13.5 %mixed_back.1 = (bf16[2,8,64,512]{3,2,1,0:T(8,128)(2,1)S(1)}, bf16[2,8,64,512]{3,2,1,0:T(8,128)(2,1)S(1)}, bf16[2,8,64,512]{3,2,1,0:T(8,128)(2,1)S(1)}, bf16[2,8...) custom-call(s32[4,16,2]{2,1,0:T(8,128)S(1)} %add_add_fusion.spots, bf16[8,64,1024]{2,1,0:T(8,128)(2,1)} %copy-done.9, ...), custom_call_target="tpu_custom_call" | custom-call | flops 5153960960 | bytes 45298484 | tf_op jit(solution)/shard_map/mixed_back/pallas_call | solution.py:451
  241.0 4.0 %output_outer.1 = (bf16[8,1,128,256]{3,2,1,0:T(8,128)(2,1)S(1)}, bf16[8,1,128,256]{3,2,1,0:T(8,128)(2,1)S(1)}) custom-call(s32[4,16,2]{2,1,0:T(8,128)S(1)} %add_add_fusion.spots, bf16[8,64,1024]{2,1,0:T(8,128)(2,1)S(1)} %copy-done.10, bf16[8,64,1024]{2,1,0:T(8,128)(2,1)} %collective-permute-done.42.far, bf16[2,8,64,512]{3,2,1,0:T(8,128)(2,1)S(1)} %copy-done.38), custom_call_target="tpu_custom_call" | custom-call | flops 2576980480 | bytes 10066329 | tf_op jit(solution)/shard_map/output_outer/pallas_call | solution.py:451
  245.1 4.3 %query_outer.1 = (bf16[8,2,128,256]{3,2,1,0:T(8,128)(2,1)S(1)}, bf16[8,2,128,256]{3,2,1,0:T(8,128)(2,1)S(1)}) custom-call(s32[4,16,2]{2,1,0:T(8,128)S(1)} %add_add_fusion.spots, bf16[8,64,1024]{2,1,0:T(8,128)(2,1)S(1)} %copy-done.7, bf16[8,64,1024]{2,1,0:T(8,128)(2,1)S(1)} %copy-done.22, bf16[2,8,64,512]{3,2,1,0:T(8,128)(2,1)S(1)} %get-tuple-element.212.refs_0_.query_grad, ...), custom_call_target="tpu_custom_call" | custom-call | flops 5153960960 | bytes 15099494 | tf_op jit(solution)/shard_map/query_outer/pallas_call | solution.py:451
  260.8 6.4 %collective-permute-start.50 = (bf16[2,4,128,128]{3,2,1,0:T(8,128)(2,1)S(1)}, bf16[2,4,128,128]{3,2,1,0:T(8,128)(2,1)S(1)}, u32[]{:S(2)}, u32[]{:S(2)}) collective-permute-start(bf16[2,4,128,128]{3,2,1,0:T(8,128)(2,1)S(1)} %fusion.43), channel_id=1, source_target_pairs={{16,0},{17,1},{18,2},{19,3},{20,4},{21,5},{22,6},{23,7},{24,8},{25... | collective-permute-start | bytes 786440 | tf_op jit(solution)/shard_map/ppermute | solution.py:50
  267.4 3.6 %collective-permute-done.50 = bf16[2,4,128,128]{3,2,1,0:T(8,128)(2,1)S(1)} collective-permute-done((bf16[2,4,128,128]{3,2,1,0:T(8,128)(2,1)S(1)}, bf16[2,4,128,128]{3,2,1,0:T(8,128)(2,1)S(1)}, u32[]{:S(2)}, u32[]{:S(2)}) %collective-permute-start.50) | collective-permute-done | bytes 262176 | tf_op jit(solution)/shard_map/ppermute | solution.py:50
  271.0 8.2 %collective-permute-done.52 = bf16[8,1,128,256]{3,2,1,0:T(8,128)(2,1)S(1)} collective-permute-done((bf16[8,1,128,256]{3,2,1,0:T(8,128)(2,1)S(1)}, bf16[8,1,128,256]{3,2,1,0:T(8,128)(2,1)S(1)}, u32[]{:S(2)}, u32[]{:S(2)}) %collective-permute-start.52) | collective-permute-done | bytes 524320 | tf_op jit(solution)/shard_map/ppermute | solution.py:38
  289.2 3.9 %collective-permute-done.56.g3 = bf16[2,4,128,128]{3,2,1,0:T(8,128)(2,1)S(1)} collective-permute-done((bf16[2,4,128,128]{3,2,1,0:T(8,128)(2,1)S(1)}, bf16[2,4,128,128]{3,2,1,0:T(8,128)(2,1)S(1)}, u32[]{:S(2)}, u32[]{:S(2)}) %collective-permute-start.56) | collective-permute-done | bytes 262176 | tf_op jit(solution)/shard_map/ppermute | solution.py:38
  294.9 4.7 %key_back.1 = (bf16[2,8,64,512]{3,2,1,0:T(8,128)(2,1)S(1)}, bf16[2,8,64,512]{3,2,1,0:T(8,128)(2,1)S(1)}) custom-call(s32[4,16,2]{2,1,0:T(8,128)S(1)} %add_add_fusion.spots, bf16[2,8,64,512]{3,2,1,0:T(8,128)(2,1)S(1)} %get-tuple-element.220.key_grad, bf16[2,8,64,512]{3,2,1,0:T(8,128)(2,1)S(1)} %get-tuple-element.221.value_grad, ...), custom_call_target="tpu_custom_call" | custom-call | flops 1288490240 | bytes 22649240 | tf_op jit(solution)/shard_map/key_back/pallas_call | solution.py:451
  299.6 4.3 %key_value_outer.1 = (bf16[8,1,128,256]{3,2,1,0:T(8,128)(2,1)S(1)}, bf16[8,1,128,256]{3,2,1,0:T(8,128)(2,1)S(1)}, bf16[8,1,128,256]{3,2,1,0:T(8,128)(2,1)S(1)}, bf16[8,1,128,256]{3,2,1,0:T(8,128)(2,1)S(1)}) custom-call(s32[4,16,2]{2,1,0:T(8,128)S(1)} %add_add_fusion.spots, bf16[8,64,1024]{2,1,0:T(8,128)(2,1)S(1)} %copy-done.7, ...), custom_call_target="tpu_custom_call" | custom-call | flops 5153960960 | bytes 15099494 | tf_op jit(solution)/shard_map/key_value_outer/pallas_call | solution.py:451
  315.3 8.5 %rows.1 = (f32[8,64,1024]{2,1,0:T(8,128)S(1)}, bf16[8,64,1024]{2,1,0:T(8,128)(2,1)S(1)}) custom-call(s32[4,16,2]{2,1,0:T(8,128)S(1)} %add_add_fusion.spots, bf16[2,8,64,512]{3,2,1,0:T(8,128)(2,1)S(1)} %get-tuple-element.212.refs_0_.query_grad, bf16[2,8,64,512]{3,2,1,0:T(8,128)(2,1)S(1)} %get-tuple-element.213.refs_1_.modulate_grad, ...), custom_call_target="tpu_custom_call" | custom-call | flops 10307921920 | bytes 27682406 | tf_op jit(solution)/shard_map/rows/pallas_call | solution.py:451
  335.5 10.6 %collective-permute-done.69 = bf16[1,3,128,256]{3,2,1,0:T(8,128)(2,1)S(1)} collective-permute-done((bf16[1,3,128,256]{3,2,1,0:T(8,128)(2,1)S(1)}, bf16[1,3,128,256]{3,2,1,0:T(8,128)(2,1)S(1)}, u32[]{:S(2)}, u32[]{:S(2)}) %collective-permute-start.69) | collective-permute-done | bytes 196640 | tf_op jit(solution)/shard_map/ppermute | solution.py:38
  (447 shorter events, 159.2 us)
Async XLA Ops:
  0.7 21.0 %collective-permute-start = (f32[2]{0:T(128)}, f32[2]{0:T(128)}, u32[]{:S(2)}, u32[]{:S(2)}) collective-permute-start(f32[2]{0:T(128)} %param.25), channel_id=1, source_target_pairs={{0,2},{1,3},{2,0},{3,1},{4,6},{5,7},{6,4},{7,5},{8,10},{9,11},{10,... | collective-permute-start | bytes 32 | tf_op jit(solution)/shard_map/ppermute | solution.py:38
  14.7 24.9 %collective-permute-start.1 = (bf16[8,64,1024]{2,1,0:T(8,128)(2,1)S(1)}, bf16[8,64,1024]{2,1,0:T(8,128)(2,1)S(1)}, u32[]{:S(2)}, u32[]{:S(2)}) collective-permute-start(bf16[8,64,1024]{2,1,0:T(8,128)(2,1)S(1)} %fusion.10.near), channel_id=1, source_target_pairs={{0,1},{1,0},{2,3},{3,2},{4,5},{5,4},{6,7},{7,6},{8,9},{9,8},{10,11... | collective-permute-start | bytes 3145736 | tf_op jit(solution)/shard_map/ppermute | solution.py:38
  49.8 16.2 %collective-permute-start.20 = (bf16[1,2,88,1024]{3,2,1,0:T(8,128)(2,1)S(1)}, bf16[1,2,88,1024]{3,2,1,0:T(8,128)(2,1)S(1)}, u32[]{:S(2)}, u32[]{:S(2)}) collective-permute-start(bf16[1,2,88,1024]{3,2,1,0:T(8,128)(2,1)S(1)} %maximum_bitcast_fusion), channel_id=1, source_target_pairs={{0,16},{1,17},{2,18},{3,19},{4,20},{5,21},{6,22},{7,23},{8,24},{9,... | collective-permute-start | bytes 1081352 | tf_op jit(solution)/shard_map/ppermute | solution.py:38
  68.9 26.8 %collective-permute-start.22 = (bf16[8,2,128,256]{3,2,1,0:T(8,128)(2,1)S(1)}, bf16[8,2,128,256]{3,2,1,0:T(8,128)(2,1)S(1)}, u32[]{:S(2)}, u32[]{:S(2)}) collective-permute-start(bf16[8,2,128,256]{3,2,1,0:T(8,128)(2,1)S(1)} %constant_dynamic-update-slice_fusion.3.w0), channel_id=1, source_target_pairs={{0,4},{1,5},{2,6},{3,7},{4,0},{5,1},{6,2},{7,3},{8,12},{9,13},{10,... | collective-permute-start | bytes 3145736 | tf_op jit(solution)/shard_map/ppermute | solution.py:38
  71.9 23.9 %collective-permute-start.24 = (bf16[2,2,88,1024]{3,2,1,0:T(8,128)(2,1)S(1)}, bf16[2,2,88,1024]{3,2,1,0:T(8,128)(2,1)S(1)}, u32[]{:S(2)}, u32[]{:S(2)}) collective-permute-start(bf16[2,2,88,1024]{3,2,1,0:T(8,128)(2,1)S(1)} %pad_maximum_fusion.5), channel_id=1, source_target_pairs={{0,8},{1,9},{2,10},{3,11},{4,12},{5,13},{6,14},{7,15},{8,0},{9,1},... | collective-permute-start | bytes 2162696 | tf_op jit(solution)/shard_map/ppermute | solution.py:38
  75.1 20.7 %collective-permute-start.25 = (bf16[4,64,1024]{2,1,0:T(8,128)(2,1)S(1)}, bf16[4,64,1024]{2,1,0:T(8,128)(2,1)S(1)}, u32[]{:S(2)}, u32[]{:S(2)}) collective-permute-start(bf16[4,64,1024]{2,1,0:T(8,128)(2,1)S(1)} %copy-done.62), channel_id=1, source_target_pairs={{0,2},{1,3},{2,0},{3,1},{4,6},{5,7},{6,4},{7,5},{8,10},{9,11},{10,... | collective-permute-start | bytes 1572872 | tf_op jit(solution)/shard_map/ppermute | solution.py:38
  116.8 35.7 %collective-permute-start.35 = (bf16[8,64,1024]{2,1,0:T(8,128)(2,1)S(1)}, bf16[8,64,1024]{2,1,0:T(8,128)(2,1)S(1)}, u32[]{:S(2)}, u32[]{:S(2)}) collective-permute-start(bf16[8,64,1024]{2,1,0:T(8,128)(2,1)S(1)} %copy-done), channel_id=1, source_target_pairs={{0,1},{1,0},{2,3},{3,2},{4,5},{5,4},{6,7},{7,6},{8,9},{9,8},{10,11... | collective-permute-start | bytes 3145736 | tf_op jit(solution)/shard_map/ppermute | solution.py:38
  117.8 33.4 %collective-permute-start.32 = (bf16[4,2,88,1024]{3,2,0,1:T(8,128)(2,1)S(1)}, bf16[4,2,88,1024]{3,2,0,1:T(8,128)(2,1)S(1)}, u32[]{:S(2)}, u32[]{:S(2)}) collective-permute-start(bf16[4,2,88,1024]{3,2,0,1:T(8,128)(2,1)S(1)} %copy.67), channel_id=1, source_target_pairs={{0,4},{1,5},{2,6},{3,7},{4,0},{5,1},{6,2},{7,3},{8,12},{9,13},{10,... | collective-permute-start | bytes 4325384 | tf_op jit(solution)/shard_map/ppermute | solution.py:38
  120.2 31.1 %collective-permute-start.31 = (bf16[8,64,1024]{2,1,0:T(8,128)(2,1)S(1)}, bf16[8,64,1024]{2,1,0:T(8,128)(2,1)S(1)}, u32[]{:S(2)}, u32[]{:S(2)}) collective-permute-start(bf16[8,64,1024]{2,1,0:T(8,128)(2,1)S(1)} %multiply_convert_fusion.1.n0), channel_id=1, source_target_pairs={{0,2},{1,3},{2,0},{3,1},{4,6},{5,7},{6,4},{7,5},{8,10},{9,11},{10,... | collective-permute-start | bytes 3145736 | tf_op jit(solution)/shard_map/ppermute | solution.py:38
  120.8 31.0 %collective-permute-start.37 = (bf16[4,88,1024]{2,1,0:T(8,128)(2,1)S(1)}, bf16[4,88,1024]{2,1,0:T(8,128)(2,1)S(1)}, u32[]{:S(2)}, u32[]{:S(2)}) collective-permute-start(bf16[4,88,1024]{2,1,0:T(8,128)(2,1)S(1)} %pad_maximum_fusion.6), channel_id=1, source_target_pairs={{0,8},{1,9},{2,10},{3,11},{4,12},{5,13},{6,14},{7,15},{8,0},{9,1},... | collective-permute-start | bytes 2162696 | tf_op jit(solution)/shard_map/ppermute | solution.py:38
  122.0 30.5 %collective-permute-start.36 = (bf16[8,64,1024]{2,1,0:T(8,128)(2,1)S(1)}, bf16[8,64,1024]{2,1,0:T(8,128)(2,1)S(1)}, u32[]{:S(2)}, u32[]{:S(2)}) collective-permute-start(bf16[8,64,1024]{2,1,0:T(8,128)(2,1)S(1)} %constant_dynamic-update-slice_fusion.10.b1), channel_id=1, source_target_pairs={{0,1},{1,0},{2,3},{3,2},{4,5},{5,4},{6,7},{7,6},{8,9},{9,8},{10,11... | collective-permute-start | bytes 3145736 | tf_op jit(solution)/shard_map/ppermute | solution.py:38
  181.3 18.4 %collective-permute-start.38 = (bf16[2,8,64,1024]{3,2,1,0:T(8,128)(2,1)}, bf16[2,8,64,1024]{3,2,1,0:T(8,128)(2,1)S(1)}, u32[]{:S(2)}, u32[]{:S(2)}) collective-permute-start(bf16[2,8,64,1024]{3,2,1,0:T(8,128)(2,1)} %get-tuple-element.190), channel_id=1, source_target_pairs={{0,1},{1,0},{2,3},{3,2},{4,5},{5,4},{6,7},{7,6},{8,9},{9,8},{10,11... | collective-permute-start | bytes 6291464 | tf_op jit(solution)/shard_map/ppermute | solution.py:38
  185.7 25.3 %collective-permute-start.40 = (bf16[8,64,1024]{2,1,0:T(8,128)(2,1)S(1)}, bf16[8,64,1024]{2,1,0:T(8,128)(2,1)S(1)}, u32[]{:S(2)}, u32[]{:S(2)}) collective-permute-start(bf16[8,64,1024]{2,1,0:T(8,128)(2,1)S(1)} %fusion.32), channel_id=1, source_target_pairs={{0,2},{1,3},{2,0},{3,1},{4,6},{5,7},{6,4},{7,5},{8,10},{9,11},{10,... | collective-permute-start | bytes 3145736 | tf_op jit(solution)/shard_map/ppermute | solution.py:38
  192.4 18.1 %collective-permute-start.41 = (bf16[4,88,1024]{2,1,0:T(8,128)(2,1)S(1)}, bf16[4,88,1024]{2,1,0:T(8,128)(2,1)S(1)}, u32[]{:S(2)}, u32[]{:S(2)}) collective-permute-start(bf16[4,88,1024]{2,1,0:T(8,128)(2,1)S(1)} %bitcast.192), channel_id=1, source_target_pairs={{0,4},{1,5},{2,6},{3,7},{4,0},{5,1},{6,2},{7,3},{8,12},{9,13},{10,... | collective-permute-start | bytes 2162696 | tf_op jit(solution)/shard_map/ppermute | solution.py:38
  213.7 22.3 %collective-permute-start.43 = (bf16[4,88,1024]{2,1,0:T(8,128)(2,1)}, bf16[4,88,1024]{2,1,0:T(8,128)(2,1)}, u32[]{:S(2)}, u32[]{:S(2)}) collective-permute-start(bf16[4,88,1024]{2,1,0:T(8,128)(2,1)} %bitcast.51), channel_id=1, source_target_pairs={{0,4},{1,5},{2,6},{3,7},{4,0},{5,1},{6,2},{7,3},{8,12},{9,13},{10,... | collective-permute-start | bytes 2162696 | tf_op jit(solution)/shard_map/ppermute | solution.py:38
  214.1 36.7 %collective-permute-start.48 = (bf16[8,64,1024]{2,1,0:T(8,128)(2,1)}, bf16[8,64,1024]{2,1,0:T(8,128)(2,1)S(1)}, u32[]{:S(2)}, u32[]{:S(2)}) collective-permute-start(bf16[8,64,1024]{2,1,0:T(8,128)(2,1)} %fusion.33), channel_id=1, source_target_pairs={{0,2},{1,3},{2,0},{3,1},{4,6},{5,7},{6,4},{7,5},{8,10},{9,11},{10,... | collective-permute-start | bytes 3145736 | tf_op jit(solution)/shard_map/ppermute | solution.py:38
  215.6 35.2 %collective-permute-start.47 = (bf16[2,2,88,1024]{3,2,0,1:T(8,128)(2,1)}, bf16[2,2,88,1024]{3,2,0,1:T(8,128)(2,1)S(1)}, u32[]{:S(2)}, u32[]{:S(2)}) collective-permute-start(bf16[2,2,88,1024]{3,2,0,1:T(8,128)(2,1)} %bitcast.191), channel_id=1, source_target_pairs={{0,8},{1,9},{2,10},{3,11},{4,12},{5,13},{6,14},{7,15},{8,0},{9,1},... | collective-permute-start | bytes 2162696 | tf_op jit(solution)/shard_map/ppermute | solution.py:38
  260.0 19.3 %collective-permute-start.52 = (bf16[8,1,128,256]{3,2,1,0:T(8,128)(2,1)S(1)}, bf16[8,1,128,256]{3,2,1,0:T(8,128)(2,1)S(1)}, u32[]{:S(2)}, u32[]{:S(2)}) collective-permute-start(bf16[8,1,128,256]{3,2,1,0:T(8,128)(2,1)S(1)} %get-tuple-element.229), channel_id=1, source_target_pairs={{0,4},{1,5},{2,6},{3,7},{4,0},{5,1},{6,2},{7,3},{8,12},{9,13},{10,... | collective-permute-start | bytes 1572872 | tf_op jit(solution)/shard_map/ppermute | solution.py:38
  284.0 23.5 %collective-permute-start.57 = (bf16[2,2,88,1024]{3,2,1,0:T(8,128)(2,1)S(1)}, bf16[2,2,88,1024]{3,2,1,0:T(8,128)(2,1)S(1)}, u32[]{:S(2)}, u32[]{:S(2)}) collective-permute-start(bf16[2,2,88,1024]{3,2,1,0:T(8,128)(2,1)S(1)} %slice.186), channel_id=1, source_target_pairs={{0,8},{1,9},{2,10},{3,11},{4,12},{5,13},{6,14},{7,15},{8,0},{9,1},... | collective-permute-start | bytes 2162696 | tf_op jit(solution)/shard_map/ppermute | solution.py:38
  286.2 20.6 %collective-permute-start.58 = (bf16[2,88,1024]{2,1,0:T(8,128)(2,1)S(1)}, bf16[2,88,1024]{2,1,0:T(8,128)(2,1)S(1)}, u32[]{:S(2)}, u32[]{:S(2)}) collective-permute-start(bf16[2,88,1024]{2,1,0:T(8,128)(2,1)S(1)} %slice_bitcast_fusion.8), channel_id=1, source_target_pairs={{0,16},{1,17},{2,18},{3,19},{4,20},{5,21},{6,22},{7,23},{8,24},{9,... | collective-permute-start | bytes 1081352 | tf_op jit(solution)/shard_map/ppermute | solution.py:38
  307.5 16.2 %collective-permute-start.61 = (bf16[8,1,128,256]{3,2,1,0:T(8,128)(2,1)S(1)}, bf16[8,1,128,256]{3,2,1,0:T(8,128)(2,1)S(1)}, u32[]{:S(2)}, u32[]{:S(2)}) collective-permute-start(bf16[8,1,128,256]{3,2,1,0:T(8,128)(2,1)S(1)} %get-tuple-element.254), channel_id=1, source_target_pairs={{0,4},{1,5},{2,6},{3,7},{4,0},{5,1},{6,2},{7,3},{8,12},{9,13},{10,... | collective-permute-start | bytes 1572872 | tf_op jit(solution)/shard_map/ppermute | solution.py:38
  308.4 15.4 %collective-permute-start.62 = (bf16[8,1,128,256]{3,2,1,0:T(8,128)(2,1)S(1)}, bf16[8,1,128,256]{3,2,1,0:T(8,128)(2,1)S(1)}, u32[]{:S(2)}, u32[]{:S(2)}) collective-permute-start(bf16[8,1,128,256]{3,2,1,0:T(8,128)(2,1)S(1)} %get-tuple-element.255), channel_id=1, source_target_pairs={{0,2},{1,3},{2,0},{3,1},{4,6},{5,7},{6,4},{7,5},{8,10},{9,11},{10,... | collective-permute-start | bytes 1572872 | tf_op jit(solution)/shard_map/ppermute | solution.py:38
  310.2 17.3 %collective-permute-start.68 = (bf16[2,88,1024]{2,1,0:T(8,128)(2,1)S(1)}, bf16[2,88,1024]{2,1,0:T(8,128)(2,1)S(1)}, u32[]{:S(2)}, u32[]{:S(2)}) collective-permute-start(bf16[2,88,1024]{2,1,0:T(8,128)(2,1)S(1)} %slice_bitcast_fusion.7), channel_id=1, source_target_pairs={{0,16},{1,17},{2,18},{3,19},{4,20},{5,21},{6,22},{7,23},{8,24},{9,... | collective-permute-start | bytes 1081352 | tf_op jit(solution)/shard_map/ppermute | solution.py:38
  327.5 19.5 %collective-permute-start.63 = (bf16[8,64,1024]{2,1,0:T(8,128)(2,1)S(1)}, bf16[8,64,1024]{2,1,0:T(8,128)(2,1)S(1)}, u32[]{:S(2)}, u32[]{:S(2)}) collective-permute-start(bf16[8,64,1024]{2,1,0:T(8,128)(2,1)S(1)} %get-tuple-element.260), channel_id=1, source_target_pairs={{0,1},{1,0},{2,3},{3,2},{4,5},{5,4},{6,7},{7,6},{8,9},{9,8},{10,11... | collective-permute-start | bytes 3145736 | tf_op jit(solution)/shard_map/ppermute | solution.py:38
  (131 other events, 1200.1 us)
